TPU v7x, 512 devices: a whole 4x8x8 slice. The times are simulated.
512 devices in a mesh: seq: 64 (over y, z), head: 8 (over x, core).
Axes of the slice: x: 4, y: 8, z: 8, core: 2. Of those that a mesh axis runs over, the one named last changes fastest.
Arguments:
- tokens: bfloat16 [32768, 3072], P(('seq', 'head')), may hold values from -6 to 6
- qkv_weight: bfloat16 [3072, 3, 4096], P('seq', None, 'head'), may hold values from -0.109375 to 0.109375
- log_decay: float32 [32, 32768], P('head', 'seq'), may hold values from -1 to 0
- norm_gain: float32 [4096], P('head'), may hold values from 0.1 to 1.9
Outputs:
- attended: bfloat16 [32768, 4096], P(('seq', 'head'))
All inputs are finite; a program needn't handle non-finite values.
Results may differ from a plain program's by a relative error of at most 0.0061.
Values may be sent and summed in bfloat16 or wider, within the bound.
No kernel may reach another device: no remote copies, remote signals or barrier semaphores. Data moves between devices by JAX's collectives and lax.ppermute only.
A program may use at most 64 MiB of HBM per device.

v0:
```python
import jax
import jax.numpy as jnp
from jax import lax
from jax.sharding import PartitionSpec as P

BLK = 128


epsilon = 1e-05


def carried_in(value, axis, join, neutral):
    count, mine = (lax.axis_size(axis), lax.axis_index(axis))
    pieces = jax.tree.map(lambda part: lax.all_gather(part, axis), value)
    running = jax.tree.map(
        lambda part, zero: jnp.full_like(part, 0) + jnp.asarray(zero, part.dtype), value, neutral
    )

    def turn(position, running):
        longer = join(running, jax.tree.map(lambda part: part[position], pieces))
        return jax.tree.map(lambda new, old: jnp.where(position < mine, new, old), longer, running)

    return lax.fori_loop(0, count - 1, turn, running)


def combine(earlier, newer):
    return (earlier[0] + newer[0], jnp.exp(newer[0])[:, None, None] * earlier[1] + newer[1])


def on_device(tokens, qkv_weight, log_decay, norm_gain):
    high = lax.Precision.HIGHEST
    gathered = lax.all_gather(tokens, "head", axis=0, tiled=True)
    tok_rows = gathered.shape[0]
    number_heads = log_decay.shape[0]
    width = qkv_weight.shape[2] // number_heads
    full_weight = lax.all_gather(qkv_weight, "seq", axis=0, tiled=True)
    projected = jnp.einsum("td,dcf->tcf", gathered, full_weight, preferred_element_type=jnp.float32)
    projected = projected.astype(jnp.bfloat16)
    block_count = tok_rows // BLK
    shaped = projected.reshape(block_count, BLK, 3, number_heads, width)
    queries = shaped[:, :, 0]
    key_rows = shaped[:, :, 1]
    values = shaped[:, :, 2]
    cumulative = jnp.cumsum(log_decay.reshape(number_heads, block_count, BLK), axis=2)
    last_decay = cumulative[:, :, -1]
    causal_mask = jnp.arange(BLK)[:, None] >= jnp.arange(BLK)[None, :]
    gaps = cumulative[:, :, :, None] - cumulative[:, :, None, :]
    weights = jnp.exp(jnp.where(causal_mask[None, None], gaps, -1e30))
    scores = (
        jnp.einsum("nihe,njhe->hnij", queries, key_rows, preferred_element_type=jnp.float32)
        * weights
    )
    local_part = jnp.einsum("hnij,njhe->nihe", scores, values.astype(jnp.float32), precision=high)
    key_scale = jnp.exp(last_decay[:, :, None] - cumulative).transpose(1, 2, 0)
    scaled_k = key_rows * key_scale[..., None]
    states = jnp.einsum("njhe,njhf->nhef", scaled_k, values.astype(jnp.float32), precision=high)

    def chain(running, items):
        return (combine(running, items), running)

    start = (
        jnp.zeros((number_heads,), jnp.float32),
        jnp.zeros((number_heads, width, width), jnp.float32),
    )
    totals, prefixes = lax.scan(chain, start, (last_decay.T, states))
    identity = (
        jnp.zeros((number_heads,), jnp.float32),
        jnp.zeros((number_heads, width, width), jnp.float32),
    )
    incoming = carried_in(totals, "seq", combine, identity)
    decayed_state, local_prefix = prefixes
    prefix_states = jnp.exp(decayed_state)[:, :, None, None] * incoming[1][None] + local_prefix
    query_scale = jnp.exp(cumulative).transpose(1, 2, 0)
    scaled_q = queries * query_scale[..., None]
    carried_part = jnp.einsum("nihe,nhef->nihf", scaled_q, prefix_states, precision=high)
    output = local_part + carried_part
    meansq = jnp.mean(output * output, axis=3, keepdims=True)
    gained = (
        output / jnp.sqrt(meansq + epsilon) * norm_gain.reshape(number_heads, width)[None, None]
    )
    flat_out = gained.reshape(tok_rows, number_heads * width).astype(jnp.bfloat16)
    return lax.all_to_all(flat_out, "head", split_axis=0, concat_axis=1, tiled=True)


def solution(mesh):
    return jax.shard_map(
        on_device,
        mesh=mesh,
        in_specs=(P(("seq", "head"), None), P("seq", None, "head"), P("head", "seq"), P("head")),
        out_specs=P(("seq", "head"), None),
        check_vma=False,
    )
```

profile of v0, /device:TPU:1, one launch (start us, length us, event | category | flops | bytes accessed | tf_op | source)
XLA Modules:
  0.0 413.7 jit_solution(11845919447751319366)
XLA Ops:
  8.8 1.2 reduce_window_sum.13
  10.4 38.2 %all-gather.6.cloned.1.call-done = bf16[512,3072]{1,0:T(8,128)(2,1)} async-done(((bf16[64,3072]{1,0:T(8,128)(2,1)}), bf16[512,3072]{1,0:T(8,128)(2,1)}) %all-gather.6.cloned.1.call-update) | async-done | bytes 3145744 | tf_op jit(solution)/shard_map/all_gather | solution.py:32
  48.6 107.2 %all-gather.8.cloned.1.call-done = bf16[3072,3,512]{2,0,1:T(8,128)(2,1)} async-done(((bf16[48,3,512]{2,0,1:T(8,128)(2,1)}), bf16[3072,3,512]{2,0,1:T(8,128)(2,1)}) %all-gather.8.cloned.1.call-update) | async-done | bytes 9437200 | tf_op jit(solution)/shard_map/all_gather | solution.py:36
  155.7 9.4 %fusion.7 = bf16[512,3,512]{2,0,1:T(8,128)(2,1)S(1)} fusion(bf16[3072,3,512]{2,0,1:T(8,128)(2,1)} %all-gather.8.cloned.1.call-done, bf16[512,3072]{1,0:T(8,128)(2,1)} %all-gather.6.cloned.1.call-done), kind=kOutput, calls=%fused_computation.13 | convolution fusion | flops 4832624640 | bytes 14155776 | tf_op jit(solution)/shard_map/td,dcf->tcf/dot_general | solution.py:37
  166.5 1.3 fusion.15
  167.8 3.6 while.31
  172.2 1.3 dynamic-slice
  174.4 115.4 %all-reduce = f32[256]{0:T(256)S(1)} all-reduce(f32[256]{0:T(256)S(1)} %dynamic-update-slice), channel_id=2, replica_groups=mesh['seq'=64,'head'=8] {'seq'}, use_global_device_ids=true, to_apply=%add | all-reduce | flops 256 | bytes 2048
  290.4 1.2 fusion.19
  291.7 20.4 %all-gather.10.cloned.1.call-done = f32[256,128,128]{2,1,0:T(8,128)} async-done(((f32[4,128,128]{2,1,0:T(8,128)}), f32[256,128,128]{2,1,0:T(8,128)}) %all-gather.10.cloned.1.call-update) | async-done | bytes 16777232 | tf_op jit(solution)/shard_map/all_gather | solution.py:14
  312.0 69.2 %while.32 = (s32[]{:T(128)}, f32[4,128,128]{2,1,0:T(8,128)S(1)}, s32[]{:T(128)}, f32[64,4]{1,0:T(8,128)S(1)}, f32[64,4,128,128]{3,2,1,0:T(8,128)}, /*index=5*/s32[]{:T(128)}, s32[]{:T(128)}) while((s32[]{:T(128)}, f32[4,128,128]{2,1,0:T(8,128)S(1)}, s32[]{:T(128)}, f32[64,4]{1,0:T(8,128)S(1)}, f32[64,4,128,128]{3,2,1,0:T(8,128)}, ...), condition=%wide.region_4.5_spmd.clone, body=%wide.region_3.4_spmd.clone.sunk | while | flops 262148 | bytes 786593 | solution.py:23
  312.0 1.1 fusion.32
  313.1 1.1 fusion.32
  314.2 1.1 fusion.32
  315.3 1.1 fusion.32
  316.4 1.1 fusion.32
  317.5 1.1 fusion.32
  318.6 1.1 fusion.32
  319.7 1.1 fusion.32
  320.8 1.1 fusion.32
  324.1 1.1 fusion.32
  327.4 1.1 fusion.32
  328.5 1.1 fusion.32
  330.7 1.1 fusion.32
  331.8 1.1 fusion.32
  334.0 1.1 fusion.32
  335.1 1.1 fusion.32
  338.4 1.1 fusion.32
  341.7 1.1 fusion.32
  345.0 1.1 fusion.32
  348.3 1.1 fusion.32
  349.4 1.1 fusion.32
  351.6 1.1 fusion.32
  352.7 1.1 fusion.32
  354.9 1.1 fusion.32
  356.0 1.1 fusion.32
  359.3 1.1 fusion.32
  362.6 1.1 fusion.32
  365.9 1.1 fusion.32
  369.2 1.1 fusion.32
  370.3 1.1 fusion.32
  372.5 1.1 fusion.32
  373.6 1.1 fusion.32
  375.8 1.1 fusion.32
  376.9 1.1 fusion.32
  380.2 1.1 fusion.32
  381.3 2.2 multiply_reduce_fusion
  384.2 22.1 %all_to_all.16 = bf16[8,64,512]{2,1,0:T(8,128)(2,1)S(1)} all-to-all(bf16[8,64,512]{2,1,0:T(8,128)(2,1)S(1)} %convert_element_type.22), channel_id=1, replica_groups=mesh['seq'=64,'head'=8] {'head'}, dimensions={0} | all-to-all | bytes 1048576 | tf_op jit(solution)/shard_map/all_to_all | solution.py:82
  (145 shorter events, 40.8 us)
Async XLA Ops:
  6.5 42.0 %all-gather.6.cloned.1.call-start = ((), (), s32[]{:S(2)}) async-start(), calls=%async_computation.1 | async-start | bytes 3538944 | tf_op jit(solution)/shard_map/all_gather | solution.py:32
  7.3 148.5 %all-gather.8.cloned.1.call-start = ((), (), s32[]{:S(2)}) async-start(), calls=%async_computation.2 | async-start | bytes 9584640 | tf_op jit(solution)/shard_map/all_gather | solution.py:36
  8.0 304.0 %all-gather.10.cloned.1.call-start = ((), (), s32[]{:S(2)}) async-start(), calls=%async_computation.3 | async-start | bytes 17039360 | tf_op jit(solution)/shard_map/all_gather | solution.py:14
  171.4 0.7 copy-start
  290.4 90.8 %copy-start.1 = (f32[4,4,128,128]{3,2,1,0:T(8,128)S(1)}, f32[4,4,128,128]{3,2,1,0:T(8,128)}, u32[]{:S(2)}) copy-start(f32[4,4,128,128]{3,2,1,0:T(8,128)} %get-tuple-element.143) | copy-start | bytes 3145732
  312.0 71.5 %copy-start.2 = (f32[512]{0:T(512)S(1)}, f32[512]{0:T(512)}, u32[]{:S(2)}) copy-start(f32[512]{0:T(512)} %param.11) | copy-start | bytes 6148
Sparse Core Ops, SparseCore 0:
  9.5 39.0 all-gather.5
  51.6 104.1 all-gather.7
  172.3 139.7 all-gather.9
where the time goes:
time: 416 us; the launch traced here: 414 us
  waiting for transfers between devices  167 us (40%)
  blocking collectives  138 us (33%)
  other arithmetic  71.3 us (17%)
  matrix products  14.6 us (4%)
  between operations  14 us (3%)
  local copies, waits for them, and re-layouts  6.97 us (2%)
    unnamed x1, blocking collectives  115 us
    all_gather x1, waiting for transfers between devices, on_device(): full_weight = lax.all_gather(qkv_weight, 'seq', axis=0, tiled=True)  107 us
    select_n x63, other arithmetic, turn(): jnp.where(position < mine, new, old)  66.5 us
    all_gather x1, waiting for transfers between devices, on_device(): gathered = lax.all_gather(tokens, 'head', axis=0, tiled=True)  38.2 us
    all_to_all x1, blocking collectives, on_device(): lax.all_to_all(flat_out, 'head', split_axis=0, concat_axis=1, tiled=True)  22.1 us
    all_gather x1, waiting for transfers between devices, carried_in(): pieces = jax.tree.map(lambda part: lax.all_gather(part, axis), value)  20.4 us
    dot_general x1, matrix products, on_device(): jnp.einsum('td,dcf->tcf', gathered, full_weight, preferred_element_type=j...  9.39 us
  transfers between devices with their start and end apart: 3, of which 3 were waited for; matrix products, arithmetic and copies ran while one was open for 1% of the time, Pallas kernels for 0%

commit v1 on v0

v1 whole, which is shorter than its diff:
```python
import functools

import jax
import jax.numpy as jnp
from jax import lax
from jax.experimental import pallas as pl
from jax.experimental.pallas import tpu as pltpu
from jax.sharding import PartitionSpec as P

BLK = 128
E = 128
EPS = 1e-05
NY = 8
NZ = 8
NH = 8
EXTRA = 16
F32 = jnp.float32
BF16 = jnp.bfloat16
VMEM = pltpu.VMEM

Z_GROUPS = [[y * NZ + z for z in range(NZ)] for y in range(NY)]
OUT_GROUPS = [[g * 16 + i for i in range(16)] for g in range(NY * NZ // 2)]


def z_shift(d):
    return [(y * NZ + z, y * NZ + (z + d) % NZ) for y in range(NY) for z in range(NZ)]


def y_shift(d):
    return [(y * NZ + z, ((y + d) % NY) * NZ + z) for y in range(NY) for z in range(NZ)]


def y_later(d):
    return [(y * NZ + z, (y + d) * NZ + z) for y in range(NY - d) for z in range(NZ)]


PAIR = [(s, s ^ 1) for s in range(NY * NZ)]


def after(value, *earlier):
    return lax.optimization_barrier((value,) + earlier)[0]


def whole(count):
    return [pl.BlockSpec(memory_space=VMEM)] * count


def mm(a, b, dims=(((1,), (0,)), ((), ()))):
    return lax.dot_general(a, b, dims, preferred_element_type=F32)


def write_message(ref, head, state, decay):
    ref[head, :E, :] = state.astype(BF16)
    decay = jnp.broadcast_to(decay, (EXTRA, E))
    high = decay.astype(BF16)
    rest = decay - high.astype(F32)
    middle = rest.astype(BF16)
    low = (rest - middle.astype(F32)).astype(BF16)
    row = lax.broadcasted_iota(jnp.int32, (EXTRA, E), 0)
    part = jnp.where(row == 0, high.astype(F32), jnp.where(row == 1, middle.astype(F32), low.astype(F32)))
    ref[head, E:, :] = part.astype(BF16)


def read_decay(ref, head):
    rows = ref[head, E:, :].astype(F32)
    return (rows[0:1] + rows[1:2]) + rows[2:3]


def pieces_kernel(weight_ref, out_ref):
    for c in range(3):
        for i in range(NZ):
            half = slice((i % 2) * 256, (i % 2 + 1) * 256)
            out_ref[i, :, c * 256 : (c + 1) * 256] = weight_ref[c, :, half]


def order_kernel(sent_ref, out_ref):
    for s in range(2):
        for h in range(NH):
            out_ref[:, (h * 2 + s) * 256 : (h * 2 + s + 1) * 256] = sent_ref[s * NH + h]


def states_kernel(side_ref, own_ref, other_ref, col_ref, row_ref, proj_ref, prefix_ref, total_ref, message_ref):
    side = side_ref[0]
    proj_ref[side] = own_ref[...].astype(BF16)
    proj_ref[1 - side] = other_ref[...].astype(BF16)
    for head in range(2):
        state = jnp.zeros((E, E), F32)
        decay = jnp.zeros((1, 1), F32)
        for n in range(8):
            at = head * 8 + n
            rows = slice((n % 4) * BLK, (n % 4 + 1) * BLK)
            keys = proj_ref[n // 4, rows, 256 + head * E : 256 + (head + 1) * E]
            values = proj_ref[n // 4, rows, 512 + head * E : 512 + (head + 1) * E]
            last = row_ref[at : at + 1, BLK - 1 : BLK]
            scale = jnp.exp(last - col_ref[:, at : at + 1])
            prefix_ref[at] = state.astype(BF16)
            scaled = (keys.astype(F32) * scale).astype(BF16)
            state = jnp.exp(last) * state + mm(scaled, values, (((0,), (0,)), ((), ())))
            decay = decay + last
        total_ref[head] = state
        write_message(message_ref, head, state, decay)


def local_kernel(proj_ref, prefix_ref, col_ref, row_ref, out_ref):
    causal = lax.broadcasted_iota(jnp.int32, (BLK, BLK), 0) >= lax.broadcasted_iota(jnp.int32, (BLK, BLK), 1)
    for head in range(2):
        for n in range(8):
            at = head * 8 + n
            rows = slice((n % 4) * BLK, (n % 4 + 1) * BLK)
            queries = proj_ref[n // 4, rows, head * E : (head + 1) * E]
            keys = proj_ref[n // 4, rows, 256 + head * E : 256 + (head + 1) * E]
            values = proj_ref[n // 4, rows, 512 + head * E : 512 + (head + 1) * E]
            col = col_ref[:, at : at + 1]
            gaps = col - row_ref[at : at + 1, :]
            weights = jnp.exp(jnp.where(causal, gaps, -1e30))
            scores = mm(queries, keys, (((1,), (1,)), ((), ()))) * weights
            scaled = (queries.astype(F32) * jnp.exp(col)).astype(BF16)
            out_ref[at] = mm(scores.astype(BF16), values) + mm(scaled, prefix_ref[at])


def row_kernel(place_ref, total_ref, own_ref, m1_ref, m2_ref, m3_ref, before_ref, decay_ref, message_ref):
    place = place_ref[0]
    messages = (None, m1_ref, m2_ref, m3_ref)
    for head in range(2):
        mine = read_decay(own_ref, head)
        decays = [mine] + [read_decay(messages[k], head) for k in range(1, 4)]
        before = jnp.zeros((E, E), F32)
        later = jnp.zeros((E, E), F32)
        gone_before = jnp.zeros((1, E), F32)
        gone_later = jnp.zeros((1, E), F32)
        for k in range(1, 4):
            block = messages[k][head, :E, :].astype(F32)
            early = place >= k
            before = before + jnp.where(early, jnp.exp(gone_before), 0.0) * block
            later = later + jnp.where(early, 0.0, jnp.exp(gone_later)) * block
            gone_before = gone_before + jnp.where(early, decays[k], 0.0)
            gone_later = gone_later + jnp.where(early, 0.0, decays[k])
        through = jnp.exp(mine) * before + total_ref[head]
        before_ref[head] = before
        decay_ref[head] = jnp.broadcast_to(gone_before, (8, E))
        write_message(message_ref, head, later + jnp.exp(gone_later) * through, gone_before + mine + gone_later)


def final_kernel(*refs):
    messages = refs[:7]
    before_ref, decay_ref, part_ref, proj_ref, col_ref, start_ref, gain_ref, out_ref = refs[7:]
    for head in range(2):
        carried = jnp.zeros((E, E), F32)
        gone = jnp.zeros((1, E), F32)
        for ref in messages:
            carried = carried + jnp.exp(gone) * ref[head, :E, :].astype(F32)
            gone = gone + read_decay(ref, head)
        incoming = (jnp.exp(decay_ref[head, 0:1, :]) * carried + before_ref[head]).astype(BF16)
        gain = gain_ref[0:1, head * E : (head + 1) * E]
        for n in range(8):
            at = head * 8 + n
            rows = slice((n % 4) * BLK, (n % 4 + 1) * BLK)
            queries = proj_ref[n // 4, rows, head * E : (head + 1) * E]
            scale = jnp.exp(col_ref[:, at : at + 1] + start_ref[0:1, at : at + 1])
            scaled = (queries.astype(F32) * scale).astype(BF16)
            output = part_ref[at] + mm(scaled, incoming)
            meansq = jnp.mean(output * output, axis=1, keepdims=True)
            gained = output / jnp.sqrt(meansq + EPS) * gain
            out_ref[n * BLK : (n + 1) * BLK, head * E : (head + 1) * E] = gained.astype(BF16)


def call(kernel, outs, scalars, *args, flops=0):
    shapes = [jax.ShapeDtypeStruct(s, d) for s, d in outs]
    smem = [pl.BlockSpec(memory_space=pltpu.SMEM)] * len(scalars)
    moved = sum(a.size * a.dtype.itemsize for a in args)
    return pl.pallas_call(
        kernel,
        out_shape=shapes,
        in_specs=smem + whole(len(args)),
        out_specs=whole(len(outs)),
        cost_estimate=pl.CostEstimate(flops=flops, bytes_accessed=moved, transcendentals=0),
        compiler_params=pltpu.CompilerParams(vmem_limit_bytes=32 * 1024 * 1024),
    )(*scalars, *args)


def on_device(tokens, qkv_weight, log_decay, norm_gain):
    seq = lax.axis_index("seq")
    y, z = seq // NZ, seq % NZ
    side = z % 2
    place = z // 2
    side1 = side.reshape(1).astype(jnp.int32)
    place1 = place.reshape(1).astype(jnp.int32)

    pair_tokens = lax.ppermute(tokens, "seq", PAIR)
    own_rows = lax.all_gather(tokens, "head", axis=0, tiled=True)
    other_rows = lax.all_gather(pair_tokens, "head", axis=0, tiled=True)

    mine = lax.dynamic_slice_in_dim(log_decay, side * 2, 2, 0)
    theirs = lax.ppermute(lax.dynamic_slice_in_dim(log_decay, (1 - side) * 2, 2, 0), "seq", PAIR)
    both = jnp.where(side == 0, jnp.concatenate([mine, theirs], 1), jnp.concatenate([theirs, mine], 1))
    rows = jnp.cumsum(both.reshape(2, 8, BLK), axis=2)
    ends = rows[:, :, -1]
    starts = (jnp.cumsum(ends, axis=1) - ends).reshape(1, 16)
    rows = rows.reshape(16, BLK)
    cols = rows.T
    gain = lax.dynamic_slice_in_dim(norm_gain, side * 256, 256, 0).reshape(1, 256)

    (pieces,) = call(pieces_kernel, [((NZ, 48, 768), BF16)], [], qkv_weight.transpose(1, 0, 2))
    block = lax.all_to_all(pieces, "seq", split_axis=0, concat_axis=0, tiled=True, axis_index_groups=Z_GROUPS)
    block, rows, cols, starts, gain = lax.optimization_barrier((block, rows, cols, starts, gain))

    def add(total, tok, part, offset):
        x = lax.dynamic_slice_in_dim(tok, ((y + offset) % NY) * (NZ * 48), NZ * 48, 1)
        d = jnp.dot(x, part.reshape(NZ * 48, 768), preferred_element_type=F32)
        return d if total is None else total + d

    ups, downs = [block], [block]

    def hop(*earlier):
        up, down = lax.optimization_barrier((ups[-1], downs[-1]) + earlier)[:2]
        ups.append(lax.ppermute(up, "seq", y_shift(1)))
        downs.append(lax.ppermute(down, "seq", y_shift(-1)))

    def add_step(total, tok, step):
        if step == 0:
            return add(total, tok, block, 0)
        return add(add(total, tok, ups[step], -step), tok, downs[step], step)

    hop()
    own = add_step(None, own_rows, 0)
    hop(own)
    own = add_step(own, own_rows, 1)
    hop(own)
    own = add_step(own, own_rows, 2)
    other = add_step(add_step(None, other_rows, 0), other_rows, 1)
    up, down = lax.optimization_barrier((ups[3], downs[3], own, other))[:2]
    up4 = lax.ppermute(up[:4], "seq", y_shift(1))
    down4 = lax.ppermute(down[4:], "seq", y_shift(-1))
    own = add_step(own, own_rows, 3)
    other = add_step(add_step(other, other_rows, 2), other_rows, 3)
    up4, down4, own, other = lax.optimization_barrier((up4, down4, own, other))
    last = jnp.concatenate([up4, down4], 0)
    own = add(own, own_rows, last, 4)
    other = add(other, other_rows, last, 4)

    proj, prefix, total, message = call(
        states_kernel,
        [((2, 512, 768), BF16), ((16, E, E), BF16), ((2, E, E), F32), ((2, E + EXTRA, E), BF16)],
        [side1], own, other, cols, rows, flops=16 * 2 * E**3,
    )
    m1 = lax.ppermute(message, "seq", z_shift(2))
    m3 = lax.ppermute(message, "seq", z_shift(-2))
    m2 = lax.ppermute(message, "seq", z_shift(4))
    (part,) = call(local_kernel, [((16, BLK, E), F32)], [], proj, prefix, cols, rows, flops=16 * 6 * E**3)
    before, gone, row_message = call(
        row_kernel,
        [((2, E, E), F32), ((2, 8, E), F32), ((2, E + EXTRA, E), BF16)],
        [place1], total, message, m1, m2, m3,
    )
    earlier = [lax.ppermute(row_message, "seq", y_later(k)) for k in range(1, NY)]
    (flat,) = call(
        final_kernel, [((1024, 256), BF16)], [], *earlier, before, gone, part, proj, cols, starts, gain,
        flops=16 * 2 * E**3,
    )
    sent = lax.all_to_all(
        flat.reshape(16, 64, 256), ("seq", "head"), split_axis=0, concat_axis=0, tiled=True,
        axis_index_groups=OUT_GROUPS,
    )
    (out,) = call(order_kernel, [((64, 4096), BF16)], [], sent)
    return out


def solution(mesh):
    return jax.shard_map(
        on_device,
        mesh=mesh,
        in_specs=(P(("seq", "head"), None), P("seq", None, "head"), P("head", "seq"), P("head")),
        out_specs=P(("seq", "head"), None),
        check_vma=False,
    )
```

time: 416 us -> 190 us (0.46)
  blocking collectives: 138 us -> 14.1 us
  waiting for transfers between devices: 167 us -> 49.8 us
  starting transfers between devices: 0.08 us -> 83.7 us
  other arithmetic: 71.3 us -> 1.21 us
  Pallas kernels: 0 us -> 7.22 us
  local copies, waits for them, and re-layouts: 6.97 us -> 2.24 us
    all_gather x3 -> x2, waiting for transfers between devices: 166 us -> 6.01 us  [the longest x1 5.99 us: on_device(): other_rows = lax.all_gather(pair_tokens, 'head', axis=0, tiled=True)]
    unnamed x1 -> x0, blocking collectives: 115 us -> none
    ppermute x0 -> x20, starting transfers between devices: none -> 70.9 us  [the longest x7 16.1 us: on_device(): lax.ppermute(row_message, 'seq', y_later(k))]
    select_n x63 -> x1, other arithmetic: 66.5 us -> 0.01 us  [on_device(): jnp.where(side == 0, jnp.concatenate([mine, theirs], 1), jnp.concatenate(...]
    ppermute x0 -> x20, waiting for transfers between devices: none -> 38.6 us  [the longest x3 13.5 us: hop(): ups.append(lax.ppermute(up, 'seq', y_shift(1)))]
    all_to_all x0 -> x1, starting transfers between devices: none -> 12.8 us  [on_device(): lax.all_to_all(pieces, 'seq', split_axis=0, concat_axis=0, tiled=True, ax...]
    all_to_all x1, blocking collectives: 22.1 us -> 14.1 us  [on_device(): lax.all_to_all(flat.reshape(16, 64, 256), ('seq', 'head'), split_axis=0,...]
    pallas_call x0 -> x6, Pallas kernels: none -> 7.22 us  [call(): pl.pallas_call(kernel, out_shape=shapes, in_specs=smem + whole(len(args))...]
  transfers between devices with their start and end apart: 3 -> 23, of which waited for: 3 -> 13; matrix products, arithmetic and copies ran while one was open for 1% -> 9% of each run, Pallas kernels for 0% -> 1%
where the time goes in v1:
time: 190 us; the launch traced here: 189 us
  starting transfers between devices  83.7 us (44%)
  waiting for transfers between devices  49.8 us (26%)
  matrix products  16.8 us (9%)
  blocking collectives  14.1 us (7%)
  between operations  14 us (7%)
  Pallas kernels  7.22 us (4%)
  local copies, waits for them, and re-layouts  2.24 us (1%)
    dot_general x16, matrix products, add(): d = jnp.dot(x, part.reshape(NZ * 48, 768), preferred_element_type=F32)  16.8 us
    ppermute x7, starting transfers between devices, on_device(): lax.ppermute(row_message, 'seq', y_later(k))  16.1 us
    all_to_all x1, blocking collectives, on_device(): lax.all_to_all(flat.reshape(16, 64, 256), ('seq', 'head'), split_axis=0,...  14.1 us
    ppermute x3, waiting for transfers between devices, hop(): ups.append(lax.ppermute(up, 'seq', y_shift(1)))  13.5 us
    all_to_all x1, starting transfers between devices, on_device(): lax.all_to_all(pieces, 'seq', split_axis=0, concat_axis=0, tiled=True, ax...  12.8 us
    ppermute x3, starting transfers between devices, hop(): downs.append(lax.ppermute(down, 'seq', y_shift(-1)))  11.1 us
    ppermute x3, starting transfers between devices, hop(): ups.append(lax.ppermute(up, 'seq', y_shift(1)))  9.63 us
    ppermute x1, waiting for transfers between devices, on_device(): lax.ppermute(lax.dynamic_slice_in_dim(log_decay, (1 - side) * 2, 2, 0), '...  8.15 us
  transfers between devices with their start and end apart: 23, of which 13 were waited for; matrix products, arithmetic and copies ran while one was open for 9% of the time, Pallas kernels for 1%

profile of v1, /device:TPU:1, one launch (start us, length us, event | category | flops | bytes accessed | tf_op | source)
XLA Modules:
  0.0 189.1 jit_solution(17403155712260180918)
XLA Ops:
  6.5 0.7 all-gather.3.cloned.1.call-update
  7.3 4.8 %collective-permute-start.7 = (bf16[64,3072]{1,0:T(8,128)(2,1)}, bf16[64,3072]{1,0:T(8,128)(2,1)S(1)}, u32[]{:S(2)}, u32[]{:S(2)}) collective-permute-start(bf16[64,3072]{1,0:T(8,128)(2,1)} %param.4), channel_id=1, source_target_pairs={{0,8},{8,0},{16,24},{24,16},{32,40},{40,32},{48,56},{56,48},{64,72... | collective-permute-start | bytes 1179656 | tf_op jit(solution)/shard_map/ppermute | solution.py:189
  12.1 5.4 %collective-permute-done.7 = bf16[64,3072]{1,0:T(8,128)(2,1)S(1)} collective-permute-done((bf16[64,3072]{1,0:T(8,128)(2,1)}, bf16[64,3072]{1,0:T(8,128)(2,1)S(1)}, u32[]{:S(2)}, u32[]{:S(2)}) %collective-permute-start.7) | collective-permute-done | bytes 393248 | tf_op jit(solution)/shard_map/ppermute | solution.py:189
  17.5 0.7 copy-done.3
  18.3 0.9 copy-done
  19.2 0.9 shard_map.46
  20.1 12.8 %all-to-all-start = ((bf16[8,48,768]{2,1,0:T(8,128)(2,1)}), bf16[8,48,768]{2,1,0:T(8,128)(2,1)S(1)}, u32[]{:S(2)}, u32[]{:S(2)}) async-start(bf16[8,48,768]{2,1,0:T(8,128)(2,1)} %shard_map.46), calls=%async_computation | async-start | bytes 1179648 | tf_op jit(solution)/shard_map/all_to_all | solution.py:204
  32.8 3.4 %collective-permute-start = (f32[2,512]{1,0:T(2,128)S(1)}, f32[2,512]{1,0:T(2,128)S(1)}, u32[]{:S(2)}, u32[]{:S(2)}) collective-permute-start(f32[2,512]{1,0:T(2,128)S(1)} %get-tuple-element.54), channel_id=1, source_target_pairs={{0,8},{8,0},{16,24},{24,16},{32,40},{40,32},{48,56},{56,48},{64,72... | collective-permute-start | bytes 12296 | tf_op jit(solution)/shard_map/ppermute | solution.py:194
  36.3 8.1 %collective-permute-done = f32[2,512]{1,0:T(2,128)S(1)} collective-permute-done((f32[2,512]{1,0:T(2,128)S(1)}, f32[2,512]{1,0:T(2,128)S(1)}, u32[]{:S(2)}, u32[]{:S(2)}) %collective-permute-start) | collective-permute-done | bytes 4128 | tf_op jit(solution)/shard_map/ppermute | solution.py:194
  45.7 4.5 %all-to-all-done = bf16[8,48,768]{2,1,0:T(8,128)(2,1)S(1)} async-done(((bf16[8,48,768]{2,1,0:T(8,128)(2,1)}), bf16[8,48,768]{2,1,0:T(8,128)(2,1)S(1)}, u32[]{:S(2)}, u32[]{:S(2)}) %all-to-all-start) | async-done | bytes 589856 | tf_op jit(solution)/shard_map/all_to_all | solution.py:204
  50.2 3.2 %collective-permute-start.1 = (bf16[8,48,768]{2,1,0:T(8,128)(2,1)S(1)}, bf16[8,48,768]{2,1,0:T(8,128)(2,1)}, u32[]{:S(2)}, u32[]{:S(2)}) collective-permute-start(bf16[8,48,768]{2,1,0:T(8,128)(2,1)S(1)} %all-to-all-done), channel_id=1, source_target_pairs={{0,64},{8,72},{16,80},{24,88},{32,96},{40,104},{48,112},{56,120},{... | collective-permute-start | bytes 1769480 | tf_op jit(solution)/shard_map/ppermute | solution.py:216
  53.4 3.8 %collective-permute-start.2 = (bf16[8,48,768]{2,1,0:T(8,128)(2,1)S(1)}, bf16[8,48,768]{2,1,0:T(8,128)(2,1)S(1)}, u32[]{:S(2)}, u32[]{:S(2)}) collective-permute-start(bf16[8,48,768]{2,1,0:T(8,128)(2,1)S(1)} %all-to-all-done), channel_id=1, source_target_pairs={{0,448},{8,456},{16,464},{24,472},{32,480},{40,488},{48,496},{56,5... | collective-permute-start | bytes 1769480 | tf_op jit(solution)/shard_map/ppermute | solution.py:217
  57.4 1.6 fusion.37
  59.0 7.5 %collective-permute-done.1 = bf16[8,48,768]{2,1,0:T(8,128)(2,1)} collective-permute-done((bf16[8,48,768]{2,1,0:T(8,128)(2,1)S(1)}, bf16[8,48,768]{2,1,0:T(8,128)(2,1)}, u32[]{:S(2)}, u32[]{:S(2)}) %collective-permute-start.1) | collective-permute-done | bytes 589856 | tf_op jit(solution)/shard_map/ppermute | solution.py:216
  66.4 0.9 collective-permute-done.2
  67.4 3.2 %collective-permute-start.3 = (bf16[8,48,768]{2,1,0:T(8,128)(2,1)}, bf16[8,48,768]{2,1,0:T(8,128)(2,1)}, u32[]{:S(2)}, u32[]{:S(2)}) collective-permute-start(bf16[8,48,768]{2,1,0:T(8,128)(2,1)} %collective-permute-done.1), channel_id=1, source_target_pairs={{0,64},{8,72},{16,80},{24,88},{32,96},{40,104},{48,112},{56,120},{... | collective-permute-start | bytes 1769480 | tf_op jit(solution)/shard_map/ppermute | solution.py:216
  70.6 3.9 %collective-permute-start.4 = (bf16[8,48,768]{2,1,0:T(8,128)(2,1)S(1)}, bf16[8,48,768]{2,1,0:T(8,128)(2,1)S(1)}, u32[]{:S(2)}, u32[]{:S(2)}) collective-permute-start(bf16[8,48,768]{2,1,0:T(8,128)(2,1)S(1)} %collective-permute-done.2), channel_id=1, source_target_pairs={{0,448},{8,456},{16,464},{24,472},{32,480},{40,488},{48,496},{56,5... | collective-permute-start | bytes 1769480 | tf_op jit(solution)/shard_map/ppermute | solution.py:217
  74.5 1.8 fusion.35
  76.2 1.6 add_add_fusion.4
  77.8 6.0 %all-gather.5.cloned.1.call-done = bf16[512,3072]{1,0:T(8,128)(2,1)} async-done(((bf16[64,3072]{1,0:T(8,128)(2,1)}), bf16[512,3072]{1,0:T(8,128)(2,1)}) %all-gather.5.cloned.1.call-update) | async-done | bytes 3145744 | tf_op jit(solution)/shard_map/all_gather | solution.py:191
  83.8 1.7 fusion.26
  85.5 1.8 fusion.24
  87.9 3.2 %collective-permute-start.5 = (bf16[8,48,768]{2,1,0:T(8,128)(2,1)}, bf16[8,48,768]{2,1,0:T(8,128)(2,1)S(1)}, u32[]{:S(2)}, u32[]{:S(2)}) collective-permute-start(bf16[8,48,768]{2,1,0:T(8,128)(2,1)} %collective-permute-done.3), channel_id=1, source_target_pairs={{0,64},{8,72},{16,80},{24,88},{32,96},{40,104},{48,112},{56,120},{... | collective-permute-start | bytes 1769480 | tf_op jit(solution)/shard_map/ppermute | solution.py:216
  91.2 3.4 %collective-permute-start.6 = (bf16[8,48,768]{2,1,0:T(8,128)(2,1)S(1)}, bf16[8,48,768]{2,1,0:T(8,128)(2,1)S(1)}, u32[]{:S(2)}, u32[]{:S(2)}) collective-permute-start(bf16[8,48,768]{2,1,0:T(8,128)(2,1)S(1)} %collective-permute-done.4), channel_id=1, source_target_pairs={{0,448},{8,456},{16,464},{24,472},{32,480},{40,488},{48,496},{56,5... | collective-permute-start | bytes 1769480 | tf_op jit(solution)/shard_map/ppermute | solution.py:217
  94.6 1.6 fusion.32
  96.2 1.6 fusion.12
  99.0 6.0 %collective-permute-done.5 = bf16[8,48,768]{2,1,0:T(8,128)(2,1)S(1)} collective-permute-done((bf16[8,48,768]{2,1,0:T(8,128)(2,1)}, bf16[8,48,768]{2,1,0:T(8,128)(2,1)S(1)}, u32[]{:S(2)}, u32[]{:S(2)}) %collective-permute-start.5) | collective-permute-done | bytes 589856 | tf_op jit(solution)/shard_map/ppermute | solution.py:216
  105.7 2.3 %collective-permute-start.8 = (bf16[4,48,768]{2,1,0:T(8,128)(2,1)S(1)}, bf16[4,48,768]{2,1,0:T(8,128)(2,1)S(1)}, u32[]{:S(2)}, u32[]{:S(2)}) collective-permute-start(bf16[4,48,768]{2,1,0:T(8,128)(2,1)S(1)} %slice.10), channel_id=1, source_target_pairs={{0,64},{8,72},{16,80},{24,88},{32,96},{40,104},{48,112},{56,120},{... | collective-permute-start | bytes 884744 | tf_op jit(solution)/shard_map/ppermute | solution.py:232
  108.0 4.9 %collective-permute-start.9 = (bf16[4,48,768]{2,1,0:T(8,128)(2,1)S(1)}, bf16[4,48,768]{2,1,0:T(8,128)(2,1)S(1)}, u32[]{:S(2)}, u32[]{:S(2)}) collective-permute-start(bf16[4,48,768]{2,1,0:T(8,128)(2,1)S(1)} %slice.11), channel_id=1, source_target_pairs={{0,448},{8,456},{16,464},{24,472},{32,480},{40,488},{48,496},{56,5... | collective-permute-start | bytes 884744 | tf_op jit(solution)/shard_map/ppermute | solution.py:233
  115.6 1.8 collective-permute-done.9
  119.0 2.0 %shard_map.47 = (bf16[2,512,768]{2,1,0:T(8,128)(2,1)S(1)}, bf16[16,128,128]{2,1,0:T(8,128)(2,1)S(1)}, f32[2,128,128]{2,1,0:T(8,128)S(1)}, bf16[2,144,128]{2,1,0:T(8,128)(2,1)S(1)}) custom-call(s32[1]{0:T(128)} %bitcast.1.side_ref, f32[512,768]{1,0:T(8,128)S(1)} %add.192.own_ref, f32[512,768]{1,0:T(8,128)S(1)} %add.193.other_ref, f32[128,16]{1,0:T(8,128)S(1)} %bitcast.32, ...), custom_call_target="tpu_custom_call" | custom-call | flops 67108864 | bytes 3162112 | tf_op jit(solution)/shard_map/pallas_call | solution.py:171
  121.0 7.8 %collective-permute-start.10 = (bf16[2,144,128]{2,1,0:T(8,128)(2,1)S(1)}, bf16[2,144,128]{2,1,0:T(8,128)(2,1)S(1)}, u32[]{:S(2)}, u32[]{:S(2)}) collective-permute-start(bf16[2,144,128]{2,1,0:T(8,128)(2,1)S(1)} %get-tuple-element.45.own_ref), channel_id=1, source_target_pairs={{0,16},{8,24},{16,32},{24,40},{32,48},{40,56},{48,0},{56,8},{64,80... | collective-permute-start | bytes 221192 | tf_op jit(solution)/shard_map/ppermute | solution.py:246
  128.9 5.9 %collective-permute-start.11 = (bf16[2,144,128]{2,1,0:T(8,128)(2,1)S(1)}, bf16[2,144,128]{2,1,0:T(8,128)(2,1)S(1)}, u32[]{:S(2)}, u32[]{:S(2)}) collective-permute-start(bf16[2,144,128]{2,1,0:T(8,128)(2,1)S(1)} %get-tuple-element.45.own_ref), channel_id=1, source_target_pairs={{0,32},{8,40},{16,48},{24,56},{32,0},{40,8},{48,16},{56,24},{64,96... | collective-permute-start | bytes 221192 | tf_op jit(solution)/shard_map/ppermute | solution.py:248
  134.8 4.8 %collective-permute-start.12 = (bf16[2,144,128]{2,1,0:T(8,128)(2,1)S(1)}, bf16[2,144,128]{2,1,0:T(8,128)(2,1)S(1)}, u32[]{:S(2)}, u32[]{:S(2)}) collective-permute-start(bf16[2,144,128]{2,1,0:T(8,128)(2,1)S(1)} %get-tuple-element.45.own_ref), channel_id=1, source_target_pairs={{0,48},{8,56},{16,0},{24,8},{32,16},{40,24},{48,32},{56,40},{64,11... | collective-permute-start | bytes 221192 | tf_op jit(solution)/shard_map/ppermute | solution.py:247
  139.7 2.0 %collective-permute-done.12.m3_ref = bf16[2,144,128]{2,1,0:T(8,128)(2,1)S(1)} collective-permute-done((bf16[2,144,128]{2,1,0:T(8,128)(2,1)S(1)}, bf16[2,144,128]{2,1,0:T(8,128)(2,1)S(1)}, u32[]{:S(2)}, u32[]{:S(2)}) %collective-permute-start.12) | collective-permute-done | bytes 73760 | tf_op jit(solution)/shard_map/ppermute | solution.py:247
  141.8 3.9 %collective-permute-start.13 = (bf16[2,144,128]{2,1,0:T(8,128)(2,1)S(1)}, bf16[2,144,128]{2,1,0:T(8,128)(2,1)S(1)}, u32[]{:S(2)}, u32[]{:S(2)}) collective-permute-start(bf16[2,144,128]{2,1,0:T(8,128)(2,1)S(1)} %get-tuple-element.46), channel_id=1, source_target_pairs={{0,64},{8,72},{16,80},{24,88},{32,96},{40,104},{48,112},{56,120},{... | collective-permute-start | bytes 221192 | tf_op jit(solution)/shard_map/ppermute | solution.py:255
  145.8 4.3 %collective-permute-start.14 = (bf16[2,144,128]{2,1,0:T(8,128)(2,1)S(1)}, bf16[2,144,128]{2,1,0:T(8,128)(2,1)S(1)}, u32[]{:S(2)}, u32[]{:S(2)}) collective-permute-start(bf16[2,144,128]{2,1,0:T(8,128)(2,1)S(1)} %get-tuple-element.46), channel_id=1, source_target_pairs={{0,128},{8,136},{16,144},{24,152},{32,160},{40,168},{48,176},{56,1... | collective-permute-start | bytes 221192 | tf_op jit(solution)/shard_map/ppermute | solution.py:255
  150.1 1.6 collective-permute-start.15
  151.7 2.2 %collective-permute-start.16 = (bf16[2,144,128]{2,1,0:T(8,128)(2,1)S(1)}, bf16[2,144,128]{2,1,0:T(8,128)(2,1)S(1)}, u32[]{:S(2)}, u32[]{:S(2)}) collective-permute-start(bf16[2,144,128]{2,1,0:T(8,128)(2,1)S(1)} %get-tuple-element.46), channel_id=1, source_target_pairs={{0,256},{8,264},{16,272},{24,280},{32,288},{40,296},{48,304},{56,3... | collective-permute-start | bytes 221192 | tf_op jit(solution)/shard_map/ppermute | solution.py:255
  154.0 1.3 collective-permute-start.17
  155.3 1.3 collective-permute-start.18
  156.6 1.5 collective-permute-start.19
  158.1 0.9 shard_map.49.refs_9_
  159.0 4.1 %collective-permute-done.18.refs_5_ = bf16[2,144,128]{2,1,0:T(8,128)(2,1)S(1)} collective-permute-done((bf16[2,144,128]{2,1,0:T(8,128)(2,1)S(1)}, bf16[2,144,128]{2,1,0:T(8,128)(2,1)S(1)}, u32[]{:S(2)}, u32[]{:S(2)}) %collective-permute-start.18) | collective-permute-done | bytes 73760 | tf_op jit(solution)/shard_map/ppermute | solution.py:255
  163.1 1.7 collective-permute-done.19.refs_6_
  164.8 2.5 %shard_map.50 = bf16[1024,256]{1,0:T(8,128)(2,1)S(1)} custom-call(bf16[2,144,128]{2,1,0:T(8,128)(2,1)S(1)} %collective-permute-done.13.refs_0_, bf16[2,144,128]{2,1,0:T(8,128)(2,1)S(1)} %collective-permute-done.14.refs_1_, bf16[2,144,128]{2,1,0:T(8,128)(2,1)S(1)} %collective-permute-done.15.refs_2_, ...), custom_call_target="tpu_custom_call" | custom-call | flops 67108864 | bytes 3286080 | tf_op jit(solution)/shard_map/pallas_call | solution.py:171
  167.3 14.1 %all_to_all.10.sent_ref = bf16[16,64,256]{2,1,0:T(8,128)(2,1)S(1)} all-to-all(bf16[16,64,256]{2,1,0:T(8,128)(2,1)S(1)} %bitcast.31), channel_id=1, replica_groups={{0,1,2,3,4,5,6,7,8,9,10,11,12,13,14,15},{16,17,18,19,20,21,22,23,24,25,..., dimensions={0} | all-to-all | bytes 1048576 | tf_op jit(solution)/shard_map/all_to_all | solution.py:260
  181.4 0.8 shard_map.51
  (52 shorter events, 8.2 us)
Async XLA Ops:
  6.5 26.3 %copy-start.4 = (f32[4,512]{1,0:T(4,128)S(1)}, f32[4,512]{1,0:T(4,128)}, u32[]{:S(2)}) copy-start(f32[4,512]{1,0:T(4,128)} %param.6) | copy-start | bytes 24580
  6.5 29.7 %copy-start.5 = (f32[512]{0:T(512)S(1)}, f32[512]{0:T(512)}, u32[]{:S(2)}) copy-start(f32[512]{0:T(512)} %param.7) | copy-start | bytes 6148
  6.5 50.9 %all-gather.3.cloned.1.call-start = ((), (), s32[]{:S(2)}) async-start(), calls=%async_computation.2 | async-start | bytes 3538944 | tf_op jit(solution)/shard_map/all_gather | solution.py:190
  7.3 76.6 %all-gather.5.cloned.1.call-start = ((), (), s32[]{:S(2)}) async-start(), calls=%async_computation.3 | async-start | bytes 3538944 | tf_op jit(solution)/shard_map/all_gather | solution.py:191
  7.3 10.2 %collective-permute-start.7 = (bf16[64,3072]{1,0:T(8,128)(2,1)}, bf16[64,3072]{1,0:T(8,128)(2,1)S(1)}, u32[]{:S(2)}, u32[]{:S(2)}) collective-permute-start(bf16[64,3072]{1,0:T(8,128)(2,1)} %param.4), channel_id=1, source_target_pairs={{0,8},{8,0},{16,24},{24,16},{32,40},{40,32},{48,56},{56,48},{64,72... | collective-permute-start | bytes 1179656 | tf_op jit(solution)/shard_map/ppermute | solution.py:189
  17.5 0.7 copy-start.3
  18.3 0.9 copy-start
  20.1 30.1 %all-to-all-start = ((bf16[8,48,768]{2,1,0:T(8,128)(2,1)}), bf16[8,48,768]{2,1,0:T(8,128)(2,1)S(1)}, u32[]{:S(2)}, u32[]{:S(2)}) async-start(bf16[8,48,768]{2,1,0:T(8,128)(2,1)} %shard_map.46), calls=%async_computation | async-start | bytes 1179648 | tf_op jit(solution)/shard_map/all_to_all | solution.py:204
  32.8 11.6 %collective-permute-start = (f32[2,512]{1,0:T(2,128)S(1)}, f32[2,512]{1,0:T(2,128)S(1)}, u32[]{:S(2)}, u32[]{:S(2)}) collective-permute-start(f32[2,512]{1,0:T(2,128)S(1)} %get-tuple-element.54), channel_id=1, source_target_pairs={{0,8},{8,0},{16,24},{24,16},{32,40},{40,32},{48,56},{56,48},{64,72... | collective-permute-start | bytes 12296 | tf_op jit(solution)/shard_map/ppermute | solution.py:194
  50.2 16.3 %collective-permute-start.1 = (bf16[8,48,768]{2,1,0:T(8,128)(2,1)S(1)}, bf16[8,48,768]{2,1,0:T(8,128)(2,1)}, u32[]{:S(2)}, u32[]{:S(2)}) collective-permute-start(bf16[8,48,768]{2,1,0:T(8,128)(2,1)S(1)} %all-to-all-done), channel_id=1, source_target_pairs={{0,64},{8,72},{16,80},{24,88},{32,96},{40,104},{48,112},{56,120},{... | collective-permute-start | bytes 1769480 | tf_op jit(solution)/shard_map/ppermute | solution.py:216
  53.4 14.0 %collective-permute-start.2 = (bf16[8,48,768]{2,1,0:T(8,128)(2,1)S(1)}, bf16[8,48,768]{2,1,0:T(8,128)(2,1)S(1)}, u32[]{:S(2)}, u32[]{:S(2)}) collective-permute-start(bf16[8,48,768]{2,1,0:T(8,128)(2,1)S(1)} %all-to-all-done), channel_id=1, source_target_pairs={{0,448},{8,456},{16,464},{24,472},{32,480},{40,488},{48,496},{56,5... | collective-permute-start | bytes 1769480 | tf_op jit(solution)/shard_map/ppermute | solution.py:217
  67.4 20.5 %collective-permute-start.3 = (bf16[8,48,768]{2,1,0:T(8,128)(2,1)}, bf16[8,48,768]{2,1,0:T(8,128)(2,1)}, u32[]{:S(2)}, u32[]{:S(2)}) collective-permute-start(bf16[8,48,768]{2,1,0:T(8,128)(2,1)} %collective-permute-done.1), channel_id=1, source_target_pairs={{0,64},{8,72},{16,80},{24,88},{32,96},{40,104},{48,112},{56,120},{... | collective-permute-start | bytes 1769480 | tf_op jit(solution)/shard_map/ppermute | solution.py:216
  70.6 17.3 %collective-permute-start.4 = (bf16[8,48,768]{2,1,0:T(8,128)(2,1)S(1)}, bf16[8,48,768]{2,1,0:T(8,128)(2,1)S(1)}, u32[]{:S(2)}, u32[]{:S(2)}) collective-permute-start(bf16[8,48,768]{2,1,0:T(8,128)(2,1)S(1)} %collective-permute-done.2), channel_id=1, source_target_pairs={{0,448},{8,456},{16,464},{24,472},{32,480},{40,488},{48,496},{56,5... | collective-permute-start | bytes 1769480 | tf_op jit(solution)/shard_map/ppermute | solution.py:217
  83.8 3.5 %copy-start.1 = (bf16[512,3072]{1,0:T(8,128)(2,1)S(1)}, bf16[512,3072]{1,0:T(8,128)(2,1)}, u32[]{:S(2)}) copy-start(bf16[512,3072]{1,0:T(8,128)(2,1)} %all-gather.5.cloned.1.call-done) | copy-start | bytes 9437188
  87.3 7.2 %copy-start.2 = (bf16[512,3072]{1,0:T(8,128)(2,1)S(1)}, bf16[512,3072]{1,0:T(8,128)(2,1)}, u32[]{:S(2)}) copy-start(bf16[512,3072]{1,0:T(8,128)(2,1)} %all-gather.3.cloned.1.call-done) | copy-start | bytes 9437188
  87.9 17.1 %collective-permute-start.5 = (bf16[8,48,768]{2,1,0:T(8,128)(2,1)}, bf16[8,48,768]{2,1,0:T(8,128)(2,1)S(1)}, u32[]{:S(2)}, u32[]{:S(2)}) collective-permute-start(bf16[8,48,768]{2,1,0:T(8,128)(2,1)} %collective-permute-done.3), channel_id=1, source_target_pairs={{0,64},{8,72},{16,80},{24,88},{32,96},{40,104},{48,112},{56,120},{... | collective-permute-start | bytes 1769480 | tf_op jit(solution)/shard_map/ppermute | solution.py:216
  91.2 14.5 %collective-permute-start.6 = (bf16[8,48,768]{2,1,0:T(8,128)(2,1)S(1)}, bf16[8,48,768]{2,1,0:T(8,128)(2,1)S(1)}, u32[]{:S(2)}, u32[]{:S(2)}) collective-permute-start(bf16[8,48,768]{2,1,0:T(8,128)(2,1)S(1)} %collective-permute-done.4), channel_id=1, source_target_pairs={{0,448},{8,456},{16,464},{24,472},{32,480},{40,488},{48,496},{56,5... | collective-permute-start | bytes 1769480 | tf_op jit(solution)/shard_map/ppermute | solution.py:217
  105.7 10.0 %collective-permute-start.8 = (bf16[4,48,768]{2,1,0:T(8,128)(2,1)S(1)}, bf16[4,48,768]{2,1,0:T(8,128)(2,1)S(1)}, u32[]{:S(2)}, u32[]{:S(2)}) collective-permute-start(bf16[4,48,768]{2,1,0:T(8,128)(2,1)S(1)} %slice.10), channel_id=1, source_target_pairs={{0,64},{8,72},{16,80},{24,88},{32,96},{40,104},{48,112},{56,120},{... | collective-permute-start | bytes 884744 | tf_op jit(solution)/shard_map/ppermute | solution.py:232
  108.0 9.4 %collective-permute-start.9 = (bf16[4,48,768]{2,1,0:T(8,128)(2,1)S(1)}, bf16[4,48,768]{2,1,0:T(8,128)(2,1)S(1)}, u32[]{:S(2)}, u32[]{:S(2)}) collective-permute-start(bf16[4,48,768]{2,1,0:T(8,128)(2,1)S(1)} %slice.11), channel_id=1, source_target_pairs={{0,448},{8,456},{16,464},{24,472},{32,480},{40,488},{48,496},{56,5... | collective-permute-start | bytes 884744 | tf_op jit(solution)/shard_map/ppermute | solution.py:233
  121.0 18.7 %collective-permute-start.10 = (bf16[2,144,128]{2,1,0:T(8,128)(2,1)S(1)}, bf16[2,144,128]{2,1,0:T(8,128)(2,1)S(1)}, u32[]{:S(2)}, u32[]{:S(2)}) collective-permute-start(bf16[2,144,128]{2,1,0:T(8,128)(2,1)S(1)} %get-tuple-element.45.own_ref), channel_id=1, source_target_pairs={{0,16},{8,24},{16,32},{24,40},{32,48},{40,56},{48,0},{56,8},{64,80... | collective-permute-start | bytes 221192 | tf_op jit(solution)/shard_map/ppermute | solution.py:246
  128.9 10.8 %collective-permute-start.11 = (bf16[2,144,128]{2,1,0:T(8,128)(2,1)S(1)}, bf16[2,144,128]{2,1,0:T(8,128)(2,1)S(1)}, u32[]{:S(2)}, u32[]{:S(2)}) collective-permute-start(bf16[2,144,128]{2,1,0:T(8,128)(2,1)S(1)} %get-tuple-element.45.own_ref), channel_id=1, source_target_pairs={{0,32},{8,40},{16,48},{24,56},{32,0},{40,8},{48,16},{56,24},{64,96... | collective-permute-start | bytes 221192 | tf_op jit(solution)/shard_map/ppermute | solution.py:248
  134.8 6.9 %collective-permute-start.12 = (bf16[2,144,128]{2,1,0:T(8,128)(2,1)S(1)}, bf16[2,144,128]{2,1,0:T(8,128)(2,1)S(1)}, u32[]{:S(2)}, u32[]{:S(2)}) collective-permute-start(bf16[2,144,128]{2,1,0:T(8,128)(2,1)S(1)} %get-tuple-element.45.own_ref), channel_id=1, source_target_pairs={{0,48},{8,56},{16,0},{24,8},{32,16},{40,24},{48,32},{56,40},{64,11... | collective-permute-start | bytes 221192 | tf_op jit(solution)/shard_map/ppermute | solution.py:247
  141.8 13.4 %collective-permute-start.13 = (bf16[2,144,128]{2,1,0:T(8,128)(2,1)S(1)}, bf16[2,144,128]{2,1,0:T(8,128)(2,1)S(1)}, u32[]{:S(2)}, u32[]{:S(2)}) collective-permute-start(bf16[2,144,128]{2,1,0:T(8,128)(2,1)S(1)} %get-tuple-element.46), channel_id=1, source_target_pairs={{0,64},{8,72},{16,80},{24,88},{32,96},{40,104},{48,112},{56,120},{... | collective-permute-start | bytes 221192 | tf_op jit(solution)/shard_map/ppermute | solution.py:255
  145.8 10.8 %collective-permute-start.14 = (bf16[2,144,128]{2,1,0:T(8,128)(2,1)S(1)}, bf16[2,144,128]{2,1,0:T(8,128)(2,1)S(1)}, u32[]{:S(2)}, u32[]{:S(2)}) collective-permute-start(bf16[2,144,128]{2,1,0:T(8,128)(2,1)S(1)} %get-tuple-element.46), channel_id=1, source_target_pairs={{0,128},{8,136},{16,144},{24,152},{32,160},{40,168},{48,176},{56,1... | collective-permute-start | bytes 221192 | tf_op jit(solution)/shard_map/ppermute | solution.py:255
  150.1 8.9 %collective-permute-start.15 = (bf16[2,144,128]{2,1,0:T(8,128)(2,1)S(1)}, bf16[2,144,128]{2,1,0:T(8,128)(2,1)S(1)}, u32[]{:S(2)}, u32[]{:S(2)}) collective-permute-start(bf16[2,144,128]{2,1,0:T(8,128)(2,1)S(1)} %get-tuple-element.46), channel_id=1, source_target_pairs={{0,192},{8,200},{16,208},{24,216},{32,224},{40,232},{48,240},{56,2... | collective-permute-start | bytes 221192 | tf_op jit(solution)/shard_map/ppermute | solution.py:255
  151.7 7.2 %collective-permute-start.16 = (bf16[2,144,128]{2,1,0:T(8,128)(2,1)S(1)}, bf16[2,144,128]{2,1,0:T(8,128)(2,1)S(1)}, u32[]{:S(2)}, u32[]{:S(2)}) collective-permute-start(bf16[2,144,128]{2,1,0:T(8,128)(2,1)S(1)} %get-tuple-element.46), channel_id=1, source_target_pairs={{0,256},{8,264},{16,272},{24,280},{32,288},{40,296},{48,304},{56,3... | collective-permute-start | bytes 221192 | tf_op jit(solution)/shard_map/ppermute | solution.py:255
  154.0 5.0 %collective-permute-start.17 = (bf16[2,144,128]{2,1,0:T(8,128)(2,1)S(1)}, bf16[2,144,128]{2,1,0:T(8,128)(2,1)S(1)}, u32[]{:S(2)}, u32[]{:S(2)}) collective-permute-start(bf16[2,144,128]{2,1,0:T(8,128)(2,1)S(1)} %get-tuple-element.46), channel_id=1, source_target_pairs={{0,320},{8,328},{16,336},{24,344},{32,352},{40,360},{48,368},{56,3... | collective-permute-start | bytes 221192 | tf_op jit(solution)/shard_map/ppermute | solution.py:255
  155.3 7.8 %collective-permute-start.18 = (bf16[2,144,128]{2,1,0:T(8,128)(2,1)S(1)}, bf16[2,144,128]{2,1,0:T(8,128)(2,1)S(1)}, u32[]{:S(2)}, u32[]{:S(2)}) collective-permute-start(bf16[2,144,128]{2,1,0:T(8,128)(2,1)S(1)} %get-tuple-element.46), channel_id=1, source_target_pairs={{0,384},{8,392},{16,400},{24,408},{32,416},{40,424},{48,432},{56,4... | collective-permute-start | bytes 221192 | tf_op jit(solution)/shard_map/ppermute | solution.py:255
  156.6 8.2 %collective-permute-start.19 = (bf16[2,144,128]{2,1,0:T(8,128)(2,1)S(1)}, bf16[2,144,128]{2,1,0:T(8,128)(2,1)S(1)}, u32[]{:S(2)}, u32[]{:S(2)}) collective-permute-start(bf16[2,144,128]{2,1,0:T(8,128)(2,1)S(1)} %get-tuple-element.46), channel_id=1, source_target_pairs={{0,448},{8,456},{16,464},{24,472},{32,480},{40,488},{48,496},{56,5... | collective-permute-start | bytes 221192 | tf_op jit(solution)/shard_map/ppermute | solution.py:255
Sparse Core Ops, SparseCore 0:
  9.5 38.9 all-gather.2
  50.6 33.1 all-gather.4

commit v2 on v1

--- a/solution.py
+++ b/solution.py
@@ -19,11 +19,8 @@
 VMEM = pltpu.VMEM
 
 Z_GROUPS = [[y * NZ + z for z in range(NZ)] for y in range(NY)]
+ROW_GROUPS = [[y * NZ + p + 2 * i for i in range(4)] for y in range(NY) for p in range(2)]
 OUT_GROUPS = [[g * 16 + i for i in range(16)] for g in range(NY * NZ // 2)]
-
-
-def z_shift(d):
-    return [(y * NZ + z, y * NZ + (z + d) % NZ) for y in range(NY) for z in range(NZ)]
 
 
 def y_shift(d):
@@ -79,7 +76,7 @@
             out_ref[:, (h * 2 + s) * 256 : (h * 2 + s + 1) * 256] = sent_ref[s * NH + h]
 
 
-def states_kernel(side_ref, own_ref, other_ref, col_ref, row_ref, proj_ref, prefix_ref, total_ref, message_ref):
+def states_kernel(side_ref, own_ref, other_ref, col_ref, row_ref, proj_ref, prefix_ref, message_ref):
     side = side_ref[0]
     proj_ref[side] = own_ref[...].astype(BF16)
     proj_ref[1 - side] = other_ref[...].astype(BF16)
@@ -97,8 +94,8 @@
             scaled = (keys.astype(F32) * scale).astype(BF16)
             state = jnp.exp(last) * state + mm(scaled, values, (((0,), (0,)), ((), ())))
             decay = decay + last
-        total_ref[head] = state
-        write_message(message_ref, head, state, decay)
+        for copy in range(4):
+            write_message(message_ref.at[copy], head, state, decay)
 
 
 def local_kernel(proj_ref, prefix_ref, col_ref, row_ref, out_ref):
@@ -118,27 +115,24 @@
             out_ref[at] = mm(scores.astype(BF16), values) + mm(scaled, prefix_ref[at])
 
 
-def row_kernel(place_ref, total_ref, own_ref, m1_ref, m2_ref, m3_ref, before_ref, decay_ref, message_ref):
+def row_kernel(place_ref, messages_ref, before_ref, decay_ref, message_ref):
     place = place_ref[0]
-    messages = (None, m1_ref, m2_ref, m3_ref)
-    for head in range(2):
-        mine = read_decay(own_ref, head)
-        decays = [mine] + [read_decay(messages[k], head) for k in range(1, 4)]
+    for head in range(2):
         before = jnp.zeros((E, E), F32)
-        later = jnp.zeros((E, E), F32)
+        total = jnp.zeros((E, E), F32)
         gone_before = jnp.zeros((1, E), F32)
-        gone_later = jnp.zeros((1, E), F32)
-        for k in range(1, 4):
-            block = messages[k][head, :E, :].astype(F32)
-            early = place >= k
+        gone = jnp.zeros((1, E), F32)
+        for k in (3, 2, 1, 0):
+            block = messages_ref[k, head, :E, :].astype(F32)
+            decay = read_decay(messages_ref.at[k], head)
+            total = total + jnp.exp(gone) * block
+            gone = gone + decay
+            early = k < place
             before = before + jnp.where(early, jnp.exp(gone_before), 0.0) * block
-            later = later + jnp.where(early, 0.0, jnp.exp(gone_later)) * block
-            gone_before = gone_before + jnp.where(early, decays[k], 0.0)
-            gone_later = gone_later + jnp.where(early, 0.0, decays[k])
-        through = jnp.exp(mine) * before + total_ref[head]
+            gone_before = gone_before + jnp.where(early, decay, 0.0)
         before_ref[head] = before
         decay_ref[head] = jnp.broadcast_to(gone_before, (8, E))
-        write_message(message_ref, head, later + jnp.exp(gone_later) * through, gone_before + mine + gone_later)
+        write_message(message_ref, head, total, gone)
 
 
 def final_kernel(*refs):
@@ -186,12 +180,35 @@
     side1 = side.reshape(1).astype(jnp.int32)
     place1 = place.reshape(1).astype(jnp.int32)
 
-    pair_tokens = lax.ppermute(tokens, "seq", PAIR)
+    (pieces,) = call(pieces_kernel, [((NZ, 48, 768), BF16)], [], qkv_weight.transpose(1, 0, 2))
+    block = lax.all_to_all(pieces, "seq", split_axis=0, concat_axis=0, tiled=True, axis_index_groups=Z_GROUPS)
+
     own_rows = lax.all_gather(tokens, "head", axis=0, tiled=True)
-    other_rows = lax.all_gather(pair_tokens, "head", axis=0, tiled=True)
+
+
+    def add(total, tok, part, offset):
+        x = lax.dynamic_slice_in_dim(tok, ((y + offset) % NY) * (NZ * 48), NZ * 48, 1)
+        d = jnp.dot(x, part.reshape(NZ * 48, 768), preferred_element_type=F32)
+        return d if total is None else total + d
+
+    ups, downs = [block], [block]
+
+    def hop(*earlier):
+        ups.append(lax.ppermute(after(ups[-1], *earlier), "seq", y_shift(1)))
+        downs.append(lax.ppermute(after(downs[-1], *earlier), "seq", y_shift(-1)))
+
+    def add_step(total, tok, step):
+        if step == 0:
+            return add(total, tok, block, 0)
+        return add(add(total, tok, ups[step], -step), tok, downs[step], step)
+
+    hop()
+    pair_tokens = lax.ppermute(after(tokens, block), "seq", PAIR)
+    own = add_step(None, own_rows, 0)
 
     mine = lax.dynamic_slice_in_dim(log_decay, side * 2, 2, 0)
-    theirs = lax.ppermute(lax.dynamic_slice_in_dim(log_decay, (1 - side) * 2, 2, 0), "seq", PAIR)
+    wanted = lax.dynamic_slice_in_dim(log_decay, (1 - side) * 2, 2, 0)
+    theirs = lax.ppermute(after(wanted, block), "seq", PAIR)
     both = jnp.where(side == 0, jnp.concatenate([mine, theirs], 1), jnp.concatenate([theirs, mine], 1))
     rows = jnp.cumsum(both.reshape(2, 8, BLK), axis=2)
     ends = rows[:, :, -1]
@@ -200,57 +217,34 @@
     cols = rows.T
     gain = lax.dynamic_slice_in_dim(norm_gain, side * 256, 256, 0).reshape(1, 256)
 
-    (pieces,) = call(pieces_kernel, [((NZ, 48, 768), BF16)], [], qkv_weight.transpose(1, 0, 2))
-    block = lax.all_to_all(pieces, "seq", split_axis=0, concat_axis=0, tiled=True, axis_index_groups=Z_GROUPS)
-    block, rows, cols, starts, gain = lax.optimization_barrier((block, rows, cols, starts, gain))
-
-    def add(total, tok, part, offset):
-        x = lax.dynamic_slice_in_dim(tok, ((y + offset) % NY) * (NZ * 48), NZ * 48, 1)
-        d = jnp.dot(x, part.reshape(NZ * 48, 768), preferred_element_type=F32)
-        return d if total is None else total + d
-
-    ups, downs = [block], [block]
-
-    def hop(*earlier):
-        up, down = lax.optimization_barrier((ups[-1], downs[-1]) + earlier)[:2]
-        ups.append(lax.ppermute(up, "seq", y_shift(1)))
-        downs.append(lax.ppermute(down, "seq", y_shift(-1)))
-
-    def add_step(total, tok, step):
-        if step == 0:
-            return add(total, tok, block, 0)
-        return add(add(total, tok, ups[step], -step), tok, downs[step], step)
-
+    first = (ups[1], downs[1], own, rows, cols, starts, gain)
+    other_rows = lax.all_gather(after(pair_tokens, *first), "head", axis=0, tiled=True)
     hop()
-    own = add_step(None, own_rows, 0)
-    hop(own)
     own = add_step(own, own_rows, 1)
     hop(own)
     own = add_step(own, own_rows, 2)
-    other = add_step(add_step(None, other_rows, 0), other_rows, 1)
-    up, down = lax.optimization_barrier((ups[3], downs[3], own, other))[:2]
-    up4 = lax.ppermute(up[:4], "seq", y_shift(1))
-    down4 = lax.ppermute(down[4:], "seq", y_shift(-1))
+    up4 = lax.ppermute(after(ups[3], own)[:4], "seq", y_shift(1))
+    down4 = lax.ppermute(after(downs[3], own)[4:], "seq", y_shift(-1))
     own = add_step(own, own_rows, 3)
-    other = add_step(add_step(other, other_rows, 2), other_rows, 3)
+    other = None
+    for step in range(4):
+        other = add_step(other, other_rows, step)
     up4, down4, own, other = lax.optimization_barrier((up4, down4, own, other))
     last = jnp.concatenate([up4, down4], 0)
     own = add(own, own_rows, last, 4)
     other = add(other, other_rows, last, 4)
 
-    proj, prefix, total, message = call(
+    proj, prefix, messages = call(
         states_kernel,
-        [((2, 512, 768), BF16), ((16, E, E), BF16), ((2, E, E), F32), ((2, E + EXTRA, E), BF16)],
+        [((2, 512, 768), BF16), ((16, E, E), BF16), ((4, 2, E + EXTRA, E), BF16)],
         [side1], own, other, cols, rows, flops=16 * 2 * E**3,
     )
-    m1 = lax.ppermute(message, "seq", z_shift(2))
-    m3 = lax.ppermute(message, "seq", z_shift(-2))
-    m2 = lax.ppermute(message, "seq", z_shift(4))
+    messages = lax.all_to_all(messages, "seq", split_axis=0, concat_axis=0, tiled=True, axis_index_groups=ROW_GROUPS)
     (part,) = call(local_kernel, [((16, BLK, E), F32)], [], proj, prefix, cols, rows, flops=16 * 6 * E**3)
     before, gone, row_message = call(
         row_kernel,
         [((2, E, E), F32), ((2, 8, E), F32), ((2, E + EXTRA, E), BF16)],
-        [place1], total, message, m1, m2, m3,
+        [place1], messages,
     )
     earlier = [lax.ppermute(row_message, "seq", y_later(k)) for k in range(1, NY)]
     (flat,) = call(

time: 190 us -> 178 us (0.937)
  starting transfers between devices: 83.7 us -> 60.8 us
  blocking collectives: 14.1 us -> 18.4 us
  waiting for transfers between devices: 49.8 us -> 53.5 us
    ppermute x13 -> x10, starting transfers between devices: 54.8 us -> 30.5 us  [the longest x3 11.9 us: hop(): downs.append(lax.ppermute(after(downs[-1], *earlier), 'seq', y_shift(-1)))]
    all_to_all x1, waiting for transfers between devices: 4.47 us -> 19.3 us  [on_device(): lax.all_to_all(pieces, 'seq', split_axis=0, concat_axis=0, tiled=True, ax...]
    ppermute x13 -> x10, waiting for transfers between devices: 32.8 us -> 19.6 us  [the longest x3 12.9 us: hop(): ups.append(lax.ppermute(after(ups[-1], *earlier), 'seq', y_shift(1)))]
    all_to_all x0 -> x1, waiting for transfers between devices: none -> 8.84 us  [on_device(): lax.all_to_all(messages, 'seq', split_axis=0, concat_axis=0, tiled=True,...]
    all_gather x1, waiting for transfers between devices: 5.99 us -> 0.02 us  [on_device(): lax.all_gather(after(pair_tokens, *first), 'head', axis=0, tiled=True)]
    all_to_all x1, blocking collectives: 14.1 us -> 18.4 us  [on_device(): lax.all_to_all(flat.reshape(16, 64, 256), ('seq', 'head'), split_axis=0,...]
    all_to_all x0 -> x1, starting transfers between devices: none -> 3.45 us  [on_device(): lax.all_to_all(messages, 'seq', split_axis=0, concat_axis=0, tiled=True,...]
  transfers between devices with their start and end apart: 23 -> 21, of which waited for: 13 -> 9; matrix products, arithmetic and copies ran while one was open for 9% -> 9% of each run, Pallas kernels for 1% -> 1%
where the time goes in v2:
time: 178 us; the launch traced here: 177 us
  starting transfers between devices  60.8 us (34%)
  waiting for transfers between devices  53.5 us (30%)
  blocking collectives  18.4 us (10%)
  matrix products  15.7 us (9%)
  between operations  14.1 us (8%)
  Pallas kernels  7.89 us (4%)
  local copies, waits for them, and re-layouts  3.97 us (2%)
  other arithmetic  2.31 us (1%)
    all_to_all x1, waiting for transfers between devices, on_device(): lax.all_to_all(pieces, 'seq', split_axis=0, concat_axis=0, tiled=True, ax...  19.3 us
    all_to_all x1, blocking collectives, on_device(): lax.all_to_all(flat.reshape(16, 64, 256), ('seq', 'head'), split_axis=0,...  18.4 us
    ppermute x7, starting transfers between devices, on_device(): lax.ppermute(row_message, 'seq', y_later(k))  16 us
    dot_general x16, matrix products, add(): d = jnp.dot(x, part.reshape(NZ * 48, 768), preferred_element_type=F32)  15.7 us
    ppermute x3, waiting for transfers between devices, hop(): ups.append(lax.ppermute(after(ups[-1], *earlier), 'seq', y_shift(1)))  12.9 us
    ppermute x3, starting transfers between devices, hop(): downs.append(lax.ppermute(after(downs[-1], *earlier), 'seq', y_shift(-1)))  11.9 us
    all_to_all x1, starting transfers between devices, on_device(): lax.all_to_all(pieces, 'seq', split_axis=0, concat_axis=0, tiled=True, ax...  10.9 us
    all_to_all x1, waiting for transfers between devices, on_device(): lax.all_to_all(messages, 'seq', split_axis=0, concat_axis=0, tiled=True,...  8.84 us
  transfers between devices with their start and end apart: 21, of which 9 were waited for; matrix products, arithmetic and copies ran while one was open for 9% of the time, Pallas kernels for 1%

profile of v2, /device:TPU:1, one launch (start us, length us, event | category | flops | bytes accessed | tf_op | source)
XLA Modules:
  0.0 176.8 jit_solution(8806815080873365975)
XLA Ops:
  6.5 0.7 all-gather.3.cloned.1.call-update
  7.3 0.9 copy-done
  8.2 0.9 shard_map.46
  9.0 10.9 %all-to-all-start = ((bf16[8,48,768]{2,1,0:T(8,128)(2,1)}), bf16[8,48,768]{2,1,0:T(8,128)(2,1)S(1)}, u32[]{:S(2)}, u32[]{:S(2)}) async-start(bf16[8,48,768]{2,1,0:T(8,128)(2,1)} %shard_map.46), calls=%async_computation | async-start | bytes 1179648 | tf_op jit(solution)/shard_map/all_to_all | solution.py:184
  20.0 19.3 %all-to-all-done = bf16[8,48,768]{2,1,0:T(8,128)(2,1)S(1)} async-done(((bf16[8,48,768]{2,1,0:T(8,128)(2,1)}), bf16[8,48,768]{2,1,0:T(8,128)(2,1)S(1)}, u32[]{:S(2)}, u32[]{:S(2)}) %all-to-all-start) | async-done | bytes 589856 | tf_op jit(solution)/shard_map/all_to_all | solution.py:184
  39.3 3.2 %collective-permute-start = (bf16[8,48,768]{2,1,0:T(8,128)(2,1)S(1)}, bf16[8,48,768]{2,1,0:T(8,128)(2,1)S(1)}, u32[]{:S(2)}, u32[]{:S(2)}) collective-permute-start(bf16[8,48,768]{2,1,0:T(8,128)(2,1)S(1)} %all-to-all-done), channel_id=1, source_target_pairs={{0,64},{8,72},{16,80},{24,88},{32,96},{40,104},{48,112},{56,120},{... | collective-permute-start | bytes 1769480 | tf_op jit(solution)/shard_map/ppermute | solution.py:197
  42.5 3.8 %collective-permute-start.2 = (bf16[8,48,768]{2,1,0:T(8,128)(2,1)S(1)}, bf16[8,48,768]{2,1,0:T(8,128)(2,1)S(1)}, u32[]{:S(2)}, u32[]{:S(2)}) collective-permute-start(bf16[8,48,768]{2,1,0:T(8,128)(2,1)S(1)} %all-to-all-done), channel_id=1, source_target_pairs={{0,448},{8,456},{16,464},{24,472},{32,480},{40,488},{48,496},{56,5... | collective-permute-start | bytes 1769480 | tf_op jit(solution)/shard_map/ppermute | solution.py:198
  46.3 1.9 %collective-permute-start.9 = (f32[2,512]{1,0:T(2,128)S(1)}, f32[2,512]{1,0:T(2,128)S(1)}, u32[]{:S(2)}, u32[]{:S(2)}) collective-permute-start(f32[2,512]{1,0:T(2,128)S(1)} %get-tuple-element.27), channel_id=1, source_target_pairs={{0,8},{8,0},{16,24},{24,16},{32,40},{40,32},{48,56},{56,48},{64,72... | collective-permute-start | bytes 12296 | tf_op jit(solution)/shard_map/ppermute | solution.py:211
  48.4 3.4 %collective-permute-start.8 = (bf16[64,3072]{1,0:T(8,128)(2,1)}, bf16[64,3072]{1,0:T(8,128)(2,1)}, u32[]{:S(2)}, u32[]{:S(2)}) collective-permute-start(bf16[64,3072]{1,0:T(8,128)(2,1)} %param.4), channel_id=1, source_target_pairs={{0,8},{8,0},{16,24},{24,16},{32,40},{40,32},{48,56},{56,48},{64,72... | collective-permute-start | bytes 1179656 | tf_op jit(solution)/shard_map/ppermute | solution.py:206
  51.8 0.6 reduce_window_sum.24
  53.0 1.6 fusion.35
  54.6 5.3 %collective-permute-done.8 = bf16[64,3072]{1,0:T(8,128)(2,1)} collective-permute-done((bf16[64,3072]{1,0:T(8,128)(2,1)}, bf16[64,3072]{1,0:T(8,128)(2,1)}, u32[]{:S(2)}, u32[]{:S(2)}) %collective-permute-start.8) | collective-permute-done | bytes 393248 | tf_op jit(solution)/shard_map/ppermute | solution.py:206
  60.1 1.9 %collective-permute-start.1 = (bf16[8,48,768]{2,1,0:T(8,128)(2,1)S(1)}, bf16[8,48,768]{2,1,0:T(8,128)(2,1)S(1)}, u32[]{:S(2)}, u32[]{:S(2)}) collective-permute-start(bf16[8,48,768]{2,1,0:T(8,128)(2,1)S(1)} %collective-permute-done), channel_id=1, source_target_pairs={{0,64},{8,72},{16,80},{24,88},{32,96},{40,104},{48,112},{56,120},{... | collective-permute-start | bytes 1769480 | tf_op jit(solution)/shard_map/ppermute | solution.py:197
  62.0 4.6 %collective-permute-start.4 = (bf16[8,48,768]{2,1,0:T(8,128)(2,1)S(1)}, bf16[8,48,768]{2,1,0:T(8,128)(2,1)S(1)}, u32[]{:S(2)}, u32[]{:S(2)}) collective-permute-start(bf16[8,48,768]{2,1,0:T(8,128)(2,1)S(1)} %collective-permute-done.2), channel_id=1, source_target_pairs={{0,448},{8,456},{16,464},{24,472},{32,480},{40,488},{48,496},{56,5... | collective-permute-start | bytes 1769480 | tf_op jit(solution)/shard_map/ppermute | solution.py:198
  66.6 1.6 fusion.33
  68.2 1.7 add_add_fusion.3
  69.9 5.8 %collective-permute-done.1 = bf16[8,48,768]{2,1,0:T(8,128)(2,1)S(1)} collective-permute-done((bf16[8,48,768]{2,1,0:T(8,128)(2,1)S(1)}, bf16[8,48,768]{2,1,0:T(8,128)(2,1)S(1)}, u32[]{:S(2)}, u32[]{:S(2)}) %collective-permute-start.1) | collective-permute-done | bytes 589856 | tf_op jit(solution)/shard_map/ppermute | solution.py:197
  75.7 2.1 %collective-permute-start.3 = (bf16[8,48,768]{2,1,0:T(8,128)(2,1)S(1)}, bf16[8,48,768]{2,1,0:T(8,128)(2,1)S(1)}, u32[]{:S(2)}, u32[]{:S(2)}) collective-permute-start(bf16[8,48,768]{2,1,0:T(8,128)(2,1)S(1)} %collective-permute-done.1), channel_id=1, source_target_pairs={{0,64},{8,72},{16,80},{24,88},{32,96},{40,104},{48,112},{56,120},{... | collective-permute-start | bytes 1769480 | tf_op jit(solution)/shard_map/ppermute | solution.py:197
  77.9 0.9 collective-permute-done.4
  78.7 3.5 %collective-permute-start.6 = (bf16[8,48,768]{2,1,0:T(8,128)(2,1)S(1)}, bf16[8,48,768]{2,1,0:T(8,128)(2,1)S(1)}, u32[]{:S(2)}, u32[]{:S(2)}) collective-permute-start(bf16[8,48,768]{2,1,0:T(8,128)(2,1)S(1)} %collective-permute-done.4), channel_id=1, source_target_pairs={{0,448},{8,456},{16,464},{24,472},{32,480},{40,488},{48,496},{56,5... | collective-permute-start | bytes 1769480 | tf_op jit(solution)/shard_map/ppermute | solution.py:198
  82.3 0.6 fusion.30
  83.4 7.1 %collective-permute-done.3 = bf16[8,48,768]{2,1,0:T(8,128)(2,1)S(1)} collective-permute-done((bf16[8,48,768]{2,1,0:T(8,128)(2,1)S(1)}, bf16[8,48,768]{2,1,0:T(8,128)(2,1)S(1)}, u32[]{:S(2)}, u32[]{:S(2)}) %collective-permute-start.3) | collective-permute-done | bytes 589856 | tf_op jit(solution)/shard_map/ppermute | solution.py:197
  90.5 0.7 slice.9
  91.2 1.9 %collective-permute-start.5 = (bf16[4,48,768]{2,1,0:T(8,128)(2,1)}, bf16[4,48,768]{2,1,0:T(8,128)(2,1)}, u32[]{:S(2)}, u32[]{:S(2)}) collective-permute-start(bf16[4,48,768]{2,1,0:T(8,128)(2,1)} %slice.9), channel_id=1, source_target_pairs={{0,64},{8,72},{16,80},{24,88},{32,96},{40,104},{48,112},{56,120},{... | collective-permute-start | bytes 884744 | tf_op jit(solution)/shard_map/ppermute | solution.py:226
  93.6 0.8 slice.10
  94.4 4.1 %collective-permute-start.7 = (bf16[4,48,768]{2,1,0:T(8,128)(2,1)}, bf16[4,48,768]{2,1,0:T(8,128)(2,1)}, u32[]{:S(2)}, u32[]{:S(2)}) collective-permute-start(bf16[4,48,768]{2,1,0:T(8,128)(2,1)} %slice.10), channel_id=1, source_target_pairs={{0,448},{8,456},{16,464},{24,472},{32,480},{40,488},{48,496},{56,5... | collective-permute-start | bytes 884744 | tf_op jit(solution)/shard_map/ppermute | solution.py:227
  99.1 0.6 add_add_fusion.1
  99.7 1.7 fusion.8
  101.4 1.8 %fusion.10 = f32[512,768]{1,0:T(8,128)S(1)} fusion(bf16[384,768]{1,0:T(8,128)(2,1)} %bitcast.51, bf16[512,3072]{1,0:T(8,128)(2,1)} %all-gather.5.cloned.1.call-done, s32[]{:T(128)S(6)} %select_n.129), kind=kOutput, calls=%fused_computation.13 | convolution fusion | flops 301989888 | bytes 2555908 | tf_op jit(solution)/shard_map/dot_general | solution.py:191
  103.3 0.6 fusion.12
  106.5 0.7 add_add_fusion
  107.3 1.1 pad_maximum_fusion
  108.4 1.6 fusion.2
  110.9 2.7 %shard_map.47 = (bf16[2,512,768]{2,1,0:T(8,128)(2,1)S(1)}, bf16[16,128,128]{2,1,0:T(8,128)(2,1)S(1)}, bf16[4,2,144,128]{3,2,1,0:T(8,128)(2,1)}) custom-call(s32[1]{0:T(128)} %bitcast.1.side_ref, f32[512,768]{1,0:T(8,128)S(1)} %add.192.own_ref, f32[512,768]{1,0:T(8,128)S(1)} %add.193.other_ref, f32[128,16]{1,0:T(8,128)S(1)} %bitcast.32, f32[16,128]{1,0:T(8,128)S(1)} %bitcast.36), custom_call_target="tpu_custom_call" | custom-call | flops 67108864 | bytes 3162112 | tf_op jit(solution)/shard_map/pallas_call | solution.py:165
  113.6 3.5 %all-to-all-start.1 = ((bf16[4,2,144,128]{3,2,1,0:T(8,128)(2,1)}), bf16[4,2,144,128]{3,2,1,0:T(8,128)(2,1)S(1)}, u32[]{:S(2)}, u32[]{:S(2)}) async-start(bf16[4,2,144,128]{3,2,1,0:T(8,128)(2,1)} %get-tuple-element.33), calls=%async_computation.1 | async-start | bytes 589824 | tf_op jit(solution)/shard_map/all_to_all | solution.py:242
  117.1 8.8 %all-to-all-done.1.messages_ref = bf16[4,2,144,128]{3,2,1,0:T(8,128)(2,1)S(1)} async-done(((bf16[4,2,144,128]{3,2,1,0:T(8,128)(2,1)}), bf16[4,2,144,128]{3,2,1,0:T(8,128)(2,1)S(1)}, u32[]{:S(2)}, u32[]{:S(2)}) %all-to-all-start.1) | async-done | bytes 294944 | tf_op jit(solution)/shard_map/all_to_all | solution.py:242
  126.1 1.6 collective-permute-start.10
  127.6 4.4 %collective-permute-start.11 = (bf16[2,144,128]{2,1,0:T(8,128)(2,1)S(1)}, bf16[2,144,128]{2,1,0:T(8,128)(2,1)S(1)}, u32[]{:S(2)}, u32[]{:S(2)}) collective-permute-start(bf16[2,144,128]{2,1,0:T(8,128)(2,1)S(1)} %get-tuple-element.34), channel_id=1, source_target_pairs={{0,128},{8,136},{16,144},{24,152},{32,160},{40,168},{48,176},{56,1... | collective-permute-start | bytes 221192 | tf_op jit(solution)/shard_map/ppermute | solution.py:249
  132.1 4.3 %collective-permute-start.12 = (bf16[2,144,128]{2,1,0:T(8,128)(2,1)S(1)}, bf16[2,144,128]{2,1,0:T(8,128)(2,1)S(1)}, u32[]{:S(2)}, u32[]{:S(2)}) collective-permute-start(bf16[2,144,128]{2,1,0:T(8,128)(2,1)S(1)} %get-tuple-element.34), channel_id=1, source_target_pairs={{0,192},{8,200},{16,208},{24,216},{32,224},{40,232},{48,240},{56,2... | collective-permute-start | bytes 221192 | tf_op jit(solution)/shard_map/ppermute | solution.py:249
  136.4 1.6 collective-permute-start.13
  138.1 1.3 collective-permute-start.14
  139.4 1.3 collective-permute-start.15
  140.7 1.5 collective-permute-start.16
  142.2 0.9 shard_map.49.refs_9_
  143.4 4.7 %collective-permute-done.16.refs_6_ = bf16[2,144,128]{2,1,0:T(8,128)(2,1)S(1)} collective-permute-done((bf16[2,144,128]{2,1,0:T(8,128)(2,1)S(1)}, bf16[2,144,128]{2,1,0:T(8,128)(2,1)S(1)}, u32[]{:S(2)}, u32[]{:S(2)}) %collective-permute-start.16) | collective-permute-done | bytes 73760 | tf_op jit(solution)/shard_map/ppermute | solution.py:249
  148.2 2.5 %shard_map.50 = bf16[1024,256]{1,0:T(8,128)(2,1)S(1)} custom-call(bf16[2,144,128]{2,1,0:T(8,128)(2,1)S(1)} %collective-permute-done.10.refs_0_, bf16[2,144,128]{2,1,0:T(8,128)(2,1)S(1)} %collective-permute-done.11.refs_1_, bf16[2,144,128]{2,1,0:T(8,128)(2,1)S(1)} %collective-permute-done.12.refs_2_, ...), custom_call_target="tpu_custom_call" | custom-call | flops 67108864 | bytes 3286080 | tf_op jit(solution)/shard_map/pallas_call | solution.py:165
  150.7 18.4 %all_to_all.15.sent_ref = bf16[16,64,256]{2,1,0:T(8,128)(2,1)S(1)} all-to-all(bf16[16,64,256]{2,1,0:T(8,128)(2,1)S(1)} %bitcast.31), channel_id=1, replica_groups={{0,1,2,3,4,5,6,7,8,9,10,11,12,13,14,15},{16,17,18,19,20,21,22,23,24,25,..., dimensions={0} | all-to-all | bytes 1048576 | tf_op jit(solution)/shard_map/all_to_all | solution.py:254
  169.1 0.8 shard_map.51
  (60 shorter events, 6.6 us)
Async XLA Ops:
  6.5 39.7 %copy-start.10 = (f32[4,512]{1,0:T(4,128)S(1)}, f32[4,512]{1,0:T(4,128)}, u32[]{:S(2)}) copy-start(f32[4,512]{1,0:T(4,128)} %param.6) | copy-start | bytes 24580
  6.5 41.8 %copy-start.11 = (f32[512]{0:T(512)S(1)}, f32[512]{0:T(512)}, u32[]{:S(2)}) copy-start(f32[512]{0:T(512)} %param.7) | copy-start | bytes 6148
  6.5 46.5 %all-gather.3.cloned.1.call-start = ((), (), s32[]{:S(2)}) async-start(), calls=%async_computation.3 | async-start | bytes 3538944 | tf_op jit(solution)/shard_map/all_gather | solution.py:186
  7.3 0.9 copy-start
  9.0 30.2 %all-to-all-start = ((bf16[8,48,768]{2,1,0:T(8,128)(2,1)}), bf16[8,48,768]{2,1,0:T(8,128)(2,1)S(1)}, u32[]{:S(2)}, u32[]{:S(2)}) async-start(bf16[8,48,768]{2,1,0:T(8,128)(2,1)} %shard_map.46), calls=%async_computation | async-start | bytes 1179648 | tf_op jit(solution)/shard_map/all_to_all | solution.py:184
  19.9 79.8 %all-gather.5.cloned.1.call-start = ((), (), s32[]{:S(2)}) async-start(), calls=%async_computation.4 | async-start | bytes 3538944 | tf_op jit(solution)/shard_map/all_gather | solution.py:221
  39.3 20.6 %collective-permute-start = (bf16[8,48,768]{2,1,0:T(8,128)(2,1)S(1)}, bf16[8,48,768]{2,1,0:T(8,128)(2,1)S(1)}, u32[]{:S(2)}, u32[]{:S(2)}) collective-permute-start(bf16[8,48,768]{2,1,0:T(8,128)(2,1)S(1)} %all-to-all-done), channel_id=1, source_target_pairs={{0,64},{8,72},{16,80},{24,88},{32,96},{40,104},{48,112},{56,120},{... | collective-permute-start | bytes 1769480 | tf_op jit(solution)/shard_map/ppermute | solution.py:197
  42.5 17.4 %collective-permute-start.2 = (bf16[8,48,768]{2,1,0:T(8,128)(2,1)S(1)}, bf16[8,48,768]{2,1,0:T(8,128)(2,1)S(1)}, u32[]{:S(2)}, u32[]{:S(2)}) collective-permute-start(bf16[8,48,768]{2,1,0:T(8,128)(2,1)S(1)} %all-to-all-done), channel_id=1, source_target_pairs={{0,448},{8,456},{16,464},{24,472},{32,480},{40,488},{48,496},{56,5... | collective-permute-start | bytes 1769480 | tf_op jit(solution)/shard_map/ppermute | solution.py:198
  46.3 5.4 %collective-permute-start.9 = (f32[2,512]{1,0:T(2,128)S(1)}, f32[2,512]{1,0:T(2,128)S(1)}, u32[]{:S(2)}, u32[]{:S(2)}) collective-permute-start(f32[2,512]{1,0:T(2,128)S(1)} %get-tuple-element.27), channel_id=1, source_target_pairs={{0,8},{8,0},{16,24},{24,16},{32,40},{40,32},{48,56},{56,48},{64,72... | collective-permute-start | bytes 12296 | tf_op jit(solution)/shard_map/ppermute | solution.py:211
  48.4 11.5 %collective-permute-start.8 = (bf16[64,3072]{1,0:T(8,128)(2,1)}, bf16[64,3072]{1,0:T(8,128)(2,1)}, u32[]{:S(2)}, u32[]{:S(2)}) collective-permute-start(bf16[64,3072]{1,0:T(8,128)(2,1)} %param.4), channel_id=1, source_target_pairs={{0,8},{8,0},{16,24},{24,16},{32,40},{40,32},{48,56},{56,48},{64,72... | collective-permute-start | bytes 1179656 | tf_op jit(solution)/shard_map/ppermute | solution.py:206
  59.9 8.3 %copy-start.6 = (bf16[8,48,768]{2,1,0:T(8,128)(2,1)}, bf16[8,48,768]{2,1,0:T(8,128)(2,1)S(1)}, u32[]{:S(2)}) copy-start(bf16[8,48,768]{2,1,0:T(8,128)(2,1)S(1)} %collective-permute-done) | copy-start | bytes 1769476
  60.1 15.7 %collective-permute-start.1 = (bf16[8,48,768]{2,1,0:T(8,128)(2,1)S(1)}, bf16[8,48,768]{2,1,0:T(8,128)(2,1)S(1)}, u32[]{:S(2)}, u32[]{:S(2)}) collective-permute-start(bf16[8,48,768]{2,1,0:T(8,128)(2,1)S(1)} %collective-permute-done), channel_id=1, source_target_pairs={{0,64},{8,72},{16,80},{24,88},{32,96},{40,104},{48,112},{56,120},{... | collective-permute-start | bytes 1769480 | tf_op jit(solution)/shard_map/ppermute | solution.py:197
  62.0 16.7 %collective-permute-start.4 = (bf16[8,48,768]{2,1,0:T(8,128)(2,1)S(1)}, bf16[8,48,768]{2,1,0:T(8,128)(2,1)S(1)}, u32[]{:S(2)}, u32[]{:S(2)}) collective-permute-start(bf16[8,48,768]{2,1,0:T(8,128)(2,1)S(1)} %collective-permute-done.2), channel_id=1, source_target_pairs={{0,448},{8,456},{16,464},{24,472},{32,480},{40,488},{48,496},{56,5... | collective-permute-start | bytes 1769480 | tf_op jit(solution)/shard_map/ppermute | solution.py:198
  68.1 14.1 %copy-start.3 = (bf16[512,3072]{1,0:T(8,128)(2,1)S(1)}, bf16[512,3072]{1,0:T(8,128)(2,1)}, u32[]{:S(2)}) copy-start(bf16[512,3072]{1,0:T(8,128)(2,1)} %all-gather.3.cloned.1.call-done) | copy-start | bytes 9437188
  75.7 7.7 %copy-start.8 = (bf16[8,48,768]{2,1,0:T(8,128)(2,1)}, bf16[8,48,768]{2,1,0:T(8,128)(2,1)S(1)}, u32[]{:S(2)}) copy-start(bf16[8,48,768]{2,1,0:T(8,128)(2,1)S(1)} %collective-permute-done.1) | copy-start | bytes 1769476
  75.7 14.7 %collective-permute-start.3 = (bf16[8,48,768]{2,1,0:T(8,128)(2,1)S(1)}, bf16[8,48,768]{2,1,0:T(8,128)(2,1)S(1)}, u32[]{:S(2)}, u32[]{:S(2)}) collective-permute-start(bf16[8,48,768]{2,1,0:T(8,128)(2,1)S(1)} %collective-permute-done.1), channel_id=1, source_target_pairs={{0,64},{8,72},{16,80},{24,88},{32,96},{40,104},{48,112},{56,120},{... | collective-permute-start | bytes 1769480 | tf_op jit(solution)/shard_map/ppermute | solution.py:197
  78.7 4.7 %copy-start.5 = (bf16[8,48,768]{2,1,0:T(8,128)(2,1)}, bf16[8,48,768]{2,1,0:T(8,128)(2,1)S(1)}, u32[]{:S(2)}) copy-start(bf16[8,48,768]{2,1,0:T(8,128)(2,1)S(1)} %collective-permute-done.4) | copy-start | bytes 1769476
  78.7 14.9 %collective-permute-start.6 = (bf16[8,48,768]{2,1,0:T(8,128)(2,1)S(1)}, bf16[8,48,768]{2,1,0:T(8,128)(2,1)S(1)}, u32[]{:S(2)}, u32[]{:S(2)}) collective-permute-start(bf16[8,48,768]{2,1,0:T(8,128)(2,1)S(1)} %collective-permute-done.4), channel_id=1, source_target_pairs={{0,448},{8,456},{16,464},{24,472},{32,480},{40,488},{48,496},{56,5... | collective-permute-start | bytes 1769480 | tf_op jit(solution)/shard_map/ppermute | solution.py:198
  91.2 16.0 %collective-permute-start.5 = (bf16[4,48,768]{2,1,0:T(8,128)(2,1)}, bf16[4,48,768]{2,1,0:T(8,128)(2,1)}, u32[]{:S(2)}, u32[]{:S(2)}) collective-permute-start(bf16[4,48,768]{2,1,0:T(8,128)(2,1)} %slice.9), channel_id=1, source_target_pairs={{0,64},{8,72},{16,80},{24,88},{32,96},{40,104},{48,112},{56,120},{... | collective-permute-start | bytes 884744 | tf_op jit(solution)/shard_map/ppermute | solution.py:226
  93.6 5.5 %copy-start.1 = (bf16[8,48,768]{2,1,0:T(8,128)(2,1)}, bf16[8,48,768]{2,1,0:T(8,128)(2,1)S(1)}, u32[]{:S(2)}) copy-start(bf16[8,48,768]{2,1,0:T(8,128)(2,1)S(1)} %collective-permute-done.6) | copy-start | bytes 1769476
  94.4 12.9 %collective-permute-start.7 = (bf16[4,48,768]{2,1,0:T(8,128)(2,1)}, bf16[4,48,768]{2,1,0:T(8,128)(2,1)}, u32[]{:S(2)}, u32[]{:S(2)}) collective-permute-start(bf16[4,48,768]{2,1,0:T(8,128)(2,1)} %slice.10), channel_id=1, source_target_pairs={{0,448},{8,456},{16,464},{24,472},{32,480},{40,488},{48,496},{56,5... | collective-permute-start | bytes 884744 | tf_op jit(solution)/shard_map/ppermute | solution.py:227
  99.7 3.6 %copy-start.4 = (bf16[512,3072]{1,0:T(8,128)(2,1)S(1)}, bf16[512,3072]{1,0:T(8,128)(2,1)}, u32[]{:S(2)}) copy-start(bf16[512,3072]{1,0:T(8,128)(2,1)} %all-gather.5.cloned.1.call-done) | copy-start | bytes 9437188
  101.4 1.8 %copy-start.9 = (bf16[8,48,768]{2,1,0:T(8,128)(2,1)S(1)}, bf16[8,48,768]{2,1,0:T(8,128)(2,1)}, u32[]{:S(2)}) copy-start(bf16[8,48,768]{2,1,0:T(8,128)(2,1)} %copy-done.8) | copy-start | bytes 1769476
  104.4 1.1 copy-start.7
  105.5 1.1 copy-start.2
  113.6 12.3 %all-to-all-start.1 = ((bf16[4,2,144,128]{3,2,1,0:T(8,128)(2,1)}), bf16[4,2,144,128]{3,2,1,0:T(8,128)(2,1)S(1)}, u32[]{:S(2)}, u32[]{:S(2)}) async-start(bf16[4,2,144,128]{3,2,1,0:T(8,128)(2,1)} %get-tuple-element.33), calls=%async_computation.1 | async-start | bytes 589824 | tf_op jit(solution)/shard_map/all_to_all | solution.py:242
  126.1 13.3 %collective-permute-start.10 = (bf16[2,144,128]{2,1,0:T(8,128)(2,1)S(1)}, bf16[2,144,128]{2,1,0:T(8,128)(2,1)S(1)}, u32[]{:S(2)}, u32[]{:S(2)}) collective-permute-start(bf16[2,144,128]{2,1,0:T(8,128)(2,1)S(1)} %get-tuple-element.34), channel_id=1, source_target_pairs={{0,64},{8,72},{16,80},{24,88},{32,96},{40,104},{48,112},{56,120},{... | collective-permute-start | bytes 221192 | tf_op jit(solution)/shard_map/ppermute | solution.py:249
  127.6 13.0 %collective-permute-start.11 = (bf16[2,144,128]{2,1,0:T(8,128)(2,1)S(1)}, bf16[2,144,128]{2,1,0:T(8,128)(2,1)S(1)}, u32[]{:S(2)}, u32[]{:S(2)}) collective-permute-start(bf16[2,144,128]{2,1,0:T(8,128)(2,1)S(1)} %get-tuple-element.34), channel_id=1, source_target_pairs={{0,128},{8,136},{16,144},{24,152},{32,160},{40,168},{48,176},{56,1... | collective-permute-start | bytes 221192 | tf_op jit(solution)/shard_map/ppermute | solution.py:249
  132.1 11.0 %collective-permute-start.12 = (bf16[2,144,128]{2,1,0:T(8,128)(2,1)S(1)}, bf16[2,144,128]{2,1,0:T(8,128)(2,1)S(1)}, u32[]{:S(2)}, u32[]{:S(2)}) collective-permute-start(bf16[2,144,128]{2,1,0:T(8,128)(2,1)S(1)} %get-tuple-element.34), channel_id=1, source_target_pairs={{0,192},{8,200},{16,208},{24,216},{32,224},{40,232},{48,240},{56,2... | collective-permute-start | bytes 221192 | tf_op jit(solution)/shard_map/ppermute | solution.py:249
  136.4 6.7 %collective-permute-start.13 = (bf16[2,144,128]{2,1,0:T(8,128)(2,1)S(1)}, bf16[2,144,128]{2,1,0:T(8,128)(2,1)S(1)}, u32[]{:S(2)}, u32[]{:S(2)}) collective-permute-start(bf16[2,144,128]{2,1,0:T(8,128)(2,1)S(1)} %get-tuple-element.34), channel_id=1, source_target_pairs={{0,256},{8,264},{16,272},{24,280},{32,288},{40,296},{48,304},{56,3... | collective-permute-start | bytes 221192 | tf_op jit(solution)/shard_map/ppermute | solution.py:249
  138.1 5.0 %collective-permute-start.14 = (bf16[2,144,128]{2,1,0:T(8,128)(2,1)S(1)}, bf16[2,144,128]{2,1,0:T(8,128)(2,1)S(1)}, u32[]{:S(2)}, u32[]{:S(2)}) collective-permute-start(bf16[2,144,128]{2,1,0:T(8,128)(2,1)S(1)} %get-tuple-element.34), channel_id=1, source_target_pairs={{0,320},{8,328},{16,336},{24,344},{32,352},{40,360},{48,368},{56,3... | collective-permute-start | bytes 221192 | tf_op jit(solution)/shard_map/ppermute | solution.py:249
  139.4 4.1 %collective-permute-start.15 = (bf16[2,144,128]{2,1,0:T(8,128)(2,1)S(1)}, bf16[2,144,128]{2,1,0:T(8,128)(2,1)S(1)}, u32[]{:S(2)}, u32[]{:S(2)}) collective-permute-start(bf16[2,144,128]{2,1,0:T(8,128)(2,1)S(1)} %get-tuple-element.34), channel_id=1, source_target_pairs={{0,384},{8,392},{16,400},{24,408},{32,416},{40,424},{48,432},{56,4... | collective-permute-start | bytes 221192 | tf_op jit(solution)/shard_map/ppermute | solution.py:249
  140.7 7.5 %collective-permute-start.16 = (bf16[2,144,128]{2,1,0:T(8,128)(2,1)S(1)}, bf16[2,144,128]{2,1,0:T(8,128)(2,1)S(1)}, u32[]{:S(2)}, u32[]{:S(2)}) collective-permute-start(bf16[2,144,128]{2,1,0:T(8,128)(2,1)S(1)} %get-tuple-element.34), channel_id=1, source_target_pairs={{0,448},{8,456},{16,464},{24,472},{32,480},{40,488},{48,496},{56,5... | collective-permute-start | bytes 221192 | tf_op jit(solution)/shard_map/ppermute | solution.py:249
Sparse Core Ops, SparseCore 0:
  9.5 38.9 all-gather.2
  60.0 31.8 all-gather.4

commit v3 on v2

--- a/solution.py
+++ b/solution.py
@@ -76,10 +76,9 @@
             out_ref[:, (h * 2 + s) * 256 : (h * 2 + s + 1) * 256] = sent_ref[s * NH + h]
 
 
-def states_kernel(side_ref, own_ref, other_ref, col_ref, row_ref, proj_ref, prefix_ref, message_ref):
-    side = side_ref[0]
-    proj_ref[side] = own_ref[...].astype(BF16)
-    proj_ref[1 - side] = other_ref[...].astype(BF16)
+def states_kernel(total_ref, col_ref, row_ref, proj_ref, prefix_ref, message_ref):
+    for half in range(2):
+        proj_ref[half] = total_ref[half * 512 : (half + 1) * 512].astype(BF16)
     for head in range(2):
         state = jnp.zeros((E, E), F32)
         decay = jnp.zeros((1, 1), F32)
@@ -177,17 +176,16 @@
     y, z = seq // NZ, seq % NZ
     side = z % 2
     place = z // 2
-    side1 = side.reshape(1).astype(jnp.int32)
     place1 = place.reshape(1).astype(jnp.int32)
 
     (pieces,) = call(pieces_kernel, [((NZ, 48, 768), BF16)], [], qkv_weight.transpose(1, 0, 2))
     block = lax.all_to_all(pieces, "seq", split_axis=0, concat_axis=0, tiled=True, axis_index_groups=Z_GROUPS)
 
-    own_rows = lax.all_gather(tokens, "head", axis=0, tiled=True)
-
-
-    def add(total, tok, part, offset):
-        x = lax.dynamic_slice_in_dim(tok, ((y + offset) % NY) * (NZ * 48), NZ * 48, 1)
+    all_rows = lax.all_gather(tokens, ("seq", "head"), axis=0, tiled=True, axis_index_groups=OUT_GROUPS)
+
+
+    def add(total, part, offset):
+        x = lax.dynamic_slice_in_dim(all_rows, ((y + offset) % NY) * (NZ * 48), NZ * 48, 1)
         d = jnp.dot(x, part.reshape(NZ * 48, 768), preferred_element_type=F32)
         return d if total is None else total + d
 
@@ -197,14 +195,10 @@
         ups.append(lax.ppermute(after(ups[-1], *earlier), "seq", y_shift(1)))
         downs.append(lax.ppermute(after(downs[-1], *earlier), "seq", y_shift(-1)))
 
-    def add_step(total, tok, step):
-        if step == 0:
-            return add(total, tok, block, 0)
-        return add(add(total, tok, ups[step], -step), tok, downs[step], step)
+    def add_step(total, step):
+        return add(add(total, ups[step], -step), downs[step], step)
 
     hop()
-    pair_tokens = lax.ppermute(after(tokens, block), "seq", PAIR)
-    own = add_step(None, own_rows, 0)
 
     mine = lax.dynamic_slice_in_dim(log_decay, side * 2, 2, 0)
     wanted = lax.dynamic_slice_in_dim(log_decay, (1 - side) * 2, 2, 0)
@@ -217,27 +211,19 @@
     cols = rows.T
     gain = lax.dynamic_slice_in_dim(norm_gain, side * 256, 256, 0).reshape(1, 256)
 
-    first = (ups[1], downs[1], own, rows, cols, starts, gain)
-    other_rows = lax.all_gather(after(pair_tokens, *first), "head", axis=0, tiled=True)
     hop()
-    own = add_step(own, own_rows, 1)
-    hop(own)
-    own = add_step(own, own_rows, 2)
-    up4 = lax.ppermute(after(ups[3], own)[:4], "seq", y_shift(1))
-    down4 = lax.ppermute(after(downs[3], own)[4:], "seq", y_shift(-1))
-    own = add_step(own, own_rows, 3)
-    other = None
-    for step in range(4):
-        other = add_step(other, other_rows, step)
-    up4, down4, own, other = lax.optimization_barrier((up4, down4, own, other))
-    last = jnp.concatenate([up4, down4], 0)
-    own = add(own, own_rows, last, 4)
-    other = add(other, other_rows, last, 4)
+    hop(all_rows, rows, cols, starts, gain)
+    total = add_step(add(None, block, 0), 1)
+    up4 = lax.ppermute(after(ups[3], total)[:4], "seq", y_shift(1))
+    down4 = lax.ppermute(after(downs[3], total)[4:], "seq", y_shift(-1))
+    total = add_step(add_step(total, 2), 3)
+    up4, down4, total = lax.optimization_barrier((up4, down4, total))
+    total = add(total, jnp.concatenate([up4, down4], 0), 4)
 
     proj, prefix, messages = call(
         states_kernel,
         [((2, 512, 768), BF16), ((16, E, E), BF16), ((4, 2, E + EXTRA, E), BF16)],
-        [side1], own, other, cols, rows, flops=16 * 2 * E**3,
+        [], total, cols, rows, flops=16 * 2 * E**3,
     )
     messages = lax.all_to_all(messages, "seq", split_axis=0, concat_axis=0, tiled=True, axis_index_groups=ROW_GROUPS)
     (part,) = call(local_kernel, [((16, BLK, E), F32)], [], proj, prefix, cols, rows, flops=16 * 6 * E**3)

time: 178 us -> 164 us (0.921)
  blocking collectives: 18.4 us -> 50 us
  waiting for transfers between devices: 53.5 us -> 22.8 us
  starting transfers between devices: 60.8 us -> 55.2 us
  matrix products: 15.7 us -> 10.3 us
    all_to_all x0 -> x1, blocking collectives: none -> 28 us  [on_device(): lax.all_to_all(pieces, 'seq', split_axis=0, concat_axis=0, tiled=True, ax...]
    all_to_all x1 -> x0, waiting for transfers between devices: 19.3 us -> none  [on_device(): lax.all_to_all(pieces, 'seq', split_axis=0, concat_axis=0, tiled=True, ax...]
    all_to_all x1 -> x0, starting transfers between devices: 10.9 us -> none  [on_device(): lax.all_to_all(pieces, 'seq', split_axis=0, concat_axis=0, tiled=True, ax...]
    dot_general x16 -> x8, matrix products: 15.7 us -> 10.3 us  [add(): d = jnp.dot(x, part.reshape(NZ * 48, 768), preferred_element_type=F32)]
    ppermute x3, waiting for transfers between devices: 12.9 us -> 7.69 us  [hop(): ups.append(lax.ppermute(after(ups[-1], *earlier), 'seq', y_shift(1)))]
    ppermute x7, waiting for transfers between devices: 5.12 us -> 0.65 us  [on_device(): lax.ppermute(row_message, 'seq', y_later(k))]
    all_to_all x1, starting transfers between devices: 3.45 us -> 7.53 us  [on_device(): lax.all_to_all(messages, 'seq', split_axis=0, concat_axis=0, tiled=True,...]
    ppermute x3 -> x2, waiting for transfers between devices: 5.32 us -> 1.6 us  [the longest x1 1.52 us: on_device(): down4 = lax.ppermute(after(downs[3], total)[4:], 'seq', y_shift(-1))]
  transfers between devices with their start and end apart: 21 -> 18, of which waited for: 9 -> 7; matrix products, arithmetic and copies ran while one was open for 9% -> 7% of each run, Pallas kernels for 1% -> 1%
where the time goes in v3:
time: 164 us; the launch traced here: 163 us
  starting transfers between devices  55.2 us (34%)
  blocking collectives  50 us (30%)
  waiting for transfers between devices  22.8 us (14%)
  between operations  13.9 us (8%)
  matrix products  10.3 us (6%)
  Pallas kernels  7.03 us (4%)
  local copies, waits for them, and re-layouts  2.94 us (2%)
    all_to_all x1, blocking collectives, on_device(): lax.all_to_all(pieces, 'seq', split_axis=0, concat_axis=0, tiled=True, ax...  28 us
    all_to_all x1, blocking collectives, on_device(): lax.all_to_all(flat.reshape(16, 64, 256), ('seq', 'head'), split_axis=0,...  22 us
    ppermute x7, starting transfers between devices, on_device(): lax.ppermute(row_message, 'seq', y_later(k))  17.5 us
    ppermute x3, starting transfers between devices, hop(): downs.append(lax.ppermute(after(downs[-1], *earlier), 'seq', y_shift(-1)))  12.4 us
    dot_general x8, matrix products, add(): d = jnp.dot(x, part.reshape(NZ * 48, 768), preferred_element_type=F32)  10.3 us
    all_to_all x1, waiting for transfers between devices, on_device(): lax.all_to_all(messages, 'seq', split_axis=0, concat_axis=0, tiled=True,...  8.9 us
    ppermute x3, starting transfers between devices, hop(): ups.append(lax.ppermute(after(ups[-1], *earlier), 'seq', y_shift(1)))  8.27 us
    ppermute x3, waiting for transfers between devices, hop(): ups.append(lax.ppermute(after(ups[-1], *earlier), 'seq', y_shift(1)))  7.69 us
  transfers between devices with their start and end apart: 18, of which 7 were waited for; matrix products, arithmetic and copies ran while one was open for 7% of the time, Pallas kernels for 1%

profile of v3, /device:TPU:1, one launch (start us, length us, event | category | flops | bytes accessed | tf_op | source)
XLA Modules:
  0.0 163.4 jit_solution(10147607779367224853)
XLA Ops:
  6.5 0.7 all-gather.2.cloned.1.call-update
  7.3 0.9 copy-done
  8.2 28.0 %all_to_all.15 = bf16[8,48,768]{2,1,0:T(8,128)(2,1)S(1)} all-to-all(bf16[8,48,768]{2,1,0:T(8,128)(2,1)S(1)} %shard_map.46), channel_id=1, replica_groups={{0,8,16,24,32,40,48,56},{64,72,80,88,96,104,112,120},{128,136,144,152,1..., dimensions={0} | all-to-all | bytes 1179648 | tf_op jit(solution)/shard_map/all_to_all | solution.py:182
  36.2 3.2 %collective-permute-start = (bf16[8,48,768]{2,1,0:T(8,128)(2,1)S(1)}, bf16[8,48,768]{2,1,0:T(8,128)(2,1)S(1)}, u32[]{:S(2)}, u32[]{:S(2)}) collective-permute-start(bf16[8,48,768]{2,1,0:T(8,128)(2,1)S(1)} %all_to_all.15), channel_id=1, source_target_pairs={{0,64},{8,72},{16,80},{24,88},{32,96},{40,104},{48,112},{56,120},{... | collective-permute-start | bytes 1769480 | tf_op jit(solution)/shard_map/ppermute | solution.py:195
  39.4 4.0 %collective-permute-start.4 = (bf16[8,48,768]{2,1,0:T(8,128)(2,1)S(1)}, bf16[8,48,768]{2,1,0:T(8,128)(2,1)S(1)}, u32[]{:S(2)}, u32[]{:S(2)}) collective-permute-start(bf16[8,48,768]{2,1,0:T(8,128)(2,1)S(1)} %all_to_all.15), channel_id=1, source_target_pairs={{0,448},{8,456},{16,464},{24,472},{32,480},{40,488},{48,496},{56,5... | collective-permute-start | bytes 1769480 | tf_op jit(solution)/shard_map/ppermute | solution.py:196
  43.4 7.7 %collective-permute-done = bf16[8,48,768]{2,1,0:T(8,128)(2,1)S(1)} collective-permute-done((bf16[8,48,768]{2,1,0:T(8,128)(2,1)S(1)}, bf16[8,48,768]{2,1,0:T(8,128)(2,1)S(1)}, u32[]{:S(2)}, u32[]{:S(2)}) %collective-permute-start) | collective-permute-done | bytes 589856 | tf_op jit(solution)/shard_map/ppermute | solution.py:195
  51.1 1.9 %collective-permute-start.1 = (bf16[8,48,768]{2,1,0:T(8,128)(2,1)S(1)}, bf16[8,48,768]{2,1,0:T(8,128)(2,1)S(1)}, u32[]{:S(2)}, u32[]{:S(2)}) collective-permute-start(bf16[8,48,768]{2,1,0:T(8,128)(2,1)S(1)} %collective-permute-done), channel_id=1, source_target_pairs={{0,64},{8,72},{16,80},{24,88},{32,96},{40,104},{48,112},{56,120},{... | collective-permute-start | bytes 1769480 | tf_op jit(solution)/shard_map/ppermute | solution.py:195
  53.0 4.6 %collective-permute-start.6 = (bf16[8,48,768]{2,1,0:T(8,128)(2,1)S(1)}, bf16[8,48,768]{2,1,0:T(8,128)(2,1)S(1)}, u32[]{:S(2)}, u32[]{:S(2)}) collective-permute-start(bf16[8,48,768]{2,1,0:T(8,128)(2,1)S(1)} %collective-permute-done.4), channel_id=1, source_target_pairs={{0,448},{8,456},{16,464},{24,472},{32,480},{40,488},{48,496},{56,5... | collective-permute-start | bytes 1769480 | tf_op jit(solution)/shard_map/ppermute | solution.py:196
  57.7 0.8 constant_dynamic-slice_fusion.1
  58.5 1.9 %collective-permute-start.2 = (f32[2,512]{1,0:T(2,128)S(1)}, f32[2,512]{1,0:T(2,128)S(1)}, u32[]{:S(2)}, u32[]{:S(2)}) collective-permute-start(f32[2,512]{1,0:T(2,128)S(1)} %get-tuple-element.19), channel_id=1, source_target_pairs={{0,8},{8,0},{16,24},{24,16},{32,40},{40,32},{48,56},{56,48},{64,72... | collective-permute-start | bytes 12296 | tf_op jit(solution)/shard_map/ppermute | solution.py:205
  60.5 0.8 dynamic_slice.35
  61.3 2.0 %collective-permute-done.2 = f32[2,512]{1,0:T(2,128)S(1)} collective-permute-done((f32[2,512]{1,0:T(2,128)S(1)}, f32[2,512]{1,0:T(2,128)S(1)}, u32[]{:S(2)}, u32[]{:S(2)}) %collective-permute-start.2) | collective-permute-done | bytes 4128 | tf_op jit(solution)/shard_map/ppermute | solution.py:205
  63.3 0.6 reduce_window_sum.24
  63.9 0.2 slice_reduce_fusion
  64.1 0.2 reduce_window_sum.25
  64.3 0.1 copy.8
  64.5 1.2 all-gather.2.cloned.1.call-done
  65.8 3.2 %collective-permute-start.3 = (bf16[8,48,768]{2,1,0:T(8,128)(2,1)S(1)}, bf16[8,48,768]{2,1,0:T(8,128)(2,1)S(1)}, u32[]{:S(2)}, u32[]{:S(2)}) collective-permute-start(bf16[8,48,768]{2,1,0:T(8,128)(2,1)S(1)} %collective-permute-done.1), channel_id=1, source_target_pairs={{0,64},{8,72},{16,80},{24,88},{32,96},{40,104},{48,112},{56,120},{... | collective-permute-start | bytes 1769480 | tf_op jit(solution)/shard_map/ppermute | solution.py:195
  69.0 3.8 %collective-permute-start.7 = (bf16[8,48,768]{2,1,0:T(8,128)(2,1)S(1)}, bf16[8,48,768]{2,1,0:T(8,128)(2,1)S(1)}, u32[]{:S(2)}, u32[]{:S(2)}) collective-permute-start(bf16[8,48,768]{2,1,0:T(8,128)(2,1)S(1)} %collective-permute-done.6), channel_id=1, source_target_pairs={{0,448},{8,456},{16,464},{24,472},{32,480},{40,488},{48,496},{56,5... | collective-permute-start | bytes 1769480 | tf_op jit(solution)/shard_map/ppermute | solution.py:196
  72.8 2.3 %fusion.15 = f32[1024,768]{1,0:T(8,128)S(1)} fusion(bf16[384,768]{1,0:T(8,128)(2,1)S(1)} %bitcast.31, bf16[1024,3072]{1,0:T(8,128)(2,1)} %all-gather.2.cloned.1.call-done, s32[]{:T(128)S(6)} %select_n.102), kind=kOutput, calls=%fused_computation.15 | convolution fusion | flops 603979776 | bytes 4521988 | tf_op jit(solution)/shard_map/dot_general | solution.py:189
  75.1 2.1 %fusion.13 = f32[1024,768]{1,0:T(8,128)S(1)} fusion(bf16[384,768]{1,0:T(8,128)(2,1)S(1)} %bitcast.36, bf16[1024,3072]{1,0:T(8,128)(2,1)} %all-gather.2.cloned.1.call-done, s32[]{:T(128)S(6)} %select_n.104), kind=kOutput, calls=%fused_computation.13 | convolution fusion | flops 603979776 | bytes 4521988 | tf_op jit(solution)/shard_map/dot_general | solution.py:189
  77.2 1.0 fusion.8
  78.2 1.0 fusion.10
  79.2 1.0 add_add_fusion.1
  80.2 2.7 %collective-permute-start.5 = (bf16[4,48,768]{2,1,0:T(8,128)(2,1)S(1)}, bf16[4,48,768]{2,1,0:T(8,128)(2,1)S(1)}, u32[]{:S(2)}, u32[]{:S(2)}) collective-permute-start(bf16[4,48,768]{2,1,0:T(8,128)(2,1)S(1)} %slice.10), channel_id=1, source_target_pairs={{0,64},{8,72},{16,80},{24,88},{32,96},{40,104},{48,112},{56,120},{... | collective-permute-start | bytes 884744 | tf_op jit(solution)/shard_map/ppermute | solution.py:217
  82.9 4.9 %collective-permute-start.8 = (bf16[4,48,768]{2,1,0:T(8,128)(2,1)S(1)}, bf16[4,48,768]{2,1,0:T(8,128)(2,1)S(1)}, u32[]{:S(2)}, u32[]{:S(2)}) collective-permute-start(bf16[4,48,768]{2,1,0:T(8,128)(2,1)S(1)} %slice.11), channel_id=1, source_target_pairs={{0,448},{8,456},{16,464},{24,472},{32,480},{40,488},{48,496},{56,5... | collective-permute-start | bytes 884744 | tf_op jit(solution)/shard_map/ppermute | solution.py:218
  87.8 1.0 fusion.6
  88.8 1.1 add_add_fusion
  89.9 0.1 collective-permute-done.5
  89.9 1.5 collective-permute-done.8
  91.5 1.0 fusion
  92.5 0.4 add.142.total_ref
  92.9 2.6 %shard_map.47 = (bf16[2,512,768]{2,1,0:T(8,128)(2,1)S(1)}, bf16[16,128,128]{2,1,0:T(8,128)(2,1)S(1)}, bf16[4,2,144,128]{3,2,1,0:T(8,128)(2,1)}) custom-call(f32[1024,768]{1,0:T(8,128)S(1)} %add.142.total_ref, f32[128,16]{1,0:T(8,128)S(1)} %bitcast.23, f32[16,128]{1,0:T(8,128)S(1)} %bitcast.27), custom_call_target="tpu_custom_call" | custom-call | flops 67108864 | bytes 3162112 | tf_op jit(solution)/shard_map/pallas_call | solution.py:164
  95.5 7.5 %all-to-all-start.1 = ((bf16[4,2,144,128]{3,2,1,0:T(8,128)(2,1)}), bf16[4,2,144,128]{3,2,1,0:T(8,128)(2,1)S(1)}, u32[]{:S(2)}, u32[]{:S(2)}) async-start(bf16[4,2,144,128]{3,2,1,0:T(8,128)(2,1)} %get-tuple-element.27), calls=%async_computation.1 | async-start | bytes 589824 | tf_op jit(solution)/shard_map/all_to_all | solution.py:228
  103.1 8.9 %all-to-all-done.1.messages_ref = bf16[4,2,144,128]{3,2,1,0:T(8,128)(2,1)S(1)} async-done(((bf16[4,2,144,128]{3,2,1,0:T(8,128)(2,1)}), bf16[4,2,144,128]{3,2,1,0:T(8,128)(2,1)S(1)}, u32[]{:S(2)}, u32[]{:S(2)}) %all-to-all-start.1) | async-done | bytes 294944 | tf_op jit(solution)/shard_map/all_to_all | solution.py:228
  112.0 0.1 shard_map.48
  112.1 3.5 %collective-permute-start.9 = (bf16[2,144,128]{2,1,0:T(8,128)(2,1)S(1)}, bf16[2,144,128]{2,1,0:T(8,128)(2,1)S(1)}, u32[]{:S(2)}, u32[]{:S(2)}) collective-permute-start(bf16[2,144,128]{2,1,0:T(8,128)(2,1)S(1)} %get-tuple-element.28), channel_id=1, source_target_pairs={{0,64},{8,72},{16,80},{24,88},{32,96},{40,104},{48,112},{56,120},{... | collective-permute-start | bytes 221192 | tf_op jit(solution)/shard_map/ppermute | solution.py:235
  115.6 4.7 %collective-permute-start.10 = (bf16[2,144,128]{2,1,0:T(8,128)(2,1)S(1)}, bf16[2,144,128]{2,1,0:T(8,128)(2,1)S(1)}, u32[]{:S(2)}, u32[]{:S(2)}) collective-permute-start(bf16[2,144,128]{2,1,0:T(8,128)(2,1)S(1)} %get-tuple-element.28), channel_id=1, source_target_pairs={{0,128},{8,136},{16,144},{24,152},{32,160},{40,168},{48,176},{56,1... | collective-permute-start | bytes 221192 | tf_op jit(solution)/shard_map/ppermute | solution.py:235
  120.3 3.1 %collective-permute-start.11 = (bf16[2,144,128]{2,1,0:T(8,128)(2,1)S(1)}, bf16[2,144,128]{2,1,0:T(8,128)(2,1)S(1)}, u32[]{:S(2)}, u32[]{:S(2)}) collective-permute-start(bf16[2,144,128]{2,1,0:T(8,128)(2,1)S(1)} %get-tuple-element.28), channel_id=1, source_target_pairs={{0,192},{8,200},{16,208},{24,216},{32,224},{40,232},{48,240},{56,2... | collective-permute-start | bytes 221192 | tf_op jit(solution)/shard_map/ppermute | solution.py:235
  123.4 2.2 %collective-permute-start.12 = (bf16[2,144,128]{2,1,0:T(8,128)(2,1)S(1)}, bf16[2,144,128]{2,1,0:T(8,128)(2,1)S(1)}, u32[]{:S(2)}, u32[]{:S(2)}) collective-permute-start(bf16[2,144,128]{2,1,0:T(8,128)(2,1)S(1)} %get-tuple-element.28), channel_id=1, source_target_pairs={{0,256},{8,264},{16,272},{24,280},{32,288},{40,296},{48,304},{56,3... | collective-permute-start | bytes 221192 | tf_op jit(solution)/shard_map/ppermute | solution.py:235
  125.5 1.3 collective-permute-start.13
  126.9 1.3 collective-permute-start.14
  128.2 1.5 collective-permute-start.15
  129.7 0.9 shard_map.49.refs_9_
  130.6 0.6 collective-permute-done.15.refs_6_
  131.2 2.5 %shard_map.50 = bf16[1024,256]{1,0:T(8,128)(2,1)S(1)} custom-call(bf16[2,144,128]{2,1,0:T(8,128)(2,1)S(1)} %collective-permute-done.9.refs_0_, bf16[2,144,128]{2,1,0:T(8,128)(2,1)S(1)} %collective-permute-done.10.refs_1_, bf16[2,144,128]{2,1,0:T(8,128)(2,1)S(1)} %collective-permute-done.11.refs_2_, bf16[2,144,128]{2,1,0:T(8,128)(2,1)S(1)} %collective-permute-done.12.refs_3_, ...), custom_call_target="tpu_custom_call" | custom-call | flops 67108864 | bytes 3286080 | tf_op jit(solution)/shard_map/pallas_call | solution.py:164
  133.7 22.0 %all_to_all.16.sent_ref = bf16[16,64,256]{2,1,0:T(8,128)(2,1)S(1)} all-to-all(bf16[16,64,256]{2,1,0:T(8,128)(2,1)S(1)} %bitcast.22), channel_id=1, replica_groups={{0,1,2,3,4,5,6,7,8,9,10,11,12,13,14,15},{16,17,18,19,20,21,22,23,24,25,..., dimensions={0} | all-to-all | bytes 1048576 | tf_op jit(solution)/shard_map/all_to_all | solution.py:240
  155.8 0.8 shard_map.51
  (25 shorter events, 0.4 us)
Async XLA Ops:
  6.5 59.2 %all-gather.2.cloned.1.call-start = ((), (), s32[]{:S(2)}) async-start(), calls=%async_computation.3 | async-start | bytes 6684672 | tf_op jit(solution)/shard_map/all_gather | solution.py:184
  7.3 0.9 copy-start
  36.2 14.9 %collective-permute-start = (bf16[8,48,768]{2,1,0:T(8,128)(2,1)S(1)}, bf16[8,48,768]{2,1,0:T(8,128)(2,1)S(1)}, u32[]{:S(2)}, u32[]{:S(2)}) collective-permute-start(bf16[8,48,768]{2,1,0:T(8,128)(2,1)S(1)} %all_to_all.15), channel_id=1, source_target_pairs={{0,64},{8,72},{16,80},{24,88},{32,96},{40,104},{48,112},{56,120},{... | collective-permute-start | bytes 1769480 | tf_op jit(solution)/shard_map/ppermute | solution.py:195
  39.4 13.6 %collective-permute-start.4 = (bf16[8,48,768]{2,1,0:T(8,128)(2,1)S(1)}, bf16[8,48,768]{2,1,0:T(8,128)(2,1)S(1)}, u32[]{:S(2)}, u32[]{:S(2)}) collective-permute-start(bf16[8,48,768]{2,1,0:T(8,128)(2,1)S(1)} %all_to_all.15), channel_id=1, source_target_pairs={{0,448},{8,456},{16,464},{24,472},{32,480},{40,488},{48,496},{56,5... | collective-permute-start | bytes 1769480 | tf_op jit(solution)/shard_map/ppermute | solution.py:196
  51.1 13.4 %collective-permute-start.1 = (bf16[8,48,768]{2,1,0:T(8,128)(2,1)S(1)}, bf16[8,48,768]{2,1,0:T(8,128)(2,1)S(1)}, u32[]{:S(2)}, u32[]{:S(2)}) collective-permute-start(bf16[8,48,768]{2,1,0:T(8,128)(2,1)S(1)} %collective-permute-done), channel_id=1, source_target_pairs={{0,64},{8,72},{16,80},{24,88},{32,96},{40,104},{48,112},{56,120},{... | collective-permute-start | bytes 1769480 | tf_op jit(solution)/shard_map/ppermute | solution.py:195
  53.0 16.0 %collective-permute-start.6 = (bf16[8,48,768]{2,1,0:T(8,128)(2,1)S(1)}, bf16[8,48,768]{2,1,0:T(8,128)(2,1)S(1)}, u32[]{:S(2)}, u32[]{:S(2)}) collective-permute-start(bf16[8,48,768]{2,1,0:T(8,128)(2,1)S(1)} %collective-permute-done.4), channel_id=1, source_target_pairs={{0,448},{8,456},{16,464},{24,472},{32,480},{40,488},{48,496},{56,5... | collective-permute-start | bytes 1769480 | tf_op jit(solution)/shard_map/ppermute | solution.py:196
  58.5 4.8 %collective-permute-start.2 = (f32[2,512]{1,0:T(2,128)S(1)}, f32[2,512]{1,0:T(2,128)S(1)}, u32[]{:S(2)}, u32[]{:S(2)}) collective-permute-start(f32[2,512]{1,0:T(2,128)S(1)} %get-tuple-element.19), channel_id=1, source_target_pairs={{0,8},{8,0},{16,24},{24,16},{32,40},{40,32},{48,56},{56,48},{64,72... | collective-permute-start | bytes 12296 | tf_op jit(solution)/shard_map/ppermute | solution.py:205
  65.8 14.4 %collective-permute-start.3 = (bf16[8,48,768]{2,1,0:T(8,128)(2,1)S(1)}, bf16[8,48,768]{2,1,0:T(8,128)(2,1)S(1)}, u32[]{:S(2)}, u32[]{:S(2)}) collective-permute-start(bf16[8,48,768]{2,1,0:T(8,128)(2,1)S(1)} %collective-permute-done.1), channel_id=1, source_target_pairs={{0,64},{8,72},{16,80},{24,88},{32,96},{40,104},{48,112},{56,120},{... | collective-permute-start | bytes 1769480 | tf_op jit(solution)/shard_map/ppermute | solution.py:195
  69.0 13.9 %collective-permute-start.7 = (bf16[8,48,768]{2,1,0:T(8,128)(2,1)S(1)}, bf16[8,48,768]{2,1,0:T(8,128)(2,1)S(1)}, u32[]{:S(2)}, u32[]{:S(2)}) collective-permute-start(bf16[8,48,768]{2,1,0:T(8,128)(2,1)S(1)} %collective-permute-done.6), channel_id=1, source_target_pairs={{0,448},{8,456},{16,464},{24,472},{32,480},{40,488},{48,496},{56,5... | collective-permute-start | bytes 1769480 | tf_op jit(solution)/shard_map/ppermute | solution.py:196
  72.8 4.4 %copy-start.1 = (bf16[1024,3072]{1,0:T(8,128)(2,1)S(1)}, bf16[1024,3072]{1,0:T(8,128)(2,1)}, u32[]{:S(2)}) copy-start(bf16[1024,3072]{1,0:T(8,128)(2,1)} %all-gather.2.cloned.1.call-done) | copy-start | bytes 18874372
  80.2 9.8 %collective-permute-start.5 = (bf16[4,48,768]{2,1,0:T(8,128)(2,1)S(1)}, bf16[4,48,768]{2,1,0:T(8,128)(2,1)S(1)}, u32[]{:S(2)}, u32[]{:S(2)}) collective-permute-start(bf16[4,48,768]{2,1,0:T(8,128)(2,1)S(1)} %slice.10), channel_id=1, source_target_pairs={{0,64},{8,72},{16,80},{24,88},{32,96},{40,104},{48,112},{56,120},{... | collective-permute-start | bytes 884744 | tf_op jit(solution)/shard_map/ppermute | solution.py:217
  82.9 8.6 %collective-permute-start.8 = (bf16[4,48,768]{2,1,0:T(8,128)(2,1)S(1)}, bf16[4,48,768]{2,1,0:T(8,128)(2,1)S(1)}, u32[]{:S(2)}, u32[]{:S(2)}) collective-permute-start(bf16[4,48,768]{2,1,0:T(8,128)(2,1)S(1)} %slice.11), channel_id=1, source_target_pairs={{0,448},{8,456},{16,464},{24,472},{32,480},{40,488},{48,496},{56,5... | collective-permute-start | bytes 884744 | tf_op jit(solution)/shard_map/ppermute | solution.py:218
  95.5 16.4 %all-to-all-start.1 = ((bf16[4,2,144,128]{3,2,1,0:T(8,128)(2,1)}), bf16[4,2,144,128]{3,2,1,0:T(8,128)(2,1)S(1)}, u32[]{:S(2)}, u32[]{:S(2)}) async-start(bf16[4,2,144,128]{3,2,1,0:T(8,128)(2,1)} %get-tuple-element.27), calls=%async_computation.1 | async-start | bytes 589824 | tf_op jit(solution)/shard_map/all_to_all | solution.py:228
  112.1 14.8 %collective-permute-start.9 = (bf16[2,144,128]{2,1,0:T(8,128)(2,1)S(1)}, bf16[2,144,128]{2,1,0:T(8,128)(2,1)S(1)}, u32[]{:S(2)}, u32[]{:S(2)}) collective-permute-start(bf16[2,144,128]{2,1,0:T(8,128)(2,1)S(1)} %get-tuple-element.28), channel_id=1, source_target_pairs={{0,64},{8,72},{16,80},{24,88},{32,96},{40,104},{48,112},{56,120},{... | collective-permute-start | bytes 221192 | tf_op jit(solution)/shard_map/ppermute | solution.py:235
  115.6 12.6 %collective-permute-start.10 = (bf16[2,144,128]{2,1,0:T(8,128)(2,1)S(1)}, bf16[2,144,128]{2,1,0:T(8,128)(2,1)S(1)}, u32[]{:S(2)}, u32[]{:S(2)}) collective-permute-start(bf16[2,144,128]{2,1,0:T(8,128)(2,1)S(1)} %get-tuple-element.28), channel_id=1, source_target_pairs={{0,128},{8,136},{16,144},{24,152},{32,160},{40,168},{48,176},{56,1... | collective-permute-start | bytes 221192 | tf_op jit(solution)/shard_map/ppermute | solution.py:235
  120.3 10.3 %collective-permute-start.11 = (bf16[2,144,128]{2,1,0:T(8,128)(2,1)S(1)}, bf16[2,144,128]{2,1,0:T(8,128)(2,1)S(1)}, u32[]{:S(2)}, u32[]{:S(2)}) collective-permute-start(bf16[2,144,128]{2,1,0:T(8,128)(2,1)S(1)} %get-tuple-element.28), channel_id=1, source_target_pairs={{0,192},{8,200},{16,208},{24,216},{32,224},{40,232},{48,240},{56,2... | collective-permute-start | bytes 221192 | tf_op jit(solution)/shard_map/ppermute | solution.py:235
  123.4 7.2 %collective-permute-start.12 = (bf16[2,144,128]{2,1,0:T(8,128)(2,1)S(1)}, bf16[2,144,128]{2,1,0:T(8,128)(2,1)S(1)}, u32[]{:S(2)}, u32[]{:S(2)}) collective-permute-start(bf16[2,144,128]{2,1,0:T(8,128)(2,1)S(1)} %get-tuple-element.28), channel_id=1, source_target_pairs={{0,256},{8,264},{16,272},{24,280},{32,288},{40,296},{48,304},{56,3... | collective-permute-start | bytes 221192 | tf_op jit(solution)/shard_map/ppermute | solution.py:235
  125.5 5.0 %collective-permute-start.13 = (bf16[2,144,128]{2,1,0:T(8,128)(2,1)S(1)}, bf16[2,144,128]{2,1,0:T(8,128)(2,1)S(1)}, u32[]{:S(2)}, u32[]{:S(2)}) collective-permute-start(bf16[2,144,128]{2,1,0:T(8,128)(2,1)S(1)} %get-tuple-element.28), channel_id=1, source_target_pairs={{0,320},{8,328},{16,336},{24,344},{32,352},{40,360},{48,368},{56,3... | collective-permute-start | bytes 221192 | tf_op jit(solution)/shard_map/ppermute | solution.py:235
  126.9 3.7 %collective-permute-start.14 = (bf16[2,144,128]{2,1,0:T(8,128)(2,1)S(1)}, bf16[2,144,128]{2,1,0:T(8,128)(2,1)S(1)}, u32[]{:S(2)}, u32[]{:S(2)}) collective-permute-start(bf16[2,144,128]{2,1,0:T(8,128)(2,1)S(1)} %get-tuple-element.28), channel_id=1, source_target_pairs={{0,384},{8,392},{16,400},{24,408},{32,416},{40,424},{48,432},{56,4... | collective-permute-start | bytes 221192 | tf_op jit(solution)/shard_map/ppermute | solution.py:235
  128.2 3.0 %collective-permute-start.15 = (bf16[2,144,128]{2,1,0:T(8,128)(2,1)S(1)}, bf16[2,144,128]{2,1,0:T(8,128)(2,1)S(1)}, u32[]{:S(2)}, u32[]{:S(2)}) collective-permute-start(bf16[2,144,128]{2,1,0:T(8,128)(2,1)S(1)} %get-tuple-element.28), channel_id=1, source_target_pairs={{0,448},{8,456},{16,464},{24,472},{32,480},{40,488},{48,496},{56,5... | collective-permute-start | bytes 221192 | tf_op jit(solution)/shard_map/ppermute | solution.py:235
Sparse Core Ops, SparseCore 0:
  9.5 56.2 all-gather.1

commit v4 on v3

--- a/solution.py
+++ b/solution.py
@@ -19,6 +19,7 @@
 VMEM = pltpu.VMEM
 
 Z_GROUPS = [[y * NZ + z for z in range(NZ)] for y in range(NY)]
+Y_GROUPS = [[y * NZ + z for y in range(NY)] for z in range(NZ)]
 ROW_GROUPS = [[y * NZ + p + 2 * i for i in range(4)] for y in range(NY) for p in range(2)]
 OUT_GROUPS = [[g * 16 + i for i in range(16)] for g in range(NY * NZ // 2)]
 
@@ -85,8 +86,8 @@
         for n in range(8):
             at = head * 8 + n
             rows = slice((n % 4) * BLK, (n % 4 + 1) * BLK)
-            keys = proj_ref[n // 4, rows, 256 + head * E : 256 + (head + 1) * E]
-            values = proj_ref[n // 4, rows, 512 + head * E : 512 + (head + 1) * E]
+            keys = proj_ref[n // 4, rows, head * E : (head + 1) * E]
+            values = proj_ref[n // 4, rows, 256 + head * E : 256 + (head + 1) * E]
             last = row_ref[at : at + 1, BLK - 1 : BLK]
             scale = jnp.exp(last - col_ref[:, at : at + 1])
             prefix_ref[at] = state.astype(BF16)
@@ -97,15 +98,17 @@
             write_message(message_ref.at[copy], head, state, decay)
 
 
-def local_kernel(proj_ref, prefix_ref, col_ref, row_ref, out_ref):
+def local_kernel(total_ref, proj_ref, prefix_ref, col_ref, row_ref, query_ref, out_ref):
+    for half in range(2):
+        query_ref[half] = total_ref[half * 512 : (half + 1) * 512].astype(BF16)
     causal = lax.broadcasted_iota(jnp.int32, (BLK, BLK), 0) >= lax.broadcasted_iota(jnp.int32, (BLK, BLK), 1)
     for head in range(2):
         for n in range(8):
             at = head * 8 + n
             rows = slice((n % 4) * BLK, (n % 4 + 1) * BLK)
-            queries = proj_ref[n // 4, rows, head * E : (head + 1) * E]
-            keys = proj_ref[n // 4, rows, 256 + head * E : 256 + (head + 1) * E]
-            values = proj_ref[n // 4, rows, 512 + head * E : 512 + (head + 1) * E]
+            queries = query_ref[n // 4, rows, head * E : (head + 1) * E]
+            keys = proj_ref[n // 4, rows, head * E : (head + 1) * E]
+            values = proj_ref[n // 4, rows, 256 + head * E : 256 + (head + 1) * E]
             col = col_ref[:, at : at + 1]
             gaps = col - row_ref[at : at + 1, :]
             weights = jnp.exp(jnp.where(causal, gaps, -1e30))
@@ -136,7 +139,7 @@
 
 def final_kernel(*refs):
     messages = refs[:7]
-    before_ref, decay_ref, part_ref, proj_ref, col_ref, start_ref, gain_ref, out_ref = refs[7:]
+    before_ref, decay_ref, part_ref, query_ref, col_ref, start_ref, gain_ref, out_ref = refs[7:]
     for head in range(2):
         carried = jnp.zeros((E, E), F32)
         gone = jnp.zeros((1, E), F32)
@@ -148,7 +151,7 @@
         for n in range(8):
             at = head * 8 + n
             rows = slice((n % 4) * BLK, (n % 4 + 1) * BLK)
-            queries = proj_ref[n // 4, rows, head * E : (head + 1) * E]
+            queries = query_ref[n // 4, rows, head * E : (head + 1) * E]
             scale = jnp.exp(col_ref[:, at : at + 1] + start_ref[0:1, at : at + 1])
             scaled = (queries.astype(F32) * scale).astype(BF16)
             output = part_ref[at] + mm(scaled, incoming)
@@ -186,9 +189,11 @@
 
     def add(total, part, offset):
         x = lax.dynamic_slice_in_dim(all_rows, ((y + offset) % NY) * (NZ * 48), NZ * 48, 1)
-        d = jnp.dot(x, part.reshape(NZ * 48, 768), preferred_element_type=F32)
+        d = jnp.dot(x, part.reshape(NZ * 48, 512), preferred_element_type=F32)
         return d if total is None else total + d
 
+    query_block = block[:, :, :256]
+    block = block[:, :, 256:]
     ups, downs = [block], [block]
 
     def hop(*earlier):
@@ -212,21 +217,28 @@
     gain = lax.dynamic_slice_in_dim(norm_gain, side * 256, 256, 0).reshape(1, 256)
 
     hop()
-    hop(all_rows, rows, cols, starts, gain)
-    total = add_step(add(None, block, 0), 1)
+    hop(rows, cols, starts, gain)
+    total = add(add(None, block, 0), ups[1], -1)
+    query_weight = lax.all_gather(
+        after(query_block, all_rows), "seq", axis=0, tiled=True, axis_index_groups=Y_GROUPS
+    ).reshape(NY * NZ * 48, 256)
     up4 = lax.ppermute(after(ups[3], total)[:4], "seq", y_shift(1))
     down4 = lax.ppermute(after(downs[3], total)[4:], "seq", y_shift(-1))
-    total = add_step(add_step(total, 2), 3)
+    total = add_step(add_step(add(total, downs[1], 1), 2), 3)
     up4, down4, total = lax.optimization_barrier((up4, down4, total))
     total = add(total, jnp.concatenate([up4, down4], 0), 4)
 
     proj, prefix, messages = call(
         states_kernel,
-        [((2, 512, 768), BF16), ((16, E, E), BF16), ((4, 2, E + EXTRA, E), BF16)],
+        [((2, 512, 512), BF16), ((16, E, E), BF16), ((4, 2, E + EXTRA, E), BF16)],
         [], total, cols, rows, flops=16 * 2 * E**3,
     )
     messages = lax.all_to_all(messages, "seq", split_axis=0, concat_axis=0, tiled=True, axis_index_groups=ROW_GROUPS)
-    (part,) = call(local_kernel, [((16, BLK, E), F32)], [], proj, prefix, cols, rows, flops=16 * 6 * E**3)
+    query_total = jnp.dot(all_rows, after(query_weight, messages), preferred_element_type=F32)
+    query, part = call(
+        local_kernel, [((2, 512, 256), BF16), ((16, BLK, E), F32)], [], query_total, proj, prefix, cols, rows,
+        flops=16 * 6 * E**3,
+    )
     before, gone, row_message = call(
         row_kernel,
         [((2, E, E), F32), ((2, 8, E), F32), ((2, E + EXTRA, E), BF16)],
@@ -234,7 +246,7 @@
     )
     earlier = [lax.ppermute(row_message, "seq", y_later(k)) for k in range(1, NY)]
     (flat,) = call(
-        final_kernel, [((1024, 256), BF16)], [], *earlier, before, gone, part, proj, cols, starts, gain,
+        final_kernel, [((1024, 256), BF16)], [], *earlier, before, gone, part, query, cols, starts, gain,
         flops=16 * 2 * E**3,
     )
     sent = lax.all_to_all(

time: 164 us -> 156 us (0.951)
  waiting for transfers between devices: 22.8 us -> 14.1 us
  matrix products: 10.3 us -> 13.4 us
  starting transfers between devices: 55.2 us -> 52.3 us
    ppermute x3, waiting for transfers between devices: 7.69 us -> 3.23 us  [hop(): ups.append(lax.ppermute(after(ups[-1], *earlier), 'seq', y_shift(1)))]
    dot_general x8 -> x9, matrix products: 10.3 us -> 13.4 us  [the longest x8 8.35 us: add(): d = jnp.dot(x, part.reshape(NZ * 48, 512), preferred_element_type=F32)]
  transfers between devices with their start and end apart: 18 -> 19, of which waited for: 7 -> 3; matrix products, arithmetic and copies ran while one was open for 7% -> 10% of each run, Pallas kernels for 1% -> 2%
where the time goes in v4:
time: 156 us
  starting transfers between devices  52.3 us (34%)
  blocking collectives  51.4 us (33%)
  waiting for transfers between devices  14.1 us (9%)
  between operations  14 us (9%)
  matrix products  13.4 us (9%)
  Pallas kernels  7.06 us (5%)
  local copies, waits for them, and re-layouts  2.25 us (1%)
    all_to_all x1, blocking collectives, on_device(): lax.all_to_all(pieces, 'seq', split_axis=0, concat_axis=0, tiled=True, ax...  28 us
    all_to_all x1, blocking collectives, on_device(): lax.all_to_all(flat.reshape(16, 64, 256), ('seq', 'head'), split_axis=0,...  23.4 us
    ppermute x7, starting transfers between devices, on_device(): lax.ppermute(row_message, 'seq', y_later(k))  16.7 us
    ppermute x3, starting transfers between devices, hop(): downs.append(lax.ppermute(after(downs[-1], *earlier), 'seq', y_shift(-1)))  13.2 us
    dot_general x8, matrix products, add(): d = jnp.dot(x, part.reshape(NZ * 48, 512), preferred_element_type=F32)  8.35 us
    all_to_all x1, waiting for transfers between devices, on_device(): lax.all_to_all(messages, 'seq', split_axis=0, concat_axis=0, tiled=True,...  8.11 us
    pallas_call x6, Pallas kernels, call(): pl.pallas_call(kernel, out_shape=shapes, in_specs=smem + whole(len(args))...  7.06 us
    ppermute x3, starting transfers between devices, hop(): ups.append(lax.ppermute(after(ups[-1], *earlier), 'seq', y_shift(1)))  7 us
  transfers between devices with their start and end apart: 19, of which 3 were waited for; matrix products, arithmetic and copies ran while one was open for 10% of the time, Pallas kernels for 2%

profile of v4, /device:TPU:1, one launch (start us, length us, event | category | flops | bytes accessed | tf_op | source)
XLA Modules:
  0.0 155.7 jit_solution(6959245001216740134)
XLA Ops:
  6.5 0.7 all-gather.3.cloned.1.call-update
  7.3 0.0 all-gather.5.cloned.1.call-start
  7.3 0.9 copy-done
  8.3 28.0 %all_to_all.15 = bf16[8,48,768]{2,1,0:T(8,128)(2,1)S(1)} all-to-all(bf16[8,48,768]{2,1,0:T(8,128)(2,1)S(1)} %shard_map.46), channel_id=1, replica_groups={{0,8,16,24,32,40,48,56},{64,72,80,88,96,104,112,120},{128,136,144,152,1..., dimensions={0} | all-to-all | bytes 1179648 | tf_op jit(solution)/shard_map/all_to_all | solution.py:185
  36.3 3.2 %collective-permute-start = (bf16[8,48,512]{2,1,0:T(8,128)(2,1)S(1)}, bf16[8,48,512]{2,1,0:T(8,128)(2,1)S(1)}, u32[]{:S(2)}, u32[]{:S(2)}) collective-permute-start(bf16[8,48,512]{2,1,0:T(8,128)(2,1)S(1)} %slice.20), channel_id=1, source_target_pairs={{0,64},{8,72},{16,80},{24,88},{32,96},{40,104},{48,112},{56,120},{... | collective-permute-start | bytes 1179656 | tf_op jit(solution)/shard_map/ppermute | solution.py:200
  39.5 4.0 %collective-permute-start.5 = (bf16[8,48,512]{2,1,0:T(8,128)(2,1)S(1)}, bf16[8,48,512]{2,1,0:T(8,128)(2,1)S(1)}, u32[]{:S(2)}, u32[]{:S(2)}) collective-permute-start(bf16[8,48,512]{2,1,0:T(8,128)(2,1)S(1)} %slice.20), channel_id=1, source_target_pairs={{0,448},{8,456},{16,464},{24,472},{32,480},{40,488},{48,496},{56,5... | collective-permute-start | bytes 1179656 | tf_op jit(solution)/shard_map/ppermute | solution.py:201
  43.5 3.2 %collective-permute-done = bf16[8,48,512]{2,1,0:T(8,128)(2,1)S(1)} collective-permute-done((bf16[8,48,512]{2,1,0:T(8,128)(2,1)S(1)}, bf16[8,48,512]{2,1,0:T(8,128)(2,1)S(1)}, u32[]{:S(2)}, u32[]{:S(2)}) %collective-permute-start) | collective-permute-done | bytes 393248 | tf_op jit(solution)/shard_map/ppermute | solution.py:200
  46.8 1.9 %collective-permute-start.1 = (bf16[8,48,512]{2,1,0:T(8,128)(2,1)S(1)}, bf16[8,48,512]{2,1,0:T(8,128)(2,1)S(1)}, u32[]{:S(2)}, u32[]{:S(2)}) collective-permute-start(bf16[8,48,512]{2,1,0:T(8,128)(2,1)S(1)} %collective-permute-done), channel_id=1, source_target_pairs={{0,64},{8,72},{16,80},{24,88},{32,96},{40,104},{48,112},{56,120},{... | collective-permute-start | bytes 1179656 | tf_op jit(solution)/shard_map/ppermute | solution.py:200
  48.7 4.6 %collective-permute-start.6 = (bf16[8,48,512]{2,1,0:T(8,128)(2,1)S(1)}, bf16[8,48,512]{2,1,0:T(8,128)(2,1)S(1)}, u32[]{:S(2)}, u32[]{:S(2)}) collective-permute-start(bf16[8,48,512]{2,1,0:T(8,128)(2,1)S(1)} %collective-permute-done.5), channel_id=1, source_target_pairs={{0,448},{8,456},{16,464},{24,472},{32,480},{40,488},{48,496},{56,5... | collective-permute-start | bytes 1179656 | tf_op jit(solution)/shard_map/ppermute | solution.py:201
  53.4 1.9 %collective-permute-start.2 = (f32[2,512]{1,0:T(2,128)S(1)}, f32[2,512]{1,0:T(2,128)S(1)}, u32[]{:S(2)}, u32[]{:S(2)}) collective-permute-start(f32[2,512]{1,0:T(2,128)S(1)} %get-tuple-element.23), channel_id=1, source_target_pairs={{0,8},{8,0},{16,24},{24,16},{32,40},{40,32},{48,56},{56,48},{64,72... | collective-permute-start | bytes 12296 | tf_op jit(solution)/shard_map/ppermute | solution.py:210
  55.5 0.1 dynamic_slice.35
  55.6 0.7 slice.22
  56.3 1.9 %collective-permute-done.2 = f32[2,512]{1,0:T(2,128)S(1)} collective-permute-done((f32[2,512]{1,0:T(2,128)S(1)}, f32[2,512]{1,0:T(2,128)S(1)}, u32[]{:S(2)}, u32[]{:S(2)}) %collective-permute-start.2) | collective-permute-done | bytes 4128 | tf_op jit(solution)/shard_map/ppermute | solution.py:210
  58.3 0.6 reduce_window_sum.24
  58.8 0.2 slice_reduce_fusion
  59.0 0.2 reduce_window_sum.25
  59.2 0.1 squeeze.6
  59.3 0.1 copy.11
  59.4 0.1 reduce_window_sum.26
  59.5 1.9 %collective-permute-start.3 = (bf16[8,48,512]{2,1,0:T(8,128)(2,1)S(1)}, bf16[8,48,512]{2,1,0:T(8,128)(2,1)S(1)}, u32[]{:S(2)}, u32[]{:S(2)}) collective-permute-start(bf16[8,48,512]{2,1,0:T(8,128)(2,1)S(1)} %collective-permute-done.1), channel_id=1, source_target_pairs={{0,64},{8,72},{16,80},{24,88},{32,96},{40,104},{48,112},{56,120},{... | collective-permute-start | bytes 1179656 | tf_op jit(solution)/shard_map/ppermute | solution.py:200
  61.4 4.6 %collective-permute-start.7 = (bf16[8,48,512]{2,1,0:T(8,128)(2,1)S(1)}, bf16[8,48,512]{2,1,0:T(8,128)(2,1)S(1)}, u32[]{:S(2)}, u32[]{:S(2)}) collective-permute-start(bf16[8,48,512]{2,1,0:T(8,128)(2,1)S(1)} %collective-permute-done.6), channel_id=1, source_target_pairs={{0,448},{8,456},{16,464},{24,472},{32,480},{40,488},{48,496},{56,5... | collective-permute-start | bytes 1179656 | tf_op jit(solution)/shard_map/ppermute | solution.py:201
  66.0 2.0 %fusion.15 = f32[1024,512]{1,0:T(8,128)S(1)} fusion(bf16[384,512]{1,0:T(8,128)(2,1)S(1)} %bitcast.36, bf16[1024,3072]{1,0:T(8,128)(2,1)} %all-gather.3.cloned.1.call-done, s32[]{:T(128)S(6)} %select_n.102), kind=kOutput, calls=%fused_computation.16 | convolution fusion | flops 402653184 | bytes 3276804 | tf_op jit(solution)/shard_map/dot_general | solution.py:192
  68.0 1.9 %convolution_add_fusion = f32[1024,512]{1,0:T(8,128)S(1)} fusion(f32[1024,512]{1,0:T(8,128)S(1)} %fusion.15, bf16[384,512]{1,0:T(8,128)(2,1)S(1)} %bitcast.43, bf16[1024,3072]{1,0:T(8,128)(2,1)} %all-gather.3.cloned.1.call-done, s32[]{:T(128)S(6)} %select_n.104), kind=kOutput, calls=%fused_computation.1 | convolution fusion | flops 403177472 | bytes 5373956 | tf_op jit(solution)/shard_map/dot_general | solution.py:192
  70.0 3.1 %collective-permute-start.4 = (bf16[4,48,512]{2,1,0:T(8,128)(2,1)S(1)}, bf16[4,48,512]{2,1,0:T(8,128)(2,1)S(1)}, u32[]{:S(2)}, u32[]{:S(2)}) collective-permute-start(bf16[4,48,512]{2,1,0:T(8,128)(2,1)S(1)} %slice.17), channel_id=1, source_target_pairs={{0,64},{8,72},{16,80},{24,88},{32,96},{40,104},{48,112},{56,120},{... | collective-permute-start | bytes 589832 | tf_op jit(solution)/shard_map/ppermute | solution.py:225
  73.1 3.8 %collective-permute-start.8 = (bf16[4,48,512]{2,1,0:T(8,128)(2,1)S(1)}, bf16[4,48,512]{2,1,0:T(8,128)(2,1)S(1)}, u32[]{:S(2)}, u32[]{:S(2)}) collective-permute-start(bf16[4,48,512]{2,1,0:T(8,128)(2,1)S(1)} %slice.18), channel_id=1, source_target_pairs={{0,448},{8,456},{16,464},{24,472},{32,480},{40,488},{48,496},{56,5... | collective-permute-start | bytes 589832 | tf_op jit(solution)/shard_map/ppermute | solution.py:226
  76.9 0.7 fusion.6
  77.6 0.7 fusion.8
  78.3 0.7 fusion.10
  79.0 0.7 fusion.12
  79.7 1.0 add_add_fusion
  80.8 0.7 fusion
  81.5 0.5 add.142.total_ref
  82.0 2.6 %shard_map.47 = (bf16[2,512,512]{2,1,0:T(8,128)(2,1)S(1)}, bf16[16,128,128]{2,1,0:T(8,128)(2,1)S(1)}, bf16[4,2,144,128]{3,2,1,0:T(8,128)(2,1)}) custom-call(f32[1024,512]{1,0:T(8,128)S(1)} %add.142.total_ref, f32[128,16]{1,0:T(8,128)S(1)} %bitcast.28, f32[16,128]{1,0:T(8,128)S(1)} %bitcast.32), custom_call_target="tpu_custom_call" | custom-call | flops 67108864 | bytes 2113536 | tf_op jit(solution)/shard_map/pallas_call | solution.py:167
  84.6 6.6 %all-to-all-start.1 = ((bf16[4,2,144,128]{3,2,1,0:T(8,128)(2,1)}), bf16[4,2,144,128]{3,2,1,0:T(8,128)(2,1)S(1)}, u32[]{:S(2)}, u32[]{:S(2)}) async-start(bf16[4,2,144,128]{3,2,1,0:T(8,128)(2,1)} %get-tuple-element.31), calls=%async_computation.1 | async-start | bytes 589824 | tf_op jit(solution)/shard_map/all_to_all | solution.py:236
  91.2 8.1 %all-to-all-done.1.messages_ref = bf16[4,2,144,128]{3,2,1,0:T(8,128)(2,1)S(1)} async-done(((bf16[4,2,144,128]{3,2,1,0:T(8,128)(2,1)}), bf16[4,2,144,128]{3,2,1,0:T(8,128)(2,1)S(1)}, u32[]{:S(2)}, u32[]{:S(2)}) %all-to-all-start.1) | async-done | bytes 294944 | tf_op jit(solution)/shard_map/all_to_all | solution.py:236
  99.3 0.1 shard_map.48
  99.4 1.6 %collective-permute-start.9 = (bf16[2,144,128]{2,1,0:T(8,128)(2,1)S(1)}, bf16[2,144,128]{2,1,0:T(8,128)(2,1)S(1)}, u32[]{:S(2)}, u32[]{:S(2)}) collective-permute-start(bf16[2,144,128]{2,1,0:T(8,128)(2,1)S(1)} %get-tuple-element.32), channel_id=1, source_target_pairs={{0,64},{8,72},{16,80},{24,88},{32,96},{40,104},{48,112},{56,120},{... | collective-permute-start | bytes 221192 | tf_op jit(solution)/shard_map/ppermute | solution.py:247
  101.0 6.6 %collective-permute-start.10 = (bf16[2,144,128]{2,1,0:T(8,128)(2,1)S(1)}, bf16[2,144,128]{2,1,0:T(8,128)(2,1)S(1)}, u32[]{:S(2)}, u32[]{:S(2)}) collective-permute-start(bf16[2,144,128]{2,1,0:T(8,128)(2,1)S(1)} %get-tuple-element.32), channel_id=1, source_target_pairs={{0,128},{8,136},{16,144},{24,152},{32,160},{40,168},{48,176},{56,1... | collective-permute-start | bytes 221192 | tf_op jit(solution)/shard_map/ppermute | solution.py:247
  107.6 2.5 %collective-permute-start.11 = (bf16[2,144,128]{2,1,0:T(8,128)(2,1)S(1)}, bf16[2,144,128]{2,1,0:T(8,128)(2,1)S(1)}, u32[]{:S(2)}, u32[]{:S(2)}) collective-permute-start(bf16[2,144,128]{2,1,0:T(8,128)(2,1)S(1)} %get-tuple-element.32), channel_id=1, source_target_pairs={{0,192},{8,200},{16,208},{24,216},{32,224},{40,232},{48,240},{56,2... | collective-permute-start | bytes 221192 | tf_op jit(solution)/shard_map/ppermute | solution.py:247
  110.1 2.1 %collective-permute-start.12 = (bf16[2,144,128]{2,1,0:T(8,128)(2,1)S(1)}, bf16[2,144,128]{2,1,0:T(8,128)(2,1)S(1)}, u32[]{:S(2)}, u32[]{:S(2)}) collective-permute-start(bf16[2,144,128]{2,1,0:T(8,128)(2,1)S(1)} %get-tuple-element.32), channel_id=1, source_target_pairs={{0,256},{8,264},{16,272},{24,280},{32,288},{40,296},{48,304},{56,3... | collective-permute-start | bytes 221192 | tf_op jit(solution)/shard_map/ppermute | solution.py:247
  112.2 1.3 collective-permute-start.13
  113.5 1.3 collective-permute-start.14
  114.9 1.3 collective-permute-start.15
  116.2 5.0 %convolution_bitcast_fusion.total_ref = f32[1024,256]{1,0:T(8,128)S(1)} fusion(bf16[1024,3072]{1,0:T(8,128)(2,1)} %all-gather.3.cloned.1.call-done, bf16[3072,256]{1,0:T(8,128)(2,1)} %bitcast.44), kind=kOutput, calls=%fused_computation.2 | convolution fusion | flops 1610612736 | bytes 8912896 | tf_op jit(solution)/shard_map/dot_general | solution.py:237
  121.2 0.9 shard_map.49
  122.1 2.5 %shard_map.50 = bf16[1024,256]{1,0:T(8,128)(2,1)S(1)} custom-call(bf16[2,144,128]{2,1,0:T(8,128)(2,1)S(1)} %collective-permute-done.9.refs_0_, bf16[2,144,128]{2,1,0:T(8,128)(2,1)S(1)} %collective-permute-done.10.refs_1_, bf16[2,144,128]{2,1,0:T(8,128)(2,1)S(1)} %collective-permute-done.11.refs_2_, bf16[2,144,128]{2,1,0:T(8,128)(2,1)S(1)} %collective-permute-done.12.refs_3_, ...), custom_call_target="tpu_custom_call" | custom-call | flops 67108864 | bytes 2237504 | tf_op jit(solution)/shard_map/pallas_call | solution.py:167
  124.7 23.4 %all_to_all.16.sent_ref = bf16[16,64,256]{2,1,0:T(8,128)(2,1)S(1)} all-to-all(bf16[16,64,256]{2,1,0:T(8,128)(2,1)S(1)} %bitcast.27), channel_id=1, replica_groups={{0,1,2,3,4,5,6,7,8,9,10,11,12,13,14,15},{16,17,18,19,20,21,22,23,24,25,..., dimensions={0} | all-to-all | bytes 1048576 | tf_op jit(solution)/shard_map/all_to_all | solution.py:252
  148.0 0.8 shard_map.51
  (35 shorter events, 0.3 us)
Async XLA Ops:
  6.5 46.9 %copy-start.2 = (f32[4,512]{1,0:T(4,128)S(1)}, f32[4,512]{1,0:T(4,128)}, u32[]{:S(2)}) copy-start(f32[4,512]{1,0:T(4,128)} %param.6) | copy-start | bytes 24580
  6.5 48.9 %copy-start.3 = (f32[512]{0:T(512)S(1)}, f32[512]{0:T(512)}, u32[]{:S(2)}) copy-start(f32[512]{0:T(512)} %param.7) | copy-start | bytes 6148
  6.5 59.5 %all-gather.3.cloned.1.call-start = ((), (), s32[]{:S(2)}) async-start(), calls=%async_computation.3 | async-start | bytes 6684672 | tf_op jit(solution)/shard_map/all_gather | solution.py:187
  7.3 106.3 %all-gather.5.cloned.1.call-start = ((), (), s32[]{:S(2)}) async-start(), calls=%async_computation.4 | async-start | bytes 1769472 | tf_op jit(solution)/shard_map/all_gather | solution.py:222
  7.3 0.9 copy-start
  36.3 10.5 %collective-permute-start = (bf16[8,48,512]{2,1,0:T(8,128)(2,1)S(1)}, bf16[8,48,512]{2,1,0:T(8,128)(2,1)S(1)}, u32[]{:S(2)}, u32[]{:S(2)}) collective-permute-start(bf16[8,48,512]{2,1,0:T(8,128)(2,1)S(1)} %slice.20), channel_id=1, source_target_pairs={{0,64},{8,72},{16,80},{24,88},{32,96},{40,104},{48,112},{56,120},{... | collective-permute-start | bytes 1179656 | tf_op jit(solution)/shard_map/ppermute | solution.py:200
  39.5 9.2 %collective-permute-start.5 = (bf16[8,48,512]{2,1,0:T(8,128)(2,1)S(1)}, bf16[8,48,512]{2,1,0:T(8,128)(2,1)S(1)}, u32[]{:S(2)}, u32[]{:S(2)}) collective-permute-start(bf16[8,48,512]{2,1,0:T(8,128)(2,1)S(1)} %slice.20), channel_id=1, source_target_pairs={{0,448},{8,456},{16,464},{24,472},{32,480},{40,488},{48,496},{56,5... | collective-permute-start | bytes 1179656 | tf_op jit(solution)/shard_map/ppermute | solution.py:201
  46.8 12.7 %collective-permute-start.1 = (bf16[8,48,512]{2,1,0:T(8,128)(2,1)S(1)}, bf16[8,48,512]{2,1,0:T(8,128)(2,1)S(1)}, u32[]{:S(2)}, u32[]{:S(2)}) collective-permute-start(bf16[8,48,512]{2,1,0:T(8,128)(2,1)S(1)} %collective-permute-done), channel_id=1, source_target_pairs={{0,64},{8,72},{16,80},{24,88},{32,96},{40,104},{48,112},{56,120},{... | collective-permute-start | bytes 1179656 | tf_op jit(solution)/shard_map/ppermute | solution.py:200
  48.7 12.7 %collective-permute-start.6 = (bf16[8,48,512]{2,1,0:T(8,128)(2,1)S(1)}, bf16[8,48,512]{2,1,0:T(8,128)(2,1)S(1)}, u32[]{:S(2)}, u32[]{:S(2)}) collective-permute-start(bf16[8,48,512]{2,1,0:T(8,128)(2,1)S(1)} %collective-permute-done.5), channel_id=1, source_target_pairs={{0,448},{8,456},{16,464},{24,472},{32,480},{40,488},{48,496},{56,5... | collective-permute-start | bytes 1179656 | tf_op jit(solution)/shard_map/ppermute | solution.py:201
  53.4 4.8 %collective-permute-start.2 = (f32[2,512]{1,0:T(2,128)S(1)}, f32[2,512]{1,0:T(2,128)S(1)}, u32[]{:S(2)}, u32[]{:S(2)}) collective-permute-start(f32[2,512]{1,0:T(2,128)S(1)} %get-tuple-element.23), channel_id=1, source_target_pairs={{0,8},{8,0},{16,24},{24,16},{32,40},{40,32},{48,56},{56,48},{64,72... | collective-permute-start | bytes 12296 | tf_op jit(solution)/shard_map/ppermute | solution.py:210
  59.5 10.5 %collective-permute-start.3 = (bf16[8,48,512]{2,1,0:T(8,128)(2,1)S(1)}, bf16[8,48,512]{2,1,0:T(8,128)(2,1)S(1)}, u32[]{:S(2)}, u32[]{:S(2)}) collective-permute-start(bf16[8,48,512]{2,1,0:T(8,128)(2,1)S(1)} %collective-permute-done.1), channel_id=1, source_target_pairs={{0,64},{8,72},{16,80},{24,88},{32,96},{40,104},{48,112},{56,120},{... | collective-permute-start | bytes 1179656 | tf_op jit(solution)/shard_map/ppermute | solution.py:200
  61.4 11.7 %collective-permute-start.7 = (bf16[8,48,512]{2,1,0:T(8,128)(2,1)S(1)}, bf16[8,48,512]{2,1,0:T(8,128)(2,1)S(1)}, u32[]{:S(2)}, u32[]{:S(2)}) collective-permute-start(bf16[8,48,512]{2,1,0:T(8,128)(2,1)S(1)} %collective-permute-done.6), channel_id=1, source_target_pairs={{0,448},{8,456},{16,464},{24,472},{32,480},{40,488},{48,496},{56,5... | collective-permute-start | bytes 1179656 | tf_op jit(solution)/shard_map/ppermute | solution.py:201
  66.0 10.9 %copy-start.1 = (bf16[1024,3072]{1,0:T(8,128)(2,1)S(1)}, bf16[1024,3072]{1,0:T(8,128)(2,1)}, u32[]{:S(2)}) copy-start(bf16[1024,3072]{1,0:T(8,128)(2,1)} %all-gather.3.cloned.1.call-done) | copy-start | bytes 18874372
  70.0 10.8 %collective-permute-start.4 = (bf16[4,48,512]{2,1,0:T(8,128)(2,1)S(1)}, bf16[4,48,512]{2,1,0:T(8,128)(2,1)S(1)}, u32[]{:S(2)}, u32[]{:S(2)}) collective-permute-start(bf16[4,48,512]{2,1,0:T(8,128)(2,1)S(1)} %slice.17), channel_id=1, source_target_pairs={{0,64},{8,72},{16,80},{24,88},{32,96},{40,104},{48,112},{56,120},{... | collective-permute-start | bytes 589832 | tf_op jit(solution)/shard_map/ppermute | solution.py:225
  73.1 7.6 %collective-permute-start.8 = (bf16[4,48,512]{2,1,0:T(8,128)(2,1)S(1)}, bf16[4,48,512]{2,1,0:T(8,128)(2,1)S(1)}, u32[]{:S(2)}, u32[]{:S(2)}) collective-permute-start(bf16[4,48,512]{2,1,0:T(8,128)(2,1)S(1)} %slice.18), channel_id=1, source_target_pairs={{0,448},{8,456},{16,464},{24,472},{32,480},{40,488},{48,496},{56,5... | collective-permute-start | bytes 589832 | tf_op jit(solution)/shard_map/ppermute | solution.py:226
  84.6 14.7 %all-to-all-start.1 = ((bf16[4,2,144,128]{3,2,1,0:T(8,128)(2,1)}), bf16[4,2,144,128]{3,2,1,0:T(8,128)(2,1)S(1)}, u32[]{:S(2)}, u32[]{:S(2)}) async-start(bf16[4,2,144,128]{3,2,1,0:T(8,128)(2,1)} %get-tuple-element.31), calls=%async_computation.1 | async-start | bytes 589824 | tf_op jit(solution)/shard_map/all_to_all | solution.py:236
  99.4 14.1 %collective-permute-start.9 = (bf16[2,144,128]{2,1,0:T(8,128)(2,1)S(1)}, bf16[2,144,128]{2,1,0:T(8,128)(2,1)S(1)}, u32[]{:S(2)}, u32[]{:S(2)}) collective-permute-start(bf16[2,144,128]{2,1,0:T(8,128)(2,1)S(1)} %get-tuple-element.32), channel_id=1, source_target_pairs={{0,64},{8,72},{16,80},{24,88},{32,96},{40,104},{48,112},{56,120},{... | collective-permute-start | bytes 221192 | tf_op jit(solution)/shard_map/ppermute | solution.py:247
  101.0 13.9 %collective-permute-start.10 = (bf16[2,144,128]{2,1,0:T(8,128)(2,1)S(1)}, bf16[2,144,128]{2,1,0:T(8,128)(2,1)S(1)}, u32[]{:S(2)}, u32[]{:S(2)}) collective-permute-start(bf16[2,144,128]{2,1,0:T(8,128)(2,1)S(1)} %get-tuple-element.32), channel_id=1, source_target_pairs={{0,128},{8,136},{16,144},{24,152},{32,160},{40,168},{48,176},{56,1... | collective-permute-start | bytes 221192 | tf_op jit(solution)/shard_map/ppermute | solution.py:247
  107.6 14.5 %collective-permute-start.11 = (bf16[2,144,128]{2,1,0:T(8,128)(2,1)S(1)}, bf16[2,144,128]{2,1,0:T(8,128)(2,1)S(1)}, u32[]{:S(2)}, u32[]{:S(2)}) collective-permute-start(bf16[2,144,128]{2,1,0:T(8,128)(2,1)S(1)} %get-tuple-element.32), channel_id=1, source_target_pairs={{0,192},{8,200},{16,208},{24,216},{32,224},{40,232},{48,240},{56,2... | collective-permute-start | bytes 221192 | tf_op jit(solution)/shard_map/ppermute | solution.py:247
  110.1 12.0 %collective-permute-start.12 = (bf16[2,144,128]{2,1,0:T(8,128)(2,1)S(1)}, bf16[2,144,128]{2,1,0:T(8,128)(2,1)S(1)}, u32[]{:S(2)}, u32[]{:S(2)}) collective-permute-start(bf16[2,144,128]{2,1,0:T(8,128)(2,1)S(1)} %get-tuple-element.32), channel_id=1, source_target_pairs={{0,256},{8,264},{16,272},{24,280},{32,288},{40,296},{48,304},{56,3... | collective-permute-start | bytes 221192 | tf_op jit(solution)/shard_map/ppermute | solution.py:247
  112.2 9.9 %collective-permute-start.13 = (bf16[2,144,128]{2,1,0:T(8,128)(2,1)S(1)}, bf16[2,144,128]{2,1,0:T(8,128)(2,1)S(1)}, u32[]{:S(2)}, u32[]{:S(2)}) collective-permute-start(bf16[2,144,128]{2,1,0:T(8,128)(2,1)S(1)} %get-tuple-element.32), channel_id=1, source_target_pairs={{0,320},{8,328},{16,336},{24,344},{32,352},{40,360},{48,368},{56,3... | collective-permute-start | bytes 221192 | tf_op jit(solution)/shard_map/ppermute | solution.py:247
  113.5 8.6 %collective-permute-start.14 = (bf16[2,144,128]{2,1,0:T(8,128)(2,1)S(1)}, bf16[2,144,128]{2,1,0:T(8,128)(2,1)S(1)}, u32[]{:S(2)}, u32[]{:S(2)}) collective-permute-start(bf16[2,144,128]{2,1,0:T(8,128)(2,1)S(1)} %get-tuple-element.32), channel_id=1, source_target_pairs={{0,384},{8,392},{16,400},{24,408},{32,416},{40,424},{48,432},{56,4... | collective-permute-start | bytes 221192 | tf_op jit(solution)/shard_map/ppermute | solution.py:247
  114.9 7.3 %collective-permute-start.15 = (bf16[2,144,128]{2,1,0:T(8,128)(2,1)S(1)}, bf16[2,144,128]{2,1,0:T(8,128)(2,1)S(1)}, u32[]{:S(2)}, u32[]{:S(2)}) collective-permute-start(bf16[2,144,128]{2,1,0:T(8,128)(2,1)S(1)} %get-tuple-element.32), channel_id=1, source_target_pairs={{0,448},{8,456},{16,464},{24,472},{32,480},{40,488},{48,496},{56,5... | collective-permute-start | bytes 221192 | tf_op jit(solution)/shard_map/ppermute | solution.py:247
Sparse Core Ops, SparseCore 0:
  9.5 56.3 all-gather.2
  67.9 41.8 all-gather.4

commit v5 on v4

--- a/solution.py
+++ b/solution.py
@@ -64,11 +64,12 @@
     return (rows[0:1] + rows[1:2]) + rows[2:3]
 
 
-def pieces_kernel(weight_ref, out_ref):
-    for c in range(3):
-        for i in range(NZ):
-            half = slice((i % 2) * 256, (i % 2 + 1) * 256)
-            out_ref[i, :, c * 256 : (c + 1) * 256] = weight_ref[c, :, half]
+def pieces_kernel(weight_ref, query_ref, out_ref):
+    for i in range(NZ):
+        half = slice((i % 2) * 256, (i % 2 + 1) * 256)
+        query_ref[i] = weight_ref[0, :, half]
+        for c in range(2):
+            out_ref[i, :, c * 256 : (c + 1) * 256] = weight_ref[c + 1, :, half]
 
 
 def order_kernel(sent_ref, out_ref):
@@ -77,9 +78,10 @@
             out_ref[:, (h * 2 + s) * 256 : (h * 2 + s + 1) * 256] = sent_ref[s * NH + h]
 
 
-def states_kernel(total_ref, col_ref, row_ref, proj_ref, prefix_ref, message_ref):
+def states_kernel(total_ref, last_ref, col_ref, row_ref, proj_ref, prefix_ref, message_ref):
     for half in range(2):
-        proj_ref[half] = total_ref[half * 512 : (half + 1) * 512].astype(BF16)
+        part = slice(half * 512, (half + 1) * 512)
+        proj_ref[half] = (total_ref[part] + last_ref[part]).astype(BF16)
     for head in range(2):
         state = jnp.zeros((E, E), F32)
         decay = jnp.zeros((1, 1), F32)
@@ -181,7 +183,9 @@
     place = z // 2
     place1 = place.reshape(1).astype(jnp.int32)
 
-    (pieces,) = call(pieces_kernel, [((NZ, 48, 768), BF16)], [], qkv_weight.transpose(1, 0, 2))
+    query_pieces, pieces = call(
+        pieces_kernel, [((NZ, 48, 256), BF16), ((NZ, 48, 512), BF16)], [], qkv_weight.transpose(1, 0, 2)
+    )
     block = lax.all_to_all(pieces, "seq", split_axis=0, concat_axis=0, tiled=True, axis_index_groups=Z_GROUPS)
 
     all_rows = lax.all_gather(tokens, ("seq", "head"), axis=0, tiled=True, axis_index_groups=OUT_GROUPS)
@@ -192,8 +196,6 @@
         d = jnp.dot(x, part.reshape(NZ * 48, 512), preferred_element_type=F32)
         return d if total is None else total + d
 
-    query_block = block[:, :, :256]
-    block = block[:, :, 256:]
     ups, downs = [block], [block]
 
     def hop(*earlier):
@@ -204,6 +206,9 @@
         return add(add(total, ups[step], -step), downs[step], step)
 
     hop()
+    query_block = lax.all_to_all(
+        after(query_pieces, block), "seq", split_axis=0, concat_axis=0, tiled=True, axis_index_groups=Z_GROUPS
+    )
 
     mine = lax.dynamic_slice_in_dim(log_decay, side * 2, 2, 0)
     wanted = lax.dynamic_slice_in_dim(log_decay, (1 - side) * 2, 2, 0)
@@ -226,12 +231,12 @@
     down4 = lax.ppermute(after(downs[3], total)[4:], "seq", y_shift(-1))
     total = add_step(add_step(add(total, downs[1], 1), 2), 3)
     up4, down4, total = lax.optimization_barrier((up4, down4, total))
-    total = add(total, jnp.concatenate([up4, down4], 0), 4)
+    last = add(None, jnp.concatenate([up4, down4], 0), 4)
 
     proj, prefix, messages = call(
         states_kernel,
         [((2, 512, 512), BF16), ((16, E, E), BF16), ((4, 2, E + EXTRA, E), BF16)],
-        [], total, cols, rows, flops=16 * 2 * E**3,
+        [], total, last, cols, rows, flops=16 * 2 * E**3,
     )
     messages = lax.all_to_all(messages, "seq", split_axis=0, concat_axis=0, tiled=True, axis_index_groups=ROW_GROUPS)
     query_total = jnp.dot(all_rows, after(query_weight, messages), preferred_element_type=F32)

time: 156 us -> 160 us (1.026)
  blocking collectives: 51.4 us -> 46.5 us
  starting transfers between devices: 52.3 us -> 56.5 us
  waiting for transfers between devices: 14.1 us -> 17.1 us
    all_to_all x0 -> x1, starting transfers between devices: none -> 3.91 us  [on_device(): lax.all_to_all(after(query_pieces, block), 'seq', split_axis=0, concat_ax...]
    all_to_all x1, blocking collectives: 28 us -> 24.1 us  [on_device(): lax.all_to_all(pieces, 'seq', split_axis=0, concat_axis=0, tiled=True, ax...]
    ppermute x3, waiting for transfers between devices: 3.23 us -> 5.26 us  [hop(): ups.append(lax.ppermute(after(ups[-1], *earlier), 'seq', y_shift(1)))]
  transfers between devices with their start and end apart: 19 -> 20, of which waited for: 3 -> 3; matrix products, arithmetic and copies ran while one was open for 10% -> 10% of each run, Pallas kernels for 2% -> 3%
where the time goes in v5:
time: 160 us
  starting transfers between devices  56.5 us (35%)
  blocking collectives  46.5 us (29%)
  waiting for transfers between devices  17.1 us (11%)
  between operations  14 us (9%)
  matrix products  13.4 us (8%)
  Pallas kernels  7.74 us (5%)
  local copies, waits for them, and re-layouts  3.62 us (2%)
    all_to_all x1, blocking collectives, on_device(): lax.all_to_all(pieces, 'seq', split_axis=0, concat_axis=0, tiled=True, ax...  24.1 us
    all_to_all x1, blocking collectives, on_device(): lax.all_to_all(flat.reshape(16, 64, 256), ('seq', 'head'), split_axis=0,...  22.3 us
    ppermute x7, starting transfers between devices, on_device(): lax.ppermute(row_message, 'seq', y_later(k))  16.7 us
    ppermute x3, starting transfers between devices, hop(): downs.append(lax.ppermute(after(downs[-1], *earlier), 'seq', y_shift(-1)))  13 us
    all_to_all x1, waiting for transfers between devices, on_device(): lax.all_to_all(messages, 'seq', split_axis=0, concat_axis=0, tiled=True,...  8.9 us
    dot_general x8, matrix products, add(): d = jnp.dot(x, part.reshape(NZ * 48, 512), preferred_element_type=F32)  8.36 us
    pallas_call x6, Pallas kernels, call(): pl.pallas_call(kernel, out_shape=shapes, in_specs=smem + whole(len(args))...  7.74 us
    ppermute x3, starting transfers between devices, hop(): ups.append(lax.ppermute(after(ups[-1], *earlier), 'seq', y_shift(1)))  7.04 us
  transfers between devices with their start and end apart: 20, of which 3 were waited for; matrix products, arithmetic and copies ran while one was open for 10% of the time, Pallas kernels for 3%

profile of v5, /device:TPU:1, one launch (start us, length us, event | category | flops | bytes accessed | tf_op | source)
XLA Modules:
  0.0 159.6 jit_solution(14323590196128105566)
XLA Ops:
  6.5 0.7 all-gather.3.cloned.1.call-update
  7.3 0.9 copy-done
  8.2 0.7 shard_map.46
  8.9 24.1 %all_to_all.20 = bf16[8,48,512]{2,1,0:T(8,128)(2,1)S(1)} all-to-all(bf16[8,48,512]{2,1,0:T(8,128)(2,1)S(1)} %get-tuple-element.26), channel_id=1, replica_groups={{0,8,16,24,32,40,48,56},{64,72,80,88,96,104,112,120},{128,136,144,152,1..., dimensions={0} | all-to-all | bytes 786432 | tf_op jit(solution)/shard_map/all_to_all | solution.py:189
  33.0 3.2 %collective-permute-start = (bf16[8,48,512]{2,1,0:T(8,128)(2,1)S(1)}, bf16[8,48,512]{2,1,0:T(8,128)(2,1)S(1)}, u32[]{:S(2)}, u32[]{:S(2)}) collective-permute-start(bf16[8,48,512]{2,1,0:T(8,128)(2,1)S(1)} %all_to_all.20), channel_id=1, source_target_pairs={{0,64},{8,72},{16,80},{24,88},{32,96},{40,104},{48,112},{56,120},{... | collective-permute-start | bytes 1179656 | tf_op jit(solution)/shard_map/ppermute | solution.py:202
  36.3 3.8 %collective-permute-start.5 = (bf16[8,48,512]{2,1,0:T(8,128)(2,1)S(1)}, bf16[8,48,512]{2,1,0:T(8,128)(2,1)S(1)}, u32[]{:S(2)}, u32[]{:S(2)}) collective-permute-start(bf16[8,48,512]{2,1,0:T(8,128)(2,1)S(1)} %all_to_all.20), channel_id=1, source_target_pairs={{0,448},{8,456},{16,464},{24,472},{32,480},{40,488},{48,496},{56,5... | collective-permute-start | bytes 1179656 | tf_op jit(solution)/shard_map/ppermute | solution.py:203
  40.1 5.3 %collective-permute-done = bf16[8,48,512]{2,1,0:T(8,128)(2,1)S(1)} collective-permute-done((bf16[8,48,512]{2,1,0:T(8,128)(2,1)S(1)}, bf16[8,48,512]{2,1,0:T(8,128)(2,1)S(1)}, u32[]{:S(2)}, u32[]{:S(2)}) %collective-permute-start) | collective-permute-done | bytes 393248 | tf_op jit(solution)/shard_map/ppermute | solution.py:202
  45.3 1.9 %collective-permute-start.1 = (bf16[8,48,512]{2,1,0:T(8,128)(2,1)S(1)}, bf16[8,48,512]{2,1,0:T(8,128)(2,1)S(1)}, u32[]{:S(2)}, u32[]{:S(2)}) collective-permute-start(bf16[8,48,512]{2,1,0:T(8,128)(2,1)S(1)} %collective-permute-done), channel_id=1, source_target_pairs={{0,64},{8,72},{16,80},{24,88},{32,96},{40,104},{48,112},{56,120},{... | collective-permute-start | bytes 1179656 | tf_op jit(solution)/shard_map/ppermute | solution.py:202
  47.3 4.6 %collective-permute-start.6 = (bf16[8,48,512]{2,1,0:T(8,128)(2,1)S(1)}, bf16[8,48,512]{2,1,0:T(8,128)(2,1)S(1)}, u32[]{:S(2)}, u32[]{:S(2)}) collective-permute-start(bf16[8,48,512]{2,1,0:T(8,128)(2,1)S(1)} %collective-permute-done.5), channel_id=1, source_target_pairs={{0,448},{8,456},{16,464},{24,472},{32,480},{40,488},{48,496},{56,5... | collective-permute-start | bytes 1179656 | tf_op jit(solution)/shard_map/ppermute | solution.py:203
  51.9 3.9 %all-to-all-start.2 = ((bf16[8,48,256]{2,1,0:T(8,128)(2,1)}), bf16[8,48,256]{2,1,0:T(8,128)(2,1)S(1)}, u32[]{:S(2)}, u32[]{:S(2)}) async-start(bf16[8,48,256]{2,1,0:T(8,128)(2,1)} %get-tuple-element.40), calls=%async_computation.2 | async-start | bytes 393216 | tf_op jit(solution)/shard_map/all_to_all | solution.py:209
  55.9 0.8 constant_dynamic-slice_fusion.1
  56.7 3.2 %collective-permute-start.2 = (f32[2,512]{1,0:T(2,128)S(1)}, f32[2,512]{1,0:T(2,128)S(1)}, u32[]{:S(2)}, u32[]{:S(2)}) collective-permute-start(f32[2,512]{1,0:T(2,128)S(1)} %get-tuple-element.27), channel_id=1, source_target_pairs={{0,8},{8,0},{16,24},{24,16},{32,40},{40,32},{48,56},{56,48},{64,72... | collective-permute-start | bytes 12296 | tf_op jit(solution)/shard_map/ppermute | solution.py:215
  60.1 0.8 dynamic_slice.35
  60.9 2.1 %collective-permute-done.2 = f32[2,512]{1,0:T(2,128)S(1)} collective-permute-done((f32[2,512]{1,0:T(2,128)S(1)}, f32[2,512]{1,0:T(2,128)S(1)}, u32[]{:S(2)}, u32[]{:S(2)}) %collective-permute-start.2) | collective-permute-done | bytes 4128 | tf_op jit(solution)/shard_map/ppermute | solution.py:215
  63.0 0.6 reduce_window_sum.24
  63.6 0.2 slice_reduce_fusion
  63.7 0.2 reduce_window_sum.25
  64.0 0.1 copy.11
  64.1 0.1 reduce_window_sum.26
  64.2 1.9 %collective-permute-start.3 = (bf16[8,48,512]{2,1,0:T(8,128)(2,1)S(1)}, bf16[8,48,512]{2,1,0:T(8,128)(2,1)S(1)}, u32[]{:S(2)}, u32[]{:S(2)}) collective-permute-start(bf16[8,48,512]{2,1,0:T(8,128)(2,1)S(1)} %collective-permute-done.1), channel_id=1, source_target_pairs={{0,64},{8,72},{16,80},{24,88},{32,96},{40,104},{48,112},{56,120},{... | collective-permute-start | bytes 1179656 | tf_op jit(solution)/shard_map/ppermute | solution.py:202
  66.1 4.6 %collective-permute-start.7 = (bf16[8,48,512]{2,1,0:T(8,128)(2,1)S(1)}, bf16[8,48,512]{2,1,0:T(8,128)(2,1)S(1)}, u32[]{:S(2)}, u32[]{:S(2)}) collective-permute-start(bf16[8,48,512]{2,1,0:T(8,128)(2,1)S(1)} %collective-permute-done.6), channel_id=1, source_target_pairs={{0,448},{8,456},{16,464},{24,472},{32,480},{40,488},{48,496},{56,5... | collective-permute-start | bytes 1179656 | tf_op jit(solution)/shard_map/ppermute | solution.py:203
  70.7 0.7 copy-done.2
  71.5 2.0 %fusion.15 = f32[1024,512]{1,0:T(8,128)S(1)} fusion(bf16[384,512]{1,0:T(8,128)(2,1)S(1)} %bitcast.36, bf16[1024,3072]{1,0:T(8,128)(2,1)} %all-gather.3.cloned.1.call-done, s32[]{:T(128)S(6)} %select_n.102), kind=kOutput, calls=%fused_computation.16 | convolution fusion | flops 402653184 | bytes 3276804 | tf_op jit(solution)/shard_map/dot_general | solution.py:196
  73.4 1.9 %convolution_add_fusion = f32[1024,512]{1,0:T(8,128)S(1)} fusion(f32[1024,512]{1,0:T(8,128)S(1)} %fusion.15, bf16[384,512]{1,0:T(8,128)(2,1)S(1)} %bitcast.43, bf16[1024,3072]{1,0:T(8,128)(2,1)} %all-gather.3.cloned.1.call-done, s32[]{:T(128)S(6)} %select_n.104), kind=kOutput, calls=%fused_computation.1 | convolution fusion | flops 403177472 | bytes 5373956 | tf_op jit(solution)/shard_map/dot_general | solution.py:196
  75.4 1.9 %collective-permute-start.4 = (bf16[4,48,512]{2,1,0:T(8,128)(2,1)S(1)}, bf16[4,48,512]{2,1,0:T(8,128)(2,1)S(1)}, u32[]{:S(2)}, u32[]{:S(2)}) collective-permute-start(bf16[4,48,512]{2,1,0:T(8,128)(2,1)S(1)} %slice.10), channel_id=1, source_target_pairs={{0,64},{8,72},{16,80},{24,88},{32,96},{40,104},{48,112},{56,120},{... | collective-permute-start | bytes 589832 | tf_op jit(solution)/shard_map/ppermute | solution.py:230
  77.3 4.6 %collective-permute-start.8 = (bf16[4,48,512]{2,1,0:T(8,128)(2,1)S(1)}, bf16[4,48,512]{2,1,0:T(8,128)(2,1)S(1)}, u32[]{:S(2)}, u32[]{:S(2)}) collective-permute-start(bf16[4,48,512]{2,1,0:T(8,128)(2,1)S(1)} %slice.11), channel_id=1, source_target_pairs={{0,448},{8,456},{16,464},{24,472},{32,480},{40,488},{48,496},{56,5... | collective-permute-start | bytes 589832 | tf_op jit(solution)/shard_map/ppermute | solution.py:231
  81.9 0.7 fusion.6
  82.6 0.7 fusion.8
  83.3 0.7 fusion.10
  84.1 0.7 fusion.12
  84.8 1.0 add_add_fusion.total_ref
  85.8 0.7 fusion.last_ref
  86.5 2.7 %shard_map.47 = (bf16[2,512,512]{2,1,0:T(8,128)(2,1)S(1)}, bf16[16,128,128]{2,1,0:T(8,128)(2,1)S(1)}, bf16[4,2,144,128]{3,2,1,0:T(8,128)(2,1)}) custom-call(f32[1024,512]{1,0:T(8,128)S(1)} %add_add_fusion.total_ref, f32[1024,512]{1,0:T(8,128)S(1)} %fusion.last_ref, f32[128,16]{1,0:T(8,128)S(1)} %bitcast.28, f32[16,128]{1,0:T(8,128)S(1)} %bitcast.32), custom_call_target="tpu_custom_call" | custom-call | flops 67108864 | bytes 4210688 | tf_op jit(solution)/shard_map/pallas_call | solution.py:169
  89.2 6.2 %all-to-all-start.1 = ((bf16[4,2,144,128]{3,2,1,0:T(8,128)(2,1)}), bf16[4,2,144,128]{3,2,1,0:T(8,128)(2,1)S(1)}, u32[]{:S(2)}, u32[]{:S(2)}) async-start(bf16[4,2,144,128]{3,2,1,0:T(8,128)(2,1)} %get-tuple-element.35), calls=%async_computation.1 | async-start | bytes 589824 | tf_op jit(solution)/shard_map/all_to_all | solution.py:241
  95.3 8.9 %all-to-all-done.1.messages_ref = bf16[4,2,144,128]{3,2,1,0:T(8,128)(2,1)S(1)} async-done(((bf16[4,2,144,128]{3,2,1,0:T(8,128)(2,1)}), bf16[4,2,144,128]{3,2,1,0:T(8,128)(2,1)S(1)}, u32[]{:S(2)}, u32[]{:S(2)}) %all-to-all-start.1) | async-done | bytes 294944 | tf_op jit(solution)/shard_map/all_to_all | solution.py:241
  104.2 0.1 shard_map.48
  104.3 1.3 collective-permute-start.9
  105.6 6.4 %collective-permute-start.10 = (bf16[2,144,128]{2,1,0:T(8,128)(2,1)S(1)}, bf16[2,144,128]{2,1,0:T(8,128)(2,1)S(1)}, u32[]{:S(2)}, u32[]{:S(2)}) collective-permute-start(bf16[2,144,128]{2,1,0:T(8,128)(2,1)S(1)} %get-tuple-element.36), channel_id=1, source_target_pairs={{0,128},{8,136},{16,144},{24,152},{32,160},{40,168},{48,176},{56,1... | collective-permute-start | bytes 221192 | tf_op jit(solution)/shard_map/ppermute | solution.py:252
  112.1 2.5 %collective-permute-start.11 = (bf16[2,144,128]{2,1,0:T(8,128)(2,1)S(1)}, bf16[2,144,128]{2,1,0:T(8,128)(2,1)S(1)}, u32[]{:S(2)}, u32[]{:S(2)}) collective-permute-start(bf16[2,144,128]{2,1,0:T(8,128)(2,1)S(1)} %get-tuple-element.36), channel_id=1, source_target_pairs={{0,192},{8,200},{16,208},{24,216},{32,224},{40,232},{48,240},{56,2... | collective-permute-start | bytes 221192 | tf_op jit(solution)/shard_map/ppermute | solution.py:252
  114.6 2.6 %collective-permute-start.12 = (bf16[2,144,128]{2,1,0:T(8,128)(2,1)S(1)}, bf16[2,144,128]{2,1,0:T(8,128)(2,1)S(1)}, u32[]{:S(2)}, u32[]{:S(2)}) collective-permute-start(bf16[2,144,128]{2,1,0:T(8,128)(2,1)S(1)} %get-tuple-element.36), channel_id=1, source_target_pairs={{0,256},{8,264},{16,272},{24,280},{32,288},{40,296},{48,304},{56,3... | collective-permute-start | bytes 221192 | tf_op jit(solution)/shard_map/ppermute | solution.py:252
  117.2 1.3 collective-permute-start.13
  118.5 1.3 collective-permute-start.14
  119.8 1.3 collective-permute-start.15
  121.1 5.0 %convolution_bitcast_fusion.total_ref = f32[1024,256]{1,0:T(8,128)S(1)} fusion(bf16[1024,3072]{1,0:T(8,128)(2,1)} %all-gather.3.cloned.1.call-done, bf16[3072,256]{1,0:T(8,128)(2,1)} %bitcast.44), kind=kOutput, calls=%fused_computation.2 | convolution fusion | flops 1610612736 | bytes 8912896 | tf_op jit(solution)/shard_map/dot_general | solution.py:242
  126.1 0.9 shard_map.49
  127.1 2.5 %shard_map.50 = bf16[1024,256]{1,0:T(8,128)(2,1)S(1)} custom-call(bf16[2,144,128]{2,1,0:T(8,128)(2,1)S(1)} %collective-permute-done.9.refs_0_, bf16[2,144,128]{2,1,0:T(8,128)(2,1)S(1)} %collective-permute-done.10.refs_1_, bf16[2,144,128]{2,1,0:T(8,128)(2,1)S(1)} %collective-permute-done.11.refs_2_, bf16[2,144,128]{2,1,0:T(8,128)(2,1)S(1)} %collective-permute-done.12.refs_3_, ...), custom_call_target="tpu_custom_call" | custom-call | flops 67108864 | bytes 2237504 | tf_op jit(solution)/shard_map/pallas_call | solution.py:169
  129.6 22.3 %all_to_all.21.sent_ref = bf16[16,64,256]{2,1,0:T(8,128)(2,1)S(1)} all-to-all(bf16[16,64,256]{2,1,0:T(8,128)(2,1)S(1)} %bitcast.27), channel_id=1, replica_groups={{0,1,2,3,4,5,6,7,8,9,10,11,12,13,14,15},{16,17,18,19,20,21,22,23,24,25,..., dimensions={0} | all-to-all | bytes 1048576 | tf_op jit(solution)/shard_map/all_to_all | solution.py:257
  151.9 0.8 shard_map.51
  (32 shorter events, 0.3 us)
Async XLA Ops:
  6.5 64.2 %all-gather.3.cloned.1.call-start = ((), (), s32[]{:S(2)}) async-start(), calls=%async_computation.4 | async-start | bytes 6684672 | tf_op jit(solution)/shard_map/all_gather | solution.py:191
  7.3 0.9 copy-start
  33.0 12.3 %collective-permute-start = (bf16[8,48,512]{2,1,0:T(8,128)(2,1)S(1)}, bf16[8,48,512]{2,1,0:T(8,128)(2,1)S(1)}, u32[]{:S(2)}, u32[]{:S(2)}) collective-permute-start(bf16[8,48,512]{2,1,0:T(8,128)(2,1)S(1)} %all_to_all.20), channel_id=1, source_target_pairs={{0,64},{8,72},{16,80},{24,88},{32,96},{40,104},{48,112},{56,120},{... | collective-permute-start | bytes 1179656 | tf_op jit(solution)/shard_map/ppermute | solution.py:202
  36.3 11.0 %collective-permute-start.5 = (bf16[8,48,512]{2,1,0:T(8,128)(2,1)S(1)}, bf16[8,48,512]{2,1,0:T(8,128)(2,1)S(1)}, u32[]{:S(2)}, u32[]{:S(2)}) collective-permute-start(bf16[8,48,512]{2,1,0:T(8,128)(2,1)S(1)} %all_to_all.20), channel_id=1, source_target_pairs={{0,448},{8,456},{16,464},{24,472},{32,480},{40,488},{48,496},{56,5... | collective-permute-start | bytes 1179656 | tf_op jit(solution)/shard_map/ppermute | solution.py:203
  45.3 18.8 %collective-permute-start.1 = (bf16[8,48,512]{2,1,0:T(8,128)(2,1)S(1)}, bf16[8,48,512]{2,1,0:T(8,128)(2,1)S(1)}, u32[]{:S(2)}, u32[]{:S(2)}) collective-permute-start(bf16[8,48,512]{2,1,0:T(8,128)(2,1)S(1)} %collective-permute-done), channel_id=1, source_target_pairs={{0,64},{8,72},{16,80},{24,88},{32,96},{40,104},{48,112},{56,120},{... | collective-permute-start | bytes 1179656 | tf_op jit(solution)/shard_map/ppermute | solution.py:202
  47.3 18.8 %collective-permute-start.6 = (bf16[8,48,512]{2,1,0:T(8,128)(2,1)S(1)}, bf16[8,48,512]{2,1,0:T(8,128)(2,1)S(1)}, u32[]{:S(2)}, u32[]{:S(2)}) collective-permute-start(bf16[8,48,512]{2,1,0:T(8,128)(2,1)S(1)} %collective-permute-done.5), channel_id=1, source_target_pairs={{0,448},{8,456},{16,464},{24,472},{32,480},{40,488},{48,496},{56,5... | collective-permute-start | bytes 1179656 | tf_op jit(solution)/shard_map/ppermute | solution.py:203
  51.9 18.8 %all-to-all-start.2 = ((bf16[8,48,256]{2,1,0:T(8,128)(2,1)}), bf16[8,48,256]{2,1,0:T(8,128)(2,1)S(1)}, u32[]{:S(2)}, u32[]{:S(2)}) async-start(bf16[8,48,256]{2,1,0:T(8,128)(2,1)} %get-tuple-element.40), calls=%async_computation.2 | async-start | bytes 393216 | tf_op jit(solution)/shard_map/all_to_all | solution.py:209
  55.8 62.7 %all-gather.5.cloned.1.call-start = ((), (), s32[]{:S(2)}) async-start(), calls=%async_computation.5 | async-start | bytes 1769472 | tf_op jit(solution)/shard_map/all_gather | solution.py:227
  56.7 6.2 %collective-permute-start.2 = (f32[2,512]{1,0:T(2,128)S(1)}, f32[2,512]{1,0:T(2,128)S(1)}, u32[]{:S(2)}, u32[]{:S(2)}) collective-permute-start(f32[2,512]{1,0:T(2,128)S(1)} %get-tuple-element.27), channel_id=1, source_target_pairs={{0,8},{8,0},{16,24},{24,16},{32,40},{40,32},{48,56},{56,48},{64,72... | collective-permute-start | bytes 12296 | tf_op jit(solution)/shard_map/ppermute | solution.py:215
  64.2 11.2 %collective-permute-start.3 = (bf16[8,48,512]{2,1,0:T(8,128)(2,1)S(1)}, bf16[8,48,512]{2,1,0:T(8,128)(2,1)S(1)}, u32[]{:S(2)}, u32[]{:S(2)}) collective-permute-start(bf16[8,48,512]{2,1,0:T(8,128)(2,1)S(1)} %collective-permute-done.1), channel_id=1, source_target_pairs={{0,64},{8,72},{16,80},{24,88},{32,96},{40,104},{48,112},{56,120},{... | collective-permute-start | bytes 1179656 | tf_op jit(solution)/shard_map/ppermute | solution.py:202
  66.1 11.2 %collective-permute-start.7 = (bf16[8,48,512]{2,1,0:T(8,128)(2,1)S(1)}, bf16[8,48,512]{2,1,0:T(8,128)(2,1)S(1)}, u32[]{:S(2)}, u32[]{:S(2)}) collective-permute-start(bf16[8,48,512]{2,1,0:T(8,128)(2,1)S(1)} %collective-permute-done.6), channel_id=1, source_target_pairs={{0,448},{8,456},{16,464},{24,472},{32,480},{40,488},{48,496},{56,5... | collective-permute-start | bytes 1179656 | tf_op jit(solution)/shard_map/ppermute | solution.py:203
  70.7 0.7 copy-start.2
  71.4 10.5 %copy-start.1 = (bf16[1024,3072]{1,0:T(8,128)(2,1)S(1)}, bf16[1024,3072]{1,0:T(8,128)(2,1)}, u32[]{:S(2)}) copy-start(bf16[1024,3072]{1,0:T(8,128)(2,1)} %all-gather.3.cloned.1.call-done) | copy-start | bytes 18874372
  75.4 10.4 %collective-permute-start.4 = (bf16[4,48,512]{2,1,0:T(8,128)(2,1)S(1)}, bf16[4,48,512]{2,1,0:T(8,128)(2,1)S(1)}, u32[]{:S(2)}, u32[]{:S(2)}) collective-permute-start(bf16[4,48,512]{2,1,0:T(8,128)(2,1)S(1)} %slice.10), channel_id=1, source_target_pairs={{0,64},{8,72},{16,80},{24,88},{32,96},{40,104},{48,112},{56,120},{... | collective-permute-start | bytes 589832 | tf_op jit(solution)/shard_map/ppermute | solution.py:230
  77.3 8.4 %collective-permute-start.8 = (bf16[4,48,512]{2,1,0:T(8,128)(2,1)S(1)}, bf16[4,48,512]{2,1,0:T(8,128)(2,1)S(1)}, u32[]{:S(2)}, u32[]{:S(2)}) collective-permute-start(bf16[4,48,512]{2,1,0:T(8,128)(2,1)S(1)} %slice.11), channel_id=1, source_target_pairs={{0,448},{8,456},{16,464},{24,472},{32,480},{40,488},{48,496},{56,5... | collective-permute-start | bytes 589832 | tf_op jit(solution)/shard_map/ppermute | solution.py:231
  89.2 15.1 %all-to-all-start.1 = ((bf16[4,2,144,128]{3,2,1,0:T(8,128)(2,1)}), bf16[4,2,144,128]{3,2,1,0:T(8,128)(2,1)S(1)}, u32[]{:S(2)}, u32[]{:S(2)}) async-start(bf16[4,2,144,128]{3,2,1,0:T(8,128)(2,1)} %get-tuple-element.35), calls=%async_computation.1 | async-start | bytes 589824 | tf_op jit(solution)/shard_map/all_to_all | solution.py:241
  104.3 14.2 %collective-permute-start.9 = (bf16[2,144,128]{2,1,0:T(8,128)(2,1)S(1)}, bf16[2,144,128]{2,1,0:T(8,128)(2,1)S(1)}, u32[]{:S(2)}, u32[]{:S(2)}) collective-permute-start(bf16[2,144,128]{2,1,0:T(8,128)(2,1)S(1)} %get-tuple-element.36), channel_id=1, source_target_pairs={{0,64},{8,72},{16,80},{24,88},{32,96},{40,104},{48,112},{56,120},{... | collective-permute-start | bytes 221192 | tf_op jit(solution)/shard_map/ppermute | solution.py:252
  105.6 14.2 %collective-permute-start.10 = (bf16[2,144,128]{2,1,0:T(8,128)(2,1)S(1)}, bf16[2,144,128]{2,1,0:T(8,128)(2,1)S(1)}, u32[]{:S(2)}, u32[]{:S(2)}) collective-permute-start(bf16[2,144,128]{2,1,0:T(8,128)(2,1)S(1)} %get-tuple-element.36), channel_id=1, source_target_pairs={{0,128},{8,136},{16,144},{24,152},{32,160},{40,168},{48,176},{56,1... | collective-permute-start | bytes 221192 | tf_op jit(solution)/shard_map/ppermute | solution.py:252
  112.1 14.9 %collective-permute-start.11 = (bf16[2,144,128]{2,1,0:T(8,128)(2,1)S(1)}, bf16[2,144,128]{2,1,0:T(8,128)(2,1)S(1)}, u32[]{:S(2)}, u32[]{:S(2)}) collective-permute-start(bf16[2,144,128]{2,1,0:T(8,128)(2,1)S(1)} %get-tuple-element.36), channel_id=1, source_target_pairs={{0,192},{8,200},{16,208},{24,216},{32,224},{40,232},{48,240},{56,2... | collective-permute-start | bytes 221192 | tf_op jit(solution)/shard_map/ppermute | solution.py:252
  114.6 12.5 %collective-permute-start.12 = (bf16[2,144,128]{2,1,0:T(8,128)(2,1)S(1)}, bf16[2,144,128]{2,1,0:T(8,128)(2,1)S(1)}, u32[]{:S(2)}, u32[]{:S(2)}) collective-permute-start(bf16[2,144,128]{2,1,0:T(8,128)(2,1)S(1)} %get-tuple-element.36), channel_id=1, source_target_pairs={{0,256},{8,264},{16,272},{24,280},{32,288},{40,296},{48,304},{56,3... | collective-permute-start | bytes 221192 | tf_op jit(solution)/shard_map/ppermute | solution.py:252
  117.2 9.9 %collective-permute-start.13 = (bf16[2,144,128]{2,1,0:T(8,128)(2,1)S(1)}, bf16[2,144,128]{2,1,0:T(8,128)(2,1)S(1)}, u32[]{:S(2)}, u32[]{:S(2)}) collective-permute-start(bf16[2,144,128]{2,1,0:T(8,128)(2,1)S(1)} %get-tuple-element.36), channel_id=1, source_target_pairs={{0,320},{8,328},{16,336},{24,344},{32,352},{40,360},{48,368},{56,3... | collective-permute-start | bytes 221192 | tf_op jit(solution)/shard_map/ppermute | solution.py:252
  118.5 8.5 %collective-permute-start.14 = (bf16[2,144,128]{2,1,0:T(8,128)(2,1)S(1)}, bf16[2,144,128]{2,1,0:T(8,128)(2,1)S(1)}, u32[]{:S(2)}, u32[]{:S(2)}) collective-permute-start(bf16[2,144,128]{2,1,0:T(8,128)(2,1)S(1)} %get-tuple-element.36), channel_id=1, source_target_pairs={{0,384},{8,392},{16,400},{24,408},{32,416},{40,424},{48,432},{56,4... | collective-permute-start | bytes 221192 | tf_op jit(solution)/shard_map/ppermute | solution.py:252
  119.8 7.2 %collective-permute-start.15 = (bf16[2,144,128]{2,1,0:T(8,128)(2,1)S(1)}, bf16[2,144,128]{2,1,0:T(8,128)(2,1)S(1)}, u32[]{:S(2)}, u32[]{:S(2)}) collective-permute-start(bf16[2,144,128]{2,1,0:T(8,128)(2,1)S(1)} %get-tuple-element.36), channel_id=1, source_target_pairs={{0,448},{8,456},{16,464},{24,472},{32,480},{40,488},{48,496},{56,5... | collective-permute-start | bytes 221192 | tf_op jit(solution)/shard_map/ppermute | solution.py:252
Sparse Core Ops, SparseCore 0:
  9.5 57.0 all-gather.2
  71.6 41.3 all-gather.4

commit v6 on v4

--- a/solution.py
+++ b/solution.py
@@ -77,9 +77,10 @@
             out_ref[:, (h * 2 + s) * 256 : (h * 2 + s + 1) * 256] = sent_ref[s * NH + h]
 
 
-def states_kernel(total_ref, col_ref, row_ref, proj_ref, prefix_ref, message_ref):
+def states_kernel(total_ref, last_ref, col_ref, row_ref, proj_ref, prefix_ref, message_ref):
     for half in range(2):
-        proj_ref[half] = total_ref[half * 512 : (half + 1) * 512].astype(BF16)
+        part = slice(half * 512, (half + 1) * 512)
+        proj_ref[half] = (total_ref[part] + last_ref[part]).astype(BF16)
     for head in range(2):
         state = jnp.zeros((E, E), F32)
         decay = jnp.zeros((1, 1), F32)
@@ -192,22 +193,9 @@
         d = jnp.dot(x, part.reshape(NZ * 48, 512), preferred_element_type=F32)
         return d if total is None else total + d
 
-    query_block = block[:, :, :256]
-    block = block[:, :, 256:]
-    ups, downs = [block], [block]
-
-    def hop(*earlier):
-        ups.append(lax.ppermute(after(ups[-1], *earlier), "seq", y_shift(1)))
-        downs.append(lax.ppermute(after(downs[-1], *earlier), "seq", y_shift(-1)))
-
-    def add_step(total, step):
-        return add(add(total, ups[step], -step), downs[step], step)
-
-    hop()
-
     mine = lax.dynamic_slice_in_dim(log_decay, side * 2, 2, 0)
     wanted = lax.dynamic_slice_in_dim(log_decay, (1 - side) * 2, 2, 0)
-    theirs = lax.ppermute(after(wanted, block), "seq", PAIR)
+    theirs = lax.ppermute(wanted, "seq", PAIR)
     both = jnp.where(side == 0, jnp.concatenate([mine, theirs], 1), jnp.concatenate([theirs, mine], 1))
     rows = jnp.cumsum(both.reshape(2, 8, BLK), axis=2)
     ends = rows[:, :, -1]
@@ -216,8 +204,22 @@
     cols = rows.T
     gain = lax.dynamic_slice_in_dim(norm_gain, side * 256, 256, 0).reshape(1, 256)
 
+    block, rows, cols, starts, gain = lax.optimization_barrier((block, rows, cols, starts, gain))
+    query_block = block[:, :, :256]
+    block = block[:, :, 256:]
+    ups, downs = [block], [block]
+
+    def hop(*earlier):
+        ups.append(lax.ppermute(after(ups[-1], *earlier), "seq", y_shift(1)))
+        downs.append(lax.ppermute(after(downs[-1], *earlier), "seq", y_shift(-1)))
+
+    def add_step(total, step):
+        return add(add(total, ups[step], -step), downs[step], step)
+
     hop()
-    hop(rows, cols, starts, gain)
+
+    hop()
+    hop()
     total = add(add(None, block, 0), ups[1], -1)
     query_weight = lax.all_gather(
         after(query_block, all_rows), "seq", axis=0, tiled=True, axis_index_groups=Y_GROUPS
@@ -226,12 +228,12 @@
     down4 = lax.ppermute(after(downs[3], total)[4:], "seq", y_shift(-1))
     total = add_step(add_step(add(total, downs[1], 1), 2), 3)
     up4, down4, total = lax.optimization_barrier((up4, down4, total))
-    total = add(total, jnp.concatenate([up4, down4], 0), 4)
+    last = add(None, jnp.concatenate([up4, down4], 0), 4)
 
     proj, prefix, messages = call(
         states_kernel,
         [((2, 512, 512), BF16), ((16, E, E), BF16), ((4, 2, E + EXTRA, E), BF16)],
-        [], total, cols, rows, flops=16 * 2 * E**3,
+        [], total, last, cols, rows, flops=16 * 2 * E**3,
     )
     messages = lax.all_to_all(messages, "seq", split_axis=0, concat_axis=0, tiled=True, axis_index_groups=ROW_GROUPS)
     query_total = jnp.dot(all_rows, after(query_weight, messages), preferred_element_type=F32)

time: 156 us -> 161 us (1.032)
  blocking collectives: 51.4 us -> 21.8 us
  waiting for transfers between devices: 14.1 us -> 37.6 us
  starting transfers between devices: 52.3 us -> 62.1 us
    all_to_all x1 -> x0, blocking collectives: 28 us -> none  [on_device(): lax.all_to_all(pieces, 'seq', split_axis=0, concat_axis=0, tiled=True, ax...]
    all_to_all x0 -> x1, starting transfers between devices: none -> 10.9 us  [on_device(): lax.all_to_all(pieces, 'seq', split_axis=0, concat_axis=0, tiled=True, ax...]
    ppermute x3, waiting for transfers between devices: 3.23 us -> 12.4 us  [hop(): ups.append(lax.ppermute(after(ups[-1], *earlier), 'seq', y_shift(1)))]
    ppermute x1, waiting for transfers between devices: 1.94 us -> 10.7 us  [on_device(): theirs = lax.ppermute(wanted, 'seq', PAIR)]
    all_to_all x0 -> x1, waiting for transfers between devices: none -> 4.59 us  [on_device(): lax.all_to_all(pieces, 'seq', split_axis=0, concat_axis=0, tiled=True, ax...]
    all_to_all x1, starting transfers between devices: 6.56 us -> 3.45 us  [on_device(): lax.all_to_all(messages, 'seq', split_axis=0, concat_axis=0, tiled=True,...]
  transfers between devices with their start and end apart: 19 -> 20, of which waited for: 3 -> 7; matrix products, arithmetic and copies ran while one was open for 10% -> 10% of each run, Pallas kernels for 2% -> 3%
where the time goes in v6:
time: 161 us; the launch traced here: 160 us
  starting transfers between devices  62.1 us (39%)
  waiting for transfers between devices  37.6 us (23%)
  blocking collectives  21.8 us (14%)
  between operations  14 us (9%)
  matrix products  13.4 us (8%)
  Pallas kernels  7.89 us (5%)
  local copies, waits for them, and re-layouts  2.24 us (1%)
    all_to_all x1, blocking collectives, on_device(): lax.all_to_all(flat.reshape(16, 64, 256), ('seq', 'head'), split_axis=0,...  21.8 us
    ppermute x7, starting transfers between devices, on_device(): lax.ppermute(row_message, 'seq', y_later(k))  17.7 us
    ppermute x3, starting transfers between devices, hop(): downs.append(lax.ppermute(after(downs[-1], *earlier), 'seq', y_shift(-1)))  13.2 us
    ppermute x3, waiting for transfers between devices, hop(): ups.append(lax.ppermute(after(ups[-1], *earlier), 'seq', y_shift(1)))  12.4 us
    all_to_all x1, starting transfers between devices, on_device(): lax.all_to_all(pieces, 'seq', split_axis=0, concat_axis=0, tiled=True, ax...  10.9 us
    ppermute x1, waiting for transfers between devices, on_device(): theirs = lax.ppermute(wanted, 'seq', PAIR)  10.7 us
    all_to_all x1, waiting for transfers between devices, on_device(): lax.all_to_all(messages, 'seq', split_axis=0, concat_axis=0, tiled=True,...  8.78 us
    dot_general x8, matrix products, add(): d = jnp.dot(x, part.reshape(NZ * 48, 512), preferred_element_type=F32)  8.36 us
  transfers between devices with their start and end apart: 20, of which 7 were waited for; matrix products, arithmetic and copies ran while one was open for 10% of the time, Pallas kernels for 3%

profile of v6, /device:TPU:1, one launch (start us, length us, event | category | flops | bytes accessed | tf_op | source)
XLA Modules:
  0.0 159.9 jit_solution(7221547875403660910)
XLA Ops:
  6.5 0.7 all-gather.3.cloned.1.call-update
  7.3 0.9 copy-done
  8.2 0.9 shard_map.46
  9.0 10.9 %all-to-all-start = ((bf16[8,48,768]{2,1,0:T(8,128)(2,1)}), bf16[8,48,768]{2,1,0:T(8,128)(2,1)S(1)}, u32[]{:S(2)}, u32[]{:S(2)}) async-start(bf16[8,48,768]{2,1,0:T(8,128)(2,1)} %shard_map.46), calls=%async_computation | async-start | bytes 1179648 | tf_op jit(solution)/shard_map/all_to_all | solution.py:186
  20.0 3.3 %collective-permute-start = (f32[2,512]{1,0:T(2,128)S(1)}, f32[2,512]{1,0:T(2,128)S(1)}, u32[]{:S(2)}, u32[]{:S(2)}) collective-permute-start(f32[2,512]{1,0:T(2,128)S(1)} %get-tuple-element.46), channel_id=1, source_target_pairs={{0,8},{8,0},{16,24},{24,16},{32,40},{40,32},{48,56},{56,48},{64,72... | collective-permute-start | bytes 12296 | tf_op jit(solution)/shard_map/ppermute | solution.py:198
  23.4 10.7 %collective-permute-done = f32[2,512]{1,0:T(2,128)S(1)} collective-permute-done((f32[2,512]{1,0:T(2,128)S(1)}, f32[2,512]{1,0:T(2,128)S(1)}, u32[]{:S(2)}, u32[]{:S(2)}) %collective-permute-start) | collective-permute-done | bytes 4128 | tf_op jit(solution)/shard_map/ppermute | solution.py:198
  34.2 0.6 reduce_window_sum.24
  34.8 0.2 slice_reduce_fusion
  34.9 0.2 reduce_window_sum.25
  35.2 0.1 copy.11
  35.4 4.6 %all-to-all-done = bf16[8,48,768]{2,1,0:T(8,128)(2,1)S(1)} async-done(((bf16[8,48,768]{2,1,0:T(8,128)(2,1)}), bf16[8,48,768]{2,1,0:T(8,128)(2,1)S(1)}, u32[]{:S(2)}, u32[]{:S(2)}) %all-to-all-start) | async-done | bytes 589856 | tf_op jit(solution)/shard_map/all_to_all | solution.py:186
  40.0 3.2 %collective-permute-start.1 = (bf16[8,48,512]{2,1,0:T(8,128)(2,1)S(1)}, bf16[8,48,512]{2,1,0:T(8,128)(2,1)S(1)}, u32[]{:S(2)}, u32[]{:S(2)}) collective-permute-start(bf16[8,48,512]{2,1,0:T(8,128)(2,1)S(1)} %slice.16), channel_id=1, source_target_pairs={{0,64},{8,72},{16,80},{24,88},{32,96},{40,104},{48,112},{56,120},{... | collective-permute-start | bytes 1179656 | tf_op jit(solution)/shard_map/ppermute | solution.py:213
  43.3 4.0 %collective-permute-start.5 = (bf16[8,48,512]{2,1,0:T(8,128)(2,1)S(1)}, bf16[8,48,512]{2,1,0:T(8,128)(2,1)S(1)}, u32[]{:S(2)}, u32[]{:S(2)}) collective-permute-start(bf16[8,48,512]{2,1,0:T(8,128)(2,1)S(1)} %slice.16), channel_id=1, source_target_pairs={{0,448},{8,456},{16,464},{24,472},{32,480},{40,488},{48,496},{56,5... | collective-permute-start | bytes 1179656 | tf_op jit(solution)/shard_map/ppermute | solution.py:214
  47.3 6.7 %collective-permute-done.1 = bf16[8,48,512]{2,1,0:T(8,128)(2,1)S(1)} collective-permute-done((bf16[8,48,512]{2,1,0:T(8,128)(2,1)S(1)}, bf16[8,48,512]{2,1,0:T(8,128)(2,1)S(1)}, u32[]{:S(2)}, u32[]{:S(2)}) %collective-permute-start.1) | collective-permute-done | bytes 393248 | tf_op jit(solution)/shard_map/ppermute | solution.py:213
  54.0 1.9 %collective-permute-start.2 = (bf16[8,48,512]{2,1,0:T(8,128)(2,1)S(1)}, bf16[8,48,512]{2,1,0:T(8,128)(2,1)S(1)}, u32[]{:S(2)}, u32[]{:S(2)}) collective-permute-start(bf16[8,48,512]{2,1,0:T(8,128)(2,1)S(1)} %collective-permute-done.1), channel_id=1, source_target_pairs={{0,64},{8,72},{16,80},{24,88},{32,96},{40,104},{48,112},{56,120},{... | collective-permute-start | bytes 1179656 | tf_op jit(solution)/shard_map/ppermute | solution.py:213
  55.9 4.6 %collective-permute-start.6 = (bf16[8,48,512]{2,1,0:T(8,128)(2,1)S(1)}, bf16[8,48,512]{2,1,0:T(8,128)(2,1)S(1)}, u32[]{:S(2)}, u32[]{:S(2)}) collective-permute-start(bf16[8,48,512]{2,1,0:T(8,128)(2,1)S(1)} %collective-permute-done.5), channel_id=1, source_target_pairs={{0,448},{8,456},{16,464},{24,472},{32,480},{40,488},{48,496},{56,5... | collective-permute-start | bytes 1179656 | tf_op jit(solution)/shard_map/ppermute | solution.py:214
  60.7 0.7 slice.19
  61.4 4.8 %collective-permute-done.2 = bf16[8,48,512]{2,1,0:T(8,128)(2,1)S(1)} collective-permute-done((bf16[8,48,512]{2,1,0:T(8,128)(2,1)S(1)}, bf16[8,48,512]{2,1,0:T(8,128)(2,1)S(1)}, u32[]{:S(2)}, u32[]{:S(2)}) %collective-permute-start.2) | collective-permute-done | bytes 393248 | tf_op jit(solution)/shard_map/ppermute | solution.py:213
  66.2 1.9 %collective-permute-start.3 = (bf16[8,48,512]{2,1,0:T(8,128)(2,1)S(1)}, bf16[8,48,512]{2,1,0:T(8,128)(2,1)S(1)}, u32[]{:S(2)}, u32[]{:S(2)}) collective-permute-start(bf16[8,48,512]{2,1,0:T(8,128)(2,1)S(1)} %collective-permute-done.2), channel_id=1, source_target_pairs={{0,64},{8,72},{16,80},{24,88},{32,96},{40,104},{48,112},{56,120},{... | collective-permute-start | bytes 1179656 | tf_op jit(solution)/shard_map/ppermute | solution.py:213
  68.2 4.6 %collective-permute-start.7 = (bf16[8,48,512]{2,1,0:T(8,128)(2,1)S(1)}, bf16[8,48,512]{2,1,0:T(8,128)(2,1)S(1)}, u32[]{:S(2)}, u32[]{:S(2)}) collective-permute-start(bf16[8,48,512]{2,1,0:T(8,128)(2,1)S(1)} %collective-permute-done.6), channel_id=1, source_target_pairs={{0,448},{8,456},{16,464},{24,472},{32,480},{40,488},{48,496},{56,5... | collective-permute-start | bytes 1179656 | tf_op jit(solution)/shard_map/ppermute | solution.py:214
  72.8 2.0 %fusion.15 = f32[1024,512]{1,0:T(8,128)S(1)} fusion(bf16[384,512]{1,0:T(8,128)(2,1)S(1)} %bitcast.36, bf16[1024,3072]{1,0:T(8,128)(2,1)} %all-gather.3.cloned.1.call-done, s32[]{:T(128)S(6)} %select_n.102), kind=kOutput, calls=%fused_computation.16 | convolution fusion | flops 402653184 | bytes 3276804 | tf_op jit(solution)/shard_map/dot_general | solution.py:193
  74.8 1.9 %convolution_add_fusion = f32[1024,512]{1,0:T(8,128)S(1)} fusion(f32[1024,512]{1,0:T(8,128)S(1)} %fusion.15, bf16[384,512]{1,0:T(8,128)(2,1)S(1)} %bitcast.43, bf16[1024,3072]{1,0:T(8,128)(2,1)} %all-gather.3.cloned.1.call-done, s32[]{:T(128)S(6)} %select_n.104), kind=kOutput, calls=%fused_computation.1 | convolution fusion | flops 403177472 | bytes 5373956 | tf_op jit(solution)/shard_map/dot_general | solution.py:193
  76.7 0.9 collective-permute-done.3
  77.6 1.9 %collective-permute-start.4 = (bf16[4,48,512]{2,1,0:T(8,128)(2,1)S(1)}, bf16[4,48,512]{2,1,0:T(8,128)(2,1)S(1)}, u32[]{:S(2)}, u32[]{:S(2)}) collective-permute-start(bf16[4,48,512]{2,1,0:T(8,128)(2,1)S(1)} %slice.17), channel_id=1, source_target_pairs={{0,64},{8,72},{16,80},{24,88},{32,96},{40,104},{48,112},{56,120},{... | collective-permute-start | bytes 589832 | tf_op jit(solution)/shard_map/ppermute | solution.py:227
  79.6 4.6 %collective-permute-start.8 = (bf16[4,48,512]{2,1,0:T(8,128)(2,1)S(1)}, bf16[4,48,512]{2,1,0:T(8,128)(2,1)S(1)}, u32[]{:S(2)}, u32[]{:S(2)}) collective-permute-start(bf16[4,48,512]{2,1,0:T(8,128)(2,1)S(1)} %slice.18), channel_id=1, source_target_pairs={{0,448},{8,456},{16,464},{24,472},{32,480},{40,488},{48,496},{56,5... | collective-permute-start | bytes 589832 | tf_op jit(solution)/shard_map/ppermute | solution.py:228
  84.2 0.7 fusion.6
  84.9 0.7 fusion.8
  85.6 0.7 fusion.10
  86.3 0.7 fusion.12
  87.0 1.0 add_add_fusion.total_ref
  88.0 0.3 collective-permute-done.8
  88.3 0.7 fusion.last_ref
  89.0 2.7 %shard_map.47 = (bf16[2,512,512]{2,1,0:T(8,128)(2,1)S(1)}, bf16[16,128,128]{2,1,0:T(8,128)(2,1)S(1)}, bf16[4,2,144,128]{3,2,1,0:T(8,128)(2,1)}) custom-call(f32[1024,512]{1,0:T(8,128)S(1)} %add_add_fusion.total_ref, f32[1024,512]{1,0:T(8,128)S(1)} %fusion.last_ref, f32[128,16]{1,0:T(8,128)S(1)} %bitcast.28, f32[16,128]{1,0:T(8,128)S(1)} %bitcast.32), custom_call_target="tpu_custom_call" | custom-call | flops 67108864 | bytes 4210688 | tf_op jit(solution)/shard_map/pallas_call | solution.py:168
  91.7 3.5 %all-to-all-start.1 = ((bf16[4,2,144,128]{3,2,1,0:T(8,128)(2,1)}), bf16[4,2,144,128]{3,2,1,0:T(8,128)(2,1)S(1)}, u32[]{:S(2)}, u32[]{:S(2)}) async-start(bf16[4,2,144,128]{3,2,1,0:T(8,128)(2,1)} %get-tuple-element.33), calls=%async_computation.1 | async-start | bytes 589824 | tf_op jit(solution)/shard_map/all_to_all | solution.py:238
  95.2 8.8 %all-to-all-done.1.messages_ref = bf16[4,2,144,128]{3,2,1,0:T(8,128)(2,1)S(1)} async-done(((bf16[4,2,144,128]{3,2,1,0:T(8,128)(2,1)}), bf16[4,2,144,128]{3,2,1,0:T(8,128)(2,1)S(1)}, u32[]{:S(2)}, u32[]{:S(2)}) %all-to-all-start.1) | async-done | bytes 294944 | tf_op jit(solution)/shard_map/all_to_all | solution.py:238
  103.9 0.1 shard_map.48
  104.1 1.3 collective-permute-start.9
  105.4 5.9 %collective-permute-start.10 = (bf16[2,144,128]{2,1,0:T(8,128)(2,1)S(1)}, bf16[2,144,128]{2,1,0:T(8,128)(2,1)S(1)}, u32[]{:S(2)}, u32[]{:S(2)}) collective-permute-start(bf16[2,144,128]{2,1,0:T(8,128)(2,1)S(1)} %get-tuple-element.34), channel_id=1, source_target_pairs={{0,128},{8,136},{16,144},{24,152},{32,160},{40,168},{48,176},{56,1... | collective-permute-start | bytes 221192 | tf_op jit(solution)/shard_map/ppermute | solution.py:249
  111.2 2.6 %collective-permute-start.11 = (bf16[2,144,128]{2,1,0:T(8,128)(2,1)S(1)}, bf16[2,144,128]{2,1,0:T(8,128)(2,1)S(1)}, u32[]{:S(2)}, u32[]{:S(2)}) collective-permute-start(bf16[2,144,128]{2,1,0:T(8,128)(2,1)S(1)} %get-tuple-element.34), channel_id=1, source_target_pairs={{0,192},{8,200},{16,208},{24,216},{32,224},{40,232},{48,240},{56,2... | collective-permute-start | bytes 221192 | tf_op jit(solution)/shard_map/ppermute | solution.py:249
  113.8 4.1 %collective-permute-start.12 = (bf16[2,144,128]{2,1,0:T(8,128)(2,1)S(1)}, bf16[2,144,128]{2,1,0:T(8,128)(2,1)S(1)}, u32[]{:S(2)}, u32[]{:S(2)}) collective-permute-start(bf16[2,144,128]{2,1,0:T(8,128)(2,1)S(1)} %get-tuple-element.34), channel_id=1, source_target_pairs={{0,256},{8,264},{16,272},{24,280},{32,288},{40,296},{48,304},{56,3... | collective-permute-start | bytes 221192 | tf_op jit(solution)/shard_map/ppermute | solution.py:249
  117.9 1.3 collective-permute-start.13
  119.3 1.3 collective-permute-start.14
  120.6 1.3 collective-permute-start.15
  121.9 5.0 %convolution_bitcast_fusion.total_ref = f32[1024,256]{1,0:T(8,128)S(1)} fusion(bf16[1024,3072]{1,0:T(8,128)(2,1)} %all-gather.3.cloned.1.call-done, bf16[3072,256]{1,0:T(8,128)(2,1)} %bitcast.44), kind=kOutput, calls=%fused_computation.2 | convolution fusion | flops 1610612736 | bytes 8912896 | tf_op jit(solution)/shard_map/dot_general | solution.py:239
  126.9 0.9 shard_map.49
  127.8 2.5 %shard_map.50 = bf16[1024,256]{1,0:T(8,128)(2,1)S(1)} custom-call(bf16[2,144,128]{2,1,0:T(8,128)(2,1)S(1)} %collective-permute-done.9.refs_0_, bf16[2,144,128]{2,1,0:T(8,128)(2,1)S(1)} %collective-permute-done.10.refs_1_, bf16[2,144,128]{2,1,0:T(8,128)(2,1)S(1)} %collective-permute-done.11.refs_2_, bf16[2,144,128]{2,1,0:T(8,128)(2,1)S(1)} %collective-permute-done.12.refs_3_, ...), custom_call_target="tpu_custom_call" | custom-call | flops 67108864 | bytes 2237504 | tf_op jit(solution)/shard_map/pallas_call | solution.py:168
  130.4 21.8 %all_to_all.15.sent_ref = bf16[16,64,256]{2,1,0:T(8,128)(2,1)S(1)} all-to-all(bf16[16,64,256]{2,1,0:T(8,128)(2,1)S(1)} %bitcast.27), channel_id=1, replica_groups={{0,1,2,3,4,5,6,7,8,9,10,11,12,13,14,15},{16,17,18,19,20,21,22,23,24,25,..., dimensions={0} | all-to-all | bytes 1048576 | tf_op jit(solution)/shard_map/all_to_all | solution.py:254
  152.2 0.8 shard_map.51
  (35 shorter events, 0.5 us)
Async XLA Ops:
  6.5 13.5 %copy-start.2 = (f32[4,512]{1,0:T(4,128)S(1)}, f32[4,512]{1,0:T(4,128)}, u32[]{:S(2)}) copy-start(f32[4,512]{1,0:T(4,128)} %param.6) | copy-start | bytes 24580
  6.5 16.8 %copy-start.3 = (f32[512]{0:T(512)S(1)}, f32[512]{0:T(512)}, u32[]{:S(2)}) copy-start(f32[512]{0:T(512)} %param.7) | copy-start | bytes 6148
  6.5 66.2 %all-gather.3.cloned.1.call-start = ((), (), s32[]{:S(2)}) async-start(), calls=%async_computation.3 | async-start | bytes 6684672 | tf_op jit(solution)/shard_map/all_gather | solution.py:188
  7.3 0.9 copy-start
  9.0 30.9 %all-to-all-start = ((bf16[8,48,768]{2,1,0:T(8,128)(2,1)}), bf16[8,48,768]{2,1,0:T(8,128)(2,1)S(1)}, u32[]{:S(2)}, u32[]{:S(2)}) async-start(bf16[8,48,768]{2,1,0:T(8,128)(2,1)} %shard_map.46), calls=%async_computation | async-start | bytes 1179648 | tf_op jit(solution)/shard_map/all_to_all | solution.py:186
  19.9 99.3 %all-gather.5.cloned.1.call-start = ((), (), s32[]{:S(2)}) async-start(), calls=%async_computation.4 | async-start | bytes 1769472 | tf_op jit(solution)/shard_map/all_gather | solution.py:224
  20.0 14.1 %collective-permute-start = (f32[2,512]{1,0:T(2,128)S(1)}, f32[2,512]{1,0:T(2,128)S(1)}, u32[]{:S(2)}, u32[]{:S(2)}) collective-permute-start(f32[2,512]{1,0:T(2,128)S(1)} %get-tuple-element.46), channel_id=1, source_target_pairs={{0,8},{8,0},{16,24},{24,16},{32,40},{40,32},{48,56},{56,48},{64,72... | collective-permute-start | bytes 12296 | tf_op jit(solution)/shard_map/ppermute | solution.py:198
  40.0 14.0 %collective-permute-start.1 = (bf16[8,48,512]{2,1,0:T(8,128)(2,1)S(1)}, bf16[8,48,512]{2,1,0:T(8,128)(2,1)S(1)}, u32[]{:S(2)}, u32[]{:S(2)}) collective-permute-start(bf16[8,48,512]{2,1,0:T(8,128)(2,1)S(1)} %slice.16), channel_id=1, source_target_pairs={{0,64},{8,72},{16,80},{24,88},{32,96},{40,104},{48,112},{56,120},{... | collective-permute-start | bytes 1179656 | tf_op jit(solution)/shard_map/ppermute | solution.py:213
  43.3 12.6 %collective-permute-start.5 = (bf16[8,48,512]{2,1,0:T(8,128)(2,1)S(1)}, bf16[8,48,512]{2,1,0:T(8,128)(2,1)S(1)}, u32[]{:S(2)}, u32[]{:S(2)}) collective-permute-start(bf16[8,48,512]{2,1,0:T(8,128)(2,1)S(1)} %slice.16), channel_id=1, source_target_pairs={{0,448},{8,456},{16,464},{24,472},{32,480},{40,488},{48,496},{56,5... | collective-permute-start | bytes 1179656 | tf_op jit(solution)/shard_map/ppermute | solution.py:214
  54.0 12.3 %collective-permute-start.2 = (bf16[8,48,512]{2,1,0:T(8,128)(2,1)S(1)}, bf16[8,48,512]{2,1,0:T(8,128)(2,1)S(1)}, u32[]{:S(2)}, u32[]{:S(2)}) collective-permute-start(bf16[8,48,512]{2,1,0:T(8,128)(2,1)S(1)} %collective-permute-done.1), channel_id=1, source_target_pairs={{0,64},{8,72},{16,80},{24,88},{32,96},{40,104},{48,112},{56,120},{... | collective-permute-start | bytes 1179656 | tf_op jit(solution)/shard_map/ppermute | solution.py:213
  55.9 12.3 %collective-permute-start.6 = (bf16[8,48,512]{2,1,0:T(8,128)(2,1)S(1)}, bf16[8,48,512]{2,1,0:T(8,128)(2,1)S(1)}, u32[]{:S(2)}, u32[]{:S(2)}) collective-permute-start(bf16[8,48,512]{2,1,0:T(8,128)(2,1)S(1)} %collective-permute-done.5), channel_id=1, source_target_pairs={{0,448},{8,456},{16,464},{24,472},{32,480},{40,488},{48,496},{56,5... | collective-permute-start | bytes 1179656 | tf_op jit(solution)/shard_map/ppermute | solution.py:214
  66.2 11.3 %collective-permute-start.3 = (bf16[8,48,512]{2,1,0:T(8,128)(2,1)S(1)}, bf16[8,48,512]{2,1,0:T(8,128)(2,1)S(1)}, u32[]{:S(2)}, u32[]{:S(2)}) collective-permute-start(bf16[8,48,512]{2,1,0:T(8,128)(2,1)S(1)} %collective-permute-done.2), channel_id=1, source_target_pairs={{0,64},{8,72},{16,80},{24,88},{32,96},{40,104},{48,112},{56,120},{... | collective-permute-start | bytes 1179656 | tf_op jit(solution)/shard_map/ppermute | solution.py:213
  68.2 11.4 %collective-permute-start.7 = (bf16[8,48,512]{2,1,0:T(8,128)(2,1)S(1)}, bf16[8,48,512]{2,1,0:T(8,128)(2,1)S(1)}, u32[]{:S(2)}, u32[]{:S(2)}) collective-permute-start(bf16[8,48,512]{2,1,0:T(8,128)(2,1)S(1)} %collective-permute-done.6), channel_id=1, source_target_pairs={{0,448},{8,456},{16,464},{24,472},{32,480},{40,488},{48,496},{56,5... | collective-permute-start | bytes 1179656 | tf_op jit(solution)/shard_map/ppermute | solution.py:214
  72.8 11.3 %copy-start.1 = (bf16[1024,3072]{1,0:T(8,128)(2,1)S(1)}, bf16[1024,3072]{1,0:T(8,128)(2,1)}, u32[]{:S(2)}) copy-start(bf16[1024,3072]{1,0:T(8,128)(2,1)} %all-gather.3.cloned.1.call-done) | copy-start | bytes 18874372
  77.6 10.4 %collective-permute-start.4 = (bf16[4,48,512]{2,1,0:T(8,128)(2,1)S(1)}, bf16[4,48,512]{2,1,0:T(8,128)(2,1)S(1)}, u32[]{:S(2)}, u32[]{:S(2)}) collective-permute-start(bf16[4,48,512]{2,1,0:T(8,128)(2,1)S(1)} %slice.17), channel_id=1, source_target_pairs={{0,64},{8,72},{16,80},{24,88},{32,96},{40,104},{48,112},{56,120},{... | collective-permute-start | bytes 589832 | tf_op jit(solution)/shard_map/ppermute | solution.py:227
  79.6 8.7 %collective-permute-start.8 = (bf16[4,48,512]{2,1,0:T(8,128)(2,1)S(1)}, bf16[4,48,512]{2,1,0:T(8,128)(2,1)S(1)}, u32[]{:S(2)}, u32[]{:S(2)}) collective-permute-start(bf16[4,48,512]{2,1,0:T(8,128)(2,1)S(1)} %slice.18), channel_id=1, source_target_pairs={{0,448},{8,456},{16,464},{24,472},{32,480},{40,488},{48,496},{56,5... | collective-permute-start | bytes 589832 | tf_op jit(solution)/shard_map/ppermute | solution.py:228
  91.7 12.3 %all-to-all-start.1 = ((bf16[4,2,144,128]{3,2,1,0:T(8,128)(2,1)}), bf16[4,2,144,128]{3,2,1,0:T(8,128)(2,1)S(1)}, u32[]{:S(2)}, u32[]{:S(2)}) async-start(bf16[4,2,144,128]{3,2,1,0:T(8,128)(2,1)} %get-tuple-element.33), calls=%async_computation.1 | async-start | bytes 589824 | tf_op jit(solution)/shard_map/all_to_all | solution.py:238
  104.1 15.2 %collective-permute-start.9 = (bf16[2,144,128]{2,1,0:T(8,128)(2,1)S(1)}, bf16[2,144,128]{2,1,0:T(8,128)(2,1)S(1)}, u32[]{:S(2)}, u32[]{:S(2)}) collective-permute-start(bf16[2,144,128]{2,1,0:T(8,128)(2,1)S(1)} %get-tuple-element.34), channel_id=1, source_target_pairs={{0,64},{8,72},{16,80},{24,88},{32,96},{40,104},{48,112},{56,120},{... | collective-permute-start | bytes 221192 | tf_op jit(solution)/shard_map/ppermute | solution.py:249
  105.4 15.2 %collective-permute-start.10 = (bf16[2,144,128]{2,1,0:T(8,128)(2,1)S(1)}, bf16[2,144,128]{2,1,0:T(8,128)(2,1)S(1)}, u32[]{:S(2)}, u32[]{:S(2)}) collective-permute-start(bf16[2,144,128]{2,1,0:T(8,128)(2,1)S(1)} %get-tuple-element.34), channel_id=1, source_target_pairs={{0,128},{8,136},{16,144},{24,152},{32,160},{40,168},{48,176},{56,1... | collective-permute-start | bytes 221192 | tf_op jit(solution)/shard_map/ppermute | solution.py:249
  111.2 16.5 %collective-permute-start.11 = (bf16[2,144,128]{2,1,0:T(8,128)(2,1)S(1)}, bf16[2,144,128]{2,1,0:T(8,128)(2,1)S(1)}, u32[]{:S(2)}, u32[]{:S(2)}) collective-permute-start(bf16[2,144,128]{2,1,0:T(8,128)(2,1)S(1)} %get-tuple-element.34), channel_id=1, source_target_pairs={{0,192},{8,200},{16,208},{24,216},{32,224},{40,232},{48,240},{56,2... | collective-permute-start | bytes 221192 | tf_op jit(solution)/shard_map/ppermute | solution.py:249
  113.8 14.0 %collective-permute-start.12 = (bf16[2,144,128]{2,1,0:T(8,128)(2,1)S(1)}, bf16[2,144,128]{2,1,0:T(8,128)(2,1)S(1)}, u32[]{:S(2)}, u32[]{:S(2)}) collective-permute-start(bf16[2,144,128]{2,1,0:T(8,128)(2,1)S(1)} %get-tuple-element.34), channel_id=1, source_target_pairs={{0,256},{8,264},{16,272},{24,280},{32,288},{40,296},{48,304},{56,3... | collective-permute-start | bytes 221192 | tf_op jit(solution)/shard_map/ppermute | solution.py:249
  117.9 9.9 %collective-permute-start.13 = (bf16[2,144,128]{2,1,0:T(8,128)(2,1)S(1)}, bf16[2,144,128]{2,1,0:T(8,128)(2,1)S(1)}, u32[]{:S(2)}, u32[]{:S(2)}) collective-permute-start(bf16[2,144,128]{2,1,0:T(8,128)(2,1)S(1)} %get-tuple-element.34), channel_id=1, source_target_pairs={{0,320},{8,328},{16,336},{24,344},{32,352},{40,360},{48,368},{56,3... | collective-permute-start | bytes 221192 | tf_op jit(solution)/shard_map/ppermute | solution.py:249
  119.3 8.6 %collective-permute-start.14 = (bf16[2,144,128]{2,1,0:T(8,128)(2,1)S(1)}, bf16[2,144,128]{2,1,0:T(8,128)(2,1)S(1)}, u32[]{:S(2)}, u32[]{:S(2)}) collective-permute-start(bf16[2,144,128]{2,1,0:T(8,128)(2,1)S(1)} %get-tuple-element.34), channel_id=1, source_target_pairs={{0,384},{8,392},{16,400},{24,408},{32,416},{40,424},{48,432},{56,4... | collective-permute-start | bytes 221192 | tf_op jit(solution)/shard_map/ppermute | solution.py:249
  120.6 7.2 %collective-permute-start.15 = (bf16[2,144,128]{2,1,0:T(8,128)(2,1)S(1)}, bf16[2,144,128]{2,1,0:T(8,128)(2,1)S(1)}, u32[]{:S(2)}, u32[]{:S(2)}) collective-permute-start(bf16[2,144,128]{2,1,0:T(8,128)(2,1)S(1)} %get-tuple-element.34), channel_id=1, source_target_pairs={{0,448},{8,456},{16,464},{24,472},{32,480},{40,488},{48,496},{56,5... | collective-permute-start | bytes 221192 | tf_op jit(solution)/shard_map/ppermute | solution.py:249
Sparse Core Ops, SparseCore 0:
  9.5 57.3 all-gather.2
  72.9 37.2 all-gather.4

commit v7 on v4

--- a/solution.py
+++ b/solution.py
@@ -77,9 +77,10 @@
             out_ref[:, (h * 2 + s) * 256 : (h * 2 + s + 1) * 256] = sent_ref[s * NH + h]
 
 
-def states_kernel(total_ref, col_ref, row_ref, proj_ref, prefix_ref, message_ref):
+def states_kernel(total_ref, last_ref, col_ref, row_ref, proj_ref, prefix_ref, message_ref):
     for half in range(2):
-        proj_ref[half] = total_ref[half * 512 : (half + 1) * 512].astype(BF16)
+        part = slice(half * 512, (half + 1) * 512)
+        proj_ref[half] = (total_ref[part] + last_ref[part]).astype(BF16)
     for head in range(2):
         state = jnp.zeros((E, E), F32)
         decay = jnp.zeros((1, 1), F32)
@@ -204,10 +205,11 @@
         return add(add(total, ups[step], -step), downs[step], step)
 
     hop()
-
     mine = lax.dynamic_slice_in_dim(log_decay, side * 2, 2, 0)
     wanted = lax.dynamic_slice_in_dim(log_decay, (1 - side) * 2, 2, 0)
     theirs = lax.ppermute(after(wanted, block), "seq", PAIR)
+    ups.append(lax.ppermute(ups[1], "seq", y_shift(1)))
+    downs.append(lax.ppermute(after(downs[1], theirs), "seq", y_shift(-1)))
     both = jnp.where(side == 0, jnp.concatenate([mine, theirs], 1), jnp.concatenate([theirs, mine], 1))
     rows = jnp.cumsum(both.reshape(2, 8, BLK), axis=2)
     ends = rows[:, :, -1]
@@ -216,7 +218,6 @@
     cols = rows.T
     gain = lax.dynamic_slice_in_dim(norm_gain, side * 256, 256, 0).reshape(1, 256)
 
-    hop()
     hop(rows, cols, starts, gain)
     total = add(add(None, block, 0), ups[1], -1)
     query_weight = lax.all_gather(
@@ -226,12 +227,12 @@
     down4 = lax.ppermute(after(downs[3], total)[4:], "seq", y_shift(-1))
     total = add_step(add_step(add(total, downs[1], 1), 2), 3)
     up4, down4, total = lax.optimization_barrier((up4, down4, total))
-    total = add(total, jnp.concatenate([up4, down4], 0), 4)
+    last = add(None, jnp.concatenate([up4, down4], 0), 4)
 
     proj, prefix, messages = call(
         states_kernel,
         [((2, 512, 512), BF16), ((16, E, E), BF16), ((4, 2, E + EXTRA, E), BF16)],
-        [], total, cols, rows, flops=16 * 2 * E**3,
+        [], total, last, cols, rows, flops=16 * 2 * E**3,
     )
     messages = lax.all_to_all(messages, "seq", split_axis=0, concat_axis=0, tiled=True, axis_index_groups=ROW_GROUPS)
     query_total = jnp.dot(all_rows, after(query_weight, messages), preferred_element_type=F32)

time: 156 us -> 155 us (level)
    ppermute x0 -> x2, starting transfers between devices: none -> 6.48 us  [the longest x1 4.57 us: on_device(): downs.append(lax.ppermute(after(downs[1], theirs), 'seq', y_shift(-1)))]
    ppermute x3 -> x2, starting transfers between devices: 13.2 us -> 8.62 us  [hop(): downs.append(lax.ppermute(after(downs[-1], *earlier), 'seq', y_shift(-1)))]
    all_gather x1, waiting for transfers between devices: 0.02 us -> 2.86 us  [on_device(): lax.all_gather(tokens, ('seq', 'head'), axis=0, tiled=True, axis_index_gr...]
    ppermute x3 -> x2, waiting for transfers between devices: 3.23 us -> 1.22 us  [hop(): ups.append(lax.ppermute(after(ups[-1], *earlier), 'seq', y_shift(1)))]
    ppermute x1, waiting for transfers between devices: 1.94 us -> 0.01 us  [on_device(): theirs = lax.ppermute(after(wanted, block), 'seq', PAIR)]
    ppermute x3 -> x2, starting transfers between devices: 7 us -> 5.09 us  [hop(): ups.append(lax.ppermute(after(ups[-1], *earlier), 'seq', y_shift(1)))]
    all_to_all x1, waiting for transfers between devices: 8.11 us -> 9.69 us  [on_device(): lax.all_to_all(messages, 'seq', split_axis=0, concat_axis=0, tiled=True,...]
  transfers between devices with their start and end apart: 19 -> 19, of which waited for: 3 -> 4; matrix products, arithmetic and copies ran while one was open for 10% -> 10% of each run, Pallas kernels for 2% -> 2%
where the time goes in v7:
time: 155 us; the launch traced here: 154 us
  starting transfers between devices  51.4 us (33%)
  blocking collectives  50 us (32%)
  waiting for transfers between devices  15.5 us (10%)
  between operations  14 us (9%)
  matrix products  13.4 us (9%)
  Pallas kernels  7.09 us (5%)
  local copies, waits for them, and re-layouts  2.25 us (1%)
    all_to_all x1, blocking collectives, on_device(): lax.all_to_all(pieces, 'seq', split_axis=0, concat_axis=0, tiled=True, ax...  28 us
    all_to_all x1, blocking collectives, on_device(): lax.all_to_all(flat.reshape(16, 64, 256), ('seq', 'head'), split_axis=0,...  22 us
    ppermute x7, starting transfers between devices, on_device(): lax.ppermute(row_message, 'seq', y_later(k))  16.7 us
    all_to_all x1, waiting for transfers between devices, on_device(): lax.all_to_all(messages, 'seq', split_axis=0, concat_axis=0, tiled=True,...  9.69 us
    ppermute x2, starting transfers between devices, hop(): downs.append(lax.ppermute(after(downs[-1], *earlier), 'seq', y_shift(-1)))  8.62 us
    dot_general x8, matrix products, add(): d = jnp.dot(x, part.reshape(NZ * 48, 512), preferred_element_type=F32)  8.41 us
    pallas_call x6, Pallas kernels, call(): pl.pallas_call(kernel, out_shape=shapes, in_specs=smem + whole(len(args))...  7.09 us
    all_to_all x1, starting transfers between devices, on_device(): lax.all_to_all(messages, 'seq', split_axis=0, concat_axis=0, tiled=True,...  5.45 us
  transfers between devices with their start and end apart: 19, of which 4 were waited for; matrix products, arithmetic and copies ran while one was open for 10% of the time, Pallas kernels for 2%

profile of v7, /device:TPU:1, one launch (start us, length us, event | category | flops | bytes accessed | tf_op | source)
XLA Modules:
  0.0 154.5 jit_solution(17699118203811139680)
XLA Ops:
  6.5 0.7 all-gather.3.cloned.1.call-update
  7.3 0.0 all-gather.5.cloned.1.call-start
  7.3 0.9 copy-done
  8.3 28.0 %all_to_all.15 = bf16[8,48,768]{2,1,0:T(8,128)(2,1)S(1)} all-to-all(bf16[8,48,768]{2,1,0:T(8,128)(2,1)S(1)} %shard_map.46), channel_id=1, replica_groups={{0,8,16,24,32,40,48,56},{64,72,80,88,96,104,112,120},{128,136,144,152,1..., dimensions={0} | all-to-all | bytes 1179648 | tf_op jit(solution)/shard_map/all_to_all | solution.py:186
  36.3 3.2 %collective-permute-start = (bf16[8,48,512]{2,1,0:T(8,128)(2,1)S(1)}, bf16[8,48,512]{2,1,0:T(8,128)(2,1)S(1)}, u32[]{:S(2)}, u32[]{:S(2)}) collective-permute-start(bf16[8,48,512]{2,1,0:T(8,128)(2,1)S(1)} %slice.20), channel_id=1, source_target_pairs={{0,64},{8,72},{16,80},{24,88},{32,96},{40,104},{48,112},{56,120},{... | collective-permute-start | bytes 1179656 | tf_op jit(solution)/shard_map/ppermute | solution.py:201
  39.5 4.0 %collective-permute-start.5 = (bf16[8,48,512]{2,1,0:T(8,128)(2,1)S(1)}, bf16[8,48,512]{2,1,0:T(8,128)(2,1)S(1)}, u32[]{:S(2)}, u32[]{:S(2)}) collective-permute-start(bf16[8,48,512]{2,1,0:T(8,128)(2,1)S(1)} %slice.20), channel_id=1, source_target_pairs={{0,448},{8,456},{16,464},{24,472},{32,480},{40,488},{48,496},{56,5... | collective-permute-start | bytes 1179656 | tf_op jit(solution)/shard_map/ppermute | solution.py:202
  43.6 1.9 %collective-permute-start.2 = (f32[2,512]{1,0:T(2,128)S(1)}, f32[2,512]{1,0:T(2,128)S(1)}, u32[]{:S(2)}, u32[]{:S(2)}) collective-permute-start(f32[2,512]{1,0:T(2,128)S(1)} %get-tuple-element.24), channel_id=1, source_target_pairs={{0,8},{8,0},{16,24},{24,16},{32,40},{40,32},{48,56},{56,48},{64,72... | collective-permute-start | bytes 12296 | tf_op jit(solution)/shard_map/ppermute | solution.py:210
  45.5 1.2 collective-permute-done
  46.8 1.9 %collective-permute-start.1 = (bf16[8,48,512]{2,1,0:T(8,128)(2,1)S(1)}, bf16[8,48,512]{2,1,0:T(8,128)(2,1)S(1)}, u32[]{:S(2)}, u32[]{:S(2)}) collective-permute-start(bf16[8,48,512]{2,1,0:T(8,128)(2,1)S(1)} %collective-permute-done), channel_id=1, source_target_pairs={{0,64},{8,72},{16,80},{24,88},{32,96},{40,104},{48,112},{56,120},{... | collective-permute-start | bytes 1179656 | tf_op jit(solution)/shard_map/ppermute | solution.py:211
  48.7 4.6 %collective-permute-start.6 = (bf16[8,48,512]{2,1,0:T(8,128)(2,1)S(1)}, bf16[8,48,512]{2,1,0:T(8,128)(2,1)S(1)}, u32[]{:S(2)}, u32[]{:S(2)}) collective-permute-start(bf16[8,48,512]{2,1,0:T(8,128)(2,1)S(1)} %collective-permute-done.5), channel_id=1, source_target_pairs={{0,448},{8,456},{16,464},{24,472},{32,480},{40,488},{48,496},{56,5... | collective-permute-start | bytes 1179656 | tf_op jit(solution)/shard_map/ppermute | solution.py:212
  53.5 0.1 dynamic_slice.35
  53.6 0.7 slice.22
  54.3 0.6 reduce_window_sum.24
  54.9 0.2 slice_reduce_fusion
  55.1 0.2 reduce_window_sum.25
  55.3 0.1 squeeze.6
  55.3 0.1 copy.11
  55.4 0.1 reduce_window_sum.26
  55.5 1.0 collective-permute-done.1
  56.5 1.9 %collective-permute-start.3 = (bf16[8,48,512]{2,1,0:T(8,128)(2,1)S(1)}, bf16[8,48,512]{2,1,0:T(8,128)(2,1)S(1)}, u32[]{:S(2)}, u32[]{:S(2)}) collective-permute-start(bf16[8,48,512]{2,1,0:T(8,128)(2,1)S(1)} %collective-permute-done.1), channel_id=1, source_target_pairs={{0,64},{8,72},{16,80},{24,88},{32,96},{40,104},{48,112},{56,120},{... | collective-permute-start | bytes 1179656 | tf_op jit(solution)/shard_map/ppermute | solution.py:201
  58.4 4.6 %collective-permute-start.7 = (bf16[8,48,512]{2,1,0:T(8,128)(2,1)S(1)}, bf16[8,48,512]{2,1,0:T(8,128)(2,1)S(1)}, u32[]{:S(2)}, u32[]{:S(2)}) collective-permute-start(bf16[8,48,512]{2,1,0:T(8,128)(2,1)S(1)} %collective-permute-done.6), channel_id=1, source_target_pairs={{0,448},{8,456},{16,464},{24,472},{32,480},{40,488},{48,496},{56,5... | collective-permute-start | bytes 1179656 | tf_op jit(solution)/shard_map/ppermute | solution.py:202
  63.0 2.9 %all-gather.3.cloned.1.call-done = bf16[1024,3072]{1,0:T(8,128)(2,1)} async-done(((bf16[64,3072]{1,0:T(8,128)(2,1)}), bf16[1024,3072]{1,0:T(8,128)(2,1)}) %all-gather.3.cloned.1.call-update) | async-done | bytes 6291472 | tf_op jit(solution)/shard_map/all_gather | solution.py:188
  65.9 2.0 %fusion.12 = f32[1024,512]{1,0:T(8,128)S(1)} fusion(bf16[384,512]{1,0:T(8,128)(2,1)S(1)} %bitcast.36, bf16[1024,3072]{1,0:T(8,128)(2,1)} %all-gather.3.cloned.1.call-done, s32[]{:T(128)S(6)} %select_n.102), kind=kOutput, calls=%fused_computation.15 | convolution fusion | flops 402653184 | bytes 3276804 | tf_op jit(solution)/shard_map/dot_general | solution.py:193
  67.9 1.9 %convolution_add_fusion = f32[1024,512]{1,0:T(8,128)S(1)} fusion(f32[1024,512]{1,0:T(8,128)S(1)} %fusion.12, bf16[384,512]{1,0:T(8,128)(2,1)S(1)} %bitcast.43, bf16[1024,3072]{1,0:T(8,128)(2,1)} %all-gather.3.cloned.1.call-done, s32[]{:T(128)S(6)} %select_n.104), kind=kOutput, calls=%fused_computation.1 | convolution fusion | flops 403177472 | bytes 5373956 | tf_op jit(solution)/shard_map/dot_general | solution.py:193
  69.8 3.2 %collective-permute-start.4 = (bf16[4,48,512]{2,1,0:T(8,128)(2,1)S(1)}, bf16[4,48,512]{2,1,0:T(8,128)(2,1)S(1)}, u32[]{:S(2)}, u32[]{:S(2)}) collective-permute-start(bf16[4,48,512]{2,1,0:T(8,128)(2,1)S(1)} %slice.17), channel_id=1, source_target_pairs={{0,64},{8,72},{16,80},{24,88},{32,96},{40,104},{48,112},{56,120},{... | collective-permute-start | bytes 589832 | tf_op jit(solution)/shard_map/ppermute | solution.py:226
  73.1 3.8 %collective-permute-start.8 = (bf16[4,48,512]{2,1,0:T(8,128)(2,1)S(1)}, bf16[4,48,512]{2,1,0:T(8,128)(2,1)S(1)}, u32[]{:S(2)}, u32[]{:S(2)}) collective-permute-start(bf16[4,48,512]{2,1,0:T(8,128)(2,1)S(1)} %slice.18), channel_id=1, source_target_pairs={{0,448},{8,456},{16,464},{24,472},{32,480},{40,488},{48,496},{56,5... | collective-permute-start | bytes 589832 | tf_op jit(solution)/shard_map/ppermute | solution.py:227
  76.9 0.7 fusion.2
  77.6 0.7 fusion.4
  78.3 0.7 fusion.6
  79.0 0.7 fusion.9
  79.7 1.0 add_add_fusion.total_ref
  80.8 0.7 fusion.last_ref
  81.5 2.7 %shard_map.47 = (bf16[2,512,512]{2,1,0:T(8,128)(2,1)S(1)}, bf16[16,128,128]{2,1,0:T(8,128)(2,1)S(1)}, bf16[4,2,144,128]{3,2,1,0:T(8,128)(2,1)}) custom-call(f32[1024,512]{1,0:T(8,128)S(1)} %add_add_fusion.total_ref, f32[1024,512]{1,0:T(8,128)S(1)} %fusion.last_ref, f32[128,16]{1,0:T(8,128)S(1)} %bitcast.28, f32[16,128]{1,0:T(8,128)S(1)} %bitcast.32), custom_call_target="tpu_custom_call" | custom-call | flops 67108864 | bytes 4210688 | tf_op jit(solution)/shard_map/pallas_call | solution.py:168
  84.2 5.4 %all-to-all-start.1 = ((bf16[4,2,144,128]{3,2,1,0:T(8,128)(2,1)}), bf16[4,2,144,128]{3,2,1,0:T(8,128)(2,1)S(1)}, u32[]{:S(2)}, u32[]{:S(2)}) async-start(bf16[4,2,144,128]{3,2,1,0:T(8,128)(2,1)} %get-tuple-element.33), calls=%async_computation.1 | async-start | bytes 589824 | tf_op jit(solution)/shard_map/all_to_all | solution.py:237
  89.6 9.7 %all-to-all-done.1.messages_ref = bf16[4,2,144,128]{3,2,1,0:T(8,128)(2,1)S(1)} async-done(((bf16[4,2,144,128]{3,2,1,0:T(8,128)(2,1)}), bf16[4,2,144,128]{3,2,1,0:T(8,128)(2,1)S(1)}, u32[]{:S(2)}, u32[]{:S(2)}) %all-to-all-start.1) | async-done | bytes 294944 | tf_op jit(solution)/shard_map/all_to_all | solution.py:237
  99.3 0.1 shard_map.48
  99.4 2.0 %collective-permute-start.9 = (bf16[2,144,128]{2,1,0:T(8,128)(2,1)S(1)}, bf16[2,144,128]{2,1,0:T(8,128)(2,1)S(1)}, u32[]{:S(2)}, u32[]{:S(2)}) collective-permute-start(bf16[2,144,128]{2,1,0:T(8,128)(2,1)S(1)} %get-tuple-element.34), channel_id=1, source_target_pairs={{0,64},{8,72},{16,80},{24,88},{32,96},{40,104},{48,112},{56,120},{... | collective-permute-start | bytes 221192 | tf_op jit(solution)/shard_map/ppermute | solution.py:248
  101.5 5.8 %collective-permute-start.10 = (bf16[2,144,128]{2,1,0:T(8,128)(2,1)S(1)}, bf16[2,144,128]{2,1,0:T(8,128)(2,1)S(1)}, u32[]{:S(2)}, u32[]{:S(2)}) collective-permute-start(bf16[2,144,128]{2,1,0:T(8,128)(2,1)S(1)} %get-tuple-element.34), channel_id=1, source_target_pairs={{0,128},{8,136},{16,144},{24,152},{32,160},{40,168},{48,176},{56,1... | collective-permute-start | bytes 221192 | tf_op jit(solution)/shard_map/ppermute | solution.py:248
  107.2 3.4 %collective-permute-start.11 = (bf16[2,144,128]{2,1,0:T(8,128)(2,1)S(1)}, bf16[2,144,128]{2,1,0:T(8,128)(2,1)S(1)}, u32[]{:S(2)}, u32[]{:S(2)}) collective-permute-start(bf16[2,144,128]{2,1,0:T(8,128)(2,1)S(1)} %get-tuple-element.34), channel_id=1, source_target_pairs={{0,192},{8,200},{16,208},{24,216},{32,224},{40,232},{48,240},{56,2... | collective-permute-start | bytes 221192 | tf_op jit(solution)/shard_map/ppermute | solution.py:248
  110.7 1.6 %collective-permute-start.12 = (bf16[2,144,128]{2,1,0:T(8,128)(2,1)S(1)}, bf16[2,144,128]{2,1,0:T(8,128)(2,1)S(1)}, u32[]{:S(2)}, u32[]{:S(2)}) collective-permute-start(bf16[2,144,128]{2,1,0:T(8,128)(2,1)S(1)} %get-tuple-element.34), channel_id=1, source_target_pairs={{0,256},{8,264},{16,272},{24,280},{32,288},{40,296},{48,304},{56,3... | collective-permute-start | bytes 221192 | tf_op jit(solution)/shard_map/ppermute | solution.py:248
  112.3 1.3 collective-permute-start.13
  113.7 1.3 collective-permute-start.14
  115.0 1.3 collective-permute-start.15
  116.3 5.0 %convolution_bitcast_fusion.total_ref = f32[1024,256]{1,0:T(8,128)S(1)} fusion(bf16[1024,3072]{1,0:T(8,128)(2,1)} %all-gather.3.cloned.1.call-done, bf16[3072,256]{1,0:T(8,128)(2,1)} %bitcast.44), kind=kOutput, calls=%fused_computation.2 | convolution fusion | flops 1610612736 | bytes 8912896 | tf_op jit(solution)/shard_map/dot_general | solution.py:238
  121.3 0.9 shard_map.49
  122.3 2.5 %shard_map.50 = bf16[1024,256]{1,0:T(8,128)(2,1)S(1)} custom-call(bf16[2,144,128]{2,1,0:T(8,128)(2,1)S(1)} %collective-permute-done.9.refs_0_, bf16[2,144,128]{2,1,0:T(8,128)(2,1)S(1)} %collective-permute-done.10.refs_1_, bf16[2,144,128]{2,1,0:T(8,128)(2,1)S(1)} %collective-permute-done.11.refs_2_, bf16[2,144,128]{2,1,0:T(8,128)(2,1)S(1)} %collective-permute-done.12.refs_3_, ...), custom_call_target="tpu_custom_call" | custom-call | flops 67108864 | bytes 2237504 | tf_op jit(solution)/shard_map/pallas_call | solution.py:168
  124.8 22.0 %all_to_all.16.sent_ref = bf16[16,64,256]{2,1,0:T(8,128)(2,1)S(1)} all-to-all(bf16[16,64,256]{2,1,0:T(8,128)(2,1)S(1)} %bitcast.27), channel_id=1, replica_groups={{0,1,2,3,4,5,6,7,8,9,10,11,12,13,14,15},{16,17,18,19,20,21,22,23,24,25,..., dimensions={0} | all-to-all | bytes 1048576 | tf_op jit(solution)/shard_map/all_to_all | solution.py:253
  146.8 0.8 shard_map.51
  (34 shorter events, 0.3 us)
Async XLA Ops:
  6.5 37.1 %copy-start.2 = (f32[4,512]{1,0:T(4,128)S(1)}, f32[4,512]{1,0:T(4,128)}, u32[]{:S(2)}) copy-start(f32[4,512]{1,0:T(4,128)} %param.6) | copy-start | bytes 24580
  6.5 46.9 %copy-start.3 = (f32[512]{0:T(512)S(1)}, f32[512]{0:T(512)}, u32[]{:S(2)}) copy-start(f32[512]{0:T(512)} %param.7) | copy-start | bytes 6148
  6.5 59.3 %all-gather.3.cloned.1.call-start = ((), (), s32[]{:S(2)}) async-start(), calls=%async_computation.3 | async-start | bytes 6684672 | tf_op jit(solution)/shard_map/all_gather | solution.py:188
  7.3 106.4 %all-gather.5.cloned.1.call-start = ((), (), s32[]{:S(2)}) async-start(), calls=%async_computation.4 | async-start | bytes 1769472 | tf_op jit(solution)/shard_map/all_gather | solution.py:223
  7.3 0.9 copy-start
  36.3 10.5 %collective-permute-start = (bf16[8,48,512]{2,1,0:T(8,128)(2,1)S(1)}, bf16[8,48,512]{2,1,0:T(8,128)(2,1)S(1)}, u32[]{:S(2)}, u32[]{:S(2)}) collective-permute-start(bf16[8,48,512]{2,1,0:T(8,128)(2,1)S(1)} %slice.20), channel_id=1, source_target_pairs={{0,64},{8,72},{16,80},{24,88},{32,96},{40,104},{48,112},{56,120},{... | collective-permute-start | bytes 1179656 | tf_op jit(solution)/shard_map/ppermute | solution.py:201
  39.5 9.2 %collective-permute-start.5 = (bf16[8,48,512]{2,1,0:T(8,128)(2,1)S(1)}, bf16[8,48,512]{2,1,0:T(8,128)(2,1)S(1)}, u32[]{:S(2)}, u32[]{:S(2)}) collective-permute-start(bf16[8,48,512]{2,1,0:T(8,128)(2,1)S(1)} %slice.20), channel_id=1, source_target_pairs={{0,448},{8,456},{16,464},{24,472},{32,480},{40,488},{48,496},{56,5... | collective-permute-start | bytes 1179656 | tf_op jit(solution)/shard_map/ppermute | solution.py:202
  43.6 5.1 %collective-permute-start.2 = (f32[2,512]{1,0:T(2,128)S(1)}, f32[2,512]{1,0:T(2,128)S(1)}, u32[]{:S(2)}, u32[]{:S(2)}) collective-permute-start(f32[2,512]{1,0:T(2,128)S(1)} %get-tuple-element.24), channel_id=1, source_target_pairs={{0,8},{8,0},{16,24},{24,16},{32,40},{40,32},{48,56},{56,48},{64,72... | collective-permute-start | bytes 12296 | tf_op jit(solution)/shard_map/ppermute | solution.py:210
  46.8 9.7 %collective-permute-start.1 = (bf16[8,48,512]{2,1,0:T(8,128)(2,1)S(1)}, bf16[8,48,512]{2,1,0:T(8,128)(2,1)S(1)}, u32[]{:S(2)}, u32[]{:S(2)}) collective-permute-start(bf16[8,48,512]{2,1,0:T(8,128)(2,1)S(1)} %collective-permute-done), channel_id=1, source_target_pairs={{0,64},{8,72},{16,80},{24,88},{32,96},{40,104},{48,112},{56,120},{... | collective-permute-start | bytes 1179656 | tf_op jit(solution)/shard_map/ppermute | solution.py:211
  48.7 9.7 %collective-permute-start.6 = (bf16[8,48,512]{2,1,0:T(8,128)(2,1)S(1)}, bf16[8,48,512]{2,1,0:T(8,128)(2,1)S(1)}, u32[]{:S(2)}, u32[]{:S(2)}) collective-permute-start(bf16[8,48,512]{2,1,0:T(8,128)(2,1)S(1)} %collective-permute-done.5), channel_id=1, source_target_pairs={{0,448},{8,456},{16,464},{24,472},{32,480},{40,488},{48,496},{56,5... | collective-permute-start | bytes 1179656 | tf_op jit(solution)/shard_map/ppermute | solution.py:212
  56.5 13.3 %collective-permute-start.3 = (bf16[8,48,512]{2,1,0:T(8,128)(2,1)S(1)}, bf16[8,48,512]{2,1,0:T(8,128)(2,1)S(1)}, u32[]{:S(2)}, u32[]{:S(2)}) collective-permute-start(bf16[8,48,512]{2,1,0:T(8,128)(2,1)S(1)} %collective-permute-done.1), channel_id=1, source_target_pairs={{0,64},{8,72},{16,80},{24,88},{32,96},{40,104},{48,112},{56,120},{... | collective-permute-start | bytes 1179656 | tf_op jit(solution)/shard_map/ppermute | solution.py:201
  58.4 14.6 %collective-permute-start.7 = (bf16[8,48,512]{2,1,0:T(8,128)(2,1)S(1)}, bf16[8,48,512]{2,1,0:T(8,128)(2,1)S(1)}, u32[]{:S(2)}, u32[]{:S(2)}) collective-permute-start(bf16[8,48,512]{2,1,0:T(8,128)(2,1)S(1)} %collective-permute-done.6), channel_id=1, source_target_pairs={{0,448},{8,456},{16,464},{24,472},{32,480},{40,488},{48,496},{56,5... | collective-permute-start | bytes 1179656 | tf_op jit(solution)/shard_map/ppermute | solution.py:202
  65.9 11.0 %copy-start.1 = (bf16[1024,3072]{1,0:T(8,128)(2,1)S(1)}, bf16[1024,3072]{1,0:T(8,128)(2,1)}, u32[]{:S(2)}) copy-start(bf16[1024,3072]{1,0:T(8,128)(2,1)} %all-gather.3.cloned.1.call-done) | copy-start | bytes 18874372
  69.8 10.9 %collective-permute-start.4 = (bf16[4,48,512]{2,1,0:T(8,128)(2,1)S(1)}, bf16[4,48,512]{2,1,0:T(8,128)(2,1)S(1)}, u32[]{:S(2)}, u32[]{:S(2)}) collective-permute-start(bf16[4,48,512]{2,1,0:T(8,128)(2,1)S(1)} %slice.17), channel_id=1, source_target_pairs={{0,64},{8,72},{16,80},{24,88},{32,96},{40,104},{48,112},{56,120},{... | collective-permute-start | bytes 589832 | tf_op jit(solution)/shard_map/ppermute | solution.py:226
  73.1 7.7 %collective-permute-start.8 = (bf16[4,48,512]{2,1,0:T(8,128)(2,1)S(1)}, bf16[4,48,512]{2,1,0:T(8,128)(2,1)S(1)}, u32[]{:S(2)}, u32[]{:S(2)}) collective-permute-start(bf16[4,48,512]{2,1,0:T(8,128)(2,1)S(1)} %slice.18), channel_id=1, source_target_pairs={{0,448},{8,456},{16,464},{24,472},{32,480},{40,488},{48,496},{56,5... | collective-permute-start | bytes 589832 | tf_op jit(solution)/shard_map/ppermute | solution.py:227
  84.2 15.1 %all-to-all-start.1 = ((bf16[4,2,144,128]{3,2,1,0:T(8,128)(2,1)}), bf16[4,2,144,128]{3,2,1,0:T(8,128)(2,1)S(1)}, u32[]{:S(2)}, u32[]{:S(2)}) async-start(bf16[4,2,144,128]{3,2,1,0:T(8,128)(2,1)} %get-tuple-element.33), calls=%async_computation.1 | async-start | bytes 589824 | tf_op jit(solution)/shard_map/all_to_all | solution.py:237
  99.4 14.2 %collective-permute-start.9 = (bf16[2,144,128]{2,1,0:T(8,128)(2,1)S(1)}, bf16[2,144,128]{2,1,0:T(8,128)(2,1)S(1)}, u32[]{:S(2)}, u32[]{:S(2)}) collective-permute-start(bf16[2,144,128]{2,1,0:T(8,128)(2,1)S(1)} %get-tuple-element.34), channel_id=1, source_target_pairs={{0,64},{8,72},{16,80},{24,88},{32,96},{40,104},{48,112},{56,120},{... | collective-permute-start | bytes 221192 | tf_op jit(solution)/shard_map/ppermute | solution.py:248
  101.5 13.5 %collective-permute-start.10 = (bf16[2,144,128]{2,1,0:T(8,128)(2,1)S(1)}, bf16[2,144,128]{2,1,0:T(8,128)(2,1)S(1)}, u32[]{:S(2)}, u32[]{:S(2)}) collective-permute-start(bf16[2,144,128]{2,1,0:T(8,128)(2,1)S(1)} %get-tuple-element.34), channel_id=1, source_target_pairs={{0,128},{8,136},{16,144},{24,152},{32,160},{40,168},{48,176},{56,1... | collective-permute-start | bytes 221192 | tf_op jit(solution)/shard_map/ppermute | solution.py:248
  107.2 15.0 %collective-permute-start.11 = (bf16[2,144,128]{2,1,0:T(8,128)(2,1)S(1)}, bf16[2,144,128]{2,1,0:T(8,128)(2,1)S(1)}, u32[]{:S(2)}, u32[]{:S(2)}) collective-permute-start(bf16[2,144,128]{2,1,0:T(8,128)(2,1)S(1)} %get-tuple-element.34), channel_id=1, source_target_pairs={{0,192},{8,200},{16,208},{24,216},{32,224},{40,232},{48,240},{56,2... | collective-permute-start | bytes 221192 | tf_op jit(solution)/shard_map/ppermute | solution.py:248
  110.7 11.5 %collective-permute-start.12 = (bf16[2,144,128]{2,1,0:T(8,128)(2,1)S(1)}, bf16[2,144,128]{2,1,0:T(8,128)(2,1)S(1)}, u32[]{:S(2)}, u32[]{:S(2)}) collective-permute-start(bf16[2,144,128]{2,1,0:T(8,128)(2,1)S(1)} %get-tuple-element.34), channel_id=1, source_target_pairs={{0,256},{8,264},{16,272},{24,280},{32,288},{40,296},{48,304},{56,3... | collective-permute-start | bytes 221192 | tf_op jit(solution)/shard_map/ppermute | solution.py:248
  112.3 9.9 %collective-permute-start.13 = (bf16[2,144,128]{2,1,0:T(8,128)(2,1)S(1)}, bf16[2,144,128]{2,1,0:T(8,128)(2,1)S(1)}, u32[]{:S(2)}, u32[]{:S(2)}) collective-permute-start(bf16[2,144,128]{2,1,0:T(8,128)(2,1)S(1)} %get-tuple-element.34), channel_id=1, source_target_pairs={{0,320},{8,328},{16,336},{24,344},{32,352},{40,360},{48,368},{56,3... | collective-permute-start | bytes 221192 | tf_op jit(solution)/shard_map/ppermute | solution.py:248
  113.7 8.6 %collective-permute-start.14 = (bf16[2,144,128]{2,1,0:T(8,128)(2,1)S(1)}, bf16[2,144,128]{2,1,0:T(8,128)(2,1)S(1)}, u32[]{:S(2)}, u32[]{:S(2)}) collective-permute-start(bf16[2,144,128]{2,1,0:T(8,128)(2,1)S(1)} %get-tuple-element.34), channel_id=1, source_target_pairs={{0,384},{8,392},{16,400},{24,408},{32,416},{40,424},{48,432},{56,4... | collective-permute-start | bytes 221192 | tf_op jit(solution)/shard_map/ppermute | solution.py:248
  115.0 7.3 %collective-permute-start.15 = (bf16[2,144,128]{2,1,0:T(8,128)(2,1)S(1)}, bf16[2,144,128]{2,1,0:T(8,128)(2,1)S(1)}, u32[]{:S(2)}, u32[]{:S(2)}) collective-permute-start(bf16[2,144,128]{2,1,0:T(8,128)(2,1)S(1)} %get-tuple-element.34), channel_id=1, source_target_pairs={{0,448},{8,456},{16,464},{24,472},{32,480},{40,488},{48,496},{56,5... | collective-permute-start | bytes 221192 | tf_op jit(solution)/shard_map/ppermute | solution.py:248
Sparse Core Ops, SparseCore 0:
  9.5 56.3 all-gather.2
  67.9 39.8 all-gather.4

commit v8 on v7

--- a/solution.py
+++ b/solution.py
@@ -14,6 +14,7 @@
 NZ = 8
 NH = 8
 EXTRA = 16
+SLICE = 32
 F32 = jnp.float32
 BF16 = jnp.bfloat16
 VMEM = pltpu.VMEM
@@ -48,7 +49,8 @@
 
 
 def write_message(ref, head, state, decay):
-    ref[head, :E, :] = state.astype(BF16)
+    rows = state.shape[0]
+    ref[head, :rows, :] = state.astype(BF16)
     decay = jnp.broadcast_to(decay, (EXTRA, E))
     high = decay.astype(BF16)
     rest = decay - high.astype(F32)
@@ -56,11 +58,11 @@
     low = (rest - middle.astype(F32)).astype(BF16)
     row = lax.broadcasted_iota(jnp.int32, (EXTRA, E), 0)
     part = jnp.where(row == 0, high.astype(F32), jnp.where(row == 1, middle.astype(F32), low.astype(F32)))
-    ref[head, E:, :] = part.astype(BF16)
+    ref[head, rows:, :] = part.astype(BF16)
 
 
 def read_decay(ref, head):
-    rows = ref[head, E:, :].astype(F32)
+    rows = ref[head, SLICE:, :].astype(F32)
     return (rows[0:1] + rows[1:2]) + rows[2:3]
 
 
@@ -95,8 +97,8 @@
             scaled = (keys.astype(F32) * scale).astype(BF16)
             state = jnp.exp(last) * state + mm(scaled, values, (((0,), (0,)), ((), ())))
             decay = decay + last
-        for copy in range(4):
-            write_message(message_ref.at[copy], head, state, decay)
+        for q in range(4):
+            write_message(message_ref.at[q], head, state[q * SLICE : (q + 1) * SLICE], decay)
 
 
 def local_kernel(total_ref, proj_ref, prefix_ref, col_ref, row_ref, query_ref, out_ref):
@@ -118,36 +120,36 @@
             out_ref[at] = mm(scores.astype(BF16), values) + mm(scaled, prefix_ref[at])
 
 
-def row_kernel(place_ref, messages_ref, before_ref, decay_ref, message_ref):
-    place = place_ref[0]
-    for head in range(2):
-        before = jnp.zeros((E, E), F32)
-        total = jnp.zeros((E, E), F32)
-        gone_before = jnp.zeros((1, E), F32)
+def row_kernel(messages_ref, before_ref, decay_ref, message_ref):
+    for head in range(2):
+        before = jnp.zeros((SLICE, E), F32)
         gone = jnp.zeros((1, E), F32)
-        for k in (3, 2, 1, 0):
-            block = messages_ref[k, head, :E, :].astype(F32)
+        for k in range(4):
+            before_ref[k, head] = before
+            decay_ref[k, head] = jnp.broadcast_to(gone, (8, E))
             decay = read_decay(messages_ref.at[k], head)
-            total = total + jnp.exp(gone) * block
+            before = jnp.exp(decay) * before + messages_ref[k, head, :SLICE, :].astype(F32)
             gone = gone + decay
-            early = k < place
-            before = before + jnp.where(early, jnp.exp(gone_before), 0.0) * block
-            gone_before = gone_before + jnp.where(early, decay, 0.0)
-        before_ref[head] = before
-        decay_ref[head] = jnp.broadcast_to(gone_before, (8, E))
-        write_message(message_ref, head, total, gone)
-
-
-def final_kernel(*refs):
+        write_message(message_ref, head, before, gone)
+
+
+def column_kernel(*refs):
     messages = refs[:7]
-    before_ref, decay_ref, part_ref, query_ref, col_ref, start_ref, gain_ref, out_ref = refs[7:]
-    for head in range(2):
-        carried = jnp.zeros((E, E), F32)
+    before_ref, decay_ref, incoming_ref = refs[7:]
+    for head in range(2):
+        carried = jnp.zeros((SLICE, E), F32)
         gone = jnp.zeros((1, E), F32)
         for ref in messages:
-            carried = carried + jnp.exp(gone) * ref[head, :E, :].astype(F32)
+            carried = carried + jnp.exp(gone) * ref[head, :SLICE, :].astype(F32)
             gone = gone + read_decay(ref, head)
-        incoming = (jnp.exp(decay_ref[head, 0:1, :]) * carried + before_ref[head]).astype(BF16)
+        for k in range(4):
+            incoming = jnp.exp(decay_ref[k, head, 0:1, :]) * carried + before_ref[k, head]
+            incoming_ref[k, head] = incoming.astype(BF16)
+
+
+def final_kernel(incoming_ref, part_ref, query_ref, col_ref, start_ref, gain_ref, out_ref):
+    for head in range(2):
+        incoming = incoming_ref[:, head].reshape(E, E)
         gain = gain_ref[0:1, head * E : (head + 1) * E]
         for n in range(8):
             at = head * 8 + n
@@ -179,8 +181,6 @@
     seq = lax.axis_index("seq")
     y, z = seq // NZ, seq % NZ
     side = z % 2
-    place = z // 2
-    place1 = place.reshape(1).astype(jnp.int32)
 
     (pieces,) = call(pieces_kernel, [((NZ, 48, 768), BF16)], [], qkv_weight.transpose(1, 0, 2))
     block = lax.all_to_all(pieces, "seq", split_axis=0, concat_axis=0, tiled=True, axis_index_groups=Z_GROUPS)
@@ -231,7 +231,7 @@
 
     proj, prefix, messages = call(
         states_kernel,
-        [((2, 512, 512), BF16), ((16, E, E), BF16), ((4, 2, E + EXTRA, E), BF16)],
+        [((2, 512, 512), BF16), ((16, E, E), BF16), ((4, 2, SLICE + EXTRA, E), BF16)],
         [], total, last, cols, rows, flops=16 * 2 * E**3,
     )
     messages = lax.all_to_all(messages, "seq", split_axis=0, concat_axis=0, tiled=True, axis_index_groups=ROW_GROUPS)
@@ -242,12 +242,16 @@
     )
     before, gone, row_message = call(
         row_kernel,
-        [((2, E, E), F32), ((2, 8, E), F32), ((2, E + EXTRA, E), BF16)],
-        [place1], messages,
+        [((4, 2, SLICE, E), F32), ((4, 2, 8, E), F32), ((2, SLICE + EXTRA, E), BF16)],
+        [], messages,
     )
     earlier = [lax.ppermute(row_message, "seq", y_later(k)) for k in range(1, NY)]
+    (incoming,) = call(column_kernel, [((4, 2, SLICE, E), BF16)], [], *earlier, after(before, query_total), gone)
+    incoming = lax.all_to_all(
+        incoming, "seq", split_axis=0, concat_axis=0, tiled=True, axis_index_groups=ROW_GROUPS
+    )
     (flat,) = call(
-        final_kernel, [((1024, 256), BF16)], [], *earlier, before, gone, part, query, cols, starts, gain,
+        final_kernel, [((1024, 256), BF16)], [], incoming, part, query, cols, starts, gain,
         flops=16 * 2 * E**3,
     )
     sent = lax.all_to_all(

time: 155 us -> 167 us (1.077)
  blocking collectives: 50 us -> 62.3 us
  waiting for transfers between devices: 15.5 us -> 9.99 us
  local copies, waits for them, and re-layouts: 2.25 us -> 6.01 us
  matrix products: 13.4 us -> 16.7 us
  starting transfers between devices: 51.4 us -> 48.9 us
    all_to_all x0 -> x1, blocking collectives: none -> 12.6 us  [on_device(): lax.all_to_all(messages, 'seq', split_axis=0, concat_axis=0, tiled=True,...]
    all_to_all x1, waiting for transfers between devices: 9.69 us -> 4.13 us  [on_device(): lax.all_to_all(incoming, 'seq', split_axis=0, concat_axis=0, tiled=True,...]
    dot_general x8, matrix products: 8.41 us -> 11.7 us  [add(): d = jnp.dot(x, part.reshape(NZ * 48, 512), preferred_element_type=F32)]
    unnamed x8 -> x24, local copies, waits for them, and re-layouts: 0.91 us -> 3.81 us
    all_to_all x1, starting transfers between devices: 5.45 us -> 3.28 us  [on_device(): lax.all_to_all(incoming, 'seq', split_axis=0, concat_axis=0, tiled=True,...]
    pallas_call x6 -> x7, Pallas kernels: 7.09 us -> 6.89 us  [call(): pl.pallas_call(kernel, out_shape=shapes, in_specs=smem + whole(len(args))...]
  transfers between devices with their start and end apart: 19 -> 19, of which waited for: 4 -> 4; matrix products, arithmetic and copies ran while one was open for 10% -> 12% of each run, Pallas kernels for 2% -> 2%
where the time goes in v8:
time: 167 us; the launch traced here: 166 us
  blocking collectives  62.3 us (37%)
  starting transfers between devices  48.9 us (29%)
  matrix products  16.7 us (10%)
  between operations  14.1 us (8%)
  waiting for transfers between devices  9.99 us (6%)
  Pallas kernels  6.89 us (4%)
  local copies, waits for them, and re-layouts  6.01 us (4%)
    all_to_all x1, blocking collectives, on_device(): lax.all_to_all(pieces, 'seq', split_axis=0, concat_axis=0, tiled=True, ax...  28 us
    all_to_all x1, blocking collectives, on_device(): lax.all_to_all(flat.reshape(16, 64, 256), ('seq', 'head'), split_axis=0,...  21.6 us
    ppermute x7, starting transfers between devices, on_device(): lax.ppermute(row_message, 'seq', y_later(k))  16.4 us
    all_to_all x1, blocking collectives, on_device(): lax.all_to_all(messages, 'seq', split_axis=0, concat_axis=0, tiled=True,...  12.6 us
    dot_general x8, matrix products, add(): d = jnp.dot(x, part.reshape(NZ * 48, 512), preferred_element_type=F32)  11.7 us
    ppermute x2, starting transfers between devices, hop(): downs.append(lax.ppermute(after(downs[-1], *earlier), 'seq', y_shift(-1)))  8.63 us
    pallas_call x7, Pallas kernels, call(): pl.pallas_call(kernel, out_shape=shapes, in_specs=smem + whole(len(args))...  6.89 us
    ppermute x2, starting transfers between devices, hop(): ups.append(lax.ppermute(after(ups[-1], *earlier), 'seq', y_shift(1)))  5.09 us
  transfers between devices with their start and end apart: 19, of which 4 were waited for; matrix products, arithmetic and copies ran while one was open for 12% of the time, Pallas kernels for 2%

profile of v8, /device:TPU:1, one launch (start us, length us, event | category | flops | bytes accessed | tf_op | source)
XLA Modules:
  0.0 165.7 jit_solution(8597550367559354989)
XLA Ops:
  6.5 0.7 all-gather.3.cloned.1.call-update
  7.3 0.9 copy-done.4
  8.3 28.0 %all_to_all.20 = bf16[8,48,768]{2,1,0:T(8,128)(2,1)S(1)} all-to-all(bf16[8,48,768]{2,1,0:T(8,128)(2,1)S(1)} %shard_map.46), channel_id=1, replica_groups={{0,8,16,24,32,40,48,56},{64,72,80,88,96,104,112,120},{128,136,144,152,1..., dimensions={0} | all-to-all | bytes 1179648 | tf_op jit(solution)/shard_map/all_to_all | solution.py:186
  36.3 3.2 %collective-permute-start = (bf16[8,48,512]{2,1,0:T(8,128)(2,1)S(1)}, bf16[8,48,512]{2,1,0:T(8,128)(2,1)S(1)}, u32[]{:S(2)}, u32[]{:S(2)}) collective-permute-start(bf16[8,48,512]{2,1,0:T(8,128)(2,1)S(1)} %slice.20), channel_id=1, source_target_pairs={{0,64},{8,72},{16,80},{24,88},{32,96},{40,104},{48,112},{56,120},{... | collective-permute-start | bytes 1179656 | tf_op jit(solution)/shard_map/ppermute | solution.py:201
  39.5 4.0 %collective-permute-start.5 = (bf16[8,48,512]{2,1,0:T(8,128)(2,1)S(1)}, bf16[8,48,512]{2,1,0:T(8,128)(2,1)S(1)}, u32[]{:S(2)}, u32[]{:S(2)}) collective-permute-start(bf16[8,48,512]{2,1,0:T(8,128)(2,1)S(1)} %slice.20), channel_id=1, source_target_pairs={{0,448},{8,456},{16,464},{24,472},{32,480},{40,488},{48,496},{56,5... | collective-permute-start | bytes 1179656 | tf_op jit(solution)/shard_map/ppermute | solution.py:202
  43.6 1.9 %collective-permute-start.2 = (f32[2,512]{1,0:T(2,128)S(1)}, f32[2,512]{1,0:T(2,128)S(1)}, u32[]{:S(2)}, u32[]{:S(2)}) collective-permute-start(f32[2,512]{1,0:T(2,128)S(1)} %get-tuple-element.25), channel_id=1, source_target_pairs={{0,8},{8,0},{16,24},{24,16},{32,40},{40,32},{48,56},{56,48},{64,72... | collective-permute-start | bytes 12296 | tf_op jit(solution)/shard_map/ppermute | solution.py:210
  45.5 1.2 collective-permute-done
  46.8 1.9 %collective-permute-start.1 = (bf16[8,48,512]{2,1,0:T(8,128)(2,1)S(1)}, bf16[8,48,512]{2,1,0:T(8,128)(2,1)}, u32[]{:S(2)}, u32[]{:S(2)}) collective-permute-start(bf16[8,48,512]{2,1,0:T(8,128)(2,1)S(1)} %collective-permute-done), channel_id=1, source_target_pairs={{0,64},{8,72},{16,80},{24,88},{32,96},{40,104},{48,112},{56,120},{... | collective-permute-start | bytes 1179656 | tf_op jit(solution)/shard_map/ppermute | solution.py:211
  48.7 4.6 %collective-permute-start.6 = (bf16[8,48,512]{2,1,0:T(8,128)(2,1)S(1)}, bf16[8,48,512]{2,1,0:T(8,128)(2,1)}, u32[]{:S(2)}, u32[]{:S(2)}) collective-permute-start(bf16[8,48,512]{2,1,0:T(8,128)(2,1)S(1)} %collective-permute-done.5), channel_id=1, source_target_pairs={{0,448},{8,456},{16,464},{24,472},{32,480},{40,488},{48,496},{56,5... | collective-permute-start | bytes 1179656 | tf_op jit(solution)/shard_map/ppermute | solution.py:212
  53.6 0.7 slice.22
  54.3 0.6 reduce_window_sum.24
  54.9 0.2 slice_reduce_fusion
  55.0 0.2 reduce_window_sum.25
  55.5 1.1 collective-permute-done.1
  56.6 1.9 %collective-permute-start.3 = (bf16[8,48,512]{2,1,0:T(8,128)(2,1)}, bf16[8,48,512]{2,1,0:T(8,128)(2,1)S(1)}, u32[]{:S(2)}, u32[]{:S(2)}) collective-permute-start(bf16[8,48,512]{2,1,0:T(8,128)(2,1)} %collective-permute-done.1), channel_id=1, source_target_pairs={{0,64},{8,72},{16,80},{24,88},{32,96},{40,104},{48,112},{56,120},{... | collective-permute-start | bytes 1179656 | tf_op jit(solution)/shard_map/ppermute | solution.py:201
  58.5 4.6 %collective-permute-start.7 = (bf16[8,48,512]{2,1,0:T(8,128)(2,1)}, bf16[8,48,512]{2,1,0:T(8,128)(2,1)}, u32[]{:S(2)}, u32[]{:S(2)}) collective-permute-start(bf16[8,48,512]{2,1,0:T(8,128)(2,1)} %collective-permute-done.6), channel_id=1, source_target_pairs={{0,448},{8,456},{16,464},{24,472},{32,480},{40,488},{48,496},{56,5... | collective-permute-start | bytes 1179656 | tf_op jit(solution)/shard_map/ppermute | solution.py:202
  63.1 2.7 %all-gather.3.cloned.1.call-done = bf16[1024,3072]{1,0:T(8,128)(2,1)} async-done(((bf16[64,3072]{1,0:T(8,128)(2,1)}), bf16[1024,3072]{1,0:T(8,128)(2,1)}) %all-gather.3.cloned.1.call-update) | async-done | bytes 6291472 | tf_op jit(solution)/shard_map/all_gather | solution.py:188
  65.9 2.0 %fusion.12 = f32[1024,512]{1,0:T(8,128)S(1)} fusion(bf16[384,512]{1,0:T(8,128)(2,1)S(1)} %bitcast.35, bf16[1024,3072]{1,0:T(8,128)(2,1)} %all-gather.3.cloned.1.call-done, s32[]{:T(128)S(6)} %select_n.98), kind=kOutput, calls=%fused_computation.15 | convolution fusion | flops 402653184 | bytes 3276804 | tf_op jit(solution)/shard_map/dot_general | solution.py:193
  67.9 2.0 %convolution_add_fusion = f32[1024,512]{1,0:T(8,128)S(1)} fusion(f32[1024,512]{1,0:T(8,128)S(1)} %fusion.12, bf16[384,512]{1,0:T(8,128)(2,1)S(1)} %bitcast.39, bf16[1024,3072]{1,0:T(8,128)(2,1)} %all-gather.3.cloned.1.call-done, s32[]{:T(128)S(6)} %select_n.100), kind=kOutput, calls=%fused_computation.1 | convolution fusion | flops 403177472 | bytes 5373956 | tf_op jit(solution)/shard_map/dot_general | solution.py:193
  69.9 3.2 %collective-permute-start.4 = (bf16[4,48,512]{2,1,0:T(8,128)(2,1)S(1)}, bf16[4,48,512]{2,1,0:T(8,128)(2,1)S(1)}, u32[]{:S(2)}, u32[]{:S(2)}) collective-permute-start(bf16[4,48,512]{2,1,0:T(8,128)(2,1)S(1)} %slice.17), channel_id=1, source_target_pairs={{0,64},{8,72},{16,80},{24,88},{32,96},{40,104},{48,112},{56,120},{... | collective-permute-start | bytes 589832 | tf_op jit(solution)/shard_map/ppermute | solution.py:226
  73.2 0.9 slice.18
  74.1 3.8 %collective-permute-start.8 = (bf16[4,48,512]{2,1,0:T(8,128)(2,1)S(1)}, bf16[4,48,512]{2,1,0:T(8,128)(2,1)S(1)}, u32[]{:S(2)}, u32[]{:S(2)}) collective-permute-start(bf16[4,48,512]{2,1,0:T(8,128)(2,1)S(1)} %slice.18), channel_id=1, source_target_pairs={{0,448},{8,456},{16,464},{24,472},{32,480},{40,488},{48,496},{56,5... | collective-permute-start | bytes 589832 | tf_op jit(solution)/shard_map/ppermute | solution.py:227
  77.9 1.7 %fusion.2 = f32[1024,512]{1,0:T(8,128)S(1)} fusion(bf16[384,512]{1,0:T(8,128)(2,1)} %bitcast.10, bf16[1024,3072]{1,0:T(8,128)(2,1)S(1)} %copy-done.5, s32[]{:T(128)S(6)} %select_n.110), kind=kOutput, calls=%fused_computation.5 | convolution fusion | flops 402653184 | bytes 3276804 | tf_op jit(solution)/shard_map/dot_general | solution.py:193
  79.7 0.7 fusion.4
  80.4 1.8 %fusion.6 = f32[1024,512]{1,0:T(8,128)S(1)} fusion(bf16[384,512]{1,0:T(8,128)(2,1)} %bitcast.8, bf16[1024,3072]{1,0:T(8,128)(2,1)S(1)} %copy-done.5, s32[]{:T(128)S(6)} %select_n.106), kind=kOutput, calls=%fused_computation.9 | convolution fusion | flops 402653184 | bytes 3276804 | tf_op jit(solution)/shard_map/dot_general | solution.py:193
  82.1 0.7 fusion.9
  82.8 2.2 %add_add_fusion.total_ref = f32[1024,512]{1,0:T(8,128)S(1)} fusion(f32[1024,512]{1,0:T(8,128)S(1)} %fusion.2, f32[1024,512]{1,0:T(8,128)S(1)} %fusion.4, f32[1024,512]{1,0:T(8,128)S(1)} %fusion.6, f32[1024,512]{1,0:T(8,128)S(1)} %convolution_add_fusion, f32[1024,512]{1,0:T(8,128)S(1)} %fusion.9, bf16[384,512]{1,0:T(8,128)(2,1)} %bitcast.7, ...), kind=kOutput, calls=%fused_computation | convolution fusion | flops 405274624 | bytes 13762564 | tf_op jit(solution)/shard_map/dot_general | solution.py:193
  85.1 0.7 fusion.last_ref
  85.8 1.9 %shard_map.47 = (bf16[2,512,512]{2,1,0:T(8,128)(2,1)S(1)}, bf16[16,128,128]{2,1,0:T(8,128)(2,1)S(1)}, bf16[4,2,48,128]{3,2,1,0:T(8,128)(2,1)S(1)}) custom-call(f32[1024,512]{1,0:T(8,128)S(1)} %add_add_fusion.total_ref, f32[1024,512]{1,0:T(8,128)S(1)} %fusion.last_ref, f32[128,16]{1,0:T(8,128)S(1)} %bitcast.27, f32[16,128]{1,0:T(8,128)S(1)} %bitcast.31), custom_call_target="tpu_custom_call" | custom-call | flops 67108864 | bytes 4210688 | tf_op jit(solution)/shard_map/pallas_call | solution.py:170
  87.7 12.6 %all_to_all.21.messages_ref = bf16[4,2,48,128]{3,2,1,0:T(8,128)(2,1)S(1)} all-to-all(bf16[4,2,48,128]{3,2,1,0:T(8,128)(2,1)S(1)} %get-tuple-element.34), channel_id=1, replica_groups={{0,16,32,48},{8,24,40,56},{64,80,96,112},{72,88,104,120},{128,144,160,1..., dimensions={0} | all-to-all | bytes 196608 | tf_op jit(solution)/shard_map/all_to_all | solution.py:237
  100.4 1.3 collective-permute-start.9
  101.7 5.3 %collective-permute-start.10 = (bf16[2,48,128]{2,1,0:T(8,128)(2,1)S(1)}, bf16[2,48,128]{2,1,0:T(8,128)(2,1)S(1)}, u32[]{:S(2)}, u32[]{:S(2)}) collective-permute-start(bf16[2,48,128]{2,1,0:T(8,128)(2,1)S(1)} %get-tuple-element.35), channel_id=1, source_target_pairs={{0,128},{8,136},{16,144},{24,152},{32,160},{40,168},{48,176},{56,1... | collective-permute-start | bytes 73736 | tf_op jit(solution)/shard_map/ppermute | solution.py:248
  107.0 4.2 %collective-permute-start.11 = (bf16[2,48,128]{2,1,0:T(8,128)(2,1)S(1)}, bf16[2,48,128]{2,1,0:T(8,128)(2,1)S(1)}, u32[]{:S(2)}, u32[]{:S(2)}) collective-permute-start(bf16[2,48,128]{2,1,0:T(8,128)(2,1)S(1)} %get-tuple-element.35), channel_id=1, source_target_pairs={{0,192},{8,200},{16,208},{24,216},{32,224},{40,232},{48,240},{56,2... | collective-permute-start | bytes 73736 | tf_op jit(solution)/shard_map/ppermute | solution.py:248
  111.3 1.6 collective-permute-start.12
  112.9 1.3 collective-permute-start.13
  114.3 1.3 collective-permute-start.14
  115.6 1.3 collective-permute-start.15
  116.9 5.0 %convolution_bitcast_fusion.total_ref = f32[1024,256]{1,0:T(8,128)S(1)} fusion(bf16[1024,3072]{1,0:T(8,128)(2,1)} %all-gather.3.cloned.1.call-done, bf16[3072,256]{1,0:T(8,128)(2,1)} %bitcast.40), kind=kOutput, calls=%fused_computation.2 | convolution fusion | flops 1610612736 | bytes 8912896 | tf_op jit(solution)/shard_map/dot_general | solution.py:238
  122.0 0.7 shard_map.49
  122.6 3.3 %all-to-all-start.2 = ((bf16[4,2,32,128]{3,2,1,0:T(8,128)(2,1)}), bf16[4,2,32,128]{3,2,1,0:T(8,128)(2,1)S(1)}, u32[]{:S(2)}, u32[]{:S(2)}) async-start(bf16[4,2,32,128]{3,2,1,0:T(8,128)(2,1)} %shard_map.49), calls=%async_computation.2 | async-start | bytes 131072 | tf_op jit(solution)/shard_map/all_to_all | solution.py:250
  125.9 1.0 copy-done.3
  127.0 0.9 shard_map.50
  127.9 0.8 copy-done
  128.7 4.1 %all-to-all-done.2.incoming_ref = bf16[4,2,32,128]{3,2,1,0:T(8,128)(2,1)S(1)} async-done(((bf16[4,2,32,128]{3,2,1,0:T(8,128)(2,1)}), bf16[4,2,32,128]{3,2,1,0:T(8,128)(2,1)S(1)}, u32[]{:S(2)}, u32[]{:S(2)}) %all-to-all-start.2) | async-done | bytes 65568 | tf_op jit(solution)/shard_map/all_to_all | solution.py:250
  132.8 1.0 copy-done.1
  133.8 2.5 %shard_map.51 = bf16[1024,256]{1,0:T(8,128)(2,1)S(1)} custom-call(bf16[4,2,32,128]{3,2,1,0:T(8,128)(2,1)S(1)} %all-to-all-done.2.incoming_ref, f32[16,128,128]{2,1,0:T(8,128)S(1)} %get-tuple-element.43.part_ref, bf16[2,512,256]{2,1,0:T(8,128)(2,1)S(1)} %copy-done.1, f32[128,16]{1,0:T(8,128)S(1)} %bitcast.29, f32[1,16]{1,0:T(1,128)S(1)} %sub.18.start_ref, ...), custom_call_target="tpu_custom_call" | custom-call | flops 67108864 | bytes 1647680 | tf_op jit(solution)/shard_map/pallas_call | solution.py:170
  136.3 21.6 %all_to_all.22.sent_ref = bf16[16,64,256]{2,1,0:T(8,128)(2,1)S(1)} all-to-all(bf16[16,64,256]{2,1,0:T(8,128)(2,1)S(1)} %bitcast.26), channel_id=1, replica_groups={{0,1,2,3,4,5,6,7,8,9,10,11,12,13,14,15},{16,17,18,19,20,21,22,23,24,25,..., dimensions={0} | all-to-all | bytes 1048576 | tf_op jit(solution)/shard_map/all_to_all | solution.py:257
  158.0 0.8 shard_map.52
  (52 shorter events, 0.7 us)
Async XLA Ops:
  6.5 37.1 %copy-start.10 = (f32[4,512]{1,0:T(4,128)S(1)}, f32[4,512]{1,0:T(4,128)}, u32[]{:S(2)}) copy-start(f32[4,512]{1,0:T(4,128)} %param.6) | copy-start | bytes 24580
  6.5 47.0 %copy-start.11 = (f32[512]{0:T(512)S(1)}, f32[512]{0:T(512)}, u32[]{:S(2)}) copy-start(f32[512]{0:T(512)} %param.7) | copy-start | bytes 6148
  6.5 59.3 %all-gather.3.cloned.1.call-start = ((), (), s32[]{:S(2)}) async-start(), calls=%async_computation.4 | async-start | bytes 6684672 | tf_op jit(solution)/shard_map/all_gather | solution.py:188
  7.3 107.0 %all-gather.5.cloned.1.call-start = ((), (), s32[]{:S(2)}) async-start(), calls=%async_computation.5 | async-start | bytes 1769472 | tf_op jit(solution)/shard_map/all_gather | solution.py:223
  7.3 0.9 copy-start.4
  36.3 10.5 %collective-permute-start = (bf16[8,48,512]{2,1,0:T(8,128)(2,1)S(1)}, bf16[8,48,512]{2,1,0:T(8,128)(2,1)S(1)}, u32[]{:S(2)}, u32[]{:S(2)}) collective-permute-start(bf16[8,48,512]{2,1,0:T(8,128)(2,1)S(1)} %slice.20), channel_id=1, source_target_pairs={{0,64},{8,72},{16,80},{24,88},{32,96},{40,104},{48,112},{56,120},{... | collective-permute-start | bytes 1179656 | tf_op jit(solution)/shard_map/ppermute | solution.py:201
  39.5 9.2 %collective-permute-start.5 = (bf16[8,48,512]{2,1,0:T(8,128)(2,1)S(1)}, bf16[8,48,512]{2,1,0:T(8,128)(2,1)S(1)}, u32[]{:S(2)}, u32[]{:S(2)}) collective-permute-start(bf16[8,48,512]{2,1,0:T(8,128)(2,1)S(1)} %slice.20), channel_id=1, source_target_pairs={{0,448},{8,456},{16,464},{24,472},{32,480},{40,488},{48,496},{56,5... | collective-permute-start | bytes 1179656 | tf_op jit(solution)/shard_map/ppermute | solution.py:202
  43.6 5.1 %collective-permute-start.2 = (f32[2,512]{1,0:T(2,128)S(1)}, f32[2,512]{1,0:T(2,128)S(1)}, u32[]{:S(2)}, u32[]{:S(2)}) collective-permute-start(f32[2,512]{1,0:T(2,128)S(1)} %get-tuple-element.25), channel_id=1, source_target_pairs={{0,8},{8,0},{16,24},{24,16},{32,40},{40,32},{48,56},{56,48},{64,72... | collective-permute-start | bytes 12296 | tf_op jit(solution)/shard_map/ppermute | solution.py:210
  46.8 9.8 %copy-start.8 = (bf16[8,48,512]{2,1,0:T(8,128)(2,1)}, bf16[8,48,512]{2,1,0:T(8,128)(2,1)S(1)}, u32[]{:S(2)}) copy-start(bf16[8,48,512]{2,1,0:T(8,128)(2,1)S(1)} %collective-permute-done) | copy-start | bytes 1179652
  46.8 9.8 %collective-permute-start.1 = (bf16[8,48,512]{2,1,0:T(8,128)(2,1)S(1)}, bf16[8,48,512]{2,1,0:T(8,128)(2,1)}, u32[]{:S(2)}, u32[]{:S(2)}) collective-permute-start(bf16[8,48,512]{2,1,0:T(8,128)(2,1)S(1)} %collective-permute-done), channel_id=1, source_target_pairs={{0,64},{8,72},{16,80},{24,88},{32,96},{40,104},{48,112},{56,120},{... | collective-permute-start | bytes 1179656 | tf_op jit(solution)/shard_map/ppermute | solution.py:211
  48.7 17.2 %copy-start.6 = (bf16[8,48,512]{2,1,0:T(8,128)(2,1)}, bf16[8,48,512]{2,1,0:T(8,128)(2,1)S(1)}, u32[]{:S(2)}) copy-start(bf16[8,48,512]{2,1,0:T(8,128)(2,1)S(1)} %collective-permute-done.5) | copy-start | bytes 1179652
  48.7 9.8 %collective-permute-start.6 = (bf16[8,48,512]{2,1,0:T(8,128)(2,1)S(1)}, bf16[8,48,512]{2,1,0:T(8,128)(2,1)}, u32[]{:S(2)}, u32[]{:S(2)}) collective-permute-start(bf16[8,48,512]{2,1,0:T(8,128)(2,1)S(1)} %collective-permute-done.5), channel_id=1, source_target_pairs={{0,448},{8,456},{16,464},{24,472},{32,480},{40,488},{48,496},{56,5... | collective-permute-start | bytes 1179656 | tf_op jit(solution)/shard_map/ppermute | solution.py:212
  56.6 13.3 %collective-permute-start.3 = (bf16[8,48,512]{2,1,0:T(8,128)(2,1)}, bf16[8,48,512]{2,1,0:T(8,128)(2,1)S(1)}, u32[]{:S(2)}, u32[]{:S(2)}) collective-permute-start(bf16[8,48,512]{2,1,0:T(8,128)(2,1)} %collective-permute-done.1), channel_id=1, source_target_pairs={{0,64},{8,72},{16,80},{24,88},{32,96},{40,104},{48,112},{56,120},{... | collective-permute-start | bytes 1179656 | tf_op jit(solution)/shard_map/ppermute | solution.py:201
  58.5 14.6 %collective-permute-start.7 = (bf16[8,48,512]{2,1,0:T(8,128)(2,1)}, bf16[8,48,512]{2,1,0:T(8,128)(2,1)}, u32[]{:S(2)}, u32[]{:S(2)}) collective-permute-start(bf16[8,48,512]{2,1,0:T(8,128)(2,1)} %collective-permute-done.6), channel_id=1, source_target_pairs={{0,448},{8,456},{16,464},{24,472},{32,480},{40,488},{48,496},{56,5... | collective-permute-start | bytes 1179656 | tf_op jit(solution)/shard_map/ppermute | solution.py:202
  65.9 2.0 %copy-start.9 = (bf16[8,48,512]{2,1,0:T(8,128)(2,1)S(1)}, bf16[8,48,512]{2,1,0:T(8,128)(2,1)}, u32[]{:S(2)}) copy-start(bf16[8,48,512]{2,1,0:T(8,128)(2,1)} %copy-done.8) | copy-start | bytes 1179652
  65.9 12.0 %copy-start.5 = (bf16[1024,3072]{1,0:T(8,128)(2,1)S(1)}, bf16[1024,3072]{1,0:T(8,128)(2,1)}, u32[]{:S(2)}) copy-start(bf16[1024,3072]{1,0:T(8,128)(2,1)} %all-gather.3.cloned.1.call-done) | copy-start | bytes 18874372
  69.9 15.1 %collective-permute-start.4 = (bf16[4,48,512]{2,1,0:T(8,128)(2,1)S(1)}, bf16[4,48,512]{2,1,0:T(8,128)(2,1)S(1)}, u32[]{:S(2)}, u32[]{:S(2)}) collective-permute-start(bf16[4,48,512]{2,1,0:T(8,128)(2,1)S(1)} %slice.17), channel_id=1, source_target_pairs={{0,64},{8,72},{16,80},{24,88},{32,96},{40,104},{48,112},{56,120},{... | collective-permute-start | bytes 589832 | tf_op jit(solution)/shard_map/ppermute | solution.py:226
  74.1 10.9 %collective-permute-start.8 = (bf16[4,48,512]{2,1,0:T(8,128)(2,1)S(1)}, bf16[4,48,512]{2,1,0:T(8,128)(2,1)S(1)}, u32[]{:S(2)}, u32[]{:S(2)}) collective-permute-start(bf16[4,48,512]{2,1,0:T(8,128)(2,1)S(1)} %slice.18), channel_id=1, source_target_pairs={{0,448},{8,456},{16,464},{24,472},{32,480},{40,488},{48,496},{56,5... | collective-permute-start | bytes 589832 | tf_op jit(solution)/shard_map/ppermute | solution.py:227
  80.4 1.8 %copy-start.7 = (bf16[8,48,512]{2,1,0:T(8,128)(2,1)S(1)}, bf16[8,48,512]{2,1,0:T(8,128)(2,1)}, u32[]{:S(2)}) copy-start(bf16[8,48,512]{2,1,0:T(8,128)(2,1)} %copy-done.6) | copy-start | bytes 1179652
  87.7 34.2 %copy-start.2 = (bf16[16,128,128]{2,1,0:T(8,128)(2,1)}, bf16[16,128,128]{2,1,0:T(8,128)(2,1)S(1)}, u32[]{:S(2)}) copy-start(bf16[16,128,128]{2,1,0:T(8,128)(2,1)S(1)} %get-tuple-element.42.prefix_ref) | copy-start | bytes 1572868
  100.4 13.9 %collective-permute-start.9 = (bf16[2,48,128]{2,1,0:T(8,128)(2,1)S(1)}, bf16[2,48,128]{2,1,0:T(8,128)(2,1)S(1)}, u32[]{:S(2)}, u32[]{:S(2)}) collective-permute-start(bf16[2,48,128]{2,1,0:T(8,128)(2,1)S(1)} %get-tuple-element.35), channel_id=1, source_target_pairs={{0,64},{8,72},{16,80},{24,88},{32,96},{40,104},{48,112},{56,120},{... | collective-permute-start | bytes 73736 | tf_op jit(solution)/shard_map/ppermute | solution.py:248
  101.7 13.9 %collective-permute-start.10 = (bf16[2,48,128]{2,1,0:T(8,128)(2,1)S(1)}, bf16[2,48,128]{2,1,0:T(8,128)(2,1)S(1)}, u32[]{:S(2)}, u32[]{:S(2)}) collective-permute-start(bf16[2,48,128]{2,1,0:T(8,128)(2,1)S(1)} %get-tuple-element.35), channel_id=1, source_target_pairs={{0,128},{8,136},{16,144},{24,152},{32,160},{40,168},{48,176},{56,1... | collective-permute-start | bytes 73736 | tf_op jit(solution)/shard_map/ppermute | solution.py:248
  107.0 14.9 %collective-permute-start.11 = (bf16[2,48,128]{2,1,0:T(8,128)(2,1)S(1)}, bf16[2,48,128]{2,1,0:T(8,128)(2,1)S(1)}, u32[]{:S(2)}, u32[]{:S(2)}) collective-permute-start(bf16[2,48,128]{2,1,0:T(8,128)(2,1)S(1)} %get-tuple-element.35), channel_id=1, source_target_pairs={{0,192},{8,200},{16,208},{24,216},{32,224},{40,232},{48,240},{56,2... | collective-permute-start | bytes 73736 | tf_op jit(solution)/shard_map/ppermute | solution.py:248
  111.3 10.7 %collective-permute-start.12 = (bf16[2,48,128]{2,1,0:T(8,128)(2,1)S(1)}, bf16[2,48,128]{2,1,0:T(8,128)(2,1)S(1)}, u32[]{:S(2)}, u32[]{:S(2)}) collective-permute-start(bf16[2,48,128]{2,1,0:T(8,128)(2,1)S(1)} %get-tuple-element.35), channel_id=1, source_target_pairs={{0,256},{8,264},{16,272},{24,280},{32,288},{40,296},{48,304},{56,3... | collective-permute-start | bytes 73736 | tf_op jit(solution)/shard_map/ppermute | solution.py:248
  112.9 9.0 %collective-permute-start.13 = (bf16[2,48,128]{2,1,0:T(8,128)(2,1)S(1)}, bf16[2,48,128]{2,1,0:T(8,128)(2,1)S(1)}, u32[]{:S(2)}, u32[]{:S(2)}) collective-permute-start(bf16[2,48,128]{2,1,0:T(8,128)(2,1)S(1)} %get-tuple-element.35), channel_id=1, source_target_pairs={{0,320},{8,328},{16,336},{24,344},{32,352},{40,360},{48,368},{56,3... | collective-permute-start | bytes 73736 | tf_op jit(solution)/shard_map/ppermute | solution.py:248
  114.3 7.7 %collective-permute-start.14 = (bf16[2,48,128]{2,1,0:T(8,128)(2,1)S(1)}, bf16[2,48,128]{2,1,0:T(8,128)(2,1)S(1)}, u32[]{:S(2)}, u32[]{:S(2)}) collective-permute-start(bf16[2,48,128]{2,1,0:T(8,128)(2,1)S(1)} %get-tuple-element.35), channel_id=1, source_target_pairs={{0,384},{8,392},{16,400},{24,408},{32,416},{40,424},{48,432},{56,4... | collective-permute-start | bytes 73736 | tf_op jit(solution)/shard_map/ppermute | solution.py:248
  115.6 6.4 %collective-permute-start.15 = (bf16[2,48,128]{2,1,0:T(8,128)(2,1)S(1)}, bf16[2,48,128]{2,1,0:T(8,128)(2,1)S(1)}, u32[]{:S(2)}, u32[]{:S(2)}) collective-permute-start(bf16[2,48,128]{2,1,0:T(8,128)(2,1)S(1)} %get-tuple-element.35), channel_id=1, source_target_pairs={{0,448},{8,456},{16,464},{24,472},{32,480},{40,488},{48,496},{56,5... | collective-permute-start | bytes 73736 | tf_op jit(solution)/shard_map/ppermute | solution.py:248
  122.6 10.1 %all-to-all-start.2 = ((bf16[4,2,32,128]{3,2,1,0:T(8,128)(2,1)}), bf16[4,2,32,128]{3,2,1,0:T(8,128)(2,1)S(1)}, u32[]{:S(2)}, u32[]{:S(2)}) async-start(bf16[4,2,32,128]{3,2,1,0:T(8,128)(2,1)} %shard_map.49), calls=%async_computation.2 | async-start | bytes 131072 | tf_op jit(solution)/shard_map/all_to_all | solution.py:250
  125.9 1.0 copy-start.3
  127.9 0.8 copy-start
  132.8 1.0 copy-start.1
Sparse Core Ops, SparseCore 0:
  9.5 56.3 all-gather.2
  67.9 39.7 all-gather.4

commit v9 on v7

--- a/solution.py
+++ b/solution.py
@@ -14,6 +14,7 @@
 NZ = 8
 NH = 8
 EXTRA = 16
+FAR_FIRST = (4, 3, 5, 2, 6, 1, 7)
 F32 = jnp.float32
 BF16 = jnp.bfloat16
 VMEM = pltpu.VMEM
@@ -47,8 +48,7 @@
     return lax.dot_general(a, b, dims, preferred_element_type=F32)
 
 
-def write_message(ref, head, state, decay):
-    ref[head, :E, :] = state.astype(BF16)
+def write_message(refs, head, state, decay):
     decay = jnp.broadcast_to(decay, (EXTRA, E))
     high = decay.astype(BF16)
     rest = decay - high.astype(F32)
@@ -56,7 +56,11 @@
     low = (rest - middle.astype(F32)).astype(BF16)
     row = lax.broadcasted_iota(jnp.int32, (EXTRA, E), 0)
     part = jnp.where(row == 0, high.astype(F32), jnp.where(row == 1, middle.astype(F32), low.astype(F32)))
-    ref[head, E:, :] = part.astype(BF16)
+    part = part.astype(BF16)
+    state = state.astype(BF16)
+    for ref in refs:
+        ref[head, :E, :] = state
+        ref[head, E:, :] = part
 
 
 def read_decay(ref, head):
@@ -95,8 +99,7 @@
             scaled = (keys.astype(F32) * scale).astype(BF16)
             state = jnp.exp(last) * state + mm(scaled, values, (((0,), (0,)), ((), ())))
             decay = decay + last
-        for copy in range(4):
-            write_message(message_ref.at[copy], head, state, decay)
+        write_message([message_ref.at[k] for k in range(4)], head, state, decay)
 
 
 def local_kernel(total_ref, proj_ref, prefix_ref, col_ref, row_ref, query_ref, out_ref):
@@ -135,11 +138,11 @@
             gone_before = gone_before + jnp.where(early, decay, 0.0)
         before_ref[head] = before
         decay_ref[head] = jnp.broadcast_to(gone_before, (8, E))
-        write_message(message_ref, head, total, gone)
+        write_message([message_ref], head, total, gone)
 
 
 def final_kernel(*refs):
-    messages = refs[:7]
+    messages = [refs[FAR_FIRST.index(k)] for k in range(1, NY)]
     before_ref, decay_ref, part_ref, query_ref, col_ref, start_ref, gain_ref, out_ref = refs[7:]
     for head in range(2):
         carried = jnp.zeros((E, E), F32)
@@ -245,7 +248,7 @@
         [((2, E, E), F32), ((2, 8, E), F32), ((2, E + EXTRA, E), BF16)],
         [place1], messages,
     )
-    earlier = [lax.ppermute(row_message, "seq", y_later(k)) for k in range(1, NY)]
+    earlier = [lax.ppermute(row_message, "seq", y_later(k)) for k in FAR_FIRST]
     (flat,) = call(
         final_kernel, [((1024, 256), BF16)], [], *earlier, before, gone, part, query, cols, starts, gain,
         flops=16 * 2 * E**3,

time: 155 us -> 155 us (level)
  no operation moved by 1% of the time
where the time goes in v9:
time: 155 us
  blocking collectives  51.1 us (33%)
  starting transfers between devices  50.4 us (33%)
  waiting for transfers between devices  15.5 us (10%)
  between operations  14 us (9%)
  matrix products  13.4 us (9%)
  Pallas kernels  7.09 us (5%)
  local copies, waits for them, and re-layouts  2.25 us (1%)
    all_to_all x1, blocking collectives, on_device(): lax.all_to_all(pieces, 'seq', split_axis=0, concat_axis=0, tiled=True, ax...  28 us
    all_to_all x1, blocking collectives, on_device(): lax.all_to_all(flat.reshape(16, 64, 256), ('seq', 'head'), split_axis=0,...  23.1 us
    ppermute x7, starting transfers between devices, on_device(): earlier = [lax.ppermute(row_message, 'seq', y_later(k)) for k in FAR_FIRST]  15.8 us
    all_to_all x1, waiting for transfers between devices, on_device(): lax.all_to_all(messages, 'seq', split_axis=0, concat_axis=0, tiled=True,...  9.69 us
    ppermute x2, starting transfers between devices, hop(): downs.append(lax.ppermute(after(downs[-1], *earlier), 'seq', y_shift(-1)))  8.62 us
    dot_general x8, matrix products, add(): d = jnp.dot(x, part.reshape(NZ * 48, 512), preferred_element_type=F32)  8.41 us
    pallas_call x6, Pallas kernels, call(): pl.pallas_call(kernel, out_shape=shapes, in_specs=smem + whole(len(args))...  7.09 us
    all_to_all x1, starting transfers between devices, on_device(): lax.all_to_all(messages, 'seq', split_axis=0, concat_axis=0, tiled=True,...  5.45 us
  transfers between devices with their start and end apart: 19, of which 4 were waited for; matrix products, arithmetic and copies ran while one was open for 10% of the time, Pallas kernels for 2%

profile of v9, /device:TPU:1, one launch (start us, length us, event | category | flops | bytes accessed | tf_op | source)
XLA Modules:
  0.0 154.6 jit_solution(1209993321404940281)
XLA Ops:
  6.5 0.7 all-gather.3.cloned.1.call-update
  7.3 0.0 all-gather.5.cloned.1.call-start
  7.3 0.9 copy-done
  8.3 28.0 %all_to_all.15 = bf16[8,48,768]{2,1,0:T(8,128)(2,1)S(1)} all-to-all(bf16[8,48,768]{2,1,0:T(8,128)(2,1)S(1)} %shard_map.46), channel_id=1, replica_groups={{0,8,16,24,32,40,48,56},{64,72,80,88,96,104,112,120},{128,136,144,152,1..., dimensions={0} | all-to-all | bytes 1179648 | tf_op jit(solution)/shard_map/all_to_all | solution.py:189
  36.3 3.2 %collective-permute-start = (bf16[8,48,512]{2,1,0:T(8,128)(2,1)S(1)}, bf16[8,48,512]{2,1,0:T(8,128)(2,1)S(1)}, u32[]{:S(2)}, u32[]{:S(2)}) collective-permute-start(bf16[8,48,512]{2,1,0:T(8,128)(2,1)S(1)} %slice.20), channel_id=1, source_target_pairs={{0,64},{8,72},{16,80},{24,88},{32,96},{40,104},{48,112},{56,120},{... | collective-permute-start | bytes 1179656 | tf_op jit(solution)/shard_map/ppermute | solution.py:204
  39.5 4.0 %collective-permute-start.5 = (bf16[8,48,512]{2,1,0:T(8,128)(2,1)S(1)}, bf16[8,48,512]{2,1,0:T(8,128)(2,1)S(1)}, u32[]{:S(2)}, u32[]{:S(2)}) collective-permute-start(bf16[8,48,512]{2,1,0:T(8,128)(2,1)S(1)} %slice.20), channel_id=1, source_target_pairs={{0,448},{8,456},{16,464},{24,472},{32,480},{40,488},{48,496},{56,5... | collective-permute-start | bytes 1179656 | tf_op jit(solution)/shard_map/ppermute | solution.py:205
  43.6 1.9 %collective-permute-start.2 = (f32[2,512]{1,0:T(2,128)S(1)}, f32[2,512]{1,0:T(2,128)S(1)}, u32[]{:S(2)}, u32[]{:S(2)}) collective-permute-start(f32[2,512]{1,0:T(2,128)S(1)} %get-tuple-element.24), channel_id=1, source_target_pairs={{0,8},{8,0},{16,24},{24,16},{32,40},{40,32},{48,56},{56,48},{64,72... | collective-permute-start | bytes 12296 | tf_op jit(solution)/shard_map/ppermute | solution.py:213
  45.5 1.2 collective-permute-done
  46.8 1.9 %collective-permute-start.1 = (bf16[8,48,512]{2,1,0:T(8,128)(2,1)S(1)}, bf16[8,48,512]{2,1,0:T(8,128)(2,1)S(1)}, u32[]{:S(2)}, u32[]{:S(2)}) collective-permute-start(bf16[8,48,512]{2,1,0:T(8,128)(2,1)S(1)} %collective-permute-done), channel_id=1, source_target_pairs={{0,64},{8,72},{16,80},{24,88},{32,96},{40,104},{48,112},{56,120},{... | collective-permute-start | bytes 1179656 | tf_op jit(solution)/shard_map/ppermute | solution.py:214
  48.7 4.6 %collective-permute-start.6 = (bf16[8,48,512]{2,1,0:T(8,128)(2,1)S(1)}, bf16[8,48,512]{2,1,0:T(8,128)(2,1)S(1)}, u32[]{:S(2)}, u32[]{:S(2)}) collective-permute-start(bf16[8,48,512]{2,1,0:T(8,128)(2,1)S(1)} %collective-permute-done.5), channel_id=1, source_target_pairs={{0,448},{8,456},{16,464},{24,472},{32,480},{40,488},{48,496},{56,5... | collective-permute-start | bytes 1179656 | tf_op jit(solution)/shard_map/ppermute | solution.py:215
  53.5 0.1 dynamic_slice.35
  53.6 0.7 slice.22
  54.3 0.6 reduce_window_sum.24
  54.9 0.2 slice_reduce_fusion
  55.1 0.2 reduce_window_sum.25
  55.3 0.1 squeeze.6
  55.3 0.1 copy.11
  55.4 0.1 reduce_window_sum.26
  55.5 1.0 collective-permute-done.1
  56.5 1.9 %collective-permute-start.3 = (bf16[8,48,512]{2,1,0:T(8,128)(2,1)S(1)}, bf16[8,48,512]{2,1,0:T(8,128)(2,1)S(1)}, u32[]{:S(2)}, u32[]{:S(2)}) collective-permute-start(bf16[8,48,512]{2,1,0:T(8,128)(2,1)S(1)} %collective-permute-done.1), channel_id=1, source_target_pairs={{0,64},{8,72},{16,80},{24,88},{32,96},{40,104},{48,112},{56,120},{... | collective-permute-start | bytes 1179656 | tf_op jit(solution)/shard_map/ppermute | solution.py:204
  58.4 4.6 %collective-permute-start.7 = (bf16[8,48,512]{2,1,0:T(8,128)(2,1)S(1)}, bf16[8,48,512]{2,1,0:T(8,128)(2,1)S(1)}, u32[]{:S(2)}, u32[]{:S(2)}) collective-permute-start(bf16[8,48,512]{2,1,0:T(8,128)(2,1)S(1)} %collective-permute-done.6), channel_id=1, source_target_pairs={{0,448},{8,456},{16,464},{24,472},{32,480},{40,488},{48,496},{56,5... | collective-permute-start | bytes 1179656 | tf_op jit(solution)/shard_map/ppermute | solution.py:205
  63.0 2.9 %all-gather.3.cloned.1.call-done = bf16[1024,3072]{1,0:T(8,128)(2,1)} async-done(((bf16[64,3072]{1,0:T(8,128)(2,1)}), bf16[1024,3072]{1,0:T(8,128)(2,1)}) %all-gather.3.cloned.1.call-update) | async-done | bytes 6291472 | tf_op jit(solution)/shard_map/all_gather | solution.py:191
  65.9 2.0 %fusion.12 = f32[1024,512]{1,0:T(8,128)S(1)} fusion(bf16[384,512]{1,0:T(8,128)(2,1)S(1)} %bitcast.36, bf16[1024,3072]{1,0:T(8,128)(2,1)} %all-gather.3.cloned.1.call-done, s32[]{:T(128)S(6)} %select_n.102), kind=kOutput, calls=%fused_computation.15 | convolution fusion | flops 402653184 | bytes 3276804 | tf_op jit(solution)/shard_map/dot_general | solution.py:196
  67.9 1.9 %convolution_add_fusion = f32[1024,512]{1,0:T(8,128)S(1)} fusion(f32[1024,512]{1,0:T(8,128)S(1)} %fusion.12, bf16[384,512]{1,0:T(8,128)(2,1)S(1)} %bitcast.43, bf16[1024,3072]{1,0:T(8,128)(2,1)} %all-gather.3.cloned.1.call-done, s32[]{:T(128)S(6)} %select_n.104), kind=kOutput, calls=%fused_computation.1 | convolution fusion | flops 403177472 | bytes 5373956 | tf_op jit(solution)/shard_map/dot_general | solution.py:196
  69.8 3.2 %collective-permute-start.4 = (bf16[4,48,512]{2,1,0:T(8,128)(2,1)S(1)}, bf16[4,48,512]{2,1,0:T(8,128)(2,1)S(1)}, u32[]{:S(2)}, u32[]{:S(2)}) collective-permute-start(bf16[4,48,512]{2,1,0:T(8,128)(2,1)S(1)} %slice.17), channel_id=1, source_target_pairs={{0,64},{8,72},{16,80},{24,88},{32,96},{40,104},{48,112},{56,120},{... | collective-permute-start | bytes 589832 | tf_op jit(solution)/shard_map/ppermute | solution.py:229
  73.1 3.8 %collective-permute-start.8 = (bf16[4,48,512]{2,1,0:T(8,128)(2,1)S(1)}, bf16[4,48,512]{2,1,0:T(8,128)(2,1)S(1)}, u32[]{:S(2)}, u32[]{:S(2)}) collective-permute-start(bf16[4,48,512]{2,1,0:T(8,128)(2,1)S(1)} %slice.18), channel_id=1, source_target_pairs={{0,448},{8,456},{16,464},{24,472},{32,480},{40,488},{48,496},{56,5... | collective-permute-start | bytes 589832 | tf_op jit(solution)/shard_map/ppermute | solution.py:230
  76.9 0.7 fusion.2
  77.6 0.7 fusion.4
  78.3 0.7 fusion.6
  79.0 0.7 fusion.9
  79.7 1.0 add_add_fusion.total_ref
  80.8 0.7 fusion.last_ref
  81.5 2.7 %shard_map.47 = (bf16[2,512,512]{2,1,0:T(8,128)(2,1)S(1)}, bf16[16,128,128]{2,1,0:T(8,128)(2,1)S(1)}, bf16[4,2,144,128]{3,2,1,0:T(8,128)(2,1)}) custom-call(f32[1024,512]{1,0:T(8,128)S(1)} %add_add_fusion.total_ref, f32[1024,512]{1,0:T(8,128)S(1)} %fusion.last_ref, f32[128,16]{1,0:T(8,128)S(1)} %bitcast.28, f32[16,128]{1,0:T(8,128)S(1)} %bitcast.32), custom_call_target="tpu_custom_call" | custom-call | flops 67108864 | bytes 4210688 | tf_op jit(solution)/shard_map/pallas_call | solution.py:171
  84.2 5.4 %all-to-all-start.1 = ((bf16[4,2,144,128]{3,2,1,0:T(8,128)(2,1)}), bf16[4,2,144,128]{3,2,1,0:T(8,128)(2,1)S(1)}, u32[]{:S(2)}, u32[]{:S(2)}) async-start(bf16[4,2,144,128]{3,2,1,0:T(8,128)(2,1)} %get-tuple-element.33), calls=%async_computation.1 | async-start | bytes 589824 | tf_op jit(solution)/shard_map/all_to_all | solution.py:240
  89.6 9.7 %all-to-all-done.1.messages_ref = bf16[4,2,144,128]{3,2,1,0:T(8,128)(2,1)S(1)} async-done(((bf16[4,2,144,128]{3,2,1,0:T(8,128)(2,1)}), bf16[4,2,144,128]{3,2,1,0:T(8,128)(2,1)S(1)}, u32[]{:S(2)}, u32[]{:S(2)}) %all-to-all-start.1) | async-done | bytes 294944 | tf_op jit(solution)/shard_map/all_to_all | solution.py:240
  99.3 0.1 shard_map.48
  99.4 5.5 %collective-permute-start.9 = (bf16[2,144,128]{2,1,0:T(8,128)(2,1)S(1)}, bf16[2,144,128]{2,1,0:T(8,128)(2,1)S(1)}, u32[]{:S(2)}, u32[]{:S(2)}) collective-permute-start(bf16[2,144,128]{2,1,0:T(8,128)(2,1)S(1)} %get-tuple-element.34), channel_id=1, source_target_pairs={{0,256},{8,264},{16,272},{24,280},{32,288},{40,296},{48,304},{56,3... | collective-permute-start | bytes 221192 | tf_op jit(solution)/shard_map/ppermute | solution.py:251
  104.9 2.4 %collective-permute-start.10 = (bf16[2,144,128]{2,1,0:T(8,128)(2,1)S(1)}, bf16[2,144,128]{2,1,0:T(8,128)(2,1)S(1)}, u32[]{:S(2)}, u32[]{:S(2)}) collective-permute-start(bf16[2,144,128]{2,1,0:T(8,128)(2,1)S(1)} %get-tuple-element.34), channel_id=1, source_target_pairs={{0,192},{8,200},{16,208},{24,216},{32,224},{40,232},{48,240},{56,2... | collective-permute-start | bytes 221192 | tf_op jit(solution)/shard_map/ppermute | solution.py:251
  107.3 1.3 collective-permute-start.11
  108.6 2.5 %collective-permute-start.12 = (bf16[2,144,128]{2,1,0:T(8,128)(2,1)S(1)}, bf16[2,144,128]{2,1,0:T(8,128)(2,1)S(1)}, u32[]{:S(2)}, u32[]{:S(2)}) collective-permute-start(bf16[2,144,128]{2,1,0:T(8,128)(2,1)S(1)} %get-tuple-element.34), channel_id=1, source_target_pairs={{0,128},{8,136},{16,144},{24,152},{32,160},{40,168},{48,176},{56,1... | collective-permute-start | bytes 221192 | tf_op jit(solution)/shard_map/ppermute | solution.py:251
  111.1 1.3 collective-permute-start.13
  112.4 1.6 %collective-permute-start.14 = (bf16[2,144,128]{2,1,0:T(8,128)(2,1)S(1)}, bf16[2,144,128]{2,1,0:T(8,128)(2,1)S(1)}, u32[]{:S(2)}, u32[]{:S(2)}) collective-permute-start(bf16[2,144,128]{2,1,0:T(8,128)(2,1)S(1)} %get-tuple-element.34), channel_id=1, source_target_pairs={{0,64},{8,72},{16,80},{24,88},{32,96},{40,104},{48,112},{56,120},{... | collective-permute-start | bytes 221192 | tf_op jit(solution)/shard_map/ppermute | solution.py:251
  114.0 1.3 collective-permute-start.15
  115.3 5.0 %convolution_bitcast_fusion.total_ref = f32[1024,256]{1,0:T(8,128)S(1)} fusion(bf16[1024,3072]{1,0:T(8,128)(2,1)} %all-gather.3.cloned.1.call-done, bf16[3072,256]{1,0:T(8,128)(2,1)} %bitcast.44), kind=kOutput, calls=%fused_computation.2 | convolution fusion | flops 1610612736 | bytes 8912896 | tf_op jit(solution)/shard_map/dot_general | solution.py:241
  120.3 0.9 shard_map.49
  121.3 2.5 %shard_map.50 = bf16[1024,256]{1,0:T(8,128)(2,1)S(1)} custom-call(bf16[2,144,128]{2,1,0:T(8,128)(2,1)S(1)} %collective-permute-done.9.refs_0_, bf16[2,144,128]{2,1,0:T(8,128)(2,1)S(1)} %collective-permute-done.10.refs_1_, bf16[2,144,128]{2,1,0:T(8,128)(2,1)S(1)} %collective-permute-done.11.refs_2_, bf16[2,144,128]{2,1,0:T(8,128)(2,1)S(1)} %collective-permute-done.12.refs_3_, ...), custom_call_target="tpu_custom_call" | custom-call | flops 67108864 | bytes 2237504 | tf_op jit(solution)/shard_map/pallas_call | solution.py:171
  123.8 23.1 %all_to_all.16.sent_ref = bf16[16,64,256]{2,1,0:T(8,128)(2,1)S(1)} all-to-all(bf16[16,64,256]{2,1,0:T(8,128)(2,1)S(1)} %bitcast.27), channel_id=1, replica_groups={{0,1,2,3,4,5,6,7,8,9,10,11,12,13,14,15},{16,17,18,19,20,21,22,23,24,25,..., dimensions={0} | all-to-all | bytes 1048576 | tf_op jit(solution)/shard_map/all_to_all | solution.py:256
  146.9 0.8 shard_map.51
  (34 shorter events, 0.3 us)
Async XLA Ops:
  6.5 37.1 %copy-start.2 = (f32[4,512]{1,0:T(4,128)S(1)}, f32[4,512]{1,0:T(4,128)}, u32[]{:S(2)}) copy-start(f32[4,512]{1,0:T(4,128)} %param.6) | copy-start | bytes 24580
  6.5 46.9 %copy-start.3 = (f32[512]{0:T(512)S(1)}, f32[512]{0:T(512)}, u32[]{:S(2)}) copy-start(f32[512]{0:T(512)} %param.7) | copy-start | bytes 6148
  6.5 59.3 %all-gather.3.cloned.1.call-start = ((), (), s32[]{:S(2)}) async-start(), calls=%async_computation.3 | async-start | bytes 6684672 | tf_op jit(solution)/shard_map/all_gather | solution.py:191
  7.3 105.1 %all-gather.5.cloned.1.call-start = ((), (), s32[]{:S(2)}) async-start(), calls=%async_computation.4 | async-start | bytes 1769472 | tf_op jit(solution)/shard_map/all_gather | solution.py:226
  7.3 0.9 copy-start
  36.3 10.5 %collective-permute-start = (bf16[8,48,512]{2,1,0:T(8,128)(2,1)S(1)}, bf16[8,48,512]{2,1,0:T(8,128)(2,1)S(1)}, u32[]{:S(2)}, u32[]{:S(2)}) collective-permute-start(bf16[8,48,512]{2,1,0:T(8,128)(2,1)S(1)} %slice.20), channel_id=1, source_target_pairs={{0,64},{8,72},{16,80},{24,88},{32,96},{40,104},{48,112},{56,120},{... | collective-permute-start | bytes 1179656 | tf_op jit(solution)/shard_map/ppermute | solution.py:204
  39.5 9.2 %collective-permute-start.5 = (bf16[8,48,512]{2,1,0:T(8,128)(2,1)S(1)}, bf16[8,48,512]{2,1,0:T(8,128)(2,1)S(1)}, u32[]{:S(2)}, u32[]{:S(2)}) collective-permute-start(bf16[8,48,512]{2,1,0:T(8,128)(2,1)S(1)} %slice.20), channel_id=1, source_target_pairs={{0,448},{8,456},{16,464},{24,472},{32,480},{40,488},{48,496},{56,5... | collective-permute-start | bytes 1179656 | tf_op jit(solution)/shard_map/ppermute | solution.py:205
  43.6 5.1 %collective-permute-start.2 = (f32[2,512]{1,0:T(2,128)S(1)}, f32[2,512]{1,0:T(2,128)S(1)}, u32[]{:S(2)}, u32[]{:S(2)}) collective-permute-start(f32[2,512]{1,0:T(2,128)S(1)} %get-tuple-element.24), channel_id=1, source_target_pairs={{0,8},{8,0},{16,24},{24,16},{32,40},{40,32},{48,56},{56,48},{64,72... | collective-permute-start | bytes 12296 | tf_op jit(solution)/shard_map/ppermute | solution.py:213
  46.8 9.7 %collective-permute-start.1 = (bf16[8,48,512]{2,1,0:T(8,128)(2,1)S(1)}, bf16[8,48,512]{2,1,0:T(8,128)(2,1)S(1)}, u32[]{:S(2)}, u32[]{:S(2)}) collective-permute-start(bf16[8,48,512]{2,1,0:T(8,128)(2,1)S(1)} %collective-permute-done), channel_id=1, source_target_pairs={{0,64},{8,72},{16,80},{24,88},{32,96},{40,104},{48,112},{56,120},{... | collective-permute-start | bytes 1179656 | tf_op jit(solution)/shard_map/ppermute | solution.py:214
  48.7 9.7 %collective-permute-start.6 = (bf16[8,48,512]{2,1,0:T(8,128)(2,1)S(1)}, bf16[8,48,512]{2,1,0:T(8,128)(2,1)S(1)}, u32[]{:S(2)}, u32[]{:S(2)}) collective-permute-start(bf16[8,48,512]{2,1,0:T(8,128)(2,1)S(1)} %collective-permute-done.5), channel_id=1, source_target_pairs={{0,448},{8,456},{16,464},{24,472},{32,480},{40,488},{48,496},{56,5... | collective-permute-start | bytes 1179656 | tf_op jit(solution)/shard_map/ppermute | solution.py:215
  56.5 13.3 %collective-permute-start.3 = (bf16[8,48,512]{2,1,0:T(8,128)(2,1)S(1)}, bf16[8,48,512]{2,1,0:T(8,128)(2,1)S(1)}, u32[]{:S(2)}, u32[]{:S(2)}) collective-permute-start(bf16[8,48,512]{2,1,0:T(8,128)(2,1)S(1)} %collective-permute-done.1), channel_id=1, source_target_pairs={{0,64},{8,72},{16,80},{24,88},{32,96},{40,104},{48,112},{56,120},{... | collective-permute-start | bytes 1179656 | tf_op jit(solution)/shard_map/ppermute | solution.py:204
  58.4 14.6 %collective-permute-start.7 = (bf16[8,48,512]{2,1,0:T(8,128)(2,1)S(1)}, bf16[8,48,512]{2,1,0:T(8,128)(2,1)S(1)}, u32[]{:S(2)}, u32[]{:S(2)}) collective-permute-start(bf16[8,48,512]{2,1,0:T(8,128)(2,1)S(1)} %collective-permute-done.6), channel_id=1, source_target_pairs={{0,448},{8,456},{16,464},{24,472},{32,480},{40,488},{48,496},{56,5... | collective-permute-start | bytes 1179656 | tf_op jit(solution)/shard_map/ppermute | solution.py:205
  65.9 11.0 %copy-start.1 = (bf16[1024,3072]{1,0:T(8,128)(2,1)S(1)}, bf16[1024,3072]{1,0:T(8,128)(2,1)}, u32[]{:S(2)}) copy-start(bf16[1024,3072]{1,0:T(8,128)(2,1)} %all-gather.3.cloned.1.call-done) | copy-start | bytes 18874372
  69.8 10.9 %collective-permute-start.4 = (bf16[4,48,512]{2,1,0:T(8,128)(2,1)S(1)}, bf16[4,48,512]{2,1,0:T(8,128)(2,1)S(1)}, u32[]{:S(2)}, u32[]{:S(2)}) collective-permute-start(bf16[4,48,512]{2,1,0:T(8,128)(2,1)S(1)} %slice.17), channel_id=1, source_target_pairs={{0,64},{8,72},{16,80},{24,88},{32,96},{40,104},{48,112},{56,120},{... | collective-permute-start | bytes 589832 | tf_op jit(solution)/shard_map/ppermute | solution.py:229
  73.1 7.7 %collective-permute-start.8 = (bf16[4,48,512]{2,1,0:T(8,128)(2,1)S(1)}, bf16[4,48,512]{2,1,0:T(8,128)(2,1)S(1)}, u32[]{:S(2)}, u32[]{:S(2)}) collective-permute-start(bf16[4,48,512]{2,1,0:T(8,128)(2,1)S(1)} %slice.18), channel_id=1, source_target_pairs={{0,448},{8,456},{16,464},{24,472},{32,480},{40,488},{48,496},{56,5... | collective-permute-start | bytes 589832 | tf_op jit(solution)/shard_map/ppermute | solution.py:230
  84.2 15.1 %all-to-all-start.1 = ((bf16[4,2,144,128]{3,2,1,0:T(8,128)(2,1)}), bf16[4,2,144,128]{3,2,1,0:T(8,128)(2,1)S(1)}, u32[]{:S(2)}, u32[]{:S(2)}) async-start(bf16[4,2,144,128]{3,2,1,0:T(8,128)(2,1)} %get-tuple-element.33), calls=%async_computation.1 | async-start | bytes 589824 | tf_op jit(solution)/shard_map/all_to_all | solution.py:240
  99.4 13.0 %collective-permute-start.9 = (bf16[2,144,128]{2,1,0:T(8,128)(2,1)S(1)}, bf16[2,144,128]{2,1,0:T(8,128)(2,1)S(1)}, u32[]{:S(2)}, u32[]{:S(2)}) collective-permute-start(bf16[2,144,128]{2,1,0:T(8,128)(2,1)S(1)} %get-tuple-element.34), channel_id=1, source_target_pairs={{0,256},{8,264},{16,272},{24,280},{32,288},{40,296},{48,304},{56,3... | collective-permute-start | bytes 221192 | tf_op jit(solution)/shard_map/ppermute | solution.py:251
  104.9 9.1 %collective-permute-start.10 = (bf16[2,144,128]{2,1,0:T(8,128)(2,1)S(1)}, bf16[2,144,128]{2,1,0:T(8,128)(2,1)S(1)}, u32[]{:S(2)}, u32[]{:S(2)}) collective-permute-start(bf16[2,144,128]{2,1,0:T(8,128)(2,1)S(1)} %get-tuple-element.34), channel_id=1, source_target_pairs={{0,192},{8,200},{16,208},{24,216},{32,224},{40,232},{48,240},{56,2... | collective-permute-start | bytes 221192 | tf_op jit(solution)/shard_map/ppermute | solution.py:251
  107.3 13.9 %collective-permute-start.11 = (bf16[2,144,128]{2,1,0:T(8,128)(2,1)S(1)}, bf16[2,144,128]{2,1,0:T(8,128)(2,1)S(1)}, u32[]{:S(2)}, u32[]{:S(2)}) collective-permute-start(bf16[2,144,128]{2,1,0:T(8,128)(2,1)S(1)} %get-tuple-element.34), channel_id=1, source_target_pairs={{0,320},{8,328},{16,336},{24,344},{32,352},{40,360},{48,368},{56,3... | collective-permute-start | bytes 221192 | tf_op jit(solution)/shard_map/ppermute | solution.py:251
  108.6 12.6 %collective-permute-start.12 = (bf16[2,144,128]{2,1,0:T(8,128)(2,1)S(1)}, bf16[2,144,128]{2,1,0:T(8,128)(2,1)S(1)}, u32[]{:S(2)}, u32[]{:S(2)}) collective-permute-start(bf16[2,144,128]{2,1,0:T(8,128)(2,1)S(1)} %get-tuple-element.34), channel_id=1, source_target_pairs={{0,128},{8,136},{16,144},{24,152},{32,160},{40,168},{48,176},{56,1... | collective-permute-start | bytes 221192 | tf_op jit(solution)/shard_map/ppermute | solution.py:251
  111.1 10.2 %collective-permute-start.13 = (bf16[2,144,128]{2,1,0:T(8,128)(2,1)S(1)}, bf16[2,144,128]{2,1,0:T(8,128)(2,1)S(1)}, u32[]{:S(2)}, u32[]{:S(2)}) collective-permute-start(bf16[2,144,128]{2,1,0:T(8,128)(2,1)S(1)} %get-tuple-element.34), channel_id=1, source_target_pairs={{0,384},{8,392},{16,400},{24,408},{32,416},{40,424},{48,432},{56,4... | collective-permute-start | bytes 221192 | tf_op jit(solution)/shard_map/ppermute | solution.py:251
  112.4 8.8 %collective-permute-start.14 = (bf16[2,144,128]{2,1,0:T(8,128)(2,1)S(1)}, bf16[2,144,128]{2,1,0:T(8,128)(2,1)S(1)}, u32[]{:S(2)}, u32[]{:S(2)}) collective-permute-start(bf16[2,144,128]{2,1,0:T(8,128)(2,1)S(1)} %get-tuple-element.34), channel_id=1, source_target_pairs={{0,64},{8,72},{16,80},{24,88},{32,96},{40,104},{48,112},{56,120},{... | collective-permute-start | bytes 221192 | tf_op jit(solution)/shard_map/ppermute | solution.py:251
  114.0 7.3 %collective-permute-start.15 = (bf16[2,144,128]{2,1,0:T(8,128)(2,1)S(1)}, bf16[2,144,128]{2,1,0:T(8,128)(2,1)S(1)}, u32[]{:S(2)}, u32[]{:S(2)}) collective-permute-start(bf16[2,144,128]{2,1,0:T(8,128)(2,1)S(1)} %get-tuple-element.34), channel_id=1, source_target_pairs={{0,448},{8,456},{16,464},{24,472},{32,480},{40,488},{48,496},{56,5... | collective-permute-start | bytes 221192 | tf_op jit(solution)/shard_map/ppermute | solution.py:251
Sparse Core Ops, SparseCore 0:
  9.5 56.3 all-gather.2
  67.9 41.0 all-gather.4

commit v10 on v9

--- a/solution.py
+++ b/solution.py
@@ -14,7 +14,7 @@
 NZ = 8
 NH = 8
 EXTRA = 16
-FAR_FIRST = (4, 3, 5, 2, 6, 1, 7)
+START_ORDER = (1, 7, 4, 3, 5, 2, 6)
 F32 = jnp.float32
 BF16 = jnp.bfloat16
 VMEM = pltpu.VMEM
@@ -142,7 +142,7 @@
 
 
 def final_kernel(*refs):
-    messages = [refs[FAR_FIRST.index(k)] for k in range(1, NY)]
+    messages = [refs[START_ORDER.index(k)] for k in range(1, NY)]
     before_ref, decay_ref, part_ref, query_ref, col_ref, start_ref, gain_ref, out_ref = refs[7:]
     for head in range(2):
         carried = jnp.zeros((E, E), F32)
@@ -248,7 +248,7 @@
         [((2, E, E), F32), ((2, 8, E), F32), ((2, E + EXTRA, E), BF16)],
         [place1], messages,
     )
-    earlier = [lax.ppermute(row_message, "seq", y_later(k)) for k in FAR_FIRST]
+    earlier = [lax.ppermute(row_message, "seq", y_later(k)) for k in START_ORDER]
     (flat,) = call(
         final_kernel, [((1024, 256), BF16)], [], *earlier, before, gone, part, query, cols, starts, gain,
         flops=16 * 2 * E**3,

time: 155 us -> 154 us (level)
  no operation moved by 1% of the time
where the time goes in v10:
time: 154 us; the launch traced here: 153 us
  starting transfers between devices  50.4 us (33%)
  blocking collectives  49.8 us (32%)
  waiting for transfers between devices  15.5 us (10%)
  between operations  14 us (9%)
  matrix products  13.4 us (9%)
  Pallas kernels  7.09 us (5%)
  local copies, waits for them, and re-layouts  2.25 us (1%)
    all_to_all x1, blocking collectives, on_device(): lax.all_to_all(pieces, 'seq', split_axis=0, concat_axis=0, tiled=True, ax...  28 us
    all_to_all x1, blocking collectives, on_device(): lax.all_to_all(flat.reshape(16, 64, 256), ('seq', 'head'), split_axis=0,...  21.7 us
    ppermute x7, starting transfers between devices, on_device(): lax.ppermute(row_message, 'seq', y_later(k))  15.8 us
    all_to_all x1, waiting for transfers between devices, on_device(): lax.all_to_all(messages, 'seq', split_axis=0, concat_axis=0, tiled=True,...  9.69 us
    ppermute x2, starting transfers between devices, hop(): downs.append(lax.ppermute(after(downs[-1], *earlier), 'seq', y_shift(-1)))  8.62 us
    dot_general x8, matrix products, add(): d = jnp.dot(x, part.reshape(NZ * 48, 512), preferred_element_type=F32)  8.41 us
    pallas_call x6, Pallas kernels, call(): pl.pallas_call(kernel, out_shape=shapes, in_specs=smem + whole(len(args))...  7.09 us
    all_to_all x1, starting transfers between devices, on_device(): lax.all_to_all(messages, 'seq', split_axis=0, concat_axis=0, tiled=True,...  5.45 us
  transfers between devices with their start and end apart: 19, of which 4 were waited for; matrix products, arithmetic and copies ran while one was open for 10% of the time, Pallas kernels for 2%

profile of v10, /device:TPU:1, one launch (start us, length us, event | category | flops | bytes accessed | tf_op | source)
XLA Modules:
  0.0 153.2 jit_solution(6378989095009441505)
XLA Ops:
  6.5 0.7 all-gather.3.cloned.1.call-update
  7.3 0.0 all-gather.5.cloned.1.call-start
  7.3 0.9 copy-done
  8.3 28.0 %all_to_all.15 = bf16[8,48,768]{2,1,0:T(8,128)(2,1)S(1)} all-to-all(bf16[8,48,768]{2,1,0:T(8,128)(2,1)S(1)} %shard_map.46), channel_id=1, replica_groups={{0,8,16,24,32,40,48,56},{64,72,80,88,96,104,112,120},{128,136,144,152,1..., dimensions={0} | all-to-all | bytes 1179648 | tf_op jit(solution)/shard_map/all_to_all | solution.py:189
  36.3 3.2 %collective-permute-start = (bf16[8,48,512]{2,1,0:T(8,128)(2,1)S(1)}, bf16[8,48,512]{2,1,0:T(8,128)(2,1)S(1)}, u32[]{:S(2)}, u32[]{:S(2)}) collective-permute-start(bf16[8,48,512]{2,1,0:T(8,128)(2,1)S(1)} %slice.20), channel_id=1, source_target_pairs={{0,64},{8,72},{16,80},{24,88},{32,96},{40,104},{48,112},{56,120},{... | collective-permute-start | bytes 1179656 | tf_op jit(solution)/shard_map/ppermute | solution.py:204
  39.5 4.0 %collective-permute-start.5 = (bf16[8,48,512]{2,1,0:T(8,128)(2,1)S(1)}, bf16[8,48,512]{2,1,0:T(8,128)(2,1)S(1)}, u32[]{:S(2)}, u32[]{:S(2)}) collective-permute-start(bf16[8,48,512]{2,1,0:T(8,128)(2,1)S(1)} %slice.20), channel_id=1, source_target_pairs={{0,448},{8,456},{16,464},{24,472},{32,480},{40,488},{48,496},{56,5... | collective-permute-start | bytes 1179656 | tf_op jit(solution)/shard_map/ppermute | solution.py:205
  43.6 1.9 %collective-permute-start.2 = (f32[2,512]{1,0:T(2,128)S(1)}, f32[2,512]{1,0:T(2,128)S(1)}, u32[]{:S(2)}, u32[]{:S(2)}) collective-permute-start(f32[2,512]{1,0:T(2,128)S(1)} %get-tuple-element.24), channel_id=1, source_target_pairs={{0,8},{8,0},{16,24},{24,16},{32,40},{40,32},{48,56},{56,48},{64,72... | collective-permute-start | bytes 12296 | tf_op jit(solution)/shard_map/ppermute | solution.py:213
  45.5 1.2 collective-permute-done
  46.8 1.9 %collective-permute-start.1 = (bf16[8,48,512]{2,1,0:T(8,128)(2,1)S(1)}, bf16[8,48,512]{2,1,0:T(8,128)(2,1)S(1)}, u32[]{:S(2)}, u32[]{:S(2)}) collective-permute-start(bf16[8,48,512]{2,1,0:T(8,128)(2,1)S(1)} %collective-permute-done), channel_id=1, source_target_pairs={{0,64},{8,72},{16,80},{24,88},{32,96},{40,104},{48,112},{56,120},{... | collective-permute-start | bytes 1179656 | tf_op jit(solution)/shard_map/ppermute | solution.py:214
  48.7 4.6 %collective-permute-start.6 = (bf16[8,48,512]{2,1,0:T(8,128)(2,1)S(1)}, bf16[8,48,512]{2,1,0:T(8,128)(2,1)S(1)}, u32[]{:S(2)}, u32[]{:S(2)}) collective-permute-start(bf16[8,48,512]{2,1,0:T(8,128)(2,1)S(1)} %collective-permute-done.5), channel_id=1, source_target_pairs={{0,448},{8,456},{16,464},{24,472},{32,480},{40,488},{48,496},{56,5... | collective-permute-start | bytes 1179656 | tf_op jit(solution)/shard_map/ppermute | solution.py:215
  53.5 0.1 dynamic_slice.35
  53.6 0.7 slice.22
  54.3 0.6 reduce_window_sum.24
  54.9 0.2 slice_reduce_fusion
  55.1 0.2 reduce_window_sum.25
  55.3 0.1 squeeze.6
  55.3 0.1 copy.11
  55.4 0.1 reduce_window_sum.26
  55.5 1.0 collective-permute-done.1
  56.5 1.9 %collective-permute-start.3 = (bf16[8,48,512]{2,1,0:T(8,128)(2,1)S(1)}, bf16[8,48,512]{2,1,0:T(8,128)(2,1)S(1)}, u32[]{:S(2)}, u32[]{:S(2)}) collective-permute-start(bf16[8,48,512]{2,1,0:T(8,128)(2,1)S(1)} %collective-permute-done.1), channel_id=1, source_target_pairs={{0,64},{8,72},{16,80},{24,88},{32,96},{40,104},{48,112},{56,120},{... | collective-permute-start | bytes 1179656 | tf_op jit(solution)/shard_map/ppermute | solution.py:204
  58.4 4.6 %collective-permute-start.7 = (bf16[8,48,512]{2,1,0:T(8,128)(2,1)S(1)}, bf16[8,48,512]{2,1,0:T(8,128)(2,1)S(1)}, u32[]{:S(2)}, u32[]{:S(2)}) collective-permute-start(bf16[8,48,512]{2,1,0:T(8,128)(2,1)S(1)} %collective-permute-done.6), channel_id=1, source_target_pairs={{0,448},{8,456},{16,464},{24,472},{32,480},{40,488},{48,496},{56,5... | collective-permute-start | bytes 1179656 | tf_op jit(solution)/shard_map/ppermute | solution.py:205
  63.0 2.9 %all-gather.3.cloned.1.call-done = bf16[1024,3072]{1,0:T(8,128)(2,1)} async-done(((bf16[64,3072]{1,0:T(8,128)(2,1)}), bf16[1024,3072]{1,0:T(8,128)(2,1)}) %all-gather.3.cloned.1.call-update) | async-done | bytes 6291472 | tf_op jit(solution)/shard_map/all_gather | solution.py:191
  65.9 2.0 %fusion.12 = f32[1024,512]{1,0:T(8,128)S(1)} fusion(bf16[384,512]{1,0:T(8,128)(2,1)S(1)} %bitcast.36, bf16[1024,3072]{1,0:T(8,128)(2,1)} %all-gather.3.cloned.1.call-done, s32[]{:T(128)S(6)} %select_n.102), kind=kOutput, calls=%fused_computation.15 | convolution fusion | flops 402653184 | bytes 3276804 | tf_op jit(solution)/shard_map/dot_general | solution.py:196
  67.9 1.9 %convolution_add_fusion = f32[1024,512]{1,0:T(8,128)S(1)} fusion(f32[1024,512]{1,0:T(8,128)S(1)} %fusion.12, bf16[384,512]{1,0:T(8,128)(2,1)S(1)} %bitcast.43, bf16[1024,3072]{1,0:T(8,128)(2,1)} %all-gather.3.cloned.1.call-done, s32[]{:T(128)S(6)} %select_n.104), kind=kOutput, calls=%fused_computation.1 | convolution fusion | flops 403177472 | bytes 5373956 | tf_op jit(solution)/shard_map/dot_general | solution.py:196
  69.8 3.2 %collective-permute-start.4 = (bf16[4,48,512]{2,1,0:T(8,128)(2,1)S(1)}, bf16[4,48,512]{2,1,0:T(8,128)(2,1)S(1)}, u32[]{:S(2)}, u32[]{:S(2)}) collective-permute-start(bf16[4,48,512]{2,1,0:T(8,128)(2,1)S(1)} %slice.17), channel_id=1, source_target_pairs={{0,64},{8,72},{16,80},{24,88},{32,96},{40,104},{48,112},{56,120},{... | collective-permute-start | bytes 589832 | tf_op jit(solution)/shard_map/ppermute | solution.py:229
  73.1 3.8 %collective-permute-start.8 = (bf16[4,48,512]{2,1,0:T(8,128)(2,1)S(1)}, bf16[4,48,512]{2,1,0:T(8,128)(2,1)S(1)}, u32[]{:S(2)}, u32[]{:S(2)}) collective-permute-start(bf16[4,48,512]{2,1,0:T(8,128)(2,1)S(1)} %slice.18), channel_id=1, source_target_pairs={{0,448},{8,456},{16,464},{24,472},{32,480},{40,488},{48,496},{56,5... | collective-permute-start | bytes 589832 | tf_op jit(solution)/shard_map/ppermute | solution.py:230
  76.9 0.7 fusion.2
  77.6 0.7 fusion.4
  78.3 0.7 fusion.6
  79.0 0.7 fusion.9
  79.7 1.0 add_add_fusion.total_ref
  80.8 0.7 fusion.last_ref
  81.5 2.7 %shard_map.47 = (bf16[2,512,512]{2,1,0:T(8,128)(2,1)S(1)}, bf16[16,128,128]{2,1,0:T(8,128)(2,1)S(1)}, bf16[4,2,144,128]{3,2,1,0:T(8,128)(2,1)}) custom-call(f32[1024,512]{1,0:T(8,128)S(1)} %add_add_fusion.total_ref, f32[1024,512]{1,0:T(8,128)S(1)} %fusion.last_ref, f32[128,16]{1,0:T(8,128)S(1)} %bitcast.28, f32[16,128]{1,0:T(8,128)S(1)} %bitcast.32), custom_call_target="tpu_custom_call" | custom-call | flops 67108864 | bytes 4210688 | tf_op jit(solution)/shard_map/pallas_call | solution.py:171
  84.2 5.4 %all-to-all-start.1 = ((bf16[4,2,144,128]{3,2,1,0:T(8,128)(2,1)}), bf16[4,2,144,128]{3,2,1,0:T(8,128)(2,1)S(1)}, u32[]{:S(2)}, u32[]{:S(2)}) async-start(bf16[4,2,144,128]{3,2,1,0:T(8,128)(2,1)} %get-tuple-element.33), calls=%async_computation.1 | async-start | bytes 589824 | tf_op jit(solution)/shard_map/all_to_all | solution.py:240
  89.6 9.7 %all-to-all-done.1.messages_ref = bf16[4,2,144,128]{3,2,1,0:T(8,128)(2,1)S(1)} async-done(((bf16[4,2,144,128]{3,2,1,0:T(8,128)(2,1)}), bf16[4,2,144,128]{3,2,1,0:T(8,128)(2,1)S(1)}, u32[]{:S(2)}, u32[]{:S(2)}) %all-to-all-start.1) | async-done | bytes 294944 | tf_op jit(solution)/shard_map/all_to_all | solution.py:240
  99.3 0.1 shard_map.48
  99.4 2.0 %collective-permute-start.9 = (bf16[2,144,128]{2,1,0:T(8,128)(2,1)S(1)}, bf16[2,144,128]{2,1,0:T(8,128)(2,1)S(1)}, u32[]{:S(2)}, u32[]{:S(2)}) collective-permute-start(bf16[2,144,128]{2,1,0:T(8,128)(2,1)S(1)} %get-tuple-element.34), channel_id=1, source_target_pairs={{0,64},{8,72},{16,80},{24,88},{32,96},{40,104},{48,112},{56,120},{... | collective-permute-start | bytes 221192 | tf_op jit(solution)/shard_map/ppermute | solution.py:251
  101.5 2.2 %collective-permute-start.10 = (bf16[2,144,128]{2,1,0:T(8,128)(2,1)S(1)}, bf16[2,144,128]{2,1,0:T(8,128)(2,1)S(1)}, u32[]{:S(2)}, u32[]{:S(2)}) collective-permute-start(bf16[2,144,128]{2,1,0:T(8,128)(2,1)S(1)} %get-tuple-element.34), channel_id=1, source_target_pairs={{0,448},{8,456},{16,464},{24,472},{32,480},{40,488},{48,496},{56,5... | collective-permute-start | bytes 221192 | tf_op jit(solution)/shard_map/ppermute | solution.py:251
  103.7 4.0 %collective-permute-start.11 = (bf16[2,144,128]{2,1,0:T(8,128)(2,1)S(1)}, bf16[2,144,128]{2,1,0:T(8,128)(2,1)S(1)}, u32[]{:S(2)}, u32[]{:S(2)}) collective-permute-start(bf16[2,144,128]{2,1,0:T(8,128)(2,1)S(1)} %get-tuple-element.34), channel_id=1, source_target_pairs={{0,256},{8,264},{16,272},{24,280},{32,288},{40,296},{48,304},{56,3... | collective-permute-start | bytes 221192 | tf_op jit(solution)/shard_map/ppermute | solution.py:251
  107.7 2.2 %collective-permute-start.12 = (bf16[2,144,128]{2,1,0:T(8,128)(2,1)S(1)}, bf16[2,144,128]{2,1,0:T(8,128)(2,1)S(1)}, u32[]{:S(2)}, u32[]{:S(2)}) collective-permute-start(bf16[2,144,128]{2,1,0:T(8,128)(2,1)S(1)} %get-tuple-element.34), channel_id=1, source_target_pairs={{0,192},{8,200},{16,208},{24,216},{32,224},{40,232},{48,240},{56,2... | collective-permute-start | bytes 221192 | tf_op jit(solution)/shard_map/ppermute | solution.py:251
  109.9 1.3 collective-permute-start.13
  111.2 2.7 %collective-permute-start.14 = (bf16[2,144,128]{2,1,0:T(8,128)(2,1)S(1)}, bf16[2,144,128]{2,1,0:T(8,128)(2,1)S(1)}, u32[]{:S(2)}, u32[]{:S(2)}) collective-permute-start(bf16[2,144,128]{2,1,0:T(8,128)(2,1)S(1)} %get-tuple-element.34), channel_id=1, source_target_pairs={{0,128},{8,136},{16,144},{24,152},{32,160},{40,168},{48,176},{56,1... | collective-permute-start | bytes 221192 | tf_op jit(solution)/shard_map/ppermute | solution.py:251
  114.0 1.3 collective-permute-start.15
  115.3 5.0 %convolution_bitcast_fusion.total_ref = f32[1024,256]{1,0:T(8,128)S(1)} fusion(bf16[1024,3072]{1,0:T(8,128)(2,1)} %all-gather.3.cloned.1.call-done, bf16[3072,256]{1,0:T(8,128)(2,1)} %bitcast.44), kind=kOutput, calls=%fused_computation.2 | convolution fusion | flops 1610612736 | bytes 8912896 | tf_op jit(solution)/shard_map/dot_general | solution.py:241
  120.3 0.9 shard_map.49
  121.3 2.5 %shard_map.50 = bf16[1024,256]{1,0:T(8,128)(2,1)S(1)} custom-call(bf16[2,144,128]{2,1,0:T(8,128)(2,1)S(1)} %collective-permute-done.9.refs_0_, bf16[2,144,128]{2,1,0:T(8,128)(2,1)S(1)} %collective-permute-done.10.refs_1_, bf16[2,144,128]{2,1,0:T(8,128)(2,1)S(1)} %collective-permute-done.11.refs_2_, bf16[2,144,128]{2,1,0:T(8,128)(2,1)S(1)} %collective-permute-done.12.refs_3_, ...), custom_call_target="tpu_custom_call" | custom-call | flops 67108864 | bytes 2237504 | tf_op jit(solution)/shard_map/pallas_call | solution.py:171
  123.8 21.7 %all_to_all.16.sent_ref = bf16[16,64,256]{2,1,0:T(8,128)(2,1)S(1)} all-to-all(bf16[16,64,256]{2,1,0:T(8,128)(2,1)S(1)} %bitcast.27), channel_id=1, replica_groups={{0,1,2,3,4,5,6,7,8,9,10,11,12,13,14,15},{16,17,18,19,20,21,22,23,24,25,..., dimensions={0} | all-to-all | bytes 1048576 | tf_op jit(solution)/shard_map/all_to_all | solution.py:256
  145.6 0.8 shard_map.51
  (34 shorter events, 0.3 us)
Async XLA Ops:
  6.5 37.1 %copy-start.2 = (f32[4,512]{1,0:T(4,128)S(1)}, f32[4,512]{1,0:T(4,128)}, u32[]{:S(2)}) copy-start(f32[4,512]{1,0:T(4,128)} %param.6) | copy-start | bytes 24580
  6.5 46.9 %copy-start.3 = (f32[512]{0:T(512)S(1)}, f32[512]{0:T(512)}, u32[]{:S(2)}) copy-start(f32[512]{0:T(512)} %param.7) | copy-start | bytes 6148
  6.5 59.3 %all-gather.3.cloned.1.call-start = ((), (), s32[]{:S(2)}) async-start(), calls=%async_computation.3 | async-start | bytes 6684672 | tf_op jit(solution)/shard_map/all_gather | solution.py:191
  7.3 104.0 %all-gather.5.cloned.1.call-start = ((), (), s32[]{:S(2)}) async-start(), calls=%async_computation.4 | async-start | bytes 1769472 | tf_op jit(solution)/shard_map/all_gather | solution.py:226
  7.3 0.9 copy-start
  36.3 10.5 %collective-permute-start = (bf16[8,48,512]{2,1,0:T(8,128)(2,1)S(1)}, bf16[8,48,512]{2,1,0:T(8,128)(2,1)S(1)}, u32[]{:S(2)}, u32[]{:S(2)}) collective-permute-start(bf16[8,48,512]{2,1,0:T(8,128)(2,1)S(1)} %slice.20), channel_id=1, source_target_pairs={{0,64},{8,72},{16,80},{24,88},{32,96},{40,104},{48,112},{56,120},{... | collective-permute-start | bytes 1179656 | tf_op jit(solution)/shard_map/ppermute | solution.py:204
  39.5 9.2 %collective-permute-start.5 = (bf16[8,48,512]{2,1,0:T(8,128)(2,1)S(1)}, bf16[8,48,512]{2,1,0:T(8,128)(2,1)S(1)}, u32[]{:S(2)}, u32[]{:S(2)}) collective-permute-start(bf16[8,48,512]{2,1,0:T(8,128)(2,1)S(1)} %slice.20), channel_id=1, source_target_pairs={{0,448},{8,456},{16,464},{24,472},{32,480},{40,488},{48,496},{56,5... | collective-permute-start | bytes 1179656 | tf_op jit(solution)/shard_map/ppermute | solution.py:205
  43.6 5.1 %collective-permute-start.2 = (f32[2,512]{1,0:T(2,128)S(1)}, f32[2,512]{1,0:T(2,128)S(1)}, u32[]{:S(2)}, u32[]{:S(2)}) collective-permute-start(f32[2,512]{1,0:T(2,128)S(1)} %get-tuple-element.24), channel_id=1, source_target_pairs={{0,8},{8,0},{16,24},{24,16},{32,40},{40,32},{48,56},{56,48},{64,72... | collective-permute-start | bytes 12296 | tf_op jit(solution)/shard_map/ppermute | solution.py:213
  46.8 9.7 %collective-permute-start.1 = (bf16[8,48,512]{2,1,0:T(8,128)(2,1)S(1)}, bf16[8,48,512]{2,1,0:T(8,128)(2,1)S(1)}, u32[]{:S(2)}, u32[]{:S(2)}) collective-permute-start(bf16[8,48,512]{2,1,0:T(8,128)(2,1)S(1)} %collective-permute-done), channel_id=1, source_target_pairs={{0,64},{8,72},{16,80},{24,88},{32,96},{40,104},{48,112},{56,120},{... | collective-permute-start | bytes 1179656 | tf_op jit(solution)/shard_map/ppermute | solution.py:214
  48.7 9.7 %collective-permute-start.6 = (bf16[8,48,512]{2,1,0:T(8,128)(2,1)S(1)}, bf16[8,48,512]{2,1,0:T(8,128)(2,1)S(1)}, u32[]{:S(2)}, u32[]{:S(2)}) collective-permute-start(bf16[8,48,512]{2,1,0:T(8,128)(2,1)S(1)} %collective-permute-done.5), channel_id=1, source_target_pairs={{0,448},{8,456},{16,464},{24,472},{32,480},{40,488},{48,496},{56,5... | collective-permute-start | bytes 1179656 | tf_op jit(solution)/shard_map/ppermute | solution.py:215
  56.5 13.3 %collective-permute-start.3 = (bf16[8,48,512]{2,1,0:T(8,128)(2,1)S(1)}, bf16[8,48,512]{2,1,0:T(8,128)(2,1)S(1)}, u32[]{:S(2)}, u32[]{:S(2)}) collective-permute-start(bf16[8,48,512]{2,1,0:T(8,128)(2,1)S(1)} %collective-permute-done.1), channel_id=1, source_target_pairs={{0,64},{8,72},{16,80},{24,88},{32,96},{40,104},{48,112},{56,120},{... | collective-permute-start | bytes 1179656 | tf_op jit(solution)/shard_map/ppermute | solution.py:204
  58.4 14.6 %collective-permute-start.7 = (bf16[8,48,512]{2,1,0:T(8,128)(2,1)S(1)}, bf16[8,48,512]{2,1,0:T(8,128)(2,1)S(1)}, u32[]{:S(2)}, u32[]{:S(2)}) collective-permute-start(bf16[8,48,512]{2,1,0:T(8,128)(2,1)S(1)} %collective-permute-done.6), channel_id=1, source_target_pairs={{0,448},{8,456},{16,464},{24,472},{32,480},{40,488},{48,496},{56,5... | collective-permute-start | bytes 1179656 | tf_op jit(solution)/shard_map/ppermute | solution.py:205
  65.9 11.0 %copy-start.1 = (bf16[1024,3072]{1,0:T(8,128)(2,1)S(1)}, bf16[1024,3072]{1,0:T(8,128)(2,1)}, u32[]{:S(2)}) copy-start(bf16[1024,3072]{1,0:T(8,128)(2,1)} %all-gather.3.cloned.1.call-done) | copy-start | bytes 18874372
  69.8 10.9 %collective-permute-start.4 = (bf16[4,48,512]{2,1,0:T(8,128)(2,1)S(1)}, bf16[4,48,512]{2,1,0:T(8,128)(2,1)S(1)}, u32[]{:S(2)}, u32[]{:S(2)}) collective-permute-start(bf16[4,48,512]{2,1,0:T(8,128)(2,1)S(1)} %slice.17), channel_id=1, source_target_pairs={{0,64},{8,72},{16,80},{24,88},{32,96},{40,104},{48,112},{56,120},{... | collective-permute-start | bytes 589832 | tf_op jit(solution)/shard_map/ppermute | solution.py:229
  73.1 7.7 %collective-permute-start.8 = (bf16[4,48,512]{2,1,0:T(8,128)(2,1)S(1)}, bf16[4,48,512]{2,1,0:T(8,128)(2,1)S(1)}, u32[]{:S(2)}, u32[]{:S(2)}) collective-permute-start(bf16[4,48,512]{2,1,0:T(8,128)(2,1)S(1)} %slice.18), channel_id=1, source_target_pairs={{0,448},{8,456},{16,464},{24,472},{32,480},{40,488},{48,496},{56,5... | collective-permute-start | bytes 589832 | tf_op jit(solution)/shard_map/ppermute | solution.py:230
  84.2 15.1 %all-to-all-start.1 = ((bf16[4,2,144,128]{3,2,1,0:T(8,128)(2,1)}), bf16[4,2,144,128]{3,2,1,0:T(8,128)(2,1)S(1)}, u32[]{:S(2)}, u32[]{:S(2)}) async-start(bf16[4,2,144,128]{3,2,1,0:T(8,128)(2,1)} %get-tuple-element.33), calls=%async_computation.1 | async-start | bytes 589824 | tf_op jit(solution)/shard_map/all_to_all | solution.py:240
  99.4 11.8 %collective-permute-start.9 = (bf16[2,144,128]{2,1,0:T(8,128)(2,1)S(1)}, bf16[2,144,128]{2,1,0:T(8,128)(2,1)S(1)}, u32[]{:S(2)}, u32[]{:S(2)}) collective-permute-start(bf16[2,144,128]{2,1,0:T(8,128)(2,1)S(1)} %get-tuple-element.34), channel_id=1, source_target_pairs={{0,64},{8,72},{16,80},{24,88},{32,96},{40,104},{48,112},{56,120},{... | collective-permute-start | bytes 221192 | tf_op jit(solution)/shard_map/ppermute | solution.py:251
  101.5 12.5 %collective-permute-start.10 = (bf16[2,144,128]{2,1,0:T(8,128)(2,1)S(1)}, bf16[2,144,128]{2,1,0:T(8,128)(2,1)S(1)}, u32[]{:S(2)}, u32[]{:S(2)}) collective-permute-start(bf16[2,144,128]{2,1,0:T(8,128)(2,1)S(1)} %get-tuple-element.34), channel_id=1, source_target_pairs={{0,448},{8,456},{16,464},{24,472},{32,480},{40,488},{48,496},{56,5... | collective-permute-start | bytes 221192 | tf_op jit(solution)/shard_map/ppermute | solution.py:251
  103.7 17.5 %collective-permute-start.11 = (bf16[2,144,128]{2,1,0:T(8,128)(2,1)S(1)}, bf16[2,144,128]{2,1,0:T(8,128)(2,1)S(1)}, u32[]{:S(2)}, u32[]{:S(2)}) collective-permute-start(bf16[2,144,128]{2,1,0:T(8,128)(2,1)S(1)} %get-tuple-element.34), channel_id=1, source_target_pairs={{0,256},{8,264},{16,272},{24,280},{32,288},{40,296},{48,304},{56,3... | collective-permute-start | bytes 221192 | tf_op jit(solution)/shard_map/ppermute | solution.py:251
  107.7 13.5 %collective-permute-start.12 = (bf16[2,144,128]{2,1,0:T(8,128)(2,1)S(1)}, bf16[2,144,128]{2,1,0:T(8,128)(2,1)S(1)}, u32[]{:S(2)}, u32[]{:S(2)}) collective-permute-start(bf16[2,144,128]{2,1,0:T(8,128)(2,1)S(1)} %get-tuple-element.34), channel_id=1, source_target_pairs={{0,192},{8,200},{16,208},{24,216},{32,224},{40,232},{48,240},{56,2... | collective-permute-start | bytes 221192 | tf_op jit(solution)/shard_map/ppermute | solution.py:251
  109.9 11.3 %collective-permute-start.13 = (bf16[2,144,128]{2,1,0:T(8,128)(2,1)S(1)}, bf16[2,144,128]{2,1,0:T(8,128)(2,1)S(1)}, u32[]{:S(2)}, u32[]{:S(2)}) collective-permute-start(bf16[2,144,128]{2,1,0:T(8,128)(2,1)S(1)} %get-tuple-element.34), channel_id=1, source_target_pairs={{0,320},{8,328},{16,336},{24,344},{32,352},{40,360},{48,368},{56,3... | collective-permute-start | bytes 221192 | tf_op jit(solution)/shard_map/ppermute | solution.py:251
  111.2 10.0 %collective-permute-start.14 = (bf16[2,144,128]{2,1,0:T(8,128)(2,1)S(1)}, bf16[2,144,128]{2,1,0:T(8,128)(2,1)S(1)}, u32[]{:S(2)}, u32[]{:S(2)}) collective-permute-start(bf16[2,144,128]{2,1,0:T(8,128)(2,1)S(1)} %get-tuple-element.34), channel_id=1, source_target_pairs={{0,128},{8,136},{16,144},{24,152},{32,160},{40,168},{48,176},{56,1... | collective-permute-start | bytes 221192 | tf_op jit(solution)/shard_map/ppermute | solution.py:251
  114.0 7.3 %collective-permute-start.15 = (bf16[2,144,128]{2,1,0:T(8,128)(2,1)S(1)}, bf16[2,144,128]{2,1,0:T(8,128)(2,1)S(1)}, u32[]{:S(2)}, u32[]{:S(2)}) collective-permute-start(bf16[2,144,128]{2,1,0:T(8,128)(2,1)S(1)} %get-tuple-element.34), channel_id=1, source_target_pairs={{0,384},{8,392},{16,400},{24,408},{32,416},{40,424},{48,432},{56,4... | collective-permute-start | bytes 221192 | tf_op jit(solution)/shard_map/ppermute | solution.py:251
Sparse Core Ops, SparseCore 0:
  9.5 56.3 all-gather.2
  67.9 39.8 all-gather.4

commit v11 on v10

--- a/solution.py
+++ b/solution.py
@@ -14,7 +14,7 @@
 NZ = 8
 NH = 8
 EXTRA = 16
-START_ORDER = (1, 7, 4, 3, 5, 2, 6)
+START_ORDER = (1, 2, 4, 5, 3, 6, 7)
 F32 = jnp.float32
 BF16 = jnp.bfloat16
 VMEM = pltpu.VMEM

time: 154 us -> 154 us (level)
  no operation moved by 1% of the time
where the time goes in v11:
time: 154 us
  starting transfers between devices  50.7 us (33%)
  blocking collectives  50 us (32%)
  waiting for transfers between devices  15.5 us (10%)
  between operations  14 us (9%)
  matrix products  13.4 us (9%)
  Pallas kernels  7.08 us (5%)
  local copies, waits for them, and re-layouts  2.25 us (1%)
    all_to_all x1, blocking collectives, on_device(): lax.all_to_all(pieces, 'seq', split_axis=0, concat_axis=0, tiled=True, ax...  28 us
    all_to_all x1, blocking collectives, on_device(): lax.all_to_all(flat.reshape(16, 64, 256), ('seq', 'head'), split_axis=0,...  22 us
    ppermute x7, starting transfers between devices, on_device(): lax.ppermute(row_message, 'seq', y_later(k))  16.1 us
    all_to_all x1, waiting for transfers between devices, on_device(): lax.all_to_all(messages, 'seq', split_axis=0, concat_axis=0, tiled=True,...  9.69 us
    ppermute x2, starting transfers between devices, hop(): downs.append(lax.ppermute(after(downs[-1], *earlier), 'seq', y_shift(-1)))  8.62 us
    dot_general x8, matrix products, add(): d = jnp.dot(x, part.reshape(NZ * 48, 512), preferred_element_type=F32)  8.41 us
    pallas_call x6, Pallas kernels, call(): pl.pallas_call(kernel, out_shape=shapes, in_specs=smem + whole(len(args))...  7.08 us
    all_to_all x1, starting transfers between devices, on_device(): lax.all_to_all(messages, 'seq', split_axis=0, concat_axis=0, tiled=True,...  5.45 us
  transfers between devices with their start and end apart: 19, of which 4 were waited for; matrix products, arithmetic and copies ran while one was open for 10% of the time, Pallas kernels for 2%

profile of v11, /device:TPU:1, one launch (start us, length us, event | category | flops | bytes accessed | tf_op | source)
XLA Modules:
  0.0 153.9 jit_solution(14341647754898564003)
XLA Ops:
  6.5 0.7 all-gather.3.cloned.1.call-update
  7.3 0.0 all-gather.5.cloned.1.call-start
  7.3 0.9 copy-done
  8.3 28.0 %all_to_all.15 = bf16[8,48,768]{2,1,0:T(8,128)(2,1)S(1)} all-to-all(bf16[8,48,768]{2,1,0:T(8,128)(2,1)S(1)} %shard_map.46), channel_id=1, replica_groups={{0,8,16,24,32,40,48,56},{64,72,80,88,96,104,112,120},{128,136,144,152,1..., dimensions={0} | all-to-all | bytes 1179648 | tf_op jit(solution)/shard_map/all_to_all | solution.py:189
  36.3 3.2 %collective-permute-start = (bf16[8,48,512]{2,1,0:T(8,128)(2,1)S(1)}, bf16[8,48,512]{2,1,0:T(8,128)(2,1)S(1)}, u32[]{:S(2)}, u32[]{:S(2)}) collective-permute-start(bf16[8,48,512]{2,1,0:T(8,128)(2,1)S(1)} %slice.20), channel_id=1, source_target_pairs={{0,64},{8,72},{16,80},{24,88},{32,96},{40,104},{48,112},{56,120},{... | collective-permute-start | bytes 1179656 | tf_op jit(solution)/shard_map/ppermute | solution.py:204
  39.5 4.0 %collective-permute-start.5 = (bf16[8,48,512]{2,1,0:T(8,128)(2,1)S(1)}, bf16[8,48,512]{2,1,0:T(8,128)(2,1)S(1)}, u32[]{:S(2)}, u32[]{:S(2)}) collective-permute-start(bf16[8,48,512]{2,1,0:T(8,128)(2,1)S(1)} %slice.20), channel_id=1, source_target_pairs={{0,448},{8,456},{16,464},{24,472},{32,480},{40,488},{48,496},{56,5... | collective-permute-start | bytes 1179656 | tf_op jit(solution)/shard_map/ppermute | solution.py:205
  43.6 1.9 %collective-permute-start.2 = (f32[2,512]{1,0:T(2,128)S(1)}, f32[2,512]{1,0:T(2,128)S(1)}, u32[]{:S(2)}, u32[]{:S(2)}) collective-permute-start(f32[2,512]{1,0:T(2,128)S(1)} %get-tuple-element.24), channel_id=1, source_target_pairs={{0,8},{8,0},{16,24},{24,16},{32,40},{40,32},{48,56},{56,48},{64,72... | collective-permute-start | bytes 12296 | tf_op jit(solution)/shard_map/ppermute | solution.py:213
  45.5 1.2 collective-permute-done
  46.8 1.9 %collective-permute-start.1 = (bf16[8,48,512]{2,1,0:T(8,128)(2,1)S(1)}, bf16[8,48,512]{2,1,0:T(8,128)(2,1)S(1)}, u32[]{:S(2)}, u32[]{:S(2)}) collective-permute-start(bf16[8,48,512]{2,1,0:T(8,128)(2,1)S(1)} %collective-permute-done), channel_id=1, source_target_pairs={{0,64},{8,72},{16,80},{24,88},{32,96},{40,104},{48,112},{56,120},{... | collective-permute-start | bytes 1179656 | tf_op jit(solution)/shard_map/ppermute | solution.py:214
  48.7 4.6 %collective-permute-start.6 = (bf16[8,48,512]{2,1,0:T(8,128)(2,1)S(1)}, bf16[8,48,512]{2,1,0:T(8,128)(2,1)S(1)}, u32[]{:S(2)}, u32[]{:S(2)}) collective-permute-start(bf16[8,48,512]{2,1,0:T(8,128)(2,1)S(1)} %collective-permute-done.5), channel_id=1, source_target_pairs={{0,448},{8,456},{16,464},{24,472},{32,480},{40,488},{48,496},{56,5... | collective-permute-start | bytes 1179656 | tf_op jit(solution)/shard_map/ppermute | solution.py:215
  53.5 0.1 dynamic_slice.35
  53.6 0.7 slice.22
  54.3 0.6 reduce_window_sum.24
  54.9 0.2 slice_reduce_fusion
  55.1 0.2 reduce_window_sum.25
  55.3 0.1 squeeze.6
  55.3 0.1 copy.11
  55.4 0.1 reduce_window_sum.26
  55.5 1.0 collective-permute-done.1
  56.5 1.9 %collective-permute-start.3 = (bf16[8,48,512]{2,1,0:T(8,128)(2,1)S(1)}, bf16[8,48,512]{2,1,0:T(8,128)(2,1)S(1)}, u32[]{:S(2)}, u32[]{:S(2)}) collective-permute-start(bf16[8,48,512]{2,1,0:T(8,128)(2,1)S(1)} %collective-permute-done.1), channel_id=1, source_target_pairs={{0,64},{8,72},{16,80},{24,88},{32,96},{40,104},{48,112},{56,120},{... | collective-permute-start | bytes 1179656 | tf_op jit(solution)/shard_map/ppermute | solution.py:204
  58.4 4.6 %collective-permute-start.7 = (bf16[8,48,512]{2,1,0:T(8,128)(2,1)S(1)}, bf16[8,48,512]{2,1,0:T(8,128)(2,1)S(1)}, u32[]{:S(2)}, u32[]{:S(2)}) collective-permute-start(bf16[8,48,512]{2,1,0:T(8,128)(2,1)S(1)} %collective-permute-done.6), channel_id=1, source_target_pairs={{0,448},{8,456},{16,464},{24,472},{32,480},{40,488},{48,496},{56,5... | collective-permute-start | bytes 1179656 | tf_op jit(solution)/shard_map/ppermute | solution.py:205
  63.0 2.9 %all-gather.3.cloned.1.call-done = bf16[1024,3072]{1,0:T(8,128)(2,1)} async-done(((bf16[64,3072]{1,0:T(8,128)(2,1)}), bf16[1024,3072]{1,0:T(8,128)(2,1)}) %all-gather.3.cloned.1.call-update) | async-done | bytes 6291472 | tf_op jit(solution)/shard_map/all_gather | solution.py:191
  65.9 2.0 %fusion.12 = f32[1024,512]{1,0:T(8,128)S(1)} fusion(bf16[384,512]{1,0:T(8,128)(2,1)S(1)} %bitcast.36, bf16[1024,3072]{1,0:T(8,128)(2,1)} %all-gather.3.cloned.1.call-done, s32[]{:T(128)S(6)} %select_n.102), kind=kOutput, calls=%fused_computation.15 | convolution fusion | flops 402653184 | bytes 3276804 | tf_op jit(solution)/shard_map/dot_general | solution.py:196
  67.9 1.9 %convolution_add_fusion = f32[1024,512]{1,0:T(8,128)S(1)} fusion(f32[1024,512]{1,0:T(8,128)S(1)} %fusion.12, bf16[384,512]{1,0:T(8,128)(2,1)S(1)} %bitcast.43, bf16[1024,3072]{1,0:T(8,128)(2,1)} %all-gather.3.cloned.1.call-done, s32[]{:T(128)S(6)} %select_n.104), kind=kOutput, calls=%fused_computation.1 | convolution fusion | flops 403177472 | bytes 5373956 | tf_op jit(solution)/shard_map/dot_general | solution.py:196
  69.8 3.2 %collective-permute-start.4 = (bf16[4,48,512]{2,1,0:T(8,128)(2,1)S(1)}, bf16[4,48,512]{2,1,0:T(8,128)(2,1)S(1)}, u32[]{:S(2)}, u32[]{:S(2)}) collective-permute-start(bf16[4,48,512]{2,1,0:T(8,128)(2,1)S(1)} %slice.17), channel_id=1, source_target_pairs={{0,64},{8,72},{16,80},{24,88},{32,96},{40,104},{48,112},{56,120},{... | collective-permute-start | bytes 589832 | tf_op jit(solution)/shard_map/ppermute | solution.py:229
  73.1 3.8 %collective-permute-start.8 = (bf16[4,48,512]{2,1,0:T(8,128)(2,1)S(1)}, bf16[4,48,512]{2,1,0:T(8,128)(2,1)S(1)}, u32[]{:S(2)}, u32[]{:S(2)}) collective-permute-start(bf16[4,48,512]{2,1,0:T(8,128)(2,1)S(1)} %slice.18), channel_id=1, source_target_pairs={{0,448},{8,456},{16,464},{24,472},{32,480},{40,488},{48,496},{56,5... | collective-permute-start | bytes 589832 | tf_op jit(solution)/shard_map/ppermute | solution.py:230
  76.9 0.7 fusion.2
  77.6 0.7 fusion.4
  78.3 0.7 fusion.6
  79.0 0.7 fusion.9
  79.7 1.0 add_add_fusion.total_ref
  80.8 0.7 fusion.last_ref
  81.5 2.7 %shard_map.47 = (bf16[2,512,512]{2,1,0:T(8,128)(2,1)S(1)}, bf16[16,128,128]{2,1,0:T(8,128)(2,1)S(1)}, bf16[4,2,144,128]{3,2,1,0:T(8,128)(2,1)}) custom-call(f32[1024,512]{1,0:T(8,128)S(1)} %add_add_fusion.total_ref, f32[1024,512]{1,0:T(8,128)S(1)} %fusion.last_ref, f32[128,16]{1,0:T(8,128)S(1)} %bitcast.28, f32[16,128]{1,0:T(8,128)S(1)} %bitcast.32), custom_call_target="tpu_custom_call" | custom-call | flops 67108864 | bytes 4210688 | tf_op jit(solution)/shard_map/pallas_call | solution.py:171
  84.2 5.4 %all-to-all-start.1 = ((bf16[4,2,144,128]{3,2,1,0:T(8,128)(2,1)}), bf16[4,2,144,128]{3,2,1,0:T(8,128)(2,1)S(1)}, u32[]{:S(2)}, u32[]{:S(2)}) async-start(bf16[4,2,144,128]{3,2,1,0:T(8,128)(2,1)} %get-tuple-element.33), calls=%async_computation.1 | async-start | bytes 589824 | tf_op jit(solution)/shard_map/all_to_all | solution.py:240
  89.6 9.7 %all-to-all-done.1.messages_ref = bf16[4,2,144,128]{3,2,1,0:T(8,128)(2,1)S(1)} async-done(((bf16[4,2,144,128]{3,2,1,0:T(8,128)(2,1)}), bf16[4,2,144,128]{3,2,1,0:T(8,128)(2,1)S(1)}, u32[]{:S(2)}, u32[]{:S(2)}) %all-to-all-start.1) | async-done | bytes 294944 | tf_op jit(solution)/shard_map/all_to_all | solution.py:240
  99.3 0.1 shard_map.48
  99.4 2.0 %collective-permute-start.9 = (bf16[2,144,128]{2,1,0:T(8,128)(2,1)S(1)}, bf16[2,144,128]{2,1,0:T(8,128)(2,1)S(1)}, u32[]{:S(2)}, u32[]{:S(2)}) collective-permute-start(bf16[2,144,128]{2,1,0:T(8,128)(2,1)S(1)} %get-tuple-element.34), channel_id=1, source_target_pairs={{0,64},{8,72},{16,80},{24,88},{32,96},{40,104},{48,112},{56,120},{... | collective-permute-start | bytes 221192 | tf_op jit(solution)/shard_map/ppermute | solution.py:251
  101.5 5.8 %collective-permute-start.10 = (bf16[2,144,128]{2,1,0:T(8,128)(2,1)S(1)}, bf16[2,144,128]{2,1,0:T(8,128)(2,1)S(1)}, u32[]{:S(2)}, u32[]{:S(2)}) collective-permute-start(bf16[2,144,128]{2,1,0:T(8,128)(2,1)S(1)} %get-tuple-element.34), channel_id=1, source_target_pairs={{0,128},{8,136},{16,144},{24,152},{32,160},{40,168},{48,176},{56,1... | collective-permute-start | bytes 221192 | tf_op jit(solution)/shard_map/ppermute | solution.py:251
  107.2 3.2 %collective-permute-start.11 = (bf16[2,144,128]{2,1,0:T(8,128)(2,1)S(1)}, bf16[2,144,128]{2,1,0:T(8,128)(2,1)S(1)}, u32[]{:S(2)}, u32[]{:S(2)}) collective-permute-start(bf16[2,144,128]{2,1,0:T(8,128)(2,1)S(1)} %get-tuple-element.34), channel_id=1, source_target_pairs={{0,256},{8,264},{16,272},{24,280},{32,288},{40,296},{48,304},{56,3... | collective-permute-start | bytes 221192 | tf_op jit(solution)/shard_map/ppermute | solution.py:251
  110.4 1.3 collective-permute-start.12
  111.7 1.3 collective-permute-start.13
  113.0 1.3 collective-permute-start.14
  114.4 1.3 collective-permute-start.15
  115.7 5.0 %convolution_bitcast_fusion.total_ref = f32[1024,256]{1,0:T(8,128)S(1)} fusion(bf16[1024,3072]{1,0:T(8,128)(2,1)} %all-gather.3.cloned.1.call-done, bf16[3072,256]{1,0:T(8,128)(2,1)} %bitcast.44), kind=kOutput, calls=%fused_computation.2 | convolution fusion | flops 1610612736 | bytes 8912896 | tf_op jit(solution)/shard_map/dot_general | solution.py:241
  120.7 0.9 shard_map.49
  121.6 2.5 %shard_map.50 = bf16[1024,256]{1,0:T(8,128)(2,1)S(1)} custom-call(bf16[2,144,128]{2,1,0:T(8,128)(2,1)S(1)} %collective-permute-done.9.refs_0_, bf16[2,144,128]{2,1,0:T(8,128)(2,1)S(1)} %collective-permute-done.10.refs_1_, bf16[2,144,128]{2,1,0:T(8,128)(2,1)S(1)} %collective-permute-done.11.refs_2_, bf16[2,144,128]{2,1,0:T(8,128)(2,1)S(1)} %collective-permute-done.12.refs_3_, ...), custom_call_target="tpu_custom_call" | custom-call | flops 67108864 | bytes 2237504 | tf_op jit(solution)/shard_map/pallas_call | solution.py:171
  124.2 22.0 %all_to_all.16.sent_ref = bf16[16,64,256]{2,1,0:T(8,128)(2,1)S(1)} all-to-all(bf16[16,64,256]{2,1,0:T(8,128)(2,1)S(1)} %bitcast.27), channel_id=1, replica_groups={{0,1,2,3,4,5,6,7,8,9,10,11,12,13,14,15},{16,17,18,19,20,21,22,23,24,25,..., dimensions={0} | all-to-all | bytes 1048576 | tf_op jit(solution)/shard_map/all_to_all | solution.py:256
  146.2 0.8 shard_map.51
  (34 shorter events, 0.3 us)
Async XLA Ops:
  6.5 37.1 %copy-start.2 = (f32[4,512]{1,0:T(4,128)S(1)}, f32[4,512]{1,0:T(4,128)}, u32[]{:S(2)}) copy-start(f32[4,512]{1,0:T(4,128)} %param.6) | copy-start | bytes 24580
  6.5 46.9 %copy-start.3 = (f32[512]{0:T(512)S(1)}, f32[512]{0:T(512)}, u32[]{:S(2)}) copy-start(f32[512]{0:T(512)} %param.7) | copy-start | bytes 6148
  6.5 59.3 %all-gather.3.cloned.1.call-start = ((), (), s32[]{:S(2)}) async-start(), calls=%async_computation.3 | async-start | bytes 6684672 | tf_op jit(solution)/shard_map/all_gather | solution.py:191
  7.3 105.8 %all-gather.5.cloned.1.call-start = ((), (), s32[]{:S(2)}) async-start(), calls=%async_computation.4 | async-start | bytes 1769472 | tf_op jit(solution)/shard_map/all_gather | solution.py:226
  7.3 0.9 copy-start
  36.3 10.5 %collective-permute-start = (bf16[8,48,512]{2,1,0:T(8,128)(2,1)S(1)}, bf16[8,48,512]{2,1,0:T(8,128)(2,1)S(1)}, u32[]{:S(2)}, u32[]{:S(2)}) collective-permute-start(bf16[8,48,512]{2,1,0:T(8,128)(2,1)S(1)} %slice.20), channel_id=1, source_target_pairs={{0,64},{8,72},{16,80},{24,88},{32,96},{40,104},{48,112},{56,120},{... | collective-permute-start | bytes 1179656 | tf_op jit(solution)/shard_map/ppermute | solution.py:204
  39.5 9.2 %collective-permute-start.5 = (bf16[8,48,512]{2,1,0:T(8,128)(2,1)S(1)}, bf16[8,48,512]{2,1,0:T(8,128)(2,1)S(1)}, u32[]{:S(2)}, u32[]{:S(2)}) collective-permute-start(bf16[8,48,512]{2,1,0:T(8,128)(2,1)S(1)} %slice.20), channel_id=1, source_target_pairs={{0,448},{8,456},{16,464},{24,472},{32,480},{40,488},{48,496},{56,5... | collective-permute-start | bytes 1179656 | tf_op jit(solution)/shard_map/ppermute | solution.py:205
  43.6 5.1 %collective-permute-start.2 = (f32[2,512]{1,0:T(2,128)S(1)}, f32[2,512]{1,0:T(2,128)S(1)}, u32[]{:S(2)}, u32[]{:S(2)}) collective-permute-start(f32[2,512]{1,0:T(2,128)S(1)} %get-tuple-element.24), channel_id=1, source_target_pairs={{0,8},{8,0},{16,24},{24,16},{32,40},{40,32},{48,56},{56,48},{64,72... | collective-permute-start | bytes 12296 | tf_op jit(solution)/shard_map/ppermute | solution.py:213
  46.8 9.7 %collective-permute-start.1 = (bf16[8,48,512]{2,1,0:T(8,128)(2,1)S(1)}, bf16[8,48,512]{2,1,0:T(8,128)(2,1)S(1)}, u32[]{:S(2)}, u32[]{:S(2)}) collective-permute-start(bf16[8,48,512]{2,1,0:T(8,128)(2,1)S(1)} %collective-permute-done), channel_id=1, source_target_pairs={{0,64},{8,72},{16,80},{24,88},{32,96},{40,104},{48,112},{56,120},{... | collective-permute-start | bytes 1179656 | tf_op jit(solution)/shard_map/ppermute | solution.py:214
  48.7 9.7 %collective-permute-start.6 = (bf16[8,48,512]{2,1,0:T(8,128)(2,1)S(1)}, bf16[8,48,512]{2,1,0:T(8,128)(2,1)S(1)}, u32[]{:S(2)}, u32[]{:S(2)}) collective-permute-start(bf16[8,48,512]{2,1,0:T(8,128)(2,1)S(1)} %collective-permute-done.5), channel_id=1, source_target_pairs={{0,448},{8,456},{16,464},{24,472},{32,480},{40,488},{48,496},{56,5... | collective-permute-start | bytes 1179656 | tf_op jit(solution)/shard_map/ppermute | solution.py:215
  56.5 13.3 %collective-permute-start.3 = (bf16[8,48,512]{2,1,0:T(8,128)(2,1)S(1)}, bf16[8,48,512]{2,1,0:T(8,128)(2,1)S(1)}, u32[]{:S(2)}, u32[]{:S(2)}) collective-permute-start(bf16[8,48,512]{2,1,0:T(8,128)(2,1)S(1)} %collective-permute-done.1), channel_id=1, source_target_pairs={{0,64},{8,72},{16,80},{24,88},{32,96},{40,104},{48,112},{56,120},{... | collective-permute-start | bytes 1179656 | tf_op jit(solution)/shard_map/ppermute | solution.py:204
  58.4 14.6 %collective-permute-start.7 = (bf16[8,48,512]{2,1,0:T(8,128)(2,1)S(1)}, bf16[8,48,512]{2,1,0:T(8,128)(2,1)S(1)}, u32[]{:S(2)}, u32[]{:S(2)}) collective-permute-start(bf16[8,48,512]{2,1,0:T(8,128)(2,1)S(1)} %collective-permute-done.6), channel_id=1, source_target_pairs={{0,448},{8,456},{16,464},{24,472},{32,480},{40,488},{48,496},{56,5... | collective-permute-start | bytes 1179656 | tf_op jit(solution)/shard_map/ppermute | solution.py:205
  65.9 11.0 %copy-start.1 = (bf16[1024,3072]{1,0:T(8,128)(2,1)S(1)}, bf16[1024,3072]{1,0:T(8,128)(2,1)}, u32[]{:S(2)}) copy-start(bf16[1024,3072]{1,0:T(8,128)(2,1)} %all-gather.3.cloned.1.call-done) | copy-start | bytes 18874372
  69.8 10.9 %collective-permute-start.4 = (bf16[4,48,512]{2,1,0:T(8,128)(2,1)S(1)}, bf16[4,48,512]{2,1,0:T(8,128)(2,1)S(1)}, u32[]{:S(2)}, u32[]{:S(2)}) collective-permute-start(bf16[4,48,512]{2,1,0:T(8,128)(2,1)S(1)} %slice.17), channel_id=1, source_target_pairs={{0,64},{8,72},{16,80},{24,88},{32,96},{40,104},{48,112},{56,120},{... | collective-permute-start | bytes 589832 | tf_op jit(solution)/shard_map/ppermute | solution.py:229
  73.1 7.7 %collective-permute-start.8 = (bf16[4,48,512]{2,1,0:T(8,128)(2,1)S(1)}, bf16[4,48,512]{2,1,0:T(8,128)(2,1)S(1)}, u32[]{:S(2)}, u32[]{:S(2)}) collective-permute-start(bf16[4,48,512]{2,1,0:T(8,128)(2,1)S(1)} %slice.18), channel_id=1, source_target_pairs={{0,448},{8,456},{16,464},{24,472},{32,480},{40,488},{48,496},{56,5... | collective-permute-start | bytes 589832 | tf_op jit(solution)/shard_map/ppermute | solution.py:230
  84.2 15.1 %all-to-all-start.1 = ((bf16[4,2,144,128]{3,2,1,0:T(8,128)(2,1)}), bf16[4,2,144,128]{3,2,1,0:T(8,128)(2,1)S(1)}, u32[]{:S(2)}, u32[]{:S(2)}) async-start(bf16[4,2,144,128]{3,2,1,0:T(8,128)(2,1)} %get-tuple-element.33), calls=%async_computation.1 | async-start | bytes 589824 | tf_op jit(solution)/shard_map/all_to_all | solution.py:240
  99.4 13.6 %collective-permute-start.9 = (bf16[2,144,128]{2,1,0:T(8,128)(2,1)S(1)}, bf16[2,144,128]{2,1,0:T(8,128)(2,1)S(1)}, u32[]{:S(2)}, u32[]{:S(2)}) collective-permute-start(bf16[2,144,128]{2,1,0:T(8,128)(2,1)S(1)} %get-tuple-element.34), channel_id=1, source_target_pairs={{0,64},{8,72},{16,80},{24,88},{32,96},{40,104},{48,112},{56,120},{... | collective-permute-start | bytes 221192 | tf_op jit(solution)/shard_map/ppermute | solution.py:251
  101.5 12.9 %collective-permute-start.10 = (bf16[2,144,128]{2,1,0:T(8,128)(2,1)S(1)}, bf16[2,144,128]{2,1,0:T(8,128)(2,1)S(1)}, u32[]{:S(2)}, u32[]{:S(2)}) collective-permute-start(bf16[2,144,128]{2,1,0:T(8,128)(2,1)S(1)} %get-tuple-element.34), channel_id=1, source_target_pairs={{0,128},{8,136},{16,144},{24,152},{32,160},{40,168},{48,176},{56,1... | collective-permute-start | bytes 221192 | tf_op jit(solution)/shard_map/ppermute | solution.py:251
  107.2 14.3 %collective-permute-start.11 = (bf16[2,144,128]{2,1,0:T(8,128)(2,1)S(1)}, bf16[2,144,128]{2,1,0:T(8,128)(2,1)S(1)}, u32[]{:S(2)}, u32[]{:S(2)}) collective-permute-start(bf16[2,144,128]{2,1,0:T(8,128)(2,1)S(1)} %get-tuple-element.34), channel_id=1, source_target_pairs={{0,256},{8,264},{16,272},{24,280},{32,288},{40,296},{48,304},{56,3... | collective-permute-start | bytes 221192 | tf_op jit(solution)/shard_map/ppermute | solution.py:251
  110.4 11.2 %collective-permute-start.12 = (bf16[2,144,128]{2,1,0:T(8,128)(2,1)S(1)}, bf16[2,144,128]{2,1,0:T(8,128)(2,1)S(1)}, u32[]{:S(2)}, u32[]{:S(2)}) collective-permute-start(bf16[2,144,128]{2,1,0:T(8,128)(2,1)S(1)} %get-tuple-element.34), channel_id=1, source_target_pairs={{0,320},{8,328},{16,336},{24,344},{32,352},{40,360},{48,368},{56,3... | collective-permute-start | bytes 221192 | tf_op jit(solution)/shard_map/ppermute | solution.py:251
  111.7 9.9 %collective-permute-start.13 = (bf16[2,144,128]{2,1,0:T(8,128)(2,1)S(1)}, bf16[2,144,128]{2,1,0:T(8,128)(2,1)S(1)}, u32[]{:S(2)}, u32[]{:S(2)}) collective-permute-start(bf16[2,144,128]{2,1,0:T(8,128)(2,1)S(1)} %get-tuple-element.34), channel_id=1, source_target_pairs={{0,192},{8,200},{16,208},{24,216},{32,224},{40,232},{48,240},{56,2... | collective-permute-start | bytes 221192 | tf_op jit(solution)/shard_map/ppermute | solution.py:251
  113.0 8.6 %collective-permute-start.14 = (bf16[2,144,128]{2,1,0:T(8,128)(2,1)S(1)}, bf16[2,144,128]{2,1,0:T(8,128)(2,1)S(1)}, u32[]{:S(2)}, u32[]{:S(2)}) collective-permute-start(bf16[2,144,128]{2,1,0:T(8,128)(2,1)S(1)} %get-tuple-element.34), channel_id=1, source_target_pairs={{0,384},{8,392},{16,400},{24,408},{32,416},{40,424},{48,432},{56,4... | collective-permute-start | bytes 221192 | tf_op jit(solution)/shard_map/ppermute | solution.py:251
  114.4 7.3 %collective-permute-start.15 = (bf16[2,144,128]{2,1,0:T(8,128)(2,1)S(1)}, bf16[2,144,128]{2,1,0:T(8,128)(2,1)S(1)}, u32[]{:S(2)}, u32[]{:S(2)}) collective-permute-start(bf16[2,144,128]{2,1,0:T(8,128)(2,1)S(1)} %get-tuple-element.34), channel_id=1, source_target_pairs={{0,448},{8,456},{16,464},{24,472},{32,480},{40,488},{48,496},{56,5... | collective-permute-start | bytes 221192 | tf_op jit(solution)/shard_map/ppermute | solution.py:251
Sparse Core Ops, SparseCore 0:
  9.5 56.3 all-gather.2
  67.9 39.8 all-gather.4

commit v12 on v11

--- a/solution.py
+++ b/solution.py
@@ -160,7 +160,7 @@
             scaled = (queries.astype(F32) * scale).astype(BF16)
             output = part_ref[at] + mm(scaled, incoming)
             meansq = jnp.mean(output * output, axis=1, keepdims=True)
-            gained = output / jnp.sqrt(meansq + EPS) * gain
+            gained = output * (1.0 / jnp.sqrt(meansq + EPS)) * gain
             out_ref[n * BLK : (n + 1) * BLK, head * E : (head + 1) * E] = gained.astype(BF16)
 
 

time: 154 us -> 154 us (level)
  no operation moved by 1% of the time
where the time goes in v12:
time: 154 us
  starting transfers between devices  50.7 us (33%)
  blocking collectives  50 us (32%)
  waiting for transfers between devices  15.5 us (10%)
  between operations  14 us (9%)
  matrix products  13.4 us (9%)
  Pallas kernels  7.08 us (5%)
  local copies, waits for them, and re-layouts  2.25 us (1%)
    all_to_all x1, blocking collectives, on_device(): lax.all_to_all(pieces, 'seq', split_axis=0, concat_axis=0, tiled=True, ax...  28 us
    all_to_all x1, blocking collectives, on_device(): lax.all_to_all(flat.reshape(16, 64, 256), ('seq', 'head'), split_axis=0,...  22 us
    ppermute x7, starting transfers between devices, on_device(): lax.ppermute(row_message, 'seq', y_later(k))  16.1 us
    all_to_all x1, waiting for transfers between devices, on_device(): lax.all_to_all(messages, 'seq', split_axis=0, concat_axis=0, tiled=True,...  9.69 us
    ppermute x2, starting transfers between devices, hop(): downs.append(lax.ppermute(after(downs[-1], *earlier), 'seq', y_shift(-1)))  8.62 us
    dot_general x8, matrix products, add(): d = jnp.dot(x, part.reshape(NZ * 48, 512), preferred_element_type=F32)  8.41 us
    pallas_call x6, Pallas kernels, call(): pl.pallas_call(kernel, out_shape=shapes, in_specs=smem + whole(len(args))...  7.08 us
    all_to_all x1, starting transfers between devices, on_device(): lax.all_to_all(messages, 'seq', split_axis=0, concat_axis=0, tiled=True,...  5.45 us
  transfers between devices with their start and end apart: 19, of which 4 were waited for; matrix products, arithmetic and copies ran while one was open for 10% of the time, Pallas kernels for 2%

profile of v12, /device:TPU:1, one launch (start us, length us, event | category | flops | bytes accessed | tf_op | source)
XLA Modules:
  0.0 153.9 jit_solution(14341647754898564003)
XLA Ops:
  6.5 0.7 all-gather.3.cloned.1.call-update
  7.3 0.0 all-gather.5.cloned.1.call-start
  7.3 0.9 copy-done
  8.3 28.0 %all_to_all.15 = bf16[8,48,768]{2,1,0:T(8,128)(2,1)S(1)} all-to-all(bf16[8,48,768]{2,1,0:T(8,128)(2,1)S(1)} %shard_map.46), channel_id=1, replica_groups={{0,8,16,24,32,40,48,56},{64,72,80,88,96,104,112,120},{128,136,144,152,1..., dimensions={0} | all-to-all | bytes 1179648 | tf_op jit(solution)/shard_map/all_to_all | solution.py:189
  36.3 3.2 %collective-permute-start = (bf16[8,48,512]{2,1,0:T(8,128)(2,1)S(1)}, bf16[8,48,512]{2,1,0:T(8,128)(2,1)S(1)}, u32[]{:S(2)}, u32[]{:S(2)}) collective-permute-start(bf16[8,48,512]{2,1,0:T(8,128)(2,1)S(1)} %slice.20), channel_id=1, source_target_pairs={{0,64},{8,72},{16,80},{24,88},{32,96},{40,104},{48,112},{56,120},{... | collective-permute-start | bytes 1179656 | tf_op jit(solution)/shard_map/ppermute | solution.py:204
  39.5 4.0 %collective-permute-start.5 = (bf16[8,48,512]{2,1,0:T(8,128)(2,1)S(1)}, bf16[8,48,512]{2,1,0:T(8,128)(2,1)S(1)}, u32[]{:S(2)}, u32[]{:S(2)}) collective-permute-start(bf16[8,48,512]{2,1,0:T(8,128)(2,1)S(1)} %slice.20), channel_id=1, source_target_pairs={{0,448},{8,456},{16,464},{24,472},{32,480},{40,488},{48,496},{56,5... | collective-permute-start | bytes 1179656 | tf_op jit(solution)/shard_map/ppermute | solution.py:205
  43.6 1.9 %collective-permute-start.2 = (f32[2,512]{1,0:T(2,128)S(1)}, f32[2,512]{1,0:T(2,128)S(1)}, u32[]{:S(2)}, u32[]{:S(2)}) collective-permute-start(f32[2,512]{1,0:T(2,128)S(1)} %get-tuple-element.24), channel_id=1, source_target_pairs={{0,8},{8,0},{16,24},{24,16},{32,40},{40,32},{48,56},{56,48},{64,72... | collective-permute-start | bytes 12296 | tf_op jit(solution)/shard_map/ppermute | solution.py:213
  45.5 1.2 collective-permute-done
  46.8 1.9 %collective-permute-start.1 = (bf16[8,48,512]{2,1,0:T(8,128)(2,1)S(1)}, bf16[8,48,512]{2,1,0:T(8,128)(2,1)S(1)}, u32[]{:S(2)}, u32[]{:S(2)}) collective-permute-start(bf16[8,48,512]{2,1,0:T(8,128)(2,1)S(1)} %collective-permute-done), channel_id=1, source_target_pairs={{0,64},{8,72},{16,80},{24,88},{32,96},{40,104},{48,112},{56,120},{... | collective-permute-start | bytes 1179656 | tf_op jit(solution)/shard_map/ppermute | solution.py:214
  48.7 4.6 %collective-permute-start.6 = (bf16[8,48,512]{2,1,0:T(8,128)(2,1)S(1)}, bf16[8,48,512]{2,1,0:T(8,128)(2,1)S(1)}, u32[]{:S(2)}, u32[]{:S(2)}) collective-permute-start(bf16[8,48,512]{2,1,0:T(8,128)(2,1)S(1)} %collective-permute-done.5), channel_id=1, source_target_pairs={{0,448},{8,456},{16,464},{24,472},{32,480},{40,488},{48,496},{56,5... | collective-permute-start | bytes 1179656 | tf_op jit(solution)/shard_map/ppermute | solution.py:215
  53.5 0.1 dynamic_slice.35
  53.6 0.7 slice.22
  54.3 0.6 reduce_window_sum.24
  54.9 0.2 slice_reduce_fusion
  55.1 0.2 reduce_window_sum.25
  55.3 0.1 squeeze.6
  55.3 0.1 copy.11
  55.4 0.1 reduce_window_sum.26
  55.5 1.0 collective-permute-done.1
  56.5 1.9 %collective-permute-start.3 = (bf16[8,48,512]{2,1,0:T(8,128)(2,1)S(1)}, bf16[8,48,512]{2,1,0:T(8,128)(2,1)S(1)}, u32[]{:S(2)}, u32[]{:S(2)}) collective-permute-start(bf16[8,48,512]{2,1,0:T(8,128)(2,1)S(1)} %collective-permute-done.1), channel_id=1, source_target_pairs={{0,64},{8,72},{16,80},{24,88},{32,96},{40,104},{48,112},{56,120},{... | collective-permute-start | bytes 1179656 | tf_op jit(solution)/shard_map/ppermute | solution.py:204
  58.4 4.6 %collective-permute-start.7 = (bf16[8,48,512]{2,1,0:T(8,128)(2,1)S(1)}, bf16[8,48,512]{2,1,0:T(8,128)(2,1)S(1)}, u32[]{:S(2)}, u32[]{:S(2)}) collective-permute-start(bf16[8,48,512]{2,1,0:T(8,128)(2,1)S(1)} %collective-permute-done.6), channel_id=1, source_target_pairs={{0,448},{8,456},{16,464},{24,472},{32,480},{40,488},{48,496},{56,5... | collective-permute-start | bytes 1179656 | tf_op jit(solution)/shard_map/ppermute | solution.py:205
  63.0 2.9 %all-gather.3.cloned.1.call-done = bf16[1024,3072]{1,0:T(8,128)(2,1)} async-done(((bf16[64,3072]{1,0:T(8,128)(2,1)}), bf16[1024,3072]{1,0:T(8,128)(2,1)}) %all-gather.3.cloned.1.call-update) | async-done | bytes 6291472 | tf_op jit(solution)/shard_map/all_gather | solution.py:191
  65.9 2.0 %fusion.12 = f32[1024,512]{1,0:T(8,128)S(1)} fusion(bf16[384,512]{1,0:T(8,128)(2,1)S(1)} %bitcast.36, bf16[1024,3072]{1,0:T(8,128)(2,1)} %all-gather.3.cloned.1.call-done, s32[]{:T(128)S(6)} %select_n.102), kind=kOutput, calls=%fused_computation.15 | convolution fusion | flops 402653184 | bytes 3276804 | tf_op jit(solution)/shard_map/dot_general | solution.py:196
  67.9 1.9 %convolution_add_fusion = f32[1024,512]{1,0:T(8,128)S(1)} fusion(f32[1024,512]{1,0:T(8,128)S(1)} %fusion.12, bf16[384,512]{1,0:T(8,128)(2,1)S(1)} %bitcast.43, bf16[1024,3072]{1,0:T(8,128)(2,1)} %all-gather.3.cloned.1.call-done, s32[]{:T(128)S(6)} %select_n.104), kind=kOutput, calls=%fused_computation.1 | convolution fusion | flops 403177472 | bytes 5373956 | tf_op jit(solution)/shard_map/dot_general | solution.py:196
  69.8 3.2 %collective-permute-start.4 = (bf16[4,48,512]{2,1,0:T(8,128)(2,1)S(1)}, bf16[4,48,512]{2,1,0:T(8,128)(2,1)S(1)}, u32[]{:S(2)}, u32[]{:S(2)}) collective-permute-start(bf16[4,48,512]{2,1,0:T(8,128)(2,1)S(1)} %slice.17), channel_id=1, source_target_pairs={{0,64},{8,72},{16,80},{24,88},{32,96},{40,104},{48,112},{56,120},{... | collective-permute-start | bytes 589832 | tf_op jit(solution)/shard_map/ppermute | solution.py:229
  73.1 3.8 %collective-permute-start.8 = (bf16[4,48,512]{2,1,0:T(8,128)(2,1)S(1)}, bf16[4,48,512]{2,1,0:T(8,128)(2,1)S(1)}, u32[]{:S(2)}, u32[]{:S(2)}) collective-permute-start(bf16[4,48,512]{2,1,0:T(8,128)(2,1)S(1)} %slice.18), channel_id=1, source_target_pairs={{0,448},{8,456},{16,464},{24,472},{32,480},{40,488},{48,496},{56,5... | collective-permute-start | bytes 589832 | tf_op jit(solution)/shard_map/ppermute | solution.py:230
  76.9 0.7 fusion.2
  77.6 0.7 fusion.4
  78.3 0.7 fusion.6
  79.0 0.7 fusion.9
  79.7 1.0 add_add_fusion.total_ref
  80.8 0.7 fusion.last_ref
  81.5 2.7 %shard_map.47 = (bf16[2,512,512]{2,1,0:T(8,128)(2,1)S(1)}, bf16[16,128,128]{2,1,0:T(8,128)(2,1)S(1)}, bf16[4,2,144,128]{3,2,1,0:T(8,128)(2,1)}) custom-call(f32[1024,512]{1,0:T(8,128)S(1)} %add_add_fusion.total_ref, f32[1024,512]{1,0:T(8,128)S(1)} %fusion.last_ref, f32[128,16]{1,0:T(8,128)S(1)} %bitcast.28, f32[16,128]{1,0:T(8,128)S(1)} %bitcast.32), custom_call_target="tpu_custom_call" | custom-call | flops 67108864 | bytes 4210688 | tf_op jit(solution)/shard_map/pallas_call | solution.py:171
  84.2 5.4 %all-to-all-start.1 = ((bf16[4,2,144,128]{3,2,1,0:T(8,128)(2,1)}), bf16[4,2,144,128]{3,2,1,0:T(8,128)(2,1)S(1)}, u32[]{:S(2)}, u32[]{:S(2)}) async-start(bf16[4,2,144,128]{3,2,1,0:T(8,128)(2,1)} %get-tuple-element.33), calls=%async_computation.1 | async-start | bytes 589824 | tf_op jit(solution)/shard_map/all_to_all | solution.py:240
  89.6 9.7 %all-to-all-done.1.messages_ref = bf16[4,2,144,128]{3,2,1,0:T(8,128)(2,1)S(1)} async-done(((bf16[4,2,144,128]{3,2,1,0:T(8,128)(2,1)}), bf16[4,2,144,128]{3,2,1,0:T(8,128)(2,1)S(1)}, u32[]{:S(2)}, u32[]{:S(2)}) %all-to-all-start.1) | async-done | bytes 294944 | tf_op jit(solution)/shard_map/all_to_all | solution.py:240
  99.3 0.1 shard_map.48
  99.4 2.0 %collective-permute-start.9 = (bf16[2,144,128]{2,1,0:T(8,128)(2,1)S(1)}, bf16[2,144,128]{2,1,0:T(8,128)(2,1)S(1)}, u32[]{:S(2)}, u32[]{:S(2)}) collective-permute-start(bf16[2,144,128]{2,1,0:T(8,128)(2,1)S(1)} %get-tuple-element.34), channel_id=1, source_target_pairs={{0,64},{8,72},{16,80},{24,88},{32,96},{40,104},{48,112},{56,120},{... | collective-permute-start | bytes 221192 | tf_op jit(solution)/shard_map/ppermute | solution.py:251
  101.5 5.8 %collective-permute-start.10 = (bf16[2,144,128]{2,1,0:T(8,128)(2,1)S(1)}, bf16[2,144,128]{2,1,0:T(8,128)(2,1)S(1)}, u32[]{:S(2)}, u32[]{:S(2)}) collective-permute-start(bf16[2,144,128]{2,1,0:T(8,128)(2,1)S(1)} %get-tuple-element.34), channel_id=1, source_target_pairs={{0,128},{8,136},{16,144},{24,152},{32,160},{40,168},{48,176},{56,1... | collective-permute-start | bytes 221192 | tf_op jit(solution)/shard_map/ppermute | solution.py:251
  107.2 3.2 %collective-permute-start.11 = (bf16[2,144,128]{2,1,0:T(8,128)(2,1)S(1)}, bf16[2,144,128]{2,1,0:T(8,128)(2,1)S(1)}, u32[]{:S(2)}, u32[]{:S(2)}) collective-permute-start(bf16[2,144,128]{2,1,0:T(8,128)(2,1)S(1)} %get-tuple-element.34), channel_id=1, source_target_pairs={{0,256},{8,264},{16,272},{24,280},{32,288},{40,296},{48,304},{56,3... | collective-permute-start | bytes 221192 | tf_op jit(solution)/shard_map/ppermute | solution.py:251
  110.4 1.3 collective-permute-start.12
  111.7 1.3 collective-permute-start.13
  113.0 1.3 collective-permute-start.14
  114.4 1.3 collective-permute-start.15
  115.7 5.0 %convolution_bitcast_fusion.total_ref = f32[1024,256]{1,0:T(8,128)S(1)} fusion(bf16[1024,3072]{1,0:T(8,128)(2,1)} %all-gather.3.cloned.1.call-done, bf16[3072,256]{1,0:T(8,128)(2,1)} %bitcast.44), kind=kOutput, calls=%fused_computation.2 | convolution fusion | flops 1610612736 | bytes 8912896 | tf_op jit(solution)/shard_map/dot_general | solution.py:241
  120.7 0.9 shard_map.49
  121.6 2.5 %shard_map.50 = bf16[1024,256]{1,0:T(8,128)(2,1)S(1)} custom-call(bf16[2,144,128]{2,1,0:T(8,128)(2,1)S(1)} %collective-permute-done.9.refs_0_, bf16[2,144,128]{2,1,0:T(8,128)(2,1)S(1)} %collective-permute-done.10.refs_1_, bf16[2,144,128]{2,1,0:T(8,128)(2,1)S(1)} %collective-permute-done.11.refs_2_, bf16[2,144,128]{2,1,0:T(8,128)(2,1)S(1)} %collective-permute-done.12.refs_3_, ...), custom_call_target="tpu_custom_call" | custom-call | flops 67108864 | bytes 2237504 | tf_op jit(solution)/shard_map/pallas_call | solution.py:171
  124.2 22.0 %all_to_all.16.sent_ref = bf16[16,64,256]{2,1,0:T(8,128)(2,1)S(1)} all-to-all(bf16[16,64,256]{2,1,0:T(8,128)(2,1)S(1)} %bitcast.27), channel_id=1, replica_groups={{0,1,2,3,4,5,6,7,8,9,10,11,12,13,14,15},{16,17,18,19,20,21,22,23,24,25,..., dimensions={0} | all-to-all | bytes 1048576 | tf_op jit(solution)/shard_map/all_to_all | solution.py:256
  146.2 0.8 shard_map.51
  (34 shorter events, 0.3 us)
Async XLA Ops:
  6.5 37.1 %copy-start.2 = (f32[4,512]{1,0:T(4,128)S(1)}, f32[4,512]{1,0:T(4,128)}, u32[]{:S(2)}) copy-start(f32[4,512]{1,0:T(4,128)} %param.6) | copy-start | bytes 24580
  6.5 46.9 %copy-start.3 = (f32[512]{0:T(512)S(1)}, f32[512]{0:T(512)}, u32[]{:S(2)}) copy-start(f32[512]{0:T(512)} %param.7) | copy-start | bytes 6148
  6.5 59.3 %all-gather.3.cloned.1.call-start = ((), (), s32[]{:S(2)}) async-start(), calls=%async_computation.3 | async-start | bytes 6684672 | tf_op jit(solution)/shard_map/all_gather | solution.py:191
  7.3 105.8 %all-gather.5.cloned.1.call-start = ((), (), s32[]{:S(2)}) async-start(), calls=%async_computation.4 | async-start | bytes 1769472 | tf_op jit(solution)/shard_map/all_gather | solution.py:226
  7.3 0.9 copy-start
  36.3 10.5 %collective-permute-start = (bf16[8,48,512]{2,1,0:T(8,128)(2,1)S(1)}, bf16[8,48,512]{2,1,0:T(8,128)(2,1)S(1)}, u32[]{:S(2)}, u32[]{:S(2)}) collective-permute-start(bf16[8,48,512]{2,1,0:T(8,128)(2,1)S(1)} %slice.20), channel_id=1, source_target_pairs={{0,64},{8,72},{16,80},{24,88},{32,96},{40,104},{48,112},{56,120},{... | collective-permute-start | bytes 1179656 | tf_op jit(solution)/shard_map/ppermute | solution.py:204
  39.5 9.2 %collective-permute-start.5 = (bf16[8,48,512]{2,1,0:T(8,128)(2,1)S(1)}, bf16[8,48,512]{2,1,0:T(8,128)(2,1)S(1)}, u32[]{:S(2)}, u32[]{:S(2)}) collective-permute-start(bf16[8,48,512]{2,1,0:T(8,128)(2,1)S(1)} %slice.20), channel_id=1, source_target_pairs={{0,448},{8,456},{16,464},{24,472},{32,480},{40,488},{48,496},{56,5... | collective-permute-start | bytes 1179656 | tf_op jit(solution)/shard_map/ppermute | solution.py:205
  43.6 5.1 %collective-permute-start.2 = (f32[2,512]{1,0:T(2,128)S(1)}, f32[2,512]{1,0:T(2,128)S(1)}, u32[]{:S(2)}, u32[]{:S(2)}) collective-permute-start(f32[2,512]{1,0:T(2,128)S(1)} %get-tuple-element.24), channel_id=1, source_target_pairs={{0,8},{8,0},{16,24},{24,16},{32,40},{40,32},{48,56},{56,48},{64,72... | collective-permute-start | bytes 12296 | tf_op jit(solution)/shard_map/ppermute | solution.py:213
  46.8 9.7 %collective-permute-start.1 = (bf16[8,48,512]{2,1,0:T(8,128)(2,1)S(1)}, bf16[8,48,512]{2,1,0:T(8,128)(2,1)S(1)}, u32[]{:S(2)}, u32[]{:S(2)}) collective-permute-start(bf16[8,48,512]{2,1,0:T(8,128)(2,1)S(1)} %collective-permute-done), channel_id=1, source_target_pairs={{0,64},{8,72},{16,80},{24,88},{32,96},{40,104},{48,112},{56,120},{... | collective-permute-start | bytes 1179656 | tf_op jit(solution)/shard_map/ppermute | solution.py:214
  48.7 9.7 %collective-permute-start.6 = (bf16[8,48,512]{2,1,0:T(8,128)(2,1)S(1)}, bf16[8,48,512]{2,1,0:T(8,128)(2,1)S(1)}, u32[]{:S(2)}, u32[]{:S(2)}) collective-permute-start(bf16[8,48,512]{2,1,0:T(8,128)(2,1)S(1)} %collective-permute-done.5), channel_id=1, source_target_pairs={{0,448},{8,456},{16,464},{24,472},{32,480},{40,488},{48,496},{56,5... | collective-permute-start | bytes 1179656 | tf_op jit(solution)/shard_map/ppermute | solution.py:215
  56.5 13.3 %collective-permute-start.3 = (bf16[8,48,512]{2,1,0:T(8,128)(2,1)S(1)}, bf16[8,48,512]{2,1,0:T(8,128)(2,1)S(1)}, u32[]{:S(2)}, u32[]{:S(2)}) collective-permute-start(bf16[8,48,512]{2,1,0:T(8,128)(2,1)S(1)} %collective-permute-done.1), channel_id=1, source_target_pairs={{0,64},{8,72},{16,80},{24,88},{32,96},{40,104},{48,112},{56,120},{... | collective-permute-start | bytes 1179656 | tf_op jit(solution)/shard_map/ppermute | solution.py:204
  58.4 14.6 %collective-permute-start.7 = (bf16[8,48,512]{2,1,0:T(8,128)(2,1)S(1)}, bf16[8,48,512]{2,1,0:T(8,128)(2,1)S(1)}, u32[]{:S(2)}, u32[]{:S(2)}) collective-permute-start(bf16[8,48,512]{2,1,0:T(8,128)(2,1)S(1)} %collective-permute-done.6), channel_id=1, source_target_pairs={{0,448},{8,456},{16,464},{24,472},{32,480},{40,488},{48,496},{56,5... | collective-permute-start | bytes 1179656 | tf_op jit(solution)/shard_map/ppermute | solution.py:205
  65.9 11.0 %copy-start.1 = (bf16[1024,3072]{1,0:T(8,128)(2,1)S(1)}, bf16[1024,3072]{1,0:T(8,128)(2,1)}, u32[]{:S(2)}) copy-start(bf16[1024,3072]{1,0:T(8,128)(2,1)} %all-gather.3.cloned.1.call-done) | copy-start | bytes 18874372
  69.8 10.9 %collective-permute-start.4 = (bf16[4,48,512]{2,1,0:T(8,128)(2,1)S(1)}, bf16[4,48,512]{2,1,0:T(8,128)(2,1)S(1)}, u32[]{:S(2)}, u32[]{:S(2)}) collective-permute-start(bf16[4,48,512]{2,1,0:T(8,128)(2,1)S(1)} %slice.17), channel_id=1, source_target_pairs={{0,64},{8,72},{16,80},{24,88},{32,96},{40,104},{48,112},{56,120},{... | collective-permute-start | bytes 589832 | tf_op jit(solution)/shard_map/ppermute | solution.py:229
  73.1 7.7 %collective-permute-start.8 = (bf16[4,48,512]{2,1,0:T(8,128)(2,1)S(1)}, bf16[4,48,512]{2,1,0:T(8,128)(2,1)S(1)}, u32[]{:S(2)}, u32[]{:S(2)}) collective-permute-start(bf16[4,48,512]{2,1,0:T(8,128)(2,1)S(1)} %slice.18), channel_id=1, source_target_pairs={{0,448},{8,456},{16,464},{24,472},{32,480},{40,488},{48,496},{56,5... | collective-permute-start | bytes 589832 | tf_op jit(solution)/shard_map/ppermute | solution.py:230
  84.2 15.1 %all-to-all-start.1 = ((bf16[4,2,144,128]{3,2,1,0:T(8,128)(2,1)}), bf16[4,2,144,128]{3,2,1,0:T(8,128)(2,1)S(1)}, u32[]{:S(2)}, u32[]{:S(2)}) async-start(bf16[4,2,144,128]{3,2,1,0:T(8,128)(2,1)} %get-tuple-element.33), calls=%async_computation.1 | async-start | bytes 589824 | tf_op jit(solution)/shard_map/all_to_all | solution.py:240
  99.4 13.6 %collective-permute-start.9 = (bf16[2,144,128]{2,1,0:T(8,128)(2,1)S(1)}, bf16[2,144,128]{2,1,0:T(8,128)(2,1)S(1)}, u32[]{:S(2)}, u32[]{:S(2)}) collective-permute-start(bf16[2,144,128]{2,1,0:T(8,128)(2,1)S(1)} %get-tuple-element.34), channel_id=1, source_target_pairs={{0,64},{8,72},{16,80},{24,88},{32,96},{40,104},{48,112},{56,120},{... | collective-permute-start | bytes 221192 | tf_op jit(solution)/shard_map/ppermute | solution.py:251
  101.5 12.9 %collective-permute-start.10 = (bf16[2,144,128]{2,1,0:T(8,128)(2,1)S(1)}, bf16[2,144,128]{2,1,0:T(8,128)(2,1)S(1)}, u32[]{:S(2)}, u32[]{:S(2)}) collective-permute-start(bf16[2,144,128]{2,1,0:T(8,128)(2,1)S(1)} %get-tuple-element.34), channel_id=1, source_target_pairs={{0,128},{8,136},{16,144},{24,152},{32,160},{40,168},{48,176},{56,1... | collective-permute-start | bytes 221192 | tf_op jit(solution)/shard_map/ppermute | solution.py:251
  107.2 14.3 %collective-permute-start.11 = (bf16[2,144,128]{2,1,0:T(8,128)(2,1)S(1)}, bf16[2,144,128]{2,1,0:T(8,128)(2,1)S(1)}, u32[]{:S(2)}, u32[]{:S(2)}) collective-permute-start(bf16[2,144,128]{2,1,0:T(8,128)(2,1)S(1)} %get-tuple-element.34), channel_id=1, source_target_pairs={{0,256},{8,264},{16,272},{24,280},{32,288},{40,296},{48,304},{56,3... | collective-permute-start | bytes 221192 | tf_op jit(solution)/shard_map/ppermute | solution.py:251
  110.4 11.2 %collective-permute-start.12 = (bf16[2,144,128]{2,1,0:T(8,128)(2,1)S(1)}, bf16[2,144,128]{2,1,0:T(8,128)(2,1)S(1)}, u32[]{:S(2)}, u32[]{:S(2)}) collective-permute-start(bf16[2,144,128]{2,1,0:T(8,128)(2,1)S(1)} %get-tuple-element.34), channel_id=1, source_target_pairs={{0,320},{8,328},{16,336},{24,344},{32,352},{40,360},{48,368},{56,3... | collective-permute-start | bytes 221192 | tf_op jit(solution)/shard_map/ppermute | solution.py:251
  111.7 9.9 %collective-permute-start.13 = (bf16[2,144,128]{2,1,0:T(8,128)(2,1)S(1)}, bf16[2,144,128]{2,1,0:T(8,128)(2,1)S(1)}, u32[]{:S(2)}, u32[]{:S(2)}) collective-permute-start(bf16[2,144,128]{2,1,0:T(8,128)(2,1)S(1)} %get-tuple-element.34), channel_id=1, source_target_pairs={{0,192},{8,200},{16,208},{24,216},{32,224},{40,232},{48,240},{56,2... | collective-permute-start | bytes 221192 | tf_op jit(solution)/shard_map/ppermute | solution.py:251
  113.0 8.6 %collective-permute-start.14 = (bf16[2,144,128]{2,1,0:T(8,128)(2,1)S(1)}, bf16[2,144,128]{2,1,0:T(8,128)(2,1)S(1)}, u32[]{:S(2)}, u32[]{:S(2)}) collective-permute-start(bf16[2,144,128]{2,1,0:T(8,128)(2,1)S(1)} %get-tuple-element.34), channel_id=1, source_target_pairs={{0,384},{8,392},{16,400},{24,408},{32,416},{40,424},{48,432},{56,4... | collective-permute-start | bytes 221192 | tf_op jit(solution)/shard_map/ppermute | solution.py:251
  114.4 7.3 %collective-permute-start.15 = (bf16[2,144,128]{2,1,0:T(8,128)(2,1)S(1)}, bf16[2,144,128]{2,1,0:T(8,128)(2,1)S(1)}, u32[]{:S(2)}, u32[]{:S(2)}) collective-permute-start(bf16[2,144,128]{2,1,0:T(8,128)(2,1)S(1)} %get-tuple-element.34), channel_id=1, source_target_pairs={{0,448},{8,456},{16,464},{24,472},{32,480},{40,488},{48,496},{56,5... | collective-permute-start | bytes 221192 | tf_op jit(solution)/shard_map/ppermute | solution.py:251
Sparse Core Ops, SparseCore 0:
  9.5 56.3 all-gather.2
  67.9 39.8 all-gather.4

commit v13 on v11

--- a/solution.py
+++ b/solution.py
@@ -14,7 +14,7 @@
 NZ = 8
 NH = 8
 EXTRA = 16
-START_ORDER = (1, 2, 4, 5, 3, 6, 7)
+START_ORDER = (1, 2, 4, 5, 6, 3, 7)
 F32 = jnp.float32
 BF16 = jnp.bfloat16
 VMEM = pltpu.VMEM

time: 154 us -> 154 us (level)
  no operation moved by 1% of the time
where the time goes in v13:
time: 154 us
  starting transfers between devices  50.7 us (33%)
  blocking collectives  50 us (32%)
  waiting for transfers between devices  15.5 us (10%)
  between operations  14 us (9%)
  matrix products  13.4 us (9%)
  Pallas kernels  7.08 us (5%)
  local copies, waits for them, and re-layouts  2.25 us (1%)
    all_to_all x1, blocking collectives, on_device(): lax.all_to_all(pieces, 'seq', split_axis=0, concat_axis=0, tiled=True, ax...  28 us
    all_to_all x1, blocking collectives, on_device(): lax.all_to_all(flat.reshape(16, 64, 256), ('seq', 'head'), split_axis=0,...  22 us
    ppermute x7, starting transfers between devices, on_device(): lax.ppermute(row_message, 'seq', y_later(k))  16.1 us
    all_to_all x1, waiting for transfers between devices, on_device(): lax.all_to_all(messages, 'seq', split_axis=0, concat_axis=0, tiled=True,...  9.69 us
    ppermute x2, starting transfers between devices, hop(): downs.append(lax.ppermute(after(downs[-1], *earlier), 'seq', y_shift(-1)))  8.62 us
    dot_general x8, matrix products, add(): d = jnp.dot(x, part.reshape(NZ * 48, 512), preferred_element_type=F32)  8.41 us
    pallas_call x6, Pallas kernels, call(): pl.pallas_call(kernel, out_shape=shapes, in_specs=smem + whole(len(args))...  7.08 us
    all_to_all x1, starting transfers between devices, on_device(): lax.all_to_all(messages, 'seq', split_axis=0, concat_axis=0, tiled=True,...  5.45 us
  transfers between devices with their start and end apart: 19, of which 4 were waited for; matrix products, arithmetic and copies ran while one was open for 10% of the time, Pallas kernels for 2%

profile of v13, /device:TPU:1, one launch (start us, length us, event | category | flops | bytes accessed | tf_op | source)
XLA Modules:
  0.0 153.9 jit_solution(15419852692899825277)
XLA Ops:
  6.5 0.7 all-gather.3.cloned.1.call-update
  7.3 0.0 all-gather.5.cloned.1.call-start
  7.3 0.9 copy-done
  8.3 28.0 %all_to_all.15 = bf16[8,48,768]{2,1,0:T(8,128)(2,1)S(1)} all-to-all(bf16[8,48,768]{2,1,0:T(8,128)(2,1)S(1)} %shard_map.46), channel_id=1, replica_groups={{0,8,16,24,32,40,48,56},{64,72,80,88,96,104,112,120},{128,136,144,152,1..., dimensions={0} | all-to-all | bytes 1179648 | tf_op jit(solution)/shard_map/all_to_all | solution.py:189
  36.3 3.2 %collective-permute-start = (bf16[8,48,512]{2,1,0:T(8,128)(2,1)S(1)}, bf16[8,48,512]{2,1,0:T(8,128)(2,1)S(1)}, u32[]{:S(2)}, u32[]{:S(2)}) collective-permute-start(bf16[8,48,512]{2,1,0:T(8,128)(2,1)S(1)} %slice.20), channel_id=1, source_target_pairs={{0,64},{8,72},{16,80},{24,88},{32,96},{40,104},{48,112},{56,120},{... | collective-permute-start | bytes 1179656 | tf_op jit(solution)/shard_map/ppermute | solution.py:204
  39.5 4.0 %collective-permute-start.5 = (bf16[8,48,512]{2,1,0:T(8,128)(2,1)S(1)}, bf16[8,48,512]{2,1,0:T(8,128)(2,1)S(1)}, u32[]{:S(2)}, u32[]{:S(2)}) collective-permute-start(bf16[8,48,512]{2,1,0:T(8,128)(2,1)S(1)} %slice.20), channel_id=1, source_target_pairs={{0,448},{8,456},{16,464},{24,472},{32,480},{40,488},{48,496},{56,5... | collective-permute-start | bytes 1179656 | tf_op jit(solution)/shard_map/ppermute | solution.py:205
  43.6 1.9 %collective-permute-start.2 = (f32[2,512]{1,0:T(2,128)S(1)}, f32[2,512]{1,0:T(2,128)S(1)}, u32[]{:S(2)}, u32[]{:S(2)}) collective-permute-start(f32[2,512]{1,0:T(2,128)S(1)} %get-tuple-element.24), channel_id=1, source_target_pairs={{0,8},{8,0},{16,24},{24,16},{32,40},{40,32},{48,56},{56,48},{64,72... | collective-permute-start | bytes 12296 | tf_op jit(solution)/shard_map/ppermute | solution.py:213
  45.5 1.2 collective-permute-done
  46.8 1.9 %collective-permute-start.1 = (bf16[8,48,512]{2,1,0:T(8,128)(2,1)S(1)}, bf16[8,48,512]{2,1,0:T(8,128)(2,1)S(1)}, u32[]{:S(2)}, u32[]{:S(2)}) collective-permute-start(bf16[8,48,512]{2,1,0:T(8,128)(2,1)S(1)} %collective-permute-done), channel_id=1, source_target_pairs={{0,64},{8,72},{16,80},{24,88},{32,96},{40,104},{48,112},{56,120},{... | collective-permute-start | bytes 1179656 | tf_op jit(solution)/shard_map/ppermute | solution.py:214
  48.7 4.6 %collective-permute-start.6 = (bf16[8,48,512]{2,1,0:T(8,128)(2,1)S(1)}, bf16[8,48,512]{2,1,0:T(8,128)(2,1)S(1)}, u32[]{:S(2)}, u32[]{:S(2)}) collective-permute-start(bf16[8,48,512]{2,1,0:T(8,128)(2,1)S(1)} %collective-permute-done.5), channel_id=1, source_target_pairs={{0,448},{8,456},{16,464},{24,472},{32,480},{40,488},{48,496},{56,5... | collective-permute-start | bytes 1179656 | tf_op jit(solution)/shard_map/ppermute | solution.py:215
  53.5 0.1 dynamic_slice.35
  53.6 0.7 slice.22
  54.3 0.6 reduce_window_sum.24
  54.9 0.2 slice_reduce_fusion
  55.1 0.2 reduce_window_sum.25
  55.3 0.1 squeeze.6
  55.3 0.1 copy.11
  55.4 0.1 reduce_window_sum.26
  55.5 1.0 collective-permute-done.1
  56.5 1.9 %collective-permute-start.3 = (bf16[8,48,512]{2,1,0:T(8,128)(2,1)S(1)}, bf16[8,48,512]{2,1,0:T(8,128)(2,1)S(1)}, u32[]{:S(2)}, u32[]{:S(2)}) collective-permute-start(bf16[8,48,512]{2,1,0:T(8,128)(2,1)S(1)} %collective-permute-done.1), channel_id=1, source_target_pairs={{0,64},{8,72},{16,80},{24,88},{32,96},{40,104},{48,112},{56,120},{... | collective-permute-start | bytes 1179656 | tf_op jit(solution)/shard_map/ppermute | solution.py:204
  58.4 4.6 %collective-permute-start.7 = (bf16[8,48,512]{2,1,0:T(8,128)(2,1)S(1)}, bf16[8,48,512]{2,1,0:T(8,128)(2,1)S(1)}, u32[]{:S(2)}, u32[]{:S(2)}) collective-permute-start(bf16[8,48,512]{2,1,0:T(8,128)(2,1)S(1)} %collective-permute-done.6), channel_id=1, source_target_pairs={{0,448},{8,456},{16,464},{24,472},{32,480},{40,488},{48,496},{56,5... | collective-permute-start | bytes 1179656 | tf_op jit(solution)/shard_map/ppermute | solution.py:205
  63.0 2.9 %all-gather.3.cloned.1.call-done = bf16[1024,3072]{1,0:T(8,128)(2,1)} async-done(((bf16[64,3072]{1,0:T(8,128)(2,1)}), bf16[1024,3072]{1,0:T(8,128)(2,1)}) %all-gather.3.cloned.1.call-update) | async-done | bytes 6291472 | tf_op jit(solution)/shard_map/all_gather | solution.py:191
  65.9 2.0 %fusion.12 = f32[1024,512]{1,0:T(8,128)S(1)} fusion(bf16[384,512]{1,0:T(8,128)(2,1)S(1)} %bitcast.36, bf16[1024,3072]{1,0:T(8,128)(2,1)} %all-gather.3.cloned.1.call-done, s32[]{:T(128)S(6)} %select_n.102), kind=kOutput, calls=%fused_computation.15 | convolution fusion | flops 402653184 | bytes 3276804 | tf_op jit(solution)/shard_map/dot_general | solution.py:196
  67.9 1.9 %convolution_add_fusion = f32[1024,512]{1,0:T(8,128)S(1)} fusion(f32[1024,512]{1,0:T(8,128)S(1)} %fusion.12, bf16[384,512]{1,0:T(8,128)(2,1)S(1)} %bitcast.43, bf16[1024,3072]{1,0:T(8,128)(2,1)} %all-gather.3.cloned.1.call-done, s32[]{:T(128)S(6)} %select_n.104), kind=kOutput, calls=%fused_computation.1 | convolution fusion | flops 403177472 | bytes 5373956 | tf_op jit(solution)/shard_map/dot_general | solution.py:196
  69.8 3.2 %collective-permute-start.4 = (bf16[4,48,512]{2,1,0:T(8,128)(2,1)S(1)}, bf16[4,48,512]{2,1,0:T(8,128)(2,1)S(1)}, u32[]{:S(2)}, u32[]{:S(2)}) collective-permute-start(bf16[4,48,512]{2,1,0:T(8,128)(2,1)S(1)} %slice.17), channel_id=1, source_target_pairs={{0,64},{8,72},{16,80},{24,88},{32,96},{40,104},{48,112},{56,120},{... | collective-permute-start | bytes 589832 | tf_op jit(solution)/shard_map/ppermute | solution.py:229
  73.1 3.8 %collective-permute-start.8 = (bf16[4,48,512]{2,1,0:T(8,128)(2,1)S(1)}, bf16[4,48,512]{2,1,0:T(8,128)(2,1)S(1)}, u32[]{:S(2)}, u32[]{:S(2)}) collective-permute-start(bf16[4,48,512]{2,1,0:T(8,128)(2,1)S(1)} %slice.18), channel_id=1, source_target_pairs={{0,448},{8,456},{16,464},{24,472},{32,480},{40,488},{48,496},{56,5... | collective-permute-start | bytes 589832 | tf_op jit(solution)/shard_map/ppermute | solution.py:230
  76.9 0.7 fusion.2
  77.6 0.7 fusion.4
  78.3 0.7 fusion.6
  79.0 0.7 fusion.9
  79.7 1.0 add_add_fusion.total_ref
  80.8 0.7 fusion.last_ref
  81.5 2.7 %shard_map.47 = (bf16[2,512,512]{2,1,0:T(8,128)(2,1)S(1)}, bf16[16,128,128]{2,1,0:T(8,128)(2,1)S(1)}, bf16[4,2,144,128]{3,2,1,0:T(8,128)(2,1)}) custom-call(f32[1024,512]{1,0:T(8,128)S(1)} %add_add_fusion.total_ref, f32[1024,512]{1,0:T(8,128)S(1)} %fusion.last_ref, f32[128,16]{1,0:T(8,128)S(1)} %bitcast.28, f32[16,128]{1,0:T(8,128)S(1)} %bitcast.32), custom_call_target="tpu_custom_call" | custom-call | flops 67108864 | bytes 4210688 | tf_op jit(solution)/shard_map/pallas_call | solution.py:171
  84.2 5.4 %all-to-all-start.1 = ((bf16[4,2,144,128]{3,2,1,0:T(8,128)(2,1)}), bf16[4,2,144,128]{3,2,1,0:T(8,128)(2,1)S(1)}, u32[]{:S(2)}, u32[]{:S(2)}) async-start(bf16[4,2,144,128]{3,2,1,0:T(8,128)(2,1)} %get-tuple-element.33), calls=%async_computation.1 | async-start | bytes 589824 | tf_op jit(solution)/shard_map/all_to_all | solution.py:240
  89.6 9.7 %all-to-all-done.1.messages_ref = bf16[4,2,144,128]{3,2,1,0:T(8,128)(2,1)S(1)} async-done(((bf16[4,2,144,128]{3,2,1,0:T(8,128)(2,1)}), bf16[4,2,144,128]{3,2,1,0:T(8,128)(2,1)S(1)}, u32[]{:S(2)}, u32[]{:S(2)}) %all-to-all-start.1) | async-done | bytes 294944 | tf_op jit(solution)/shard_map/all_to_all | solution.py:240
  99.3 0.1 shard_map.48
  99.4 2.0 %collective-permute-start.9 = (bf16[2,144,128]{2,1,0:T(8,128)(2,1)S(1)}, bf16[2,144,128]{2,1,0:T(8,128)(2,1)S(1)}, u32[]{:S(2)}, u32[]{:S(2)}) collective-permute-start(bf16[2,144,128]{2,1,0:T(8,128)(2,1)S(1)} %get-tuple-element.34), channel_id=1, source_target_pairs={{0,64},{8,72},{16,80},{24,88},{32,96},{40,104},{48,112},{56,120},{... | collective-permute-start | bytes 221192 | tf_op jit(solution)/shard_map/ppermute | solution.py:251
  101.5 5.8 %collective-permute-start.10 = (bf16[2,144,128]{2,1,0:T(8,128)(2,1)S(1)}, bf16[2,144,128]{2,1,0:T(8,128)(2,1)S(1)}, u32[]{:S(2)}, u32[]{:S(2)}) collective-permute-start(bf16[2,144,128]{2,1,0:T(8,128)(2,1)S(1)} %get-tuple-element.34), channel_id=1, source_target_pairs={{0,128},{8,136},{16,144},{24,152},{32,160},{40,168},{48,176},{56,1... | collective-permute-start | bytes 221192 | tf_op jit(solution)/shard_map/ppermute | solution.py:251
  107.2 3.2 %collective-permute-start.11 = (bf16[2,144,128]{2,1,0:T(8,128)(2,1)S(1)}, bf16[2,144,128]{2,1,0:T(8,128)(2,1)S(1)}, u32[]{:S(2)}, u32[]{:S(2)}) collective-permute-start(bf16[2,144,128]{2,1,0:T(8,128)(2,1)S(1)} %get-tuple-element.34), channel_id=1, source_target_pairs={{0,256},{8,264},{16,272},{24,280},{32,288},{40,296},{48,304},{56,3... | collective-permute-start | bytes 221192 | tf_op jit(solution)/shard_map/ppermute | solution.py:251
  110.4 1.3 collective-permute-start.12
  111.7 1.3 collective-permute-start.13
  113.0 1.3 collective-permute-start.14
  114.4 1.3 collective-permute-start.15
  115.7 5.0 %convolution_bitcast_fusion.total_ref = f32[1024,256]{1,0:T(8,128)S(1)} fusion(bf16[1024,3072]{1,0:T(8,128)(2,1)} %all-gather.3.cloned.1.call-done, bf16[3072,256]{1,0:T(8,128)(2,1)} %bitcast.44), kind=kOutput, calls=%fused_computation.2 | convolution fusion | flops 1610612736 | bytes 8912896 | tf_op jit(solution)/shard_map/dot_general | solution.py:241
  120.7 0.9 shard_map.49
  121.6 2.5 %shard_map.50 = bf16[1024,256]{1,0:T(8,128)(2,1)S(1)} custom-call(bf16[2,144,128]{2,1,0:T(8,128)(2,1)S(1)} %collective-permute-done.9.refs_0_, bf16[2,144,128]{2,1,0:T(8,128)(2,1)S(1)} %collective-permute-done.10.refs_1_, bf16[2,144,128]{2,1,0:T(8,128)(2,1)S(1)} %collective-permute-done.11.refs_2_, bf16[2,144,128]{2,1,0:T(8,128)(2,1)S(1)} %collective-permute-done.12.refs_3_, ...), custom_call_target="tpu_custom_call" | custom-call | flops 67108864 | bytes 2237504 | tf_op jit(solution)/shard_map/pallas_call | solution.py:171
  124.2 22.0 %all_to_all.16.sent_ref = bf16[16,64,256]{2,1,0:T(8,128)(2,1)S(1)} all-to-all(bf16[16,64,256]{2,1,0:T(8,128)(2,1)S(1)} %bitcast.27), channel_id=1, replica_groups={{0,1,2,3,4,5,6,7,8,9,10,11,12,13,14,15},{16,17,18,19,20,21,22,23,24,25,..., dimensions={0} | all-to-all | bytes 1048576 | tf_op jit(solution)/shard_map/all_to_all | solution.py:256
  146.2 0.8 shard_map.51
  (34 shorter events, 0.3 us)
Async XLA Ops:
  6.5 37.1 %copy-start.2 = (f32[4,512]{1,0:T(4,128)S(1)}, f32[4,512]{1,0:T(4,128)}, u32[]{:S(2)}) copy-start(f32[4,512]{1,0:T(4,128)} %param.6) | copy-start | bytes 24580
  6.5 46.9 %copy-start.3 = (f32[512]{0:T(512)S(1)}, f32[512]{0:T(512)}, u32[]{:S(2)}) copy-start(f32[512]{0:T(512)} %param.7) | copy-start | bytes 6148
  6.5 59.3 %all-gather.3.cloned.1.call-start = ((), (), s32[]{:S(2)}) async-start(), calls=%async_computation.3 | async-start | bytes 6684672 | tf_op jit(solution)/shard_map/all_gather | solution.py:191
  7.3 105.8 %all-gather.5.cloned.1.call-start = ((), (), s32[]{:S(2)}) async-start(), calls=%async_computation.4 | async-start | bytes 1769472 | tf_op jit(solution)/shard_map/all_gather | solution.py:226
  7.3 0.9 copy-start
  36.3 10.5 %collective-permute-start = (bf16[8,48,512]{2,1,0:T(8,128)(2,1)S(1)}, bf16[8,48,512]{2,1,0:T(8,128)(2,1)S(1)}, u32[]{:S(2)}, u32[]{:S(2)}) collective-permute-start(bf16[8,48,512]{2,1,0:T(8,128)(2,1)S(1)} %slice.20), channel_id=1, source_target_pairs={{0,64},{8,72},{16,80},{24,88},{32,96},{40,104},{48,112},{56,120},{... | collective-permute-start | bytes 1179656 | tf_op jit(solution)/shard_map/ppermute | solution.py:204
  39.5 9.2 %collective-permute-start.5 = (bf16[8,48,512]{2,1,0:T(8,128)(2,1)S(1)}, bf16[8,48,512]{2,1,0:T(8,128)(2,1)S(1)}, u32[]{:S(2)}, u32[]{:S(2)}) collective-permute-start(bf16[8,48,512]{2,1,0:T(8,128)(2,1)S(1)} %slice.20), channel_id=1, source_target_pairs={{0,448},{8,456},{16,464},{24,472},{32,480},{40,488},{48,496},{56,5... | collective-permute-start | bytes 1179656 | tf_op jit(solution)/shard_map/ppermute | solution.py:205
  43.6 5.1 %collective-permute-start.2 = (f32[2,512]{1,0:T(2,128)S(1)}, f32[2,512]{1,0:T(2,128)S(1)}, u32[]{:S(2)}, u32[]{:S(2)}) collective-permute-start(f32[2,512]{1,0:T(2,128)S(1)} %get-tuple-element.24), channel_id=1, source_target_pairs={{0,8},{8,0},{16,24},{24,16},{32,40},{40,32},{48,56},{56,48},{64,72... | collective-permute-start | bytes 12296 | tf_op jit(solution)/shard_map/ppermute | solution.py:213
  46.8 9.7 %collective-permute-start.1 = (bf16[8,48,512]{2,1,0:T(8,128)(2,1)S(1)}, bf16[8,48,512]{2,1,0:T(8,128)(2,1)S(1)}, u32[]{:S(2)}, u32[]{:S(2)}) collective-permute-start(bf16[8,48,512]{2,1,0:T(8,128)(2,1)S(1)} %collective-permute-done), channel_id=1, source_target_pairs={{0,64},{8,72},{16,80},{24,88},{32,96},{40,104},{48,112},{56,120},{... | collective-permute-start | bytes 1179656 | tf_op jit(solution)/shard_map/ppermute | solution.py:214
  48.7 9.7 %collective-permute-start.6 = (bf16[8,48,512]{2,1,0:T(8,128)(2,1)S(1)}, bf16[8,48,512]{2,1,0:T(8,128)(2,1)S(1)}, u32[]{:S(2)}, u32[]{:S(2)}) collective-permute-start(bf16[8,48,512]{2,1,0:T(8,128)(2,1)S(1)} %collective-permute-done.5), channel_id=1, source_target_pairs={{0,448},{8,456},{16,464},{24,472},{32,480},{40,488},{48,496},{56,5... | collective-permute-start | bytes 1179656 | tf_op jit(solution)/shard_map/ppermute | solution.py:215
  56.5 13.3 %collective-permute-start.3 = (bf16[8,48,512]{2,1,0:T(8,128)(2,1)S(1)}, bf16[8,48,512]{2,1,0:T(8,128)(2,1)S(1)}, u32[]{:S(2)}, u32[]{:S(2)}) collective-permute-start(bf16[8,48,512]{2,1,0:T(8,128)(2,1)S(1)} %collective-permute-done.1), channel_id=1, source_target_pairs={{0,64},{8,72},{16,80},{24,88},{32,96},{40,104},{48,112},{56,120},{... | collective-permute-start | bytes 1179656 | tf_op jit(solution)/shard_map/ppermute | solution.py:204
  58.4 14.6 %collective-permute-start.7 = (bf16[8,48,512]{2,1,0:T(8,128)(2,1)S(1)}, bf16[8,48,512]{2,1,0:T(8,128)(2,1)S(1)}, u32[]{:S(2)}, u32[]{:S(2)}) collective-permute-start(bf16[8,48,512]{2,1,0:T(8,128)(2,1)S(1)} %collective-permute-done.6), channel_id=1, source_target_pairs={{0,448},{8,456},{16,464},{24,472},{32,480},{40,488},{48,496},{56,5... | collective-permute-start | bytes 1179656 | tf_op jit(solution)/shard_map/ppermute | solution.py:205
  65.9 11.0 %copy-start.1 = (bf16[1024,3072]{1,0:T(8,128)(2,1)S(1)}, bf16[1024,3072]{1,0:T(8,128)(2,1)}, u32[]{:S(2)}) copy-start(bf16[1024,3072]{1,0:T(8,128)(2,1)} %all-gather.3.cloned.1.call-done) | copy-start | bytes 18874372
  69.8 10.9 %collective-permute-start.4 = (bf16[4,48,512]{2,1,0:T(8,128)(2,1)S(1)}, bf16[4,48,512]{2,1,0:T(8,128)(2,1)S(1)}, u32[]{:S(2)}, u32[]{:S(2)}) collective-permute-start(bf16[4,48,512]{2,1,0:T(8,128)(2,1)S(1)} %slice.17), channel_id=1, source_target_pairs={{0,64},{8,72},{16,80},{24,88},{32,96},{40,104},{48,112},{56,120},{... | collective-permute-start | bytes 589832 | tf_op jit(solution)/shard_map/ppermute | solution.py:229
  73.1 7.7 %collective-permute-start.8 = (bf16[4,48,512]{2,1,0:T(8,128)(2,1)S(1)}, bf16[4,48,512]{2,1,0:T(8,128)(2,1)S(1)}, u32[]{:S(2)}, u32[]{:S(2)}) collective-permute-start(bf16[4,48,512]{2,1,0:T(8,128)(2,1)S(1)} %slice.18), channel_id=1, source_target_pairs={{0,448},{8,456},{16,464},{24,472},{32,480},{40,488},{48,496},{56,5... | collective-permute-start | bytes 589832 | tf_op jit(solution)/shard_map/ppermute | solution.py:230
  84.2 15.1 %all-to-all-start.1 = ((bf16[4,2,144,128]{3,2,1,0:T(8,128)(2,1)}), bf16[4,2,144,128]{3,2,1,0:T(8,128)(2,1)S(1)}, u32[]{:S(2)}, u32[]{:S(2)}) async-start(bf16[4,2,144,128]{3,2,1,0:T(8,128)(2,1)} %get-tuple-element.33), calls=%async_computation.1 | async-start | bytes 589824 | tf_op jit(solution)/shard_map/all_to_all | solution.py:240
  99.4 13.6 %collective-permute-start.9 = (bf16[2,144,128]{2,1,0:T(8,128)(2,1)S(1)}, bf16[2,144,128]{2,1,0:T(8,128)(2,1)S(1)}, u32[]{:S(2)}, u32[]{:S(2)}) collective-permute-start(bf16[2,144,128]{2,1,0:T(8,128)(2,1)S(1)} %get-tuple-element.34), channel_id=1, source_target_pairs={{0,64},{8,72},{16,80},{24,88},{32,96},{40,104},{48,112},{56,120},{... | collective-permute-start | bytes 221192 | tf_op jit(solution)/shard_map/ppermute | solution.py:251
  101.5 12.9 %collective-permute-start.10 = (bf16[2,144,128]{2,1,0:T(8,128)(2,1)S(1)}, bf16[2,144,128]{2,1,0:T(8,128)(2,1)S(1)}, u32[]{:S(2)}, u32[]{:S(2)}) collective-permute-start(bf16[2,144,128]{2,1,0:T(8,128)(2,1)S(1)} %get-tuple-element.34), channel_id=1, source_target_pairs={{0,128},{8,136},{16,144},{24,152},{32,160},{40,168},{48,176},{56,1... | collective-permute-start | bytes 221192 | tf_op jit(solution)/shard_map/ppermute | solution.py:251
  107.2 14.3 %collective-permute-start.11 = (bf16[2,144,128]{2,1,0:T(8,128)(2,1)S(1)}, bf16[2,144,128]{2,1,0:T(8,128)(2,1)S(1)}, u32[]{:S(2)}, u32[]{:S(2)}) collective-permute-start(bf16[2,144,128]{2,1,0:T(8,128)(2,1)S(1)} %get-tuple-element.34), channel_id=1, source_target_pairs={{0,256},{8,264},{16,272},{24,280},{32,288},{40,296},{48,304},{56,3... | collective-permute-start | bytes 221192 | tf_op jit(solution)/shard_map/ppermute | solution.py:251
  110.4 11.2 %collective-permute-start.12 = (bf16[2,144,128]{2,1,0:T(8,128)(2,1)S(1)}, bf16[2,144,128]{2,1,0:T(8,128)(2,1)S(1)}, u32[]{:S(2)}, u32[]{:S(2)}) collective-permute-start(bf16[2,144,128]{2,1,0:T(8,128)(2,1)S(1)} %get-tuple-element.34), channel_id=1, source_target_pairs={{0,320},{8,328},{16,336},{24,344},{32,352},{40,360},{48,368},{56,3... | collective-permute-start | bytes 221192 | tf_op jit(solution)/shard_map/ppermute | solution.py:251
  111.7 9.9 %collective-permute-start.13 = (bf16[2,144,128]{2,1,0:T(8,128)(2,1)S(1)}, bf16[2,144,128]{2,1,0:T(8,128)(2,1)S(1)}, u32[]{:S(2)}, u32[]{:S(2)}) collective-permute-start(bf16[2,144,128]{2,1,0:T(8,128)(2,1)S(1)} %get-tuple-element.34), channel_id=1, source_target_pairs={{0,384},{8,392},{16,400},{24,408},{32,416},{40,424},{48,432},{56,4... | collective-permute-start | bytes 221192 | tf_op jit(solution)/shard_map/ppermute | solution.py:251
  113.0 8.6 %collective-permute-start.14 = (bf16[2,144,128]{2,1,0:T(8,128)(2,1)S(1)}, bf16[2,144,128]{2,1,0:T(8,128)(2,1)S(1)}, u32[]{:S(2)}, u32[]{:S(2)}) collective-permute-start(bf16[2,144,128]{2,1,0:T(8,128)(2,1)S(1)} %get-tuple-element.34), channel_id=1, source_target_pairs={{0,192},{8,200},{16,208},{24,216},{32,224},{40,232},{48,240},{56,2... | collective-permute-start | bytes 221192 | tf_op jit(solution)/shard_map/ppermute | solution.py:251
  114.4 7.3 %collective-permute-start.15 = (bf16[2,144,128]{2,1,0:T(8,128)(2,1)S(1)}, bf16[2,144,128]{2,1,0:T(8,128)(2,1)S(1)}, u32[]{:S(2)}, u32[]{:S(2)}) collective-permute-start(bf16[2,144,128]{2,1,0:T(8,128)(2,1)S(1)} %get-tuple-element.34), channel_id=1, source_target_pairs={{0,448},{8,456},{16,464},{24,472},{32,480},{40,488},{48,496},{56,5... | collective-permute-start | bytes 221192 | tf_op jit(solution)/shard_map/ppermute | solution.py:251
Sparse Core Ops, SparseCore 0:
  9.5 56.3 all-gather.2
  67.9 39.8 all-gather.4

commit v14 on v13

--- a/solution.py
+++ b/solution.py
@@ -14,7 +14,7 @@
 NZ = 8
 NH = 8
 EXTRA = 16
-START_ORDER = (1, 2, 4, 5, 6, 3, 7)
+START_ORDER = (1, 2, 7, 6, 5, 4, 3)
 F32 = jnp.float32
 BF16 = jnp.bfloat16
 VMEM = pltpu.VMEM

time: 154 us -> 156 us (1.013); the launches traced: 154 us -> 154 us
  no operation moved by 1% of the time
where the time goes in v14:
time: 156 us; the launch traced here: 154 us
  starting transfers between devices  50.8 us (33%)
  blocking collectives  49.7 us (32%)
  waiting for transfers between devices  15.5 us (10%)
  between operations  14 us (9%)
  matrix products  13.4 us (9%)
  Pallas kernels  7.08 us (5%)
  local copies, waits for them, and re-layouts  2.25 us (1%)
    all_to_all x1, blocking collectives, on_device(): lax.all_to_all(pieces, 'seq', split_axis=0, concat_axis=0, tiled=True, ax...  28 us
    all_to_all x1, blocking collectives, on_device(): lax.all_to_all(flat.reshape(16, 64, 256), ('seq', 'head'), split_axis=0,...  21.7 us
    ppermute x7, starting transfers between devices, on_device(): lax.ppermute(row_message, 'seq', y_later(k))  16.2 us
    all_to_all x1, waiting for transfers between devices, on_device(): lax.all_to_all(messages, 'seq', split_axis=0, concat_axis=0, tiled=True,...  9.69 us
    ppermute x2, starting transfers between devices, hop(): downs.append(lax.ppermute(after(downs[-1], *earlier), 'seq', y_shift(-1)))  8.62 us
    dot_general x8, matrix products, add(): d = jnp.dot(x, part.reshape(NZ * 48, 512), preferred_element_type=F32)  8.41 us
    pallas_call x6, Pallas kernels, call(): pl.pallas_call(kernel, out_shape=shapes, in_specs=smem + whole(len(args))...  7.08 us
    all_to_all x1, starting transfers between devices, on_device(): lax.all_to_all(messages, 'seq', split_axis=0, concat_axis=0, tiled=True,...  5.45 us
  transfers between devices with their start and end apart: 19, of which 4 were waited for; matrix products, arithmetic and copies ran while one was open for 10% of the time, Pallas kernels for 2%

profile of v14, /device:TPU:1, one launch (start us, length us, event | category | flops | bytes accessed | tf_op | source)
XLA Modules:
  0.0 153.7 jit_solution(7091112196242223288)
XLA Ops:
  6.5 0.7 all-gather.3.cloned.1.call-update
  7.3 0.0 all-gather.5.cloned.1.call-start
  7.3 0.9 copy-done
  8.3 28.0 %all_to_all.15 = bf16[8,48,768]{2,1,0:T(8,128)(2,1)S(1)} all-to-all(bf16[8,48,768]{2,1,0:T(8,128)(2,1)S(1)} %shard_map.46), channel_id=1, replica_groups={{0,8,16,24,32,40,48,56},{64,72,80,88,96,104,112,120},{128,136,144,152,1..., dimensions={0} | all-to-all | bytes 1179648 | tf_op jit(solution)/shard_map/all_to_all | solution.py:189
  36.3 3.2 %collective-permute-start = (bf16[8,48,512]{2,1,0:T(8,128)(2,1)S(1)}, bf16[8,48,512]{2,1,0:T(8,128)(2,1)S(1)}, u32[]{:S(2)}, u32[]{:S(2)}) collective-permute-start(bf16[8,48,512]{2,1,0:T(8,128)(2,1)S(1)} %slice.20), channel_id=1, source_target_pairs={{0,64},{8,72},{16,80},{24,88},{32,96},{40,104},{48,112},{56,120},{... | collective-permute-start | bytes 1179656 | tf_op jit(solution)/shard_map/ppermute | solution.py:204
  39.5 4.0 %collective-permute-start.5 = (bf16[8,48,512]{2,1,0:T(8,128)(2,1)S(1)}, bf16[8,48,512]{2,1,0:T(8,128)(2,1)S(1)}, u32[]{:S(2)}, u32[]{:S(2)}) collective-permute-start(bf16[8,48,512]{2,1,0:T(8,128)(2,1)S(1)} %slice.20), channel_id=1, source_target_pairs={{0,448},{8,456},{16,464},{24,472},{32,480},{40,488},{48,496},{56,5... | collective-permute-start | bytes 1179656 | tf_op jit(solution)/shard_map/ppermute | solution.py:205
  43.6 1.9 %collective-permute-start.2 = (f32[2,512]{1,0:T(2,128)S(1)}, f32[2,512]{1,0:T(2,128)S(1)}, u32[]{:S(2)}, u32[]{:S(2)}) collective-permute-start(f32[2,512]{1,0:T(2,128)S(1)} %get-tuple-element.24), channel_id=1, source_target_pairs={{0,8},{8,0},{16,24},{24,16},{32,40},{40,32},{48,56},{56,48},{64,72... | collective-permute-start | bytes 12296 | tf_op jit(solution)/shard_map/ppermute | solution.py:213
  45.5 1.2 collective-permute-done
  46.8 1.9 %collective-permute-start.1 = (bf16[8,48,512]{2,1,0:T(8,128)(2,1)S(1)}, bf16[8,48,512]{2,1,0:T(8,128)(2,1)S(1)}, u32[]{:S(2)}, u32[]{:S(2)}) collective-permute-start(bf16[8,48,512]{2,1,0:T(8,128)(2,1)S(1)} %collective-permute-done), channel_id=1, source_target_pairs={{0,64},{8,72},{16,80},{24,88},{32,96},{40,104},{48,112},{56,120},{... | collective-permute-start | bytes 1179656 | tf_op jit(solution)/shard_map/ppermute | solution.py:214
  48.7 4.6 %collective-permute-start.6 = (bf16[8,48,512]{2,1,0:T(8,128)(2,1)S(1)}, bf16[8,48,512]{2,1,0:T(8,128)(2,1)S(1)}, u32[]{:S(2)}, u32[]{:S(2)}) collective-permute-start(bf16[8,48,512]{2,1,0:T(8,128)(2,1)S(1)} %collective-permute-done.5), channel_id=1, source_target_pairs={{0,448},{8,456},{16,464},{24,472},{32,480},{40,488},{48,496},{56,5... | collective-permute-start | bytes 1179656 | tf_op jit(solution)/shard_map/ppermute | solution.py:215
  53.5 0.1 dynamic_slice.35
  53.6 0.7 slice.22
  54.3 0.6 reduce_window_sum.24
  54.9 0.2 slice_reduce_fusion
  55.1 0.2 reduce_window_sum.25
  55.3 0.1 squeeze.6
  55.3 0.1 copy.11
  55.4 0.1 reduce_window_sum.26
  55.5 1.0 collective-permute-done.1
  56.5 1.9 %collective-permute-start.3 = (bf16[8,48,512]{2,1,0:T(8,128)(2,1)S(1)}, bf16[8,48,512]{2,1,0:T(8,128)(2,1)S(1)}, u32[]{:S(2)}, u32[]{:S(2)}) collective-permute-start(bf16[8,48,512]{2,1,0:T(8,128)(2,1)S(1)} %collective-permute-done.1), channel_id=1, source_target_pairs={{0,64},{8,72},{16,80},{24,88},{32,96},{40,104},{48,112},{56,120},{... | collective-permute-start | bytes 1179656 | tf_op jit(solution)/shard_map/ppermute | solution.py:204
  58.4 4.6 %collective-permute-start.7 = (bf16[8,48,512]{2,1,0:T(8,128)(2,1)S(1)}, bf16[8,48,512]{2,1,0:T(8,128)(2,1)S(1)}, u32[]{:S(2)}, u32[]{:S(2)}) collective-permute-start(bf16[8,48,512]{2,1,0:T(8,128)(2,1)S(1)} %collective-permute-done.6), channel_id=1, source_target_pairs={{0,448},{8,456},{16,464},{24,472},{32,480},{40,488},{48,496},{56,5... | collective-permute-start | bytes 1179656 | tf_op jit(solution)/shard_map/ppermute | solution.py:205
  63.0 2.9 %all-gather.3.cloned.1.call-done = bf16[1024,3072]{1,0:T(8,128)(2,1)} async-done(((bf16[64,3072]{1,0:T(8,128)(2,1)}), bf16[1024,3072]{1,0:T(8,128)(2,1)}) %all-gather.3.cloned.1.call-update) | async-done | bytes 6291472 | tf_op jit(solution)/shard_map/all_gather | solution.py:191
  65.9 2.0 %fusion.12 = f32[1024,512]{1,0:T(8,128)S(1)} fusion(bf16[384,512]{1,0:T(8,128)(2,1)S(1)} %bitcast.36, bf16[1024,3072]{1,0:T(8,128)(2,1)} %all-gather.3.cloned.1.call-done, s32[]{:T(128)S(6)} %select_n.102), kind=kOutput, calls=%fused_computation.15 | convolution fusion | flops 402653184 | bytes 3276804 | tf_op jit(solution)/shard_map/dot_general | solution.py:196
  67.9 1.9 %convolution_add_fusion = f32[1024,512]{1,0:T(8,128)S(1)} fusion(f32[1024,512]{1,0:T(8,128)S(1)} %fusion.12, bf16[384,512]{1,0:T(8,128)(2,1)S(1)} %bitcast.43, bf16[1024,3072]{1,0:T(8,128)(2,1)} %all-gather.3.cloned.1.call-done, s32[]{:T(128)S(6)} %select_n.104), kind=kOutput, calls=%fused_computation.1 | convolution fusion | flops 403177472 | bytes 5373956 | tf_op jit(solution)/shard_map/dot_general | solution.py:196
  69.8 3.2 %collective-permute-start.4 = (bf16[4,48,512]{2,1,0:T(8,128)(2,1)S(1)}, bf16[4,48,512]{2,1,0:T(8,128)(2,1)S(1)}, u32[]{:S(2)}, u32[]{:S(2)}) collective-permute-start(bf16[4,48,512]{2,1,0:T(8,128)(2,1)S(1)} %slice.17), channel_id=1, source_target_pairs={{0,64},{8,72},{16,80},{24,88},{32,96},{40,104},{48,112},{56,120},{... | collective-permute-start | bytes 589832 | tf_op jit(solution)/shard_map/ppermute | solution.py:229
  73.1 3.8 %collective-permute-start.8 = (bf16[4,48,512]{2,1,0:T(8,128)(2,1)S(1)}, bf16[4,48,512]{2,1,0:T(8,128)(2,1)S(1)}, u32[]{:S(2)}, u32[]{:S(2)}) collective-permute-start(bf16[4,48,512]{2,1,0:T(8,128)(2,1)S(1)} %slice.18), channel_id=1, source_target_pairs={{0,448},{8,456},{16,464},{24,472},{32,480},{40,488},{48,496},{56,5... | collective-permute-start | bytes 589832 | tf_op jit(solution)/shard_map/ppermute | solution.py:230
  76.9 0.7 fusion.2
  77.6 0.7 fusion.4
  78.3 0.7 fusion.6
  79.0 0.7 fusion.9
  79.7 1.0 add_add_fusion.total_ref
  80.8 0.7 fusion.last_ref
  81.5 2.7 %shard_map.47 = (bf16[2,512,512]{2,1,0:T(8,128)(2,1)S(1)}, bf16[16,128,128]{2,1,0:T(8,128)(2,1)S(1)}, bf16[4,2,144,128]{3,2,1,0:T(8,128)(2,1)}) custom-call(f32[1024,512]{1,0:T(8,128)S(1)} %add_add_fusion.total_ref, f32[1024,512]{1,0:T(8,128)S(1)} %fusion.last_ref, f32[128,16]{1,0:T(8,128)S(1)} %bitcast.28, f32[16,128]{1,0:T(8,128)S(1)} %bitcast.32), custom_call_target="tpu_custom_call" | custom-call | flops 67108864 | bytes 4210688 | tf_op jit(solution)/shard_map/pallas_call | solution.py:171
  84.2 5.4 %all-to-all-start.1 = ((bf16[4,2,144,128]{3,2,1,0:T(8,128)(2,1)}), bf16[4,2,144,128]{3,2,1,0:T(8,128)(2,1)S(1)}, u32[]{:S(2)}, u32[]{:S(2)}) async-start(bf16[4,2,144,128]{3,2,1,0:T(8,128)(2,1)} %get-tuple-element.33), calls=%async_computation.1 | async-start | bytes 589824 | tf_op jit(solution)/shard_map/all_to_all | solution.py:240
  89.6 9.7 %all-to-all-done.1.messages_ref = bf16[4,2,144,128]{3,2,1,0:T(8,128)(2,1)S(1)} async-done(((bf16[4,2,144,128]{3,2,1,0:T(8,128)(2,1)}), bf16[4,2,144,128]{3,2,1,0:T(8,128)(2,1)S(1)}, u32[]{:S(2)}, u32[]{:S(2)}) %all-to-all-start.1) | async-done | bytes 294944 | tf_op jit(solution)/shard_map/all_to_all | solution.py:240
  99.3 0.1 shard_map.48
  99.4 2.0 %collective-permute-start.9 = (bf16[2,144,128]{2,1,0:T(8,128)(2,1)S(1)}, bf16[2,144,128]{2,1,0:T(8,128)(2,1)S(1)}, u32[]{:S(2)}, u32[]{:S(2)}) collective-permute-start(bf16[2,144,128]{2,1,0:T(8,128)(2,1)S(1)} %get-tuple-element.34), channel_id=1, source_target_pairs={{0,64},{8,72},{16,80},{24,88},{32,96},{40,104},{48,112},{56,120},{... | collective-permute-start | bytes 221192 | tf_op jit(solution)/shard_map/ppermute | solution.py:251
  101.5 5.8 %collective-permute-start.10 = (bf16[2,144,128]{2,1,0:T(8,128)(2,1)S(1)}, bf16[2,144,128]{2,1,0:T(8,128)(2,1)S(1)}, u32[]{:S(2)}, u32[]{:S(2)}) collective-permute-start(bf16[2,144,128]{2,1,0:T(8,128)(2,1)S(1)} %get-tuple-element.34), channel_id=1, source_target_pairs={{0,128},{8,136},{16,144},{24,152},{32,160},{40,168},{48,176},{56,1... | collective-permute-start | bytes 221192 | tf_op jit(solution)/shard_map/ppermute | solution.py:251
  107.2 1.3 collective-permute-start.11
  108.5 1.3 collective-permute-start.12
  109.8 1.3 collective-permute-start.13
  111.2 1.5 collective-permute-start.14
  112.7 3.1 %collective-permute-start.15 = (bf16[2,144,128]{2,1,0:T(8,128)(2,1)S(1)}, bf16[2,144,128]{2,1,0:T(8,128)(2,1)S(1)}, u32[]{:S(2)}, u32[]{:S(2)}) collective-permute-start(bf16[2,144,128]{2,1,0:T(8,128)(2,1)S(1)} %get-tuple-element.34), channel_id=1, source_target_pairs={{0,192},{8,200},{16,208},{24,216},{32,224},{40,232},{48,240},{56,2... | collective-permute-start | bytes 221192 | tf_op jit(solution)/shard_map/ppermute | solution.py:251
  115.8 5.0 %convolution_bitcast_fusion.total_ref = f32[1024,256]{1,0:T(8,128)S(1)} fusion(bf16[1024,3072]{1,0:T(8,128)(2,1)} %all-gather.3.cloned.1.call-done, bf16[3072,256]{1,0:T(8,128)(2,1)} %bitcast.44), kind=kOutput, calls=%fused_computation.2 | convolution fusion | flops 1610612736 | bytes 8912896 | tf_op jit(solution)/shard_map/dot_general | solution.py:241
  120.8 0.9 shard_map.49
  121.7 2.5 %shard_map.50 = bf16[1024,256]{1,0:T(8,128)(2,1)S(1)} custom-call(bf16[2,144,128]{2,1,0:T(8,128)(2,1)S(1)} %collective-permute-done.9.refs_0_, bf16[2,144,128]{2,1,0:T(8,128)(2,1)S(1)} %collective-permute-done.10.refs_1_, bf16[2,144,128]{2,1,0:T(8,128)(2,1)S(1)} %collective-permute-done.11.refs_2_, bf16[2,144,128]{2,1,0:T(8,128)(2,1)S(1)} %collective-permute-done.12.refs_3_, ...), custom_call_target="tpu_custom_call" | custom-call | flops 67108864 | bytes 2237504 | tf_op jit(solution)/shard_map/pallas_call | solution.py:171
  124.3 21.7 %all_to_all.16.sent_ref = bf16[16,64,256]{2,1,0:T(8,128)(2,1)S(1)} all-to-all(bf16[16,64,256]{2,1,0:T(8,128)(2,1)S(1)} %bitcast.27), channel_id=1, replica_groups={{0,1,2,3,4,5,6,7,8,9,10,11,12,13,14,15},{16,17,18,19,20,21,22,23,24,25,..., dimensions={0} | all-to-all | bytes 1048576 | tf_op jit(solution)/shard_map/all_to_all | solution.py:256
  146.0 0.8 shard_map.51
  (34 shorter events, 0.3 us)
Async XLA Ops:
  6.5 37.1 %copy-start.2 = (f32[4,512]{1,0:T(4,128)S(1)}, f32[4,512]{1,0:T(4,128)}, u32[]{:S(2)}) copy-start(f32[4,512]{1,0:T(4,128)} %param.6) | copy-start | bytes 24580
  6.5 46.9 %copy-start.3 = (f32[512]{0:T(512)S(1)}, f32[512]{0:T(512)}, u32[]{:S(2)}) copy-start(f32[512]{0:T(512)} %param.7) | copy-start | bytes 6148
  6.5 59.3 %all-gather.3.cloned.1.call-start = ((), (), s32[]{:S(2)}) async-start(), calls=%async_computation.3 | async-start | bytes 6684672 | tf_op jit(solution)/shard_map/all_gather | solution.py:191
  7.3 103.9 %all-gather.5.cloned.1.call-start = ((), (), s32[]{:S(2)}) async-start(), calls=%async_computation.4 | async-start | bytes 1769472 | tf_op jit(solution)/shard_map/all_gather | solution.py:226
  7.3 0.9 copy-start
  36.3 10.5 %collective-permute-start = (bf16[8,48,512]{2,1,0:T(8,128)(2,1)S(1)}, bf16[8,48,512]{2,1,0:T(8,128)(2,1)S(1)}, u32[]{:S(2)}, u32[]{:S(2)}) collective-permute-start(bf16[8,48,512]{2,1,0:T(8,128)(2,1)S(1)} %slice.20), channel_id=1, source_target_pairs={{0,64},{8,72},{16,80},{24,88},{32,96},{40,104},{48,112},{56,120},{... | collective-permute-start | bytes 1179656 | tf_op jit(solution)/shard_map/ppermute | solution.py:204
  39.5 9.2 %collective-permute-start.5 = (bf16[8,48,512]{2,1,0:T(8,128)(2,1)S(1)}, bf16[8,48,512]{2,1,0:T(8,128)(2,1)S(1)}, u32[]{:S(2)}, u32[]{:S(2)}) collective-permute-start(bf16[8,48,512]{2,1,0:T(8,128)(2,1)S(1)} %slice.20), channel_id=1, source_target_pairs={{0,448},{8,456},{16,464},{24,472},{32,480},{40,488},{48,496},{56,5... | collective-permute-start | bytes 1179656 | tf_op jit(solution)/shard_map/ppermute | solution.py:205
  43.6 5.1 %collective-permute-start.2 = (f32[2,512]{1,0:T(2,128)S(1)}, f32[2,512]{1,0:T(2,128)S(1)}, u32[]{:S(2)}, u32[]{:S(2)}) collective-permute-start(f32[2,512]{1,0:T(2,128)S(1)} %get-tuple-element.24), channel_id=1, source_target_pairs={{0,8},{8,0},{16,24},{24,16},{32,40},{40,32},{48,56},{56,48},{64,72... | collective-permute-start | bytes 12296 | tf_op jit(solution)/shard_map/ppermute | solution.py:213
  46.8 9.7 %collective-permute-start.1 = (bf16[8,48,512]{2,1,0:T(8,128)(2,1)S(1)}, bf16[8,48,512]{2,1,0:T(8,128)(2,1)S(1)}, u32[]{:S(2)}, u32[]{:S(2)}) collective-permute-start(bf16[8,48,512]{2,1,0:T(8,128)(2,1)S(1)} %collective-permute-done), channel_id=1, source_target_pairs={{0,64},{8,72},{16,80},{24,88},{32,96},{40,104},{48,112},{56,120},{... | collective-permute-start | bytes 1179656 | tf_op jit(solution)/shard_map/ppermute | solution.py:214
  48.7 9.7 %collective-permute-start.6 = (bf16[8,48,512]{2,1,0:T(8,128)(2,1)S(1)}, bf16[8,48,512]{2,1,0:T(8,128)(2,1)S(1)}, u32[]{:S(2)}, u32[]{:S(2)}) collective-permute-start(bf16[8,48,512]{2,1,0:T(8,128)(2,1)S(1)} %collective-permute-done.5), channel_id=1, source_target_pairs={{0,448},{8,456},{16,464},{24,472},{32,480},{40,488},{48,496},{56,5... | collective-permute-start | bytes 1179656 | tf_op jit(solution)/shard_map/ppermute | solution.py:215
  56.5 13.3 %collective-permute-start.3 = (bf16[8,48,512]{2,1,0:T(8,128)(2,1)S(1)}, bf16[8,48,512]{2,1,0:T(8,128)(2,1)S(1)}, u32[]{:S(2)}, u32[]{:S(2)}) collective-permute-start(bf16[8,48,512]{2,1,0:T(8,128)(2,1)S(1)} %collective-permute-done.1), channel_id=1, source_target_pairs={{0,64},{8,72},{16,80},{24,88},{32,96},{40,104},{48,112},{56,120},{... | collective-permute-start | bytes 1179656 | tf_op jit(solution)/shard_map/ppermute | solution.py:204
  58.4 14.6 %collective-permute-start.7 = (bf16[8,48,512]{2,1,0:T(8,128)(2,1)S(1)}, bf16[8,48,512]{2,1,0:T(8,128)(2,1)S(1)}, u32[]{:S(2)}, u32[]{:S(2)}) collective-permute-start(bf16[8,48,512]{2,1,0:T(8,128)(2,1)S(1)} %collective-permute-done.6), channel_id=1, source_target_pairs={{0,448},{8,456},{16,464},{24,472},{32,480},{40,488},{48,496},{56,5... | collective-permute-start | bytes 1179656 | tf_op jit(solution)/shard_map/ppermute | solution.py:205
  65.9 11.0 %copy-start.1 = (bf16[1024,3072]{1,0:T(8,128)(2,1)S(1)}, bf16[1024,3072]{1,0:T(8,128)(2,1)}, u32[]{:S(2)}) copy-start(bf16[1024,3072]{1,0:T(8,128)(2,1)} %all-gather.3.cloned.1.call-done) | copy-start | bytes 18874372
  69.8 10.9 %collective-permute-start.4 = (bf16[4,48,512]{2,1,0:T(8,128)(2,1)S(1)}, bf16[4,48,512]{2,1,0:T(8,128)(2,1)S(1)}, u32[]{:S(2)}, u32[]{:S(2)}) collective-permute-start(bf16[4,48,512]{2,1,0:T(8,128)(2,1)S(1)} %slice.17), channel_id=1, source_target_pairs={{0,64},{8,72},{16,80},{24,88},{32,96},{40,104},{48,112},{56,120},{... | collective-permute-start | bytes 589832 | tf_op jit(solution)/shard_map/ppermute | solution.py:229
  73.1 7.7 %collective-permute-start.8 = (bf16[4,48,512]{2,1,0:T(8,128)(2,1)S(1)}, bf16[4,48,512]{2,1,0:T(8,128)(2,1)S(1)}, u32[]{:S(2)}, u32[]{:S(2)}) collective-permute-start(bf16[4,48,512]{2,1,0:T(8,128)(2,1)S(1)} %slice.18), channel_id=1, source_target_pairs={{0,448},{8,456},{16,464},{24,472},{32,480},{40,488},{48,496},{56,5... | collective-permute-start | bytes 589832 | tf_op jit(solution)/shard_map/ppermute | solution.py:230
  84.2 15.1 %all-to-all-start.1 = ((bf16[4,2,144,128]{3,2,1,0:T(8,128)(2,1)}), bf16[4,2,144,128]{3,2,1,0:T(8,128)(2,1)S(1)}, u32[]{:S(2)}, u32[]{:S(2)}) async-start(bf16[4,2,144,128]{3,2,1,0:T(8,128)(2,1)} %get-tuple-element.33), calls=%async_computation.1 | async-start | bytes 589824 | tf_op jit(solution)/shard_map/all_to_all | solution.py:240
  99.4 11.7 %collective-permute-start.9 = (bf16[2,144,128]{2,1,0:T(8,128)(2,1)S(1)}, bf16[2,144,128]{2,1,0:T(8,128)(2,1)S(1)}, u32[]{:S(2)}, u32[]{:S(2)}) collective-permute-start(bf16[2,144,128]{2,1,0:T(8,128)(2,1)S(1)} %get-tuple-element.34), channel_id=1, source_target_pairs={{0,64},{8,72},{16,80},{24,88},{32,96},{40,104},{48,112},{56,120},{... | collective-permute-start | bytes 221192 | tf_op jit(solution)/shard_map/ppermute | solution.py:251
  101.5 11.2 %collective-permute-start.10 = (bf16[2,144,128]{2,1,0:T(8,128)(2,1)S(1)}, bf16[2,144,128]{2,1,0:T(8,128)(2,1)S(1)}, u32[]{:S(2)}, u32[]{:S(2)}) collective-permute-start(bf16[2,144,128]{2,1,0:T(8,128)(2,1)S(1)} %get-tuple-element.34), channel_id=1, source_target_pairs={{0,128},{8,136},{16,144},{24,152},{32,160},{40,168},{48,176},{56,1... | collective-permute-start | bytes 221192 | tf_op jit(solution)/shard_map/ppermute | solution.py:251
  107.2 14.4 %collective-permute-start.11 = (bf16[2,144,128]{2,1,0:T(8,128)(2,1)S(1)}, bf16[2,144,128]{2,1,0:T(8,128)(2,1)S(1)}, u32[]{:S(2)}, u32[]{:S(2)}) collective-permute-start(bf16[2,144,128]{2,1,0:T(8,128)(2,1)S(1)} %get-tuple-element.34), channel_id=1, source_target_pairs={{0,448},{8,456},{16,464},{24,472},{32,480},{40,488},{48,496},{56,5... | collective-permute-start | bytes 221192 | tf_op jit(solution)/shard_map/ppermute | solution.py:251
  108.5 13.1 %collective-permute-start.12 = (bf16[2,144,128]{2,1,0:T(8,128)(2,1)S(1)}, bf16[2,144,128]{2,1,0:T(8,128)(2,1)S(1)}, u32[]{:S(2)}, u32[]{:S(2)}) collective-permute-start(bf16[2,144,128]{2,1,0:T(8,128)(2,1)S(1)} %get-tuple-element.34), channel_id=1, source_target_pairs={{0,384},{8,392},{16,400},{24,408},{32,416},{40,424},{48,432},{56,4... | collective-permute-start | bytes 221192 | tf_op jit(solution)/shard_map/ppermute | solution.py:251
  109.8 11.9 %collective-permute-start.13 = (bf16[2,144,128]{2,1,0:T(8,128)(2,1)S(1)}, bf16[2,144,128]{2,1,0:T(8,128)(2,1)S(1)}, u32[]{:S(2)}, u32[]{:S(2)}) collective-permute-start(bf16[2,144,128]{2,1,0:T(8,128)(2,1)S(1)} %get-tuple-element.34), channel_id=1, source_target_pairs={{0,320},{8,328},{16,336},{24,344},{32,352},{40,360},{48,368},{56,3... | collective-permute-start | bytes 221192 | tf_op jit(solution)/shard_map/ppermute | solution.py:251
  111.2 10.5 %collective-permute-start.14 = (bf16[2,144,128]{2,1,0:T(8,128)(2,1)S(1)}, bf16[2,144,128]{2,1,0:T(8,128)(2,1)S(1)}, u32[]{:S(2)}, u32[]{:S(2)}) collective-permute-start(bf16[2,144,128]{2,1,0:T(8,128)(2,1)S(1)} %get-tuple-element.34), channel_id=1, source_target_pairs={{0,256},{8,264},{16,272},{24,280},{32,288},{40,296},{48,304},{56,3... | collective-permute-start | bytes 221192 | tf_op jit(solution)/shard_map/ppermute | solution.py:251
  112.7 9.0 %collective-permute-start.15 = (bf16[2,144,128]{2,1,0:T(8,128)(2,1)S(1)}, bf16[2,144,128]{2,1,0:T(8,128)(2,1)S(1)}, u32[]{:S(2)}, u32[]{:S(2)}) collective-permute-start(bf16[2,144,128]{2,1,0:T(8,128)(2,1)S(1)} %get-tuple-element.34), channel_id=1, source_target_pairs={{0,192},{8,200},{16,208},{24,216},{32,224},{40,232},{48,240},{56,2... | collective-permute-start | bytes 221192 | tf_op jit(solution)/shard_map/ppermute | solution.py:251
Sparse Core Ops, SparseCore 0:
  9.5 56.3 all-gather.2
  67.9 39.8 all-gather.4
